TPU v7x, 32 devices: a whole 2x2x4 slice. The times are simulated.
32 devices in a mesh: groups: 2 (over x), tiles: 16 (over z, y, core).
Axes of the slice: x: 2, y: 2, z: 4, core: 2. Of those that a mesh axis runs over, the one named last changes fastest.
Arguments:
- video_q: bfloat16 [8192, 3072], P(('groups', 'tiles')), parts along dimension 0, may hold values from -88 to 88, as said below
- video_k: bfloat16 [8192, 3072], P(('groups', 'tiles')), parts along dimension 0, may hold values from -4 to 4, as said below
- video_v: bfloat16 [8192, 3072], P(('groups', 'tiles')), parts along dimension 0, may hold values from -5 to 5
- text_q: bfloat16 [512, 3072], P('groups'), parts along dimension 0, may hold values from -88 to 88
- text_k: bfloat16 [512, 3072], P('groups'), parts along dimension 0, may hold values from -5 to 5
- text_v: bfloat16 [512, 3072], P('groups'), parts along dimension 0, may hold values from -5 to 5
- window: int32 [32, 6], P('tiles'), may hold values from 0 to 13, as said below
- counts: int32 [64], P(('groups', 'tiles')), parts along dimension 0, may hold values from 1 to 128, as said below
- text_count: int32 [2], P('groups'), parts along dimension 0, may hold values from 64 to 256
Outputs:
- video_out: bfloat16 [8192, 3072], P(('groups', 'tiles')), parts along dimension 0
- text_out: bfloat16 [512, 3072], P(('groups', 'tiles')), parts along dimension 0
There are 2 independent parts, one for each index of `groups`. A program takes and returns all parts, laid end to end along the dimension named above; an argument that names none is the same for every part. Nothing has to cross between parts.
Inputs may be any that keep to these rules, and one draw needn't show every extreme that they name: `video_q`: queries drawn for the problem. `video_k`: keys drawn for the problem. `window`: each row names 6 different codes, among them always 3, 6, 9 and 12. `counts`: valid tokens are the first slots of a tile.
All inputs are finite; a program needn't handle non-finite values.
Results may differ from a plain program's by a relative error of at most 0.003.
Values may be sent and summed in bfloat16 or wider, within the bound.
No kernel may reach another device: no remote copies, remote signals or barrier semaphores. Data moves between devices by JAX's collectives and lax.ppermute only.
A program may use at most 192 MiB of HBM per device.

v0:
```python
import math

import jax
import jax.numpy as jnp
from jax import lax
from jax.sharding import PartitionSpec as P

HEADS = 24
HD = 128
NR = 4
TEXT = 256


def passed_along(x, axis, by):
    length = lax.axis_size(axis)
    return lax.ppermute(x, axis, [(i, (i + by) % length) for i in range(length)])


def per_device(video_q, video_k, video_v, text_q, text_k, text_v, window, counts, text_count):
    columns = counts.shape[0]
    tok_tile = video_q.shape[0] // columns
    model_width = video_q.shape[1]
    score_scale = 1.0 / math.sqrt(HD)
    group_size = lax.axis_size("tiles")
    position = lax.axis_index("tiles")
    spot = (position + group_size // 2 + NR + NR // 2) % group_size
    row_pos = spot % NR
    time_pos = spot // NR
    last_time = group_size // NR - 1
    keys_own = video_k.reshape(columns, tok_tile, model_width)
    values_own = video_v.reshape(columns, tok_tile, model_width)
    earlier_side = passed_along((keys_own, values_own, counts), "tiles", NR)
    later_side = passed_along((keys_own, values_own, counts), "tiles", -NR)
    above_side = passed_along((keys_own, values_own, counts), "tiles", 1)
    below_side = passed_along((keys_own, values_own, counts), "tiles", -1)
    earlier_count = jnp.where(time_pos == 0, 0, earlier_side[2])
    later_count = jnp.where(time_pos == last_time, 0, later_side[2])
    above_count = jnp.where(row_pos == 0, 0, above_side[2])
    below_count = jnp.where(row_pos == NR - 1, 0, below_side[2])
    column_pad = ((0, 0), (1, 1), (0, 0), (0, 0))
    key_flat = jnp.pad(
        jnp.stack([keys_own, earlier_side[0], later_side[0], above_side[0], below_side[0]]),
        column_pad,
    )
    key_flat = key_flat.reshape(5 * (columns + 2), tok_tile, model_width)
    value_flat = jnp.pad(
        jnp.stack([values_own, earlier_side[1], later_side[1], above_side[1], below_side[1]]),
        column_pad,
    )
    value_flat = value_flat.reshape(5 * (columns + 2), tok_tile, model_width)
    count_flat = jnp.pad(
        jnp.stack([counts, earlier_count, later_count, above_count, below_count]), ((0, 0), (1, 1))
    ).reshape(-1)
    cell_codes = jnp.concatenate(
        [jnp.ones((columns, 1), jnp.int32), window + (window >= 1)], axis=1
    )
    flat_index = (
        cell_codes // 3 * (columns + 2)
        + jnp.arange(columns, dtype=jnp.int32)[:, None]
        + cell_codes % 3
    )
    slot_ids = jnp.arange(tok_tile, dtype=jnp.int32)
    text_valid = jnp.arange(TEXT, dtype=jnp.int32) < text_count[0]
    text_keys = text_k.reshape(TEXT, HEADS, HD)
    text_values = text_v.reshape(TEXT, HEADS, HD)
    query_tiles = video_q.reshape(columns, tok_tile, HEADS, HD)

    def one_tile(tile_items):
        q_tile, flat_row, q_count = tile_items
        keys_chosen = key_flat[flat_row].reshape(-1, HEADS, HD)
        values_chosen = value_flat[flat_row].reshape(-1, HEADS, HD)
        key_valid = (slot_ids[None, :] < count_flat[flat_row][:, None]).reshape(-1)
        video_scores = (
            jnp.einsum("qhd,khd->hqk", q_tile, keys_chosen, preferred_element_type=jnp.float32)
            * score_scale
        )
        video_scores = jnp.where(key_valid[None, None, :], video_scores, -jnp.inf)
        text_scores = (
            jnp.einsum("qhd,khd->hqk", q_tile, text_keys, preferred_element_type=jnp.float32)
            * score_scale
        )
        text_scores = jnp.where(text_valid[None, None, :], text_scores, -jnp.inf)
        row_top = jnp.maximum(jnp.max(video_scores, axis=-1), jnp.max(text_scores, axis=-1))[
            ..., None
        ]
        video_probs = jnp.exp(video_scores - row_top)
        text_probs = jnp.exp(text_scores - row_top)
        denom = jnp.sum(video_probs, axis=-1) + jnp.sum(text_probs, axis=-1)
        numer = jnp.einsum(
            "hqk,khd->qhd",
            video_probs.astype(jnp.bfloat16),
            values_chosen,
            preferred_element_type=jnp.float32,
        )
        numer = numer + jnp.einsum(
            "hqk,khd->qhd",
            text_probs.astype(jnp.bfloat16),
            text_values,
            preferred_element_type=jnp.float32,
        )
        result = numer / denom.T[:, :, None]
        query_valid = slot_ids < q_count
        return jnp.where(query_valid[:, None, None], result, 0.0).astype(jnp.bfloat16)

    video_out = lax.map(one_tile, (query_tiles, flat_index, counts)).reshape(
        columns * tok_tile, model_width
    )
    key_heads = video_k.reshape(columns * tok_tile, HEADS, HD)
    value_heads = video_v.reshape(columns * tok_tile, HEADS, HD)
    local_valid = (slot_ids[None, :] < counts[:, None]).reshape(-1)
    text_queries = text_q.reshape(TEXT, HEADS, HD)
    global_scores = (
        jnp.einsum("qhd,khd->hqk", text_queries, key_heads, preferred_element_type=jnp.float32)
        * score_scale
    )
    global_scores = jnp.where(local_valid[None, None, :], global_scores, -jnp.inf)
    local_top = jnp.max(global_scores, axis=-1)
    global_top = lax.pmax(local_top, "tiles")
    weights = jnp.exp(global_scores - global_top[..., None])
    denom_part = jnp.sum(weights, axis=-1).T
    numer_part = jnp.einsum(
        "hqk,khd->qhd",
        weights.astype(jnp.bfloat16),
        value_heads,
        preferred_element_type=jnp.float32,
    )
    numer_part = numer_part.reshape(TEXT, model_width)
    share_rows = TEXT // group_size
    numer_rows, denom_rows = (
        lax.psum_scatter(numer_part, "tiles", scatter_dimension=0, tiled=True),
        lax.psum_scatter(denom_part, "tiles", scatter_dimension=0, tiled=True),
    )
    text_result = numer_rows.reshape(share_rows, HEADS, HD) / denom_rows[:, :, None]
    row_ids = position * share_rows + jnp.arange(share_rows, dtype=jnp.int32)
    text_out = jnp.where((row_ids < text_count[0])[:, None, None], text_result, 0.0)
    text_out = text_out.astype(jnp.bfloat16).reshape(share_rows, model_width)
    return (video_out, text_out)


def solution(mesh):
    return jax.shard_map(
        per_device,
        mesh=mesh,
        in_specs=(
            P(("groups", "tiles"), None),
            P(("groups", "tiles"), None),
            P(("groups", "tiles"), None),
            P("groups", None),
            P("groups", None),
            P("groups", None),
            P("tiles", None),
            P(("groups", "tiles")),
            P("groups"),
        ),
        out_specs=(P(("groups", "tiles"), None), P(("groups", "tiles"), None)),
        check_vma=False,
    )
```

profile of v0, /device:TPU:24, one launch (start us, length us, event | category | flops | bytes accessed | tf_op | source)
XLA Modules:
  0.0 403.7 jit_solution(15297029560444386600)
XLA Ops:
  7.3 2.6 collective-permute-start.7
  9.9 1.6 collective-permute-start.4
  12.0 3.4 collective-permute-start.8
  16.1 5.2 %fusion.45 = (f32[24,256]{1,0:T(8,128)S(1)}, f32[24,256,256]{1,2,0:T(8,128)}) fusion(pred[256]{0:T(512)(128)(4,1)S(1)} %compare_bitcast_fusion, bf16[256,3072]{1,0:T(8,128)(2,1)} %param.12, bf16[256,3072]{1,0:T(8,128)(2,1)S(1)} %copy-done), kind=kOutput, calls=%fused_computation.53 | convolution fusion | flops 407365632 | bytes 9462016 | tf_op jit(solution)/shard_map/qhd,khd->hqk/dot_general | solution.py:113
  21.3 70.7 %pmax.7 = f32[24,256]{1,0:T(8,128)S(1)} all-reduce(f32[24,256]{1,0:T(8,128)S(1)} %get-tuple-element.181), channel_id=1, replica_groups=mesh['groups'=2,'tiles'=16] {'tiles'}, use_global_device_ids=true, to_apply=%region_7.8 | all-reduce | flops 6144 | bytes 49152 | tf_op jit(solution)/shard_map/pmax | solution.py:118
  91.9 4.1 %fusion.46 = f32[24,256]{1,0:T(8,128)S(1)} fusion(f32[24,256,256]{1,2,0:T(8,128)} %get-tuple-element.182, f32[24,256]{1,0:T(8,128)S(1)} %pmax.7, pred[256]{0:T(512)(128)(4,1)S(1)} %compare_bitcast_fusion), kind=kLoop, calls=%fused_computation.54 | loop fusion | flops 6285312 | bytes 6340864 | tf_op jit(solution)/shard_map/reduce_sum | solution.py:120
  96.9 1.7 copy.78
  98.6 6.1 %fusion.48 = f32[24,256,128]{1,2,0:T(8,128)} fusion(bf16[256,24,128]{0,2,1:T(8,128)(2,1)S(1)} %bitcast.162, f32[24,256,256]{1,2,0:T(8,128)} %get-tuple-element.182, f32[24,256]{1,0:T(8,128)S(1)} %pmax.7, pred[256]{0:T(512)(128)(4,1)S(1)} %compare_bitcast_fusion), kind=kOutput, calls=%fused_computation.56 | convolution fusion | flops 408944640 | bytes 11034880 | tf_op jit(solution)/shard_map/hqk,khd->qhd/dot_general | solution.py:121
  104.7 3.5 copy.74
  111.2 1.7 copy.65
  113.0 1.6 copy.68
  114.5 2.9 copy.91
  118.7 2.6 constant_dynamic-update-slice_fusion.2
  121.4 2.7 constant_dynamic-update-slice_fusion.1
  124.1 1.7 collective-permute-start.10
  126.8 11.8 %collective-permute-start = (bf16[2,128,3072]{2,1,0:T(8,128)(2,1)}, bf16[2,128,3072]{2,1,0:T(8,128)(2,1)}, u32[]{:S(2)}, u32[]{:S(2)}) collective-permute-start(bf16[2,128,3072]{2,1,0:T(8,128)(2,1)} %bitcast.1), channel_id=1, source_target_pairs={{0,4},{1,5},{2,6},{3,7},{4,8},{5,9},{6,10},{7,11},{8,12},{9,13},{1... | collective-permute-start | bytes 4718600 | tf_op jit(solution)/shard_map/ppermute | solution.py:16
  139.3 2.7 bitcast_dynamic-update-slice_fusion.3
  142.0 28.0 %collective-permute-done.9 = bf16[2,128,3072]{2,1,0:T(8,128)(2,1)} collective-permute-done((bf16[2,128,3072]{2,1,0:T(8,128)(2,1)}, bf16[2,128,3072]{2,1,0:T(8,128)(2,1)}, u32[]{:S(2)}, u32[]{:S(2)}) %collective-permute-start.9) | collective-permute-done | bytes 1572896 | tf_op jit(solution)/shard_map/ppermute | solution.py:16
  170.0 2.8 bitcast_dynamic-update-slice_fusion.2
  172.8 18.8 %collective-permute-done.10 = bf16[2,128,3072]{2,1,0:T(8,128)(2,1)} collective-permute-done((bf16[2,128,3072]{2,1,0:T(8,128)(2,1)}, bf16[2,128,3072]{2,1,0:T(8,128)(2,1)}, u32[]{:S(2)}, u32[]{:S(2)}) %collective-permute-start.10) | collective-permute-done | bytes 1572896 | tf_op jit(solution)/shard_map/ppermute | solution.py:16
  191.6 2.7 bitcast_dynamic-update-slice_fusion.1
  194.3 2.7 bitcast_dynamic-update-slice_fusion
  197.0 35.8 %collective-permute-done = bf16[2,128,3072]{2,1,0:T(8,128)(2,1)} collective-permute-done((bf16[2,128,3072]{2,1,0:T(8,128)(2,1)}, bf16[2,128,3072]{2,1,0:T(8,128)(2,1)}, u32[]{:S(2)}, u32[]{:S(2)}) %collective-permute-start) | collective-permute-done | bytes 1572896 | tf_op jit(solution)/shard_map/ppermute | solution.py:16
  232.8 1.6 bitcast_dynamic-update-slice_fusion.7
  234.3 9.1 %pad.14 = bf16[5,4,128,3072]{3,2,1,0:T(8,128)(2,1)} pad(bf16[5,2,128,3072]{3,2,1,0:T(8,128)(2,1)} %bitcast_dynamic-update-slice_fusion, bf16[]{:T(256)} %constant.82.clone.1), padding=0_0x1_1x0_0x0_0 | pad | bytes 23592962 | tf_op jit(solution)/shard_map/jit(_pad)/pad | solution.py:41
  243.5 12.5 %collective-permute-done.1 = bf16[2,128,3072]{2,1,0:T(8,128)(2,1)S(1)} collective-permute-done((bf16[2,128,3072]{2,1,0:T(8,128)(2,1)}, bf16[2,128,3072]{2,1,0:T(8,128)(2,1)S(1)}, u32[]{:S(2)}, u32[]{:S(2)}) %collective-permute-start.1) | collective-permute-done | bytes 1572896 | tf_op jit(solution)/shard_map/ppermute | solution.py:16
  256.0 20.6 %collective-permute-done.2 = bf16[2,128,3072]{2,1,0:T(8,128)(2,1)S(1)} collective-permute-done((bf16[2,128,3072]{2,1,0:T(8,128)(2,1)}, bf16[2,128,3072]{2,1,0:T(8,128)(2,1)S(1)}, u32[]{:S(2)}, u32[]{:S(2)}) %collective-permute-start.2) | collective-permute-done | bytes 1572896 | tf_op jit(solution)/shard_map/ppermute | solution.py:16
  276.9 5.8 %pad.12 = bf16[5,4,128,3072]{3,2,1,0:T(8,128)(2,1)} pad(bf16[5,2,128,3072]{3,2,1,0:T(8,128)(2,1)S(1)} %bitcast_dynamic-update-slice_fusion.4, bf16[]{:T(256)} %constant.82.clone.1), padding=0_0x1_1x0_0x0_0 | pad | bytes 23592962 | tf_op jit(solution)/shard_map/jit(_pad)/pad | solution.py:46
  282.6 108.8 %while.12 = (s32[]{:T(128)}, bf16[2,128,24,128]{3,2,1,0:T(8,128)(2,1)}, s32[2]{0:T(128)S(1)}, s32[2,7]{1,0:T(2,128)S(1)}, bf16[20,128,3072]{2,1,0:T(8,128)(2,1)}...) while((s32[]{:T(128)}, ...), condition=%wide.region_5.6_spmd.clone.clone, body=%wide.region_0.5_spmd.clone.clone.sunk | while | flops 1852436736 | bytes 173995776 | solution.py:105
  283.4 9.0 %gather_fusion.1 = bf16[7,128,3072]{2,1,0:T(8,128)(2,1)} fusion(bf16[20,128,3072]{2,1,0:T(8,128)(2,1)} %get-tuple-element.289, s32[1024]{0:T(1024)S(1)} %pad_clamp_fusion.2), kind=kCustom, calls=%fused_computation.2.clone.clone.1 | custom fusion | bytes 11010076 | tf_op jit(solution)/shard_map/while/body/eval_jaxpr/gather | solution.py:70
  292.3 4.4 %copy.137 = bf16[112,8,24,128]{3,2,1,0:T(8,128)(2,1)S(1)} copy(bf16[112,8,24,128]{3,1,2,0:T(8,128)(2,1)} %bitcast.156) | data formatting | bytes 11010048 | tf_op jit(solution)/shard_map/while
  296.8 2.5 fusion.95
  300.7 2.7 fusion.97
  304.8 2.3 fusion.96
  307.1 8.8 %gather_fusion.2 = bf16[7,128,3072]{2,1,0:T(8,128)(2,1)} fusion(bf16[20,128,3072]{2,1,0:T(8,128)(2,1)} %get-tuple-element.286, s32[1024]{0:T(1024)S(1)} %pad_clamp_fusion.2), kind=kCustom, calls=%fused_computation.clone.clone.1 | custom fusion | bytes 11010076 | tf_op jit(solution)/shard_map/while/body/eval_jaxpr/gather | solution.py:71
  315.9 6.8 %copy.138 = bf16[112,8,24,128]{3,2,1,0:T(8,128)(2,1)} copy(bf16[112,8,24,128]{3,1,2,0:T(8,128)(2,1)} %bitcast.155) | data formatting | bytes 11010048 | tf_op jit(solution)/shard_map/while
  324.0 10.5 %fusion.99 = bf16[1,128,24,128]{1,3,2,0:T(8,128)(2,1)} fusion(f32[24,128,128]{1,2,0:T(8,128)S(1)} %copy-done.4, f32[24,128,896]{2,1,0:T(8,128)} %copy-done.2, f32[24,128]{1,0:T(8,128)S(1)} %max.12, pred[896]{0:T(1024)(128)(4,1)S(1)} %fusion.94, bf16[896,24,128]{2,1,0:T(8,128)(2,1)} %bitcast.157, f32[128,24]{0,1:T(8,128)S(1)} %add_bitcast_fusion.2, ...), kind=kOutput, calls=%fused_computation.32.clone.1 | convolution fusion | flops 717225984 | bytes 18899968 | tf_op jit(solution)/shard_map/while/body/eval_jaxpr/hqk,khd->qhd/dot_general | solution.py:89
  334.6 1.5 copy.139
  337.9 8.8 %gather_fusion.1 = bf16[7,128,3072]{2,1,0:T(8,128)(2,1)} fusion(bf16[20,128,3072]{2,1,0:T(8,128)(2,1)} %get-tuple-element.289, s32[1024]{0:T(1024)S(1)} %pad_clamp_fusion.2), kind=kCustom, calls=%fused_computation.2.clone.clone.1 | custom fusion | bytes 11010076 | tf_op jit(solution)/shard_map/while/body/eval_jaxpr/gather | solution.py:70
  346.7 4.3 %copy.137 = bf16[112,8,24,128]{3,2,1,0:T(8,128)(2,1)S(1)} copy(bf16[112,8,24,128]{3,1,2,0:T(8,128)(2,1)} %bitcast.156) | data formatting | bytes 11010048 | tf_op jit(solution)/shard_map/while
  351.1 2.5 fusion.95
  355.0 2.7 fusion.97
  359.1 2.3 fusion.96
  361.4 8.8 %gather_fusion.2 = bf16[7,128,3072]{2,1,0:T(8,128)(2,1)} fusion(bf16[20,128,3072]{2,1,0:T(8,128)(2,1)} %get-tuple-element.286, s32[1024]{0:T(1024)S(1)} %pad_clamp_fusion.2), kind=kCustom, calls=%fused_computation.clone.clone.1 | custom fusion | bytes 11010076 | tf_op jit(solution)/shard_map/while/body/eval_jaxpr/gather | solution.py:71
  370.2 6.8 %copy.138 = bf16[112,8,24,128]{3,2,1,0:T(8,128)(2,1)} copy(bf16[112,8,24,128]{3,1,2,0:T(8,128)(2,1)} %bitcast.155) | data formatting | bytes 11010048 | tf_op jit(solution)/shard_map/while
  378.3 10.5 %fusion.99 = bf16[1,128,24,128]{1,3,2,0:T(8,128)(2,1)} fusion(f32[24,128,128]{1,2,0:T(8,128)S(1)} %copy-done.4, f32[24,128,896]{2,1,0:T(8,128)} %copy-done.2, f32[24,128]{1,0:T(8,128)S(1)} %max.12, pred[896]{0:T(1024)(128)(4,1)S(1)} %fusion.94, bf16[896,24,128]{2,1,0:T(8,128)(2,1)} %bitcast.157, f32[128,24]{0,1:T(8,128)S(1)} %add_bitcast_fusion.2, ...), kind=kOutput, calls=%fused_computation.32.clone.1 | convolution fusion | flops 717225984 | bytes 18899968 | tf_op jit(solution)/shard_map/while/body/eval_jaxpr/hqk,khd->qhd/dot_general | solution.py:89
  391.4 3.0 copy.125
  395.2 1.6 fusion.60
  (102 shorter events, 21.8 us)
Async XLA Ops:
  7.2 9.0 %copy-start = (bf16[256,3072]{1,0:T(8,128)(2,1)S(1)}, bf16[256,3072]{1,0:T(8,128)(2,1)}, u32[]{:S(2)}) copy-start(bf16[256,3072]{1,0:T(8,128)(2,1)} %param.14) | copy-start | bytes 4718596
  7.2 387.2 %reduce-scatter.7.cloned.1.call-start = ((), (), s32[]{:S(2)}) async-start(), calls=%async_computation.3 | async-start | bytes 139264 | tf_op jit(solution)/shard_map/reduce_scatter | solution.py:131
  7.2 116.8 %collective-permute-start.6 = (s32[2]{0:T(128)}, s32[2]{0:T(128)S(1)}, u32[]{:S(2)}, u32[]{:S(2)}) collective-permute-start(s32[2]{0:T(128)} %param.18), channel_id=1, source_target_pairs={{0,1},{1,2},{2,3},{3,4},{4,5},{5,6},{6,7},{7,8},{8,9},{9,10},{10,1... | collective-permute-start | bytes 32 | tf_op jit(solution)/shard_map/ppermute | solution.py:16
  7.3 116.8 %collective-permute-start.7 = (s32[2]{0:T(128)}, s32[2]{0:T(128)S(1)}, u32[]{:S(2)}, u32[]{:S(2)}) collective-permute-start(s32[2]{0:T(128)} %param.18), channel_id=1, source_target_pairs={{0,15},{1,0},{2,1},{3,2},{4,3},{5,4},{6,5},{7,6},{8,7},{9,8},{10,9... | collective-permute-start | bytes 32 | tf_op jit(solution)/shard_map/ppermute | solution.py:16
  9.9 115.8 %collective-permute-start.4 = (s32[2]{0:T(128)}, s32[2]{0:T(128)S(1)}, u32[]{:S(2)}, u32[]{:S(2)}) collective-permute-start(s32[2]{0:T(128)} %param.18), channel_id=1, source_target_pairs={{0,4},{1,5},{2,6},{3,7},{4,8},{5,9},{6,10},{7,11},{8,12},{9,13},{1... | collective-permute-start | bytes 32 | tf_op jit(solution)/shard_map/ppermute | solution.py:16
  11.6 115.2 %collective-permute-start.5 = (s32[2]{0:T(128)}, s32[2]{0:T(128)S(1)}, u32[]{:S(2)}, u32[]{:S(2)}) collective-permute-start(s32[2]{0:T(128)} %param.18), channel_id=1, source_target_pairs={{0,12},{1,13},{2,14},{3,15},{4,0},{5,1},{6,2},{7,3},{8,4},{9,5},{1... | collective-permute-start | bytes 32 | tf_op jit(solution)/shard_map/ppermute | solution.py:16
  12.0 127.3 %collective-permute-start.8 = (bf16[2,128,3072]{2,1,0:T(8,128)(2,1)}, bf16[2,128,3072]{2,1,0:T(8,128)(2,1)}, u32[]{:S(2)}, u32[]{:S(2)}) collective-permute-start(bf16[2,128,3072]{2,1,0:T(8,128)(2,1)} %bitcast.13), channel_id=1, source_target_pairs={{0,4},{1,5},{2,6},{3,7},{4,8},{5,9},{6,10},{7,11},{8,12},{9,13},{1... | collective-permute-start | bytes 4718600 | tf_op jit(solution)/shard_map/ppermute | solution.py:16
  96.8 297.5 %reduce-scatter.5.cloned.1.call-start = ((), (), s32[]{:S(2)}) async-start(), calls=%async_computation.2 | async-start | bytes 3342336 | tf_op jit(solution)/shard_map/reduce_scatter | solution.py:130
  108.2 0.7 copy-start.10
  108.2 1.4 copy-start.7
  113.0 4.5 %copy-start.8 = (s32[2,6]{1,0:T(2,128)S(1)}, s32[2,6]{1,0:T(2,128)}, u32[]{:S(2)}) copy-start(s32[2,6]{1,0:T(2,128)} %param.17) | copy-start | bytes 148
  124.0 45.9 %collective-permute-start.9 = (bf16[2,128,3072]{2,1,0:T(8,128)(2,1)}, bf16[2,128,3072]{2,1,0:T(8,128)(2,1)}, u32[]{:S(2)}, u32[]{:S(2)}) collective-permute-start(bf16[2,128,3072]{2,1,0:T(8,128)(2,1)} %bitcast.13), channel_id=1, source_target_pairs={{0,12},{1,13},{2,14},{3,15},{4,0},{5,1},{6,2},{7,3},{8,4},{9,5},{1... | collective-permute-start | bytes 4718600 | tf_op jit(solution)/shard_map/ppermute | solution.py:16
  124.1 67.6 %collective-permute-start.10 = (bf16[2,128,3072]{2,1,0:T(8,128)(2,1)}, bf16[2,128,3072]{2,1,0:T(8,128)(2,1)}, u32[]{:S(2)}, u32[]{:S(2)}) collective-permute-start(bf16[2,128,3072]{2,1,0:T(8,128)(2,1)} %bitcast.13), channel_id=1, source_target_pairs={{0,1},{1,2},{2,3},{3,4},{4,5},{5,6},{6,7},{7,8},{8,9},{9,10},{10,1... | collective-permute-start | bytes 4718600 | tf_op jit(solution)/shard_map/ppermute | solution.py:16
  125.7 68.5 %collective-permute-start.11 = (bf16[2,128,3072]{2,1,0:T(8,128)(2,1)}, bf16[2,128,3072]{2,1,0:T(8,128)(2,1)}, u32[]{:S(2)}, u32[]{:S(2)}) collective-permute-start(bf16[2,128,3072]{2,1,0:T(8,128)(2,1)} %bitcast.13), channel_id=1, source_target_pairs={{0,15},{1,0},{2,1},{3,2},{4,3},{5,4},{6,5},{7,6},{8,7},{9,8},{10,9... | collective-permute-start | bytes 4718600 | tf_op jit(solution)/shard_map/ppermute | solution.py:16
  126.8 106.0 %collective-permute-start = (bf16[2,128,3072]{2,1,0:T(8,128)(2,1)}, bf16[2,128,3072]{2,1,0:T(8,128)(2,1)}, u32[]{:S(2)}, u32[]{:S(2)}) collective-permute-start(bf16[2,128,3072]{2,1,0:T(8,128)(2,1)} %bitcast.1), channel_id=1, source_target_pairs={{0,4},{1,5},{2,6},{3,7},{4,8},{5,9},{6,10},{7,11},{8,12},{9,13},{1... | collective-permute-start | bytes 4718600 | tf_op jit(solution)/shard_map/ppermute | solution.py:16
  139.3 116.6 %collective-permute-start.1 = (bf16[2,128,3072]{2,1,0:T(8,128)(2,1)}, bf16[2,128,3072]{2,1,0:T(8,128)(2,1)S(1)}, u32[]{:S(2)}, u32[]{:S(2)}) collective-permute-start(bf16[2,128,3072]{2,1,0:T(8,128)(2,1)} %bitcast.1), channel_id=1, source_target_pairs={{0,12},{1,13},{2,14},{3,15},{4,0},{5,1},{6,2},{7,3},{8,4},{9,5},{1... | collective-permute-start | bytes 4718600 | tf_op jit(solution)/shard_map/ppermute | solution.py:16
  170.0 106.7 %collective-permute-start.2 = (bf16[2,128,3072]{2,1,0:T(8,128)(2,1)}, bf16[2,128,3072]{2,1,0:T(8,128)(2,1)S(1)}, u32[]{:S(2)}, u32[]{:S(2)}) collective-permute-start(bf16[2,128,3072]{2,1,0:T(8,128)(2,1)} %bitcast.1), channel_id=1, source_target_pairs={{0,1},{1,2},{2,3},{3,4},{4,5},{5,6},{6,7},{7,8},{8,9},{9,10},{10,1... | collective-permute-start | bytes 4718600 | tf_op jit(solution)/shard_map/ppermute | solution.py:16
  170.0 62.8 %copy-start.6 = (bf16[5,2,128,3072]{3,2,1,0:T(8,128)(2,1)S(1)}, bf16[5,2,128,3072]{3,2,1,0:T(8,128)(2,1)}, u32[]{:S(2)}) copy-start(bf16[5,2,128,3072]{3,2,1,0:T(8,128)(2,1)} %constant_dynamic-update-slice_fusion.1) | copy-start | bytes 23592964
  191.6 85.1 %collective-permute-start.3 = (bf16[2,128,3072]{2,1,0:T(8,128)(2,1)}, bf16[2,128,3072]{2,1,0:T(8,128)(2,1)S(1)}, u32[]{:S(2)}, u32[]{:S(2)}) collective-permute-start(bf16[2,128,3072]{2,1,0:T(8,128)(2,1)} %bitcast.1), channel_id=1, source_target_pairs={{0,15},{1,0},{2,1},{3,2},{4,3},{5,4},{6,5},{7,6},{8,7},{9,8},{10,9... | collective-permute-start | bytes 4718600 | tf_op jit(solution)/shard_map/ppermute | solution.py:16
  292.3 4.4 %copy-start.5 = (bf16[2,128,24,128]{3,2,1,0:T(8,128)(2,1)S(1)}, bf16[2,128,24,128]{3,2,1,0:T(8,128)(2,1)}, u32[]{:S(2)}) copy-start(bf16[2,128,24,128]{3,2,1,0:T(8,128)(2,1)} %get-tuple-element.288) | copy-start | bytes 4718596 | tf_op jit(solution)/shard_map/while
  299.3 4.1 %copy-start.2 = (f32[24,128,896]{2,1,0:T(8,128)}, f32[24,128,896]{2,1,0:T(8,128)S(1)}, u32[]{:S(2)}) copy-start(f32[24,128,896]{2,1,0:T(8,128)S(1)} %get-tuple-element.257) | copy-start | bytes 33030148 | tf_op jit(solution)/shard_map/while
  303.4 1.4 copy-start.3
  315.9 8.2 %copy-start.4 = (f32[24,128,128]{1,2,0:T(8,128)S(1)}, f32[24,128,128]{1,2,0:T(8,128)}, u32[]{:S(2)}) copy-start(f32[24,128,128]{1,2,0:T(8,128)} %fusion.96) | copy-start | bytes 4718596 | tf_op jit(solution)/shard_map/while
  346.7 4.3 %copy-start.5 = (bf16[2,128,24,128]{3,2,1,0:T(8,128)(2,1)S(1)}, bf16[2,128,24,128]{3,2,1,0:T(8,128)(2,1)}, u32[]{:S(2)}) copy-start(bf16[2,128,24,128]{3,2,1,0:T(8,128)(2,1)} %get-tuple-element.288) | copy-start | bytes 4718596 | tf_op jit(solution)/shard_map/while
  353.6 4.1 %copy-start.2 = (f32[24,128,896]{2,1,0:T(8,128)}, f32[24,128,896]{2,1,0:T(8,128)S(1)}, u32[]{:S(2)}) copy-start(f32[24,128,896]{2,1,0:T(8,128)S(1)} %get-tuple-element.257) | copy-start | bytes 33030148 | tf_op jit(solution)/shard_map/while
  357.7 1.4 copy-start.3
  370.2 8.2 %copy-start.4 = (f32[24,128,128]{1,2,0:T(8,128)S(1)}, f32[24,128,128]{1,2,0:T(8,128)}, u32[]{:S(2)}) copy-start(f32[24,128,128]{1,2,0:T(8,128)} %fusion.96) | copy-start | bytes 4718596 | tf_op jit(solution)/shard_map/while
  391.4 3.8 copy-start.9
  391.4 5.5 %copy-start.1 = (bf16[256,3072]{1,0:T(8,128)(2,1)S(1)}, bf16[256,3072]{1,0:T(8,128)(2,1)}, u32[]{:S(2)}) copy-start(bf16[256,3072]{1,0:T(8,128)(2,1)} %param.14) | copy-start | bytes 4718596
Sparse Core Ops, SparseCore 0:
  97.0 116.0 reduce-scatter.6
  216.9 81.8 reduce-scatter.4
where the time goes:
time: 411 us; the launch traced here: 404 us
  local copies, waits for them, and re-layouts  119 us (29%)
  waiting for transfers between devices  116 us (28%)
  blocking collectives  70.7 us (17%)
  matrix products  43.2 us (11%)
  starting transfers between devices  22.7 us (6%)
  other arithmetic  17.8 us (4%)
  between operations  14.9 us (4%)
    ppermute x12, waiting for transfers between devices, passed_along(): lax.ppermute(x, axis, [(i, (i + by) % length) for i in range(length)])  116 us
    pmax x1, blocking collectives, per_device(): global_top = lax.pmax(local_top, 'tiles')  70.7 us
    unnamed x30, local copies, waits for them, and re-layouts  28.2 us
    while x20, local copies, waits for them, and re-layouts  22.8 us
    ppermute x12, starting transfers between devices, passed_along(): lax.ppermute(x, axis, [(i, (i + by) % length) for i in range(length)])  22.7 us
    dot_general x2, matrix products, one_tile(): jnp.einsum('hqk,khd->qhd', video_probs.astype(jnp.bfloat16), values_chose...  21.1 us
    gather x2, local copies, waits for them, and re-layouts, one_tile(): keys_chosen = key_flat[flat_row].reshape(-1, HEADS, HD)  17.8 us
    gather x2, local copies, waits for them, and re-layouts, one_tile(): values_chosen = value_flat[flat_row].reshape(-1, HEADS, HD)  17.5 us
  transfers between devices with their start and end apart: 14, of which 5 were waited for; matrix products, arithmetic and copies ran while one was open for 43% of the time, Pallas kernels for 0%

commit v1 on v0

v1 whole, which is shorter than its diff:
```python
import functools
import math

import jax
import jax.numpy as jnp
from jax import lax
from jax.experimental import pallas as pl
from jax.experimental.pallas import tpu as pltpu
from jax.sharding import PartitionSpec as P

HEADS = 24
HD = 128
NR = 4
CELLS = 7
CHUNKS = 6
VMEM_BYTES = 40 * 1024 * 1024
LOG2E = 1.4426950408889634


def tile_pairs(n):
    shift = n // 2 + NR + NR // 2
    times = n // NR

    def at(t, r):
        return (t * NR + r - shift) % n

    rows = range(NR)
    pairs = {}
    pairs["earlier"] = [(at(t - 1, r), at(t, r)) for t in range(1, times) for r in rows]
    pairs["later"] = [(at(t + 1, r), at(t, r)) for t in range(times - 1) for r in rows]
    pairs["above"] = [(at(t, r - 1), at(t, r)) for t in range(times) for r in (1, 3)]
    pairs["above"].append((at(times - 1, 1), at(times - 1, 2)))
    pairs["below"] = [(at(t, r + 1), at(t, r)) for t in range(times) for r in (0, 2)]
    pairs["below"].append((at(0, 2), at(0, 1)))
    pairs["above_far"] = [(at(t + 1, 1), at(t, 2)) for t in range(times - 1)]
    pairs["below_far"] = [(at(t - 1, 2), at(t, 1)) for t in range(1, times)]
    return pairs


def dot_nt(a, b):
    return lax.dot_general(a, b, (((1,), (1,)), ((), ())), preferred_element_type=jnp.float32)


def video_kernel(table, q, k_own, v_own, earlier, later, above, below, above_far, below_far,
                 text_k, text_v, *rest):
    out, k_all, v_all, k_cat, v_cat = rest[-5:]
    tok = q.shape[0] // 2
    text = text_k.shape[0]
    video_keys = CELLS * tok
    scale = LOG2E / math.sqrt(HD)

    def put(block, k, v):
        for c in range(2):
            rows = pl.ds(c * tok, tok)
            k_all[2 * block + c] = k[rows, :]
            v_all[2 * block + c] = v[rows, :]

    def put_packed(block, ref):
        put(block, ref.at[pl.ds(0, 2 * tok)], ref.at[pl.ds(2 * tok, 2 * tok)])

    put(0, k_own, v_own)
    put_packed(1, earlier)
    put_packed(2, later)
    far_above = table[2 * CELLS * 2 + 3]
    far_below = table[2 * CELLS * 2 + 4]

    @pl.when(far_above == 1)
    def _():
        put_packed(3, above_far)

    @pl.when(far_above == 0)
    def _():
        put_packed(3, above)

    @pl.when(far_below == 1)
    def _():
        put_packed(4, below_far)

    @pl.when(far_below == 0)
    def _():
        put_packed(4, below)

    lane = lax.broadcasted_iota(jnp.int32, (1, tok), 1)
    text_lane = lax.broadcasted_iota(jnp.int32, (1, text), 1)
    text_bias = jnp.where(text_lane < table[2 * CELLS * 2 + 2], 0.0, -jnp.inf)
    slot = lax.broadcasted_iota(jnp.int32, (tok, 1), 0)
    for c in range(2):
        biases = []
        for j in range(CELLS):
            cell = table[c * CELLS + j]
            count = table[(2 + c) * CELLS + j]
            k_cat[c, pl.ds(j * tok, tok), :] = k_all[cell]
            v_cat[c, pl.ds(j * tok, tok), :] = v_all[cell]
            biases.append(jnp.where(lane < count, 0.0, -jnp.inf))
        k_cat[c, pl.ds(video_keys, text), :] = text_k[...]
        v_cat[c, pl.ds(video_keys, text), :] = text_v[...]
        biases.append(text_bias)
        bias = jnp.concatenate(biases, axis=1)
        s = dot_nt(q[pl.ds(c * tok, tok), :], k_cat[c]) + bias
        top = jnp.max(s, axis=1, keepdims=True)
        p = jnp.exp2((s - top) * scale)
        denom = jnp.sum(p, axis=1, keepdims=True)
        acc = jnp.dot(p.astype(jnp.bfloat16), v_cat[c], preferred_element_type=jnp.float32)
        valid = slot < table[2 * CELLS * 2 + c]
        out[pl.ds(c * tok, tok), :] = jnp.where(valid, acc / denom, 0.0).astype(out.dtype)


def video_call(chunk, heads, table, q, k, v, near, text_k, text_v, carried):
    rows, width = q.shape
    text = text_k.shape[0]
    tok = rows // 2
    first = chunk * heads
    whole = lambda h: (0, first + h)
    part = lambda h: (0, h)
    own_spec = pl.BlockSpec((rows, HD), whole)
    near_spec = pl.BlockSpec((2 * rows, HD), part)
    text_spec = pl.BlockSpec((text, HD), whole)
    in_specs = [pl.BlockSpec(memory_space=pltpu.SMEM), own_spec, own_spec, own_spec]
    in_specs += [near_spec] * 6 + [text_spec] * 2
    operands = [table, q, k, v, *near, text_k, text_v]
    aliases = {}
    if carried is not None:
        aliases = {len(operands): 0}
        operands.append(carried)
        in_specs.append(pl.BlockSpec(memory_space=pl.ANY))
    keys = CELLS * tok + text
    return pl.pallas_call(
        video_kernel,
        grid=(heads,),
        in_specs=in_specs,
        out_specs=pl.BlockSpec((rows, HD), whole),
        out_shape=jax.ShapeDtypeStruct((rows, width), q.dtype),
        scratch_shapes=[
            pltpu.VMEM((10, tok, HD), q.dtype),
            pltpu.VMEM((10, tok, HD), q.dtype),
            pltpu.VMEM((2, keys, HD), q.dtype),
            pltpu.VMEM((2, keys, HD), q.dtype),
        ],
        input_output_aliases=aliases,
        compiler_params=pltpu.CompilerParams(vmem_limit_bytes=VMEM_BYTES),
        cost_estimate=pl.CostEstimate(
            flops=heads * rows * keys * HD * 4,
            bytes_accessed=heads * rows * HD * 40,
            transcendentals=heads * rows * keys,
        ),
        name="video_attention",
    )(*operands)


def key_bias(counts, tok, rows):
    lane = lax.broadcasted_iota(jnp.int32, (1, tok), 1)
    return jnp.concatenate(
        [jnp.where(lane < counts[c], 0.0, -jnp.inf) for c in range(rows // tok)], axis=1
    )


def text_top_kernel(counts, q, k, top):
    h = pl.program_id(0)
    rows = k.shape[0]
    s = dot_nt(q[...], k[...]) * (1.0 / math.sqrt(HD)) + key_bias(counts, rows // 2, rows)
    lane = lax.broadcasted_iota(jnp.int32, top.shape, 1)
    own = jnp.max(s, axis=1, keepdims=True)

    @pl.when(h == 0)
    def _():
        top[...] = jnp.zeros_like(top)

    top[...] = jnp.where(lane == h, own, top[...])


def text_sum_kernel(counts, q, k, v, top, out, denoms):
    h = pl.program_id(0)
    rows = k.shape[0]
    lane = lax.broadcasted_iota(jnp.int32, top.shape, 1)

    @pl.when(h == 0)
    def _():
        denoms[...] = jnp.zeros_like(denoms)

    @pl.when(h < HEADS)
    def _():
        s = dot_nt(q[...], k[...]) * (1.0 / math.sqrt(HD)) + key_bias(counts, rows // 2, rows)
        own = jnp.sum(jnp.where(lane == h, top[...], 0.0), axis=1, keepdims=True)
        w = jnp.exp(s - own)
        denoms[...] = jnp.where(lane == h, jnp.sum(w, axis=1, keepdims=True), denoms[...])
        out[...] = jnp.dot(w.astype(jnp.bfloat16), v[...], preferred_element_type=jnp.float32)

    @pl.when(h == HEADS)
    def _():
        out[...] = denoms[...]


def text_partials(counts, q, k, v):
    text = q.shape[0]
    rows = k.shape[0]
    smem = pl.BlockSpec(memory_space=pltpu.SMEM)
    q_spec = pl.BlockSpec((text, HD), lambda h: (0, jnp.minimum(h, HEADS - 1)))
    k_spec = pl.BlockSpec((rows, HD), lambda h: (0, jnp.minimum(h, HEADS - 1)))
    flat = pl.BlockSpec((text, HD), lambda h: (0, 0))
    params = pltpu.CompilerParams(vmem_limit_bytes=VMEM_BYTES)
    work = HEADS * text * rows
    top = pl.pallas_call(
        text_top_kernel,
        grid=(HEADS,),
        in_specs=[smem, q_spec, k_spec],
        out_specs=flat,
        out_shape=jax.ShapeDtypeStruct((text, HD), jnp.float32),
        compiler_params=params,
        cost_estimate=pl.CostEstimate(
            flops=2 * work * HD, bytes_accessed=4 * text * HEADS * HD, transcendentals=0
        ),
        name="text_top",
    )(counts, q, k)
    top = lax.pmax(top, "tiles")
    return pl.pallas_call(
        text_sum_kernel,
        grid=(HEADS + 1,),
        in_specs=[smem, q_spec, k_spec, k_spec, flat],
        out_specs=pl.BlockSpec((text, HD), lambda h: (0, h)),
        out_shape=jax.ShapeDtypeStruct((text, (HEADS + 1) * HD), jnp.float32),
        scratch_shapes=[pltpu.VMEM((text, HD), jnp.float32)],
        compiler_params=params,
        cost_estimate=pl.CostEstimate(
            flops=4 * work * HD, bytes_accessed=10 * text * HEADS * HD, transcendentals=work
        ),
        name="text_sum",
    )(counts, q, k, v, top)


def cell_table(window, counts, all_counts, text_count, spot, n):
    times = n // NR
    t, r = spot // NR, spot % NR
    shift = n // 2 + NR + NR // 2
    steps_t = jnp.array([0, -1, 1, 0, 0], jnp.int32)
    steps_r = jnp.array([0, 0, 0, -1, 1], jnp.int32)
    near_t, near_r = t + steps_t, r + steps_r
    inside = (near_t >= 0) & (near_t < times) & (near_r >= 0) & (near_r < NR)
    place = (near_t * NR + near_r - shift) % n
    near_counts = jnp.where(inside[:, None], all_counts[place], 0)
    columns = counts.shape[0]
    codes = jnp.concatenate(
        [jnp.ones((columns, 1), jnp.int32), window + (window >= 1)], axis=1
    ).astype(jnp.int32)
    block = codes // 3
    column = jnp.arange(columns, dtype=jnp.int32)[:, None] + codes % 3 - 1
    held = (column >= 0) & (column < columns)
    column = jnp.clip(column, 0, columns - 1)
    cell = block * columns + column
    valid = jnp.where(held, near_counts.reshape(-1)[cell], 0)
    flags = jnp.stack([(r == 2) & (t < times - 1), (r == 1) & (t > 0)]).astype(jnp.int32)
    return jnp.concatenate([cell.reshape(-1), valid.reshape(-1), counts, text_count, flags])


def per_device(n, video_q, video_k, video_v, text_q, text_k, text_v, window, counts, text_count):
    rows, width = video_q.shape
    text = text_q.shape[0]
    pairs = tile_pairs(n)
    position = lax.axis_index("tiles")
    spot = (position + n // 2 + NR + NR // 2) % n
    all_counts = lax.all_gather(counts, "tiles")
    table = cell_table(window, counts, all_counts, text_count, spot, n)

    partials = text_partials(counts, text_q, video_k, video_v)
    sums = lax.psum_scatter(partials, "tiles", scatter_dimension=0, tiled=True)

    heads = HEADS // CHUNKS
    step = heads * HD
    video_out = None
    for chunk in range(CHUNKS):
        cols = slice(chunk * step, (chunk + 1) * step)
        packed = jnp.concatenate([video_k[:, cols], video_v[:, cols]], axis=0)
        near = {}
        for name in ("earlier", "later", "above", "below"):
            near[name] = lax.ppermute(packed, "tiles", pairs[name])
        above_far = lax.ppermute(near["earlier"], "tiles", pairs["above_far"])
        below_far = lax.ppermute(near["later"], "tiles", pairs["below_far"])
        sides = [near["earlier"], near["later"], near["above"], near["below"], above_far, below_far]
        video_out = video_call(
            chunk, heads, table, video_q, video_k, video_v, sides, text_k, text_v, video_out
        )

    share = text // n
    denoms = sums[:, width : width + HEADS]
    text_result = sums[:, :width].reshape(share, HEADS, HD) / denoms[:, :, None]
    row_ids = position * share + jnp.arange(share, dtype=jnp.int32)
    text_out = jnp.where((row_ids < text_count[0])[:, None, None], text_result, 0.0)
    text_out = text_out.astype(jnp.bfloat16).reshape(share, width)
    return (video_out, text_out)


def solution(mesh):
    tiles = mesh.shape["tiles"]
    return jax.shard_map(
        functools.partial(per_device, tiles),
        mesh=mesh,
        in_specs=(
            P(("groups", "tiles"), None),
            P(("groups", "tiles"), None),
            P(("groups", "tiles"), None),
            P("groups", None),
            P("groups", None),
            P("groups", None),
            P("tiles", None),
            P(("groups", "tiles")),
            P("groups"),
        ),
        out_specs=(P(("groups", "tiles"), None), P(("groups", "tiles"), None)),
        check_vma=False,
    )
```

time: 411 us -> 389 us (0.946); the launches traced: 404 us -> 387 us
  local copies, waits for them, and re-layouts: 119 us -> 26.2 us
  starting transfers between devices: 22.7 us -> 112 us
  Pallas kernels: 0 us -> 59.8 us
  blocking collectives: 70.7 us -> 19.2 us
  matrix products: 43.2 us -> 0 us
  waiting for transfers between devices: 116 us -> 150 us
  other arithmetic: 17.8 us -> 3.86 us
    ppermute x12 -> x36, starting transfers between devices: 22.7 us -> 112 us  [the longest x24 66.3 us: per_device(): near[name] = lax.ppermute(packed, 'tiles', pairs[name])]
    pmax x0 -> x1, waiting for transfers between devices: none -> 88.6 us  [text_partials(): top = lax.pmax(top, 'tiles')]
    pmax x1 -> x0, blocking collectives: 70.7 us -> none  [per_device(): global_top = lax.pmax(local_top, 'tiles')]
    pallas_call x0 -> x8, Pallas kernels: none -> 59.8 us  [the longest x6 39.5 us: video_call(): pl.pallas_call(video_kernel, grid=(heads,), in_specs=in_specs, out_specs=...]
    ppermute x12 -> x36, waiting for transfers between devices: 116 us -> 61.7 us  [the longest x24 61.6 us: per_device(): near[name] = lax.ppermute(packed, 'tiles', pairs[name])]
    dot_general x10 -> x0, matrix products: 43.2 us -> none  [the longest x2 21.1 us: one_tile(): jnp.einsum('hqk,khd->qhd', video_probs.astype(jnp.bfloat16), values_chose...]
    gather x6 -> x3, local copies, waits for them, and re-layouts: 36.6 us -> 1.3 us  [the longest x2 0.74 us: cell_table(): valid = jnp.where(held, near_counts.reshape(-1)[cell], 0)]
    while x20 -> x0, local copies, waits for them, and re-layouts: 22.8 us -> none
  transfers between devices with their start and end apart: 14 -> 38, of which waited for: 5 -> 5; matrix products, arithmetic and copies ran while one was open for 43% -> 2% of each run, Pallas kernels for 0% -> 10%
where the time goes in v1:
time: 389 us; the launch traced here: 387 us
  waiting for transfers between devices  150 us (39%)
  starting transfers between devices  112 us (29%)
  Pallas kernels  59.8 us (15%)
  local copies, waits for them, and re-layouts  26.2 us (7%)
  blocking collectives  19.2 us (5%)
  between operations  16.3 us (4%)
    pmax x1, waiting for transfers between devices, text_partials(): top = lax.pmax(top, 'tiles')  88.6 us
    ppermute x24, starting transfers between devices, per_device(): near[name] = lax.ppermute(packed, 'tiles', pairs[name])  66.3 us
    ppermute x24, waiting for transfers between devices, per_device(): near[name] = lax.ppermute(packed, 'tiles', pairs[name])  61.6 us
    pallas_call x6, Pallas kernels, video_call(): pl.pallas_call(video_kernel, grid=(heads,), in_specs=in_specs, out_specs=...  39.5 us
    ppermute x6, starting transfers between devices, per_device(): below_far = lax.ppermute(near['later'], 'tiles', pairs['below_far'])  37.7 us
    unnamed x111, local copies, waits for them, and re-layouts  22.4 us
    unnamed x1, blocking collectives  19.2 us
    pallas_call x1, Pallas kernels, text_partials(): pl.pallas_call(text_sum_kernel, grid=(HEADS + 1,), in_specs=[smem, q_spec...  11.1 us
  transfers between devices with their start and end apart: 38, of which 5 were waited for; matrix products, arithmetic and copies ran while one was open for 2% of the time, Pallas kernels for 10%

profile of v1, /device:TPU:24, one launch (start us, length us, event | category | flops | bytes accessed | tf_op | source)
XLA Modules:
  0.0 387.4 jit_solution(5255716972319473943)
XLA Ops:
  7.2 1.4 copy-done
  8.6 1.4 copy-done.8
  10.7 9.2 %text_top.1 = f32[256,128]{1,0:T(8,128)} custom-call(s32[2]{0:T(128)S(1)} %copy-done.43, bf16[256,3072]{1,0:T(8,128)(2,1)S(1)} %copy-done.8, bf16[256,3072]{1,0:T(8,128)(2,1)S(1)} %copy-done), custom_call_target="tpu_custom_call" | custom-call | flops 402653184 | bytes 3145728 | tf_op jit(solution)/shard_map/text_top/pallas_call | solution.py:202
  21.1 88.6 %all-reduce.4.cloned.1.call-done.top = f32[256,128]{1,0:T(8,128)} async-done(((f32[256,128]{1,0:T(8,128)}), f32[256,128]{1,0:T(8,128)}) %all-reduce.4.cloned.1.call-update) | async-done | bytes 131088 | tf_op jit(solution)/shard_map/pmax | solution.py:214
  109.7 1.4 copy-done.9
  112.0 11.1 %text_sum.1 = f32[256,3200]{1,0:T(8,128)S(1)} custom-call(s32[2]{0:T(128)S(1)} %copy-done.44, bf16[256,3072]{1,0:T(8,128)(2,1)S(1)} %copy-done.9, bf16[256,3072]{1,0:T(8,128)(2,1)S(1)} %copy-done.1, bf16[256,3072]{1,0:T(8,128)(2,1)S(1)} %copy-done.2, f32[256,128]{1,0:T(8,128)S(1)} %copy-done.42), custom_call_target="tpu_custom_call" | custom-call | flops 805306368 | bytes 7864320 | tf_op jit(solution)/shard_map/text_sum/pallas_call | solution.py:215
  123.2 1.7 copy-done.7
  125.8 2.1 collective-permute-start.30
  127.9 3.9 %collective-permute-start.31 = (bf16[512,512]{1,0:T(8,128)(2,1)S(1)}, bf16[512,512]{1,0:T(8,128)(2,1)S(1)}, u32[]{:S(2)}, u32[]{:S(2)}) collective-permute-start(bf16[512,512]{1,0:T(8,128)(2,1)S(1)} %pad_maximum_fusion.5), channel_id=1, source_target_pairs={{6,2},{7,3},{8,4},{9,5},{10,6},{11,7},{12,8},{13,9},{14,10},{15,11... | collective-permute-start | bytes 1572872 | tf_op jit(solution)/shard_map/ppermute | solution.py:274
  131.8 1.3 collective-permute-start.32
  133.2 1.3 collective-permute-start.33
  134.5 4.5 %collective-permute-start.24 = (bf16[512,512]{1,0:T(8,128)(2,1)S(1)}, bf16[512,512]{1,0:T(8,128)(2,1)S(1)}, u32[]{:S(2)}, u32[]{:S(2)}) collective-permute-start(bf16[512,512]{1,0:T(8,128)(2,1)S(1)} %pad_maximum_fusion.4), channel_id=1, source_target_pairs={{2,6},{3,7},{4,8},{5,9},{6,10},{7,11},{8,12},{9,13},{10,14},{11,15... | collective-permute-start | bytes 1572872 | tf_op jit(solution)/shard_map/ppermute | solution.py:274
  139.0 17.7 %collective-permute-done.30.earlier = bf16[512,512]{1,0:T(8,128)(2,1)S(1)} collective-permute-done((bf16[512,512]{1,0:T(8,128)(2,1)S(1)}, bf16[512,512]{1,0:T(8,128)(2,1)S(1)}, u32[]{:S(2)}, u32[]{:S(2)}) %collective-permute-start.30) | collective-permute-done | bytes 524320 | tf_op jit(solution)/shard_map/ppermute | solution.py:274
  156.7 1.9 collective-permute-start.25
  158.7 1.3 collective-permute-start.26
  160.1 1.3 collective-permute-start.27
  161.4 6.3 %collective-permute-start.18 = (bf16[512,512]{1,0:T(8,128)(2,1)S(1)}, bf16[512,512]{1,0:T(8,128)(2,1)S(1)}, u32[]{:S(2)}, u32[]{:S(2)}) collective-permute-start(bf16[512,512]{1,0:T(8,128)(2,1)S(1)} %pad_maximum_fusion.3), channel_id=1, source_target_pairs={{2,6},{3,7},{4,8},{5,9},{6,10},{7,11},{8,12},{9,13},{10,14},{11,15... | collective-permute-start | bytes 1572872 | tf_op jit(solution)/shard_map/ppermute | solution.py:274
  167.8 27.5 %collective-permute-done.24.earlier = bf16[512,512]{1,0:T(8,128)(2,1)S(1)} collective-permute-done((bf16[512,512]{1,0:T(8,128)(2,1)S(1)}, bf16[512,512]{1,0:T(8,128)(2,1)S(1)}, u32[]{:S(2)}, u32[]{:S(2)}) %collective-permute-start.24) | collective-permute-done | bytes 524320 | tf_op jit(solution)/shard_map/ppermute | solution.py:274
  195.2 1.9 collective-permute-start.19
  197.2 1.3 collective-permute-start.20
  198.6 1.3 collective-permute-start.21
  200.8 6.3 %collective-permute-start.12 = (bf16[512,512]{1,0:T(8,128)(2,1)S(1)}, bf16[512,512]{1,0:T(8,128)(2,1)S(1)}, u32[]{:S(2)}, u32[]{:S(2)}) collective-permute-start(bf16[512,512]{1,0:T(8,128)(2,1)S(1)} %pad_maximum_fusion.2), channel_id=1, source_target_pairs={{2,6},{3,7},{4,8},{5,9},{6,10},{7,11},{8,12},{9,13},{10,14},{11,15... | collective-permute-start | bytes 1572872 | tf_op jit(solution)/shard_map/ppermute | solution.py:274
  207.1 16.1 %collective-permute-done.18.earlier = bf16[512,512]{1,0:T(8,128)(2,1)S(1)} collective-permute-done((bf16[512,512]{1,0:T(8,128)(2,1)S(1)}, bf16[512,512]{1,0:T(8,128)(2,1)S(1)}, u32[]{:S(2)}, u32[]{:S(2)}) %collective-permute-start.18) | collective-permute-done | bytes 524320 | tf_op jit(solution)/shard_map/ppermute | solution.py:274
  223.2 2.9 collective-permute-start.13
  226.2 1.3 collective-permute-start.14
  232.1 5.3 %collective-permute-start.6 = (bf16[512,512]{1,0:T(8,128)(2,1)}, bf16[512,512]{1,0:T(8,128)(2,1)}, u32[]{:S(2)}, u32[]{:S(2)}) collective-permute-start(bf16[512,512]{1,0:T(8,128)(2,1)} %pad_maximum_fusion.1), channel_id=1, source_target_pairs={{2,6},{3,7},{4,8},{5,9},{6,10},{7,11},{8,12},{9,13},{10,14},{11,15... | collective-permute-start | bytes 1572872 | tf_op jit(solution)/shard_map/ppermute | solution.py:274
  237.8 5.1 %collective-permute-start.7 = (bf16[512,512]{1,0:T(8,128)(2,1)}, bf16[512,512]{1,0:T(8,128)(2,1)}, u32[]{:S(2)}, u32[]{:S(2)}) collective-permute-start(bf16[512,512]{1,0:T(8,128)(2,1)} %pad_maximum_fusion.1), channel_id=1, source_target_pairs={{6,2},{7,3},{8,4},{9,5},{10,6},{11,7},{12,8},{13,9},{14,10},{15,11... | collective-permute-start | bytes 1572872 | tf_op jit(solution)/shard_map/ppermute | solution.py:274
  243.7 2.1 collective-permute-start.8
  248.6 3.5 collective-permute-start
  253.6 19.2 %all-reduce.1 = s32[32]{0:T(128)S(1)} all-reduce(s32[32]{0:T(128)S(1)} %dynamic-update-slice), channel_id=2, replica_groups=mesh['groups'=2,'tiles'=16] {'tiles'}, use_global_device_ids=true, to_apply=%add.1 | all-reduce | flops 32 | bytes 256
  272.9 5.3 %collective-permute-start.1 = (bf16[512,512]{1,0:T(8,128)(2,1)}, bf16[512,512]{1,0:T(8,128)(2,1)}, u32[]{:S(2)}, u32[]{:S(2)}) collective-permute-start(bf16[512,512]{1,0:T(8,128)(2,1)} %pad_maximum_fusion), channel_id=1, source_target_pairs={{6,2},{7,3},{8,4},{9,5},{10,6},{11,7},{12,8},{13,9},{14,10},{15,11... | collective-permute-start | bytes 1572872 | tf_op jit(solution)/shard_map/ppermute | solution.py:274
  279.6 5.9 %collective-permute-start.35 = (bf16[512,512]{1,0:T(8,128)(2,1)}, bf16[512,512]{1,0:T(8,128)(2,1)}, u32[]{:S(2)}, u32[]{:S(2)}) collective-permute-start(bf16[512,512]{1,0:T(8,128)(2,1)} %copy-done.12), channel_id=1, source_target_pairs={{4,7},{8,11},{12,15},{20,23},{24,27},{28,31}} | collective-permute-start | bytes 1572872 | tf_op jit(solution)/shard_map/ppermute | solution.py:276
  286.7 5.9 %collective-permute-start.29 = (bf16[512,512]{1,0:T(8,128)(2,1)}, bf16[512,512]{1,0:T(8,128)(2,1)}, u32[]{:S(2)}, u32[]{:S(2)}) collective-permute-start(bf16[512,512]{1,0:T(8,128)(2,1)} %copy-done.20), channel_id=1, source_target_pairs={{4,7},{8,11},{12,15},{20,23},{24,27},{28,31}} | collective-permute-start | bytes 1572872 | tf_op jit(solution)/shard_map/ppermute | solution.py:276
  294.5 5.9 %collective-permute-start.23 = (bf16[512,512]{1,0:T(8,128)(2,1)}, bf16[512,512]{1,0:T(8,128)(2,1)}, u32[]{:S(2)}, u32[]{:S(2)}) collective-permute-start(bf16[512,512]{1,0:T(8,128)(2,1)} %copy-done.28), channel_id=1, source_target_pairs={{4,7},{8,11},{12,15},{20,23},{24,27},{28,31}} | collective-permute-start | bytes 1572872 | tf_op jit(solution)/shard_map/ppermute | solution.py:276
  301.7 5.8 %collective-permute-start.17 = (bf16[512,512]{1,0:T(8,128)(2,1)}, bf16[512,512]{1,0:T(8,128)(2,1)}, u32[]{:S(2)}, u32[]{:S(2)}) collective-permute-start(bf16[512,512]{1,0:T(8,128)(2,1)} %copy-done.36), channel_id=1, source_target_pairs={{4,7},{8,11},{12,15},{20,23},{24,27},{28,31}} | collective-permute-start | bytes 1572872 | tf_op jit(solution)/shard_map/ppermute | solution.py:276
  309.9 2.1 collective-permute-start.2
  313.3 8.4 %collective-permute-start.11 = (bf16[512,512]{1,0:T(8,128)(2,1)}, bf16[512,512]{1,0:T(8,128)(2,1)}, u32[]{:S(2)}, u32[]{:S(2)}) collective-permute-start(bf16[512,512]{1,0:T(8,128)(2,1)} %collective-permute-done.7.later), channel_id=1, source_target_pairs={{4,7},{8,11},{12,15},{20,23},{24,27},{28,31}} | collective-permute-start | bytes 1572872 | tf_op jit(solution)/shard_map/ppermute | solution.py:276
  323.0 5.9 %collective-permute-start.5 = (bf16[512,512]{1,0:T(8,128)(2,1)}, bf16[512,512]{1,0:T(8,128)(2,1)}, u32[]{:S(2)}, u32[]{:S(2)}) collective-permute-start(bf16[512,512]{1,0:T(8,128)(2,1)} %collective-permute-done.1.later), channel_id=1, source_target_pairs={{4,7},{8,11},{12,15},{20,23},{24,27},{28,31}} | collective-permute-start | bytes 1572872 | tf_op jit(solution)/shard_map/ppermute | solution.py:276
  330.0 1.4 copy-done.3
  331.4 1.4 copy-done.4
  332.8 1.4 copy-done.6
  338.4 6.6 %video_attention.6.rest_0_ = bf16[256,3072]{1,0:T(8,128)(2,1)} custom-call(s32[33]{0:T(128)S(1)} %concatenate.25.table, bf16[256,3072]{1,0:T(8,128)(2,1)S(1)} %copy-done.3, bf16[256,3072]{1,0:T(8,128)(2,1)S(1)} %copy-done.1, bf16[256,3072]{1,0:T(8,128)(2,1)S(1)} %copy-done.2, bf16[512,512]{1,0:T(8,128)(2,1)S(1)} %copy-done.11, ...), custom_call_target="tpu_custom_call" | custom-call | flops 603979776 | bytes 5242880 | tf_op jit(solution)/shard_map/video_attention/pallas_call | solution.py:127
  345.1 6.6 %video_attention.7.rest_0_ = bf16[256,3072]{1,0:T(8,128)(2,1)} custom-call(s32[33]{0:T(128)S(1)} %concatenate.25.table, bf16[256,3072]{1,0:T(8,128)(2,1)S(1)} %copy-done.3, bf16[256,3072]{1,0:T(8,128)(2,1)S(1)} %copy-done.1, bf16[256,3072]{1,0:T(8,128)(2,1)S(1)} %copy-done.2, bf16[512,512]{1,0:T(8,128)(2,1)S(1)} %copy-done.19, ...), custom_call_target="tpu_custom_call", output_to_operand_aliasing={{}: (12, {})} | custom-call | flops 603979776 | bytes 5242880 | tf_op jit(solution)/shard_map/video_attention/pallas_call | solution.py:127
  351.8 6.6 %video_attention.8.rest_0_ = bf16[256,3072]{1,0:T(8,128)(2,1)} custom-call(s32[33]{0:T(128)S(1)} %concatenate.25.table, bf16[256,3072]{1,0:T(8,128)(2,1)S(1)} %copy-done.3, bf16[256,3072]{1,0:T(8,128)(2,1)S(1)} %copy-done.1, bf16[256,3072]{1,0:T(8,128)(2,1)S(1)} %copy-done.2, bf16[512,512]{1,0:T(8,128)(2,1)S(1)} %copy-done.27, ...), custom_call_target="tpu_custom_call", output_to_operand_aliasing={{}: (12, {})} | custom-call | flops 603979776 | bytes 5242880 | tf_op jit(solution)/shard_map/video_attention/pallas_call | solution.py:127
  358.5 6.5 %video_attention.9.rest_0_ = bf16[256,3072]{1,0:T(8,128)(2,1)} custom-call(s32[33]{0:T(128)S(1)} %concatenate.25.table, bf16[256,3072]{1,0:T(8,128)(2,1)S(1)} %copy-done.3, bf16[256,3072]{1,0:T(8,128)(2,1)S(1)} %copy-done.1, bf16[256,3072]{1,0:T(8,128)(2,1)S(1)} %copy-done.2, bf16[512,512]{1,0:T(8,128)(2,1)S(1)} %copy-done.35, ...), custom_call_target="tpu_custom_call", output_to_operand_aliasing={{}: (12, {})} | custom-call | flops 603979776 | bytes 5242880 | tf_op jit(solution)/shard_map/video_attention/pallas_call | solution.py:127
  365.0 6.5 %video_attention.10.rest_0_ = bf16[256,3072]{1,0:T(8,128)(2,1)} custom-call(s32[33]{0:T(128)S(1)} %concatenate.25.table, bf16[256,3072]{1,0:T(8,128)(2,1)S(1)} %copy-done.3, bf16[256,3072]{1,0:T(8,128)(2,1)S(1)} %copy-done.1, bf16[256,3072]{1,0:T(8,128)(2,1)S(1)} %copy-done.2, ...), custom_call_target="tpu_custom_call", output_to_operand_aliasing={{}: (12, {})} | custom-call | flops 603979776 | bytes 5242880 | tf_op jit(solution)/shard_map/video_attention/pallas_call | solution.py:127
  371.5 6.5 %video_attention.11 = bf16[256,3072]{1,0:T(8,128)(2,1)} custom-call(s32[33]{0:T(128)S(1)} %concatenate.25.table, bf16[256,3072]{1,0:T(8,128)(2,1)S(1)} %copy-done.3, bf16[256,3072]{1,0:T(8,128)(2,1)S(1)} %copy-done.1, bf16[256,3072]{1,0:T(8,128)(2,1)S(1)} %copy-done.2, ...), custom_call_target="tpu_custom_call", output_to_operand_aliasing={{}: (12, {})} | custom-call | flops 603979776 | bytes 5242880 | tf_op jit(solution)/shard_map/video_attention/pallas_call | solution.py:127
  378.9 1.7 fusion.1
  (180 shorter events, 30.3 us)
Async XLA Ops:
  7.2 102.5 %all-reduce.4.cloned.1.call-start = ((), (), s32[]{:S(2)}) async-start(), calls=%async_computation.1 | async-start | bytes 262144 | tf_op jit(solution)/shard_map/pmax | solution.py:214
  19.9 89.7 %copy-start.1 = (bf16[256,3072]{1,0:T(8,128)(2,1)S(1)}, bf16[256,3072]{1,0:T(8,128)(2,1)}, u32[]{:S(2)}) copy-start(bf16[256,3072]{1,0:T(8,128)(2,1)} %k.3) | copy-start | bytes 4718596
  20.0 89.7 %copy-start.44 = (s32[2]{0:T(128)S(1)}, s32[2]{0:T(128)}, u32[]{:S(2)}) copy-start(s32[2]{0:T(128)} %counts.3) | copy-start | bytes 28
  20.0 358.1 %reduce-scatter.2.cloned.1.call-start = ((), (), s32[]{:S(2)}) async-start(), calls=%async_computation.2 | async-start | bytes 3481600 | tf_op jit(solution)/shard_map/reduce_scatter | solution.py:264
  125.8 72.7 %copy-start.46 = (bf16[256,512]{1,0:T(8,128)(2,1)S(1)}, bf16[256,512]{1,0:T(8,128)(2,1)}, u32[]{:S(2)}) copy-start(bf16[256,512]{1,0:T(8,128)(2,1)} %get-tuple-element.13) | copy-start | bytes 786436
  125.8 30.9 %collective-permute-start.30 = (bf16[512,512]{1,0:T(8,128)(2,1)S(1)}, bf16[512,512]{1,0:T(8,128)(2,1)S(1)}, u32[]{:S(2)}, u32[]{:S(2)}) collective-permute-start(bf16[512,512]{1,0:T(8,128)(2,1)S(1)} %pad_maximum_fusion.5), channel_id=1, source_target_pairs={{2,6},{3,7},{4,8},{5,9},{6,10},{7,11},{8,12},{9,13},{10,14},{11,15... | collective-permute-start | bytes 1572872 | tf_op jit(solution)/shard_map/ppermute | solution.py:274
  127.9 30.8 %collective-permute-start.31 = (bf16[512,512]{1,0:T(8,128)(2,1)S(1)}, bf16[512,512]{1,0:T(8,128)(2,1)S(1)}, u32[]{:S(2)}, u32[]{:S(2)}) collective-permute-start(bf16[512,512]{1,0:T(8,128)(2,1)S(1)} %pad_maximum_fusion.5), channel_id=1, source_target_pairs={{6,2},{7,3},{8,4},{9,5},{10,6},{11,7},{12,8},{13,9},{14,10},{15,11... | collective-permute-start | bytes 1572872 | tf_op jit(solution)/shard_map/ppermute | solution.py:274
  131.8 28.2 %collective-permute-start.32 = (bf16[512,512]{1,0:T(8,128)(2,1)S(1)}, bf16[512,512]{1,0:T(8,128)(2,1)S(1)}, u32[]{:S(2)}, u32[]{:S(2)}) collective-permute-start(bf16[512,512]{1,0:T(8,128)(2,1)S(1)} %pad_maximum_fusion.5), channel_id=1, source_target_pairs={{2,3},{4,5},{6,7},{8,9},{10,11},{12,13},{14,15},{0,1},{15,0},{18,1... | collective-permute-start | bytes 1572872 | tf_op jit(solution)/shard_map/ppermute | solution.py:274
  133.2 28.2 %collective-permute-start.33 = (bf16[512,512]{1,0:T(8,128)(2,1)S(1)}, bf16[512,512]{1,0:T(8,128)(2,1)S(1)}, u32[]{:S(2)}, u32[]{:S(2)}) collective-permute-start(bf16[512,512]{1,0:T(8,128)(2,1)S(1)} %pad_maximum_fusion.5), channel_id=1, source_target_pairs={{3,2},{5,4},{7,6},{9,8},{11,10},{13,12},{15,14},{1,0},{4,3},{19,18... | collective-permute-start | bytes 1572872 | tf_op jit(solution)/shard_map/ppermute | solution.py:274
  134.5 95.1 %copy-start.45 = (bf16[256,512]{1,0:T(8,128)(2,1)S(1)}, bf16[256,512]{1,0:T(8,128)(2,1)}, u32[]{:S(2)}) copy-start(bf16[256,512]{1,0:T(8,128)(2,1)} %get-tuple-element.14) | copy-start | bytes 786436
  134.5 60.7 %collective-permute-start.24 = (bf16[512,512]{1,0:T(8,128)(2,1)S(1)}, bf16[512,512]{1,0:T(8,128)(2,1)S(1)}, u32[]{:S(2)}, u32[]{:S(2)}) collective-permute-start(bf16[512,512]{1,0:T(8,128)(2,1)S(1)} %pad_maximum_fusion.4), channel_id=1, source_target_pairs={{2,6},{3,7},{4,8},{5,9},{6,10},{7,11},{8,12},{9,13},{10,14},{11,15... | collective-permute-start | bytes 1572872 | tf_op jit(solution)/shard_map/ppermute | solution.py:274
  156.7 73.7 %copy-start.10 = (bf16[512,512]{1,0:T(8,128)(2,1)}, bf16[512,512]{1,0:T(8,128)(2,1)S(1)}, u32[]{:S(2)}) copy-start(bf16[512,512]{1,0:T(8,128)(2,1)S(1)} %collective-permute-done.30.earlier) | copy-start | bytes 1572868
  156.7 40.4 %collective-permute-start.25 = (bf16[512,512]{1,0:T(8,128)(2,1)S(1)}, bf16[512,512]{1,0:T(8,128)(2,1)S(1)}, u32[]{:S(2)}, u32[]{:S(2)}) collective-permute-start(bf16[512,512]{1,0:T(8,128)(2,1)S(1)} %pad_maximum_fusion.4), channel_id=1, source_target_pairs={{6,2},{7,3},{8,4},{9,5},{10,6},{11,7},{12,8},{13,9},{14,10},{15,11... | collective-permute-start | bytes 1572872 | tf_op jit(solution)/shard_map/ppermute | solution.py:274
  158.7 72.6 %copy-start.12 = (bf16[512,512]{1,0:T(8,128)(2,1)}, bf16[512,512]{1,0:T(8,128)(2,1)S(1)}, u32[]{:S(2)}) copy-start(bf16[512,512]{1,0:T(8,128)(2,1)S(1)} %collective-permute-done.31.later) | copy-start | bytes 1572868
  158.7 39.9 %collective-permute-start.26 = (bf16[512,512]{1,0:T(8,128)(2,1)S(1)}, bf16[512,512]{1,0:T(8,128)(2,1)S(1)}, u32[]{:S(2)}, u32[]{:S(2)}) collective-permute-start(bf16[512,512]{1,0:T(8,128)(2,1)S(1)} %pad_maximum_fusion.4), channel_id=1, source_target_pairs={{2,3},{4,5},{6,7},{8,9},{10,11},{12,13},{14,15},{0,1},{15,0},{18,1... | collective-permute-start | bytes 1572872 | tf_op jit(solution)/shard_map/ppermute | solution.py:274
  160.1 71.2 %copy-start.14 = (bf16[512,512]{1,0:T(8,128)(2,1)}, bf16[512,512]{1,0:T(8,128)(2,1)S(1)}, u32[]{:S(2)}) copy-start(bf16[512,512]{1,0:T(8,128)(2,1)S(1)} %collective-permute-done.32.above) | copy-start | bytes 1572868
  160.1 39.8 %collective-permute-start.27 = (bf16[512,512]{1,0:T(8,128)(2,1)S(1)}, bf16[512,512]{1,0:T(8,128)(2,1)S(1)}, u32[]{:S(2)}, u32[]{:S(2)}) collective-permute-start(bf16[512,512]{1,0:T(8,128)(2,1)S(1)} %pad_maximum_fusion.4), channel_id=1, source_target_pairs={{3,2},{5,4},{7,6},{9,8},{11,10},{13,12},{15,14},{1,0},{4,3},{19,18... | collective-permute-start | bytes 1572872 | tf_op jit(solution)/shard_map/ppermute | solution.py:274
  161.4 61.8 %collective-permute-start.18 = (bf16[512,512]{1,0:T(8,128)(2,1)S(1)}, bf16[512,512]{1,0:T(8,128)(2,1)S(1)}, u32[]{:S(2)}, u32[]{:S(2)}) collective-permute-start(bf16[512,512]{1,0:T(8,128)(2,1)S(1)} %pad_maximum_fusion.3), channel_id=1, source_target_pairs={{2,6},{3,7},{4,8},{5,9},{6,10},{7,11},{8,12},{9,13},{10,14},{11,15... | collective-permute-start | bytes 1572872 | tf_op jit(solution)/shard_map/ppermute | solution.py:274
  195.2 30.9 %collective-permute-start.19 = (bf16[512,512]{1,0:T(8,128)(2,1)S(1)}, bf16[512,512]{1,0:T(8,128)(2,1)S(1)}, u32[]{:S(2)}, u32[]{:S(2)}) collective-permute-start(bf16[512,512]{1,0:T(8,128)(2,1)S(1)} %pad_maximum_fusion.3), channel_id=1, source_target_pairs={{6,2},{7,3},{8,4},{9,5},{10,6},{11,7},{12,8},{13,9},{14,10},{15,11... | collective-permute-start | bytes 1572872 | tf_op jit(solution)/shard_map/ppermute | solution.py:274
  197.2 30.3 %collective-permute-start.20 = (bf16[512,512]{1,0:T(8,128)(2,1)S(1)}, bf16[512,512]{1,0:T(8,128)(2,1)S(1)}, u32[]{:S(2)}, u32[]{:S(2)}) collective-permute-start(bf16[512,512]{1,0:T(8,128)(2,1)S(1)} %pad_maximum_fusion.3), channel_id=1, source_target_pairs={{2,3},{4,5},{6,7},{8,9},{10,11},{12,13},{14,15},{0,1},{15,0},{18,1... | collective-permute-start | bytes 1572872 | tf_op jit(solution)/shard_map/ppermute | solution.py:274
  198.5 94.1 %copy-start.50 = (s32[5]{0:T(128)S(1)}, s32[5]{0:T(128)}, u32[]{:S(2)}) copy-start(s32[5]{0:T(128)} %constant.91.clone) | copy-start | bytes 64
  198.5 94.1 %copy-start.51 = (s32[5]{0:T(128)S(1)}, s32[5]{0:T(128)}, u32[]{:S(2)}) copy-start(s32[5]{0:T(128)} %constant.92.clone) | copy-start | bytes 64
  198.5 110.4 %copy-start.52 = (s32[2,6]{1,0:T(2,128)S(1)}, s32[2,6]{1,0:T(2,128)}, u32[]{:S(2)}) copy-start(s32[2,6]{1,0:T(2,128)} %param.17) | copy-start | bytes 148
  198.6 32.7 %collective-permute-start.21 = (bf16[512,512]{1,0:T(8,128)(2,1)S(1)}, bf16[512,512]{1,0:T(8,128)(2,1)S(1)}, u32[]{:S(2)}, u32[]{:S(2)}) collective-permute-start(bf16[512,512]{1,0:T(8,128)(2,1)S(1)} %pad_maximum_fusion.3), channel_id=1, source_target_pairs={{3,2},{5,4},{7,6},{9,8},{11,10},{13,12},{15,14},{1,0},{4,3},{19,18... | collective-permute-start | bytes 1572872 | tf_op jit(solution)/shard_map/ppermute | solution.py:274
  200.8 37.0 %collective-permute-start.12 = (bf16[512,512]{1,0:T(8,128)(2,1)S(1)}, bf16[512,512]{1,0:T(8,128)(2,1)S(1)}, u32[]{:S(2)}, u32[]{:S(2)}) collective-permute-start(bf16[512,512]{1,0:T(8,128)(2,1)S(1)} %pad_maximum_fusion.2), channel_id=1, source_target_pairs={{2,6},{3,7},{4,8},{5,9},{6,10},{7,11},{8,12},{9,13},{10,14},{11,15... | collective-permute-start | bytes 1572872 | tf_op jit(solution)/shard_map/ppermute | solution.py:274
  223.2 19.7 %collective-permute-start.13 = (bf16[512,512]{1,0:T(8,128)(2,1)S(1)}, bf16[512,512]{1,0:T(8,128)(2,1)S(1)}, u32[]{:S(2)}, u32[]{:S(2)}) collective-permute-start(bf16[512,512]{1,0:T(8,128)(2,1)S(1)} %pad_maximum_fusion.2), channel_id=1, source_target_pairs={{6,2},{7,3},{8,4},{9,5},{10,6},{11,7},{12,8},{13,9},{14,10},{15,11... | collective-permute-start | bytes 1572872 | tf_op jit(solution)/shard_map/ppermute | solution.py:274
  226.2 19.6 %collective-permute-start.14 = (bf16[512,512]{1,0:T(8,128)(2,1)S(1)}, bf16[512,512]{1,0:T(8,128)(2,1)S(1)}, u32[]{:S(2)}, u32[]{:S(2)}) collective-permute-start(bf16[512,512]{1,0:T(8,128)(2,1)S(1)} %pad_maximum_fusion.2), channel_id=1, source_target_pairs={{2,3},{4,5},{6,7},{8,9},{10,11},{12,13},{14,15},{0,1},{15,0},{18,1... | collective-permute-start | bytes 1572872 | tf_op jit(solution)/shard_map/ppermute | solution.py:274
  228.3 19.5 %collective-permute-start.15 = (bf16[512,512]{1,0:T(8,128)(2,1)S(1)}, bf16[512,512]{1,0:T(8,128)(2,1)S(1)}, u32[]{:S(2)}, u32[]{:S(2)}) collective-permute-start(bf16[512,512]{1,0:T(8,128)(2,1)S(1)} %pad_maximum_fusion.2), channel_id=1, source_target_pairs={{3,2},{5,4},{7,6},{9,8},{11,10},{13,12},{15,14},{1,0},{4,3},{19,18... | collective-permute-start | bytes 1572872 | tf_op jit(solution)/shard_map/ppermute | solution.py:274
  232.1 40.8 %collective-permute-start.6 = (bf16[512,512]{1,0:T(8,128)(2,1)}, bf16[512,512]{1,0:T(8,128)(2,1)}, u32[]{:S(2)}, u32[]{:S(2)}) collective-permute-start(bf16[512,512]{1,0:T(8,128)(2,1)} %pad_maximum_fusion.1), channel_id=1, source_target_pairs={{2,6},{3,7},{4,8},{5,9},{6,10},{7,11},{8,12},{9,13},{10,14},{11,15... | collective-permute-start | bytes 1572872 | tf_op jit(solution)/shard_map/ppermute | solution.py:274
  237.8 40.5 %collective-permute-start.7 = (bf16[512,512]{1,0:T(8,128)(2,1)}, bf16[512,512]{1,0:T(8,128)(2,1)}, u32[]{:S(2)}, u32[]{:S(2)}) collective-permute-start(bf16[512,512]{1,0:T(8,128)(2,1)} %pad_maximum_fusion.1), channel_id=1, source_target_pairs={{6,2},{7,3},{8,4},{9,5},{10,6},{11,7},{12,8},{13,9},{14,10},{15,11... | collective-permute-start | bytes 1572872 | tf_op jit(solution)/shard_map/ppermute | solution.py:274
  243.7 35.9 %collective-permute-start.8 = (bf16[512,512]{1,0:T(8,128)(2,1)}, bf16[512,512]{1,0:T(8,128)(2,1)}, u32[]{:S(2)}, u32[]{:S(2)}) collective-permute-start(bf16[512,512]{1,0:T(8,128)(2,1)} %pad_maximum_fusion.1), channel_id=1, source_target_pairs={{2,3},{4,5},{6,7},{8,9},{10,11},{12,13},{14,15},{0,1},{15,0},{18,1... | collective-permute-start | bytes 1572872 | tf_op jit(solution)/shard_map/ppermute | solution.py:274
  246.5 38.9 %collective-permute-start.9 = (bf16[512,512]{1,0:T(8,128)(2,1)}, bf16[512,512]{1,0:T(8,128)(2,1)}, u32[]{:S(2)}, u32[]{:S(2)}) collective-permute-start(bf16[512,512]{1,0:T(8,128)(2,1)} %pad_maximum_fusion.1), channel_id=1, source_target_pairs={{3,2},{5,4},{7,6},{9,8},{11,10},{13,12},{15,14},{1,0},{4,3},{19,18... | collective-permute-start | bytes 1572872 | tf_op jit(solution)/shard_map/ppermute | solution.py:274
  248.6 38.1 %collective-permute-start = (bf16[512,512]{1,0:T(8,128)(2,1)}, bf16[512,512]{1,0:T(8,128)(2,1)}, u32[]{:S(2)}, u32[]{:S(2)}) collective-permute-start(bf16[512,512]{1,0:T(8,128)(2,1)} %pad_maximum_fusion), channel_id=1, source_target_pairs={{2,6},{3,7},{4,8},{5,9},{6,10},{7,11},{8,12},{9,13},{10,14},{11,15... | collective-permute-start | bytes 1572872 | tf_op jit(solution)/shard_map/ppermute | solution.py:274
  272.9 20.3 %collective-permute-start.1 = (bf16[512,512]{1,0:T(8,128)(2,1)}, bf16[512,512]{1,0:T(8,128)(2,1)}, u32[]{:S(2)}, u32[]{:S(2)}) collective-permute-start(bf16[512,512]{1,0:T(8,128)(2,1)} %pad_maximum_fusion), channel_id=1, source_target_pairs={{6,2},{7,3},{8,4},{9,5},{10,6},{11,7},{12,8},{13,9},{14,10},{15,11... | collective-permute-start | bytes 1572872 | tf_op jit(solution)/shard_map/ppermute | solution.py:274
  278.2 16.3 %collective-permute-start.34 = (bf16[512,512]{1,0:T(8,128)(2,1)}, bf16[512,512]{1,0:T(8,128)(2,1)}, u32[]{:S(2)}, u32[]{:S(2)}) collective-permute-start(bf16[512,512]{1,0:T(8,128)(2,1)} %copy-done.10), channel_id=1, source_target_pairs={{7,4},{11,8},{15,12},{23,20},{27,24},{31,28}} | collective-permute-start | bytes 1572872 | tf_op jit(solution)/shard_map/ppermute | solution.py:275
  279.6 20.8 %collective-permute-start.35 = (bf16[512,512]{1,0:T(8,128)(2,1)}, bf16[512,512]{1,0:T(8,128)(2,1)}, u32[]{:S(2)}, u32[]{:S(2)}) collective-permute-start(bf16[512,512]{1,0:T(8,128)(2,1)} %copy-done.12), channel_id=1, source_target_pairs={{4,7},{8,11},{12,15},{20,23},{24,27},{28,31}} | collective-permute-start | bytes 1572872 | tf_op jit(solution)/shard_map/ppermute | solution.py:276
  285.4 16.3 %collective-permute-start.28 = (bf16[512,512]{1,0:T(8,128)(2,1)}, bf16[512,512]{1,0:T(8,128)(2,1)}, u32[]{:S(2)}, u32[]{:S(2)}) collective-permute-start(bf16[512,512]{1,0:T(8,128)(2,1)} %copy-done.18), channel_id=1, source_target_pairs={{7,4},{11,8},{15,12},{23,20},{27,24},{31,28}} | collective-permute-start | bytes 1572872 | tf_op jit(solution)/shard_map/ppermute | solution.py:275
  286.7 20.8 %collective-permute-start.29 = (bf16[512,512]{1,0:T(8,128)(2,1)}, bf16[512,512]{1,0:T(8,128)(2,1)}, u32[]{:S(2)}, u32[]{:S(2)}) collective-permute-start(bf16[512,512]{1,0:T(8,128)(2,1)} %copy-done.20), channel_id=1, source_target_pairs={{4,7},{8,11},{12,15},{20,23},{24,27},{28,31}} | collective-permute-start | bytes 1572872 | tf_op jit(solution)/shard_map/ppermute | solution.py:276
  293.2 16.7 %collective-permute-start.22 = (bf16[512,512]{1,0:T(8,128)(2,1)}, bf16[512,512]{1,0:T(8,128)(2,1)}, u32[]{:S(2)}, u32[]{:S(2)}) collective-permute-start(bf16[512,512]{1,0:T(8,128)(2,1)} %copy-done.26), channel_id=1, source_target_pairs={{7,4},{11,8},{15,12},{23,20},{27,24},{31,28}} | collective-permute-start | bytes 1572872 | tf_op jit(solution)/shard_map/ppermute | solution.py:275
  294.5 17.5 %collective-permute-start.23 = (bf16[512,512]{1,0:T(8,128)(2,1)}, bf16[512,512]{1,0:T(8,128)(2,1)}, u32[]{:S(2)}, u32[]{:S(2)}) collective-permute-start(bf16[512,512]{1,0:T(8,128)(2,1)} %copy-done.28), channel_id=1, source_target_pairs={{4,7},{8,11},{12,15},{20,23},{24,27},{28,31}} | collective-permute-start | bytes 1572872 | tf_op jit(solution)/shard_map/ppermute | solution.py:276
  300.4 12.9 %collective-permute-start.16 = (bf16[512,512]{1,0:T(8,128)(2,1)}, bf16[512,512]{1,0:T(8,128)(2,1)}, u32[]{:S(2)}, u32[]{:S(2)}) collective-permute-start(bf16[512,512]{1,0:T(8,128)(2,1)} %copy-done.34), channel_id=1, source_target_pairs={{7,4},{11,8},{15,12},{23,20},{27,24},{31,28}} | collective-permute-start | bytes 1572872 | tf_op jit(solution)/shard_map/ppermute | solution.py:275
  301.7 20.0 %collective-permute-start.17 = (bf16[512,512]{1,0:T(8,128)(2,1)}, bf16[512,512]{1,0:T(8,128)(2,1)}, u32[]{:S(2)}, u32[]{:S(2)}) collective-permute-start(bf16[512,512]{1,0:T(8,128)(2,1)} %copy-done.36), channel_id=1, source_target_pairs={{4,7},{8,11},{12,15},{20,23},{24,27},{28,31}} | collective-permute-start | bytes 1572872 | tf_op jit(solution)/shard_map/ppermute | solution.py:276
  307.5 15.5 %collective-permute-start.10 = (bf16[512,512]{1,0:T(8,128)(2,1)}, bf16[512,512]{1,0:T(8,128)(2,1)}, u32[]{:S(2)}, u32[]{:S(2)}) collective-permute-start(bf16[512,512]{1,0:T(8,128)(2,1)} %collective-permute-done.6.earlier), channel_id=1, source_target_pairs={{7,4},{11,8},{15,12},{23,20},{27,24},{31,28}} | collective-permute-start | bytes 1572872 | tf_op jit(solution)/shard_map/ppermute | solution.py:275
  309.9 61.6 %collective-permute-start.2 = (bf16[512,512]{1,0:T(8,128)(2,1)}, bf16[512,512]{1,0:T(8,128)(2,1)}, u32[]{:S(2)}, u32[]{:S(2)}) collective-permute-start(bf16[512,512]{1,0:T(8,128)(2,1)} %pad_maximum_fusion), channel_id=1, source_target_pairs={{2,3},{4,5},{6,7},{8,9},{10,11},{12,13},{14,15},{0,1},{15,0},{18,1... | collective-permute-start | bytes 1572872 | tf_op jit(solution)/shard_map/ppermute | solution.py:274
  312.0 59.5 %collective-permute-start.3 = (bf16[512,512]{1,0:T(8,128)(2,1)}, bf16[512,512]{1,0:T(8,128)(2,1)}, u32[]{:S(2)}, u32[]{:S(2)}) collective-permute-start(bf16[512,512]{1,0:T(8,128)(2,1)} %pad_maximum_fusion), channel_id=1, source_target_pairs={{3,2},{5,4},{7,6},{9,8},{11,10},{13,12},{15,14},{1,0},{4,3},{19,18... | collective-permute-start | bytes 1572872 | tf_op jit(solution)/shard_map/ppermute | solution.py:274
  313.3 51.6 %collective-permute-start.11 = (bf16[512,512]{1,0:T(8,128)(2,1)}, bf16[512,512]{1,0:T(8,128)(2,1)}, u32[]{:S(2)}, u32[]{:S(2)}) collective-permute-start(bf16[512,512]{1,0:T(8,128)(2,1)} %collective-permute-done.7.later), channel_id=1, source_target_pairs={{4,7},{8,11},{12,15},{20,23},{24,27},{28,31}} | collective-permute-start | bytes 1572872 | tf_op jit(solution)/shard_map/ppermute | solution.py:276
  321.7 49.8 %collective-permute-start.4 = (bf16[512,512]{1,0:T(8,128)(2,1)}, bf16[512,512]{1,0:T(8,128)(2,1)}, u32[]{:S(2)}, u32[]{:S(2)}) collective-permute-start(bf16[512,512]{1,0:T(8,128)(2,1)} %collective-permute-done.earlier), channel_id=1, source_target_pairs={{7,4},{11,8},{15,12},{23,20},{27,24},{31,28}} | collective-permute-start | bytes 1572872 | tf_op jit(solution)/shard_map/ppermute | solution.py:275
  323.0 48.5 %collective-permute-start.5 = (bf16[512,512]{1,0:T(8,128)(2,1)}, bf16[512,512]{1,0:T(8,128)(2,1)}, u32[]{:S(2)}, u32[]{:S(2)}) collective-permute-start(bf16[512,512]{1,0:T(8,128)(2,1)} %collective-permute-done.1.later), channel_id=1, source_target_pairs={{4,7},{8,11},{12,15},{20,23},{24,27},{28,31}} | collective-permute-start | bytes 1572872 | tf_op jit(solution)/shard_map/ppermute | solution.py:276
  (44 other events, 418.3 us)
Sparse Core Ops, SparseCore 0:
  20.1 89.5 all-reduce.3
  125.0 96.5 reduce-scatter.1

commit v2 on v0

v2 whole, which is shorter than its diff:
```python
import functools
import math

import jax
import jax.numpy as jnp
from jax import lax
from jax.experimental import pallas as pl
from jax.experimental.pallas import tpu as pltpu
from jax.sharding import PartitionSpec as P

HEADS = 24
HD = 128
NR = 4
BLOCKS = 5
STEP_HEADS = 2
CHUNK_HEADS = (8, 6, 6, 4)
DIVERTED = (False, True, True, False)
PAD_ROWS = 16
VMEM_BYTES = 48 * 1024 * 1024
LOG2E = 1.4426950408889634
SOURCES = ("own", "earlier", "later", "relayed", "above", "below")


def spot_shift(n):
    return n // 2 + NR + NR // 2


def plan_moves(n, diverted):
    shift, times = spot_shift(n), n // NR
    last = times - 1

    def at(t, r):
        return (t * NR + r - shift) % n

    moves = {
        "earlier": {at(t - 1, r): at(t, r) for t in range(1, times) for r in range(NR)},
        "later": {at(t + 1, r): at(t, r) for t in range(last) for r in range(NR)},
        "above": {at(t, r - 1): at(t, r) for t in range(times) for r in (1, 3)},
        "below": {at(t, r + 1): at(t, r) for t in range(times) for r in (0, 2)},
    }
    relay_earlier = {at(t + 1, 1): at(t, 2) for t in range(last)}
    relay_later = {at(t - 1, 2): at(t, 1) for t in range(1, times)}
    if times == 4:
        moves["later"][at(0, 2)] = at(3, 2)
        relay_later[at(3, 2)] = at(0, 1)
        moves["later"][at(3, 3)] = at(3, 0)
        relay_later[at(3, 0)] = at(2, 3)
        if diverted:
            moves["earlier"][at(2, 2)] = at(0, 0)
            relay_earlier[at(0, 0)] = at(3, 2)
            moves["earlier"][at(2, 3)] = at(0, 1)
            relay_earlier[at(0, 1)] = at(3, 3)
            moves["earlier"][at(3, 1)] = at(3, 2)
        else:
            moves["earlier"][at(3, 1)] = at(0, 1)
            relay_earlier[at(0, 1)] = at(3, 2)
    else:
        moves["above"][at(last, 1)] = at(last, 2)
        moves["below"][at(0, 2)] = at(0, 1)
    assert not set(relay_earlier) & set(relay_later)
    moves["relayed"] = {**relay_earlier, **relay_later}
    held = {"own": {d: d for d in range(n)}}
    for name in ("earlier", "later", "above", "below"):
        held[name] = {dst: src for src, dst in moves[name].items()}
    held["relayed"] = {dst: held["earlier"].get(src) for src, dst in relay_earlier.items()}
    held["relayed"].update({dst: held["later"].get(src) for src, dst in relay_later.items()})
    choice = []
    for device in range(n):
        spot = (device + shift) % n
        t, r = spot // NR, spot % NR
        row = []
        for dt, dr in ((-1, 0), (1, 0), (0, -1), (0, 1)):
            found = -1
            if 0 <= t + dt < times and 0 <= r + dr < NR:
                wanted = at(t + dt, r + dr)
                found = [i for i, s in enumerate(SOURCES) if held[s].get(device) == wanted][0]
            row.append(found)
        choice.append(row)
    for move in moves.values():
        assert len(set(move.values())) == len(move)
    pairs = {name: sorted(move.items()) for name, move in moves.items()}
    return pairs, [int(d in relay_later) for d in range(n)], choice


def dot_nt(a, b):
    return lax.dot_general(a, b, (((1,), (1,)), ((), ())), preferred_element_type=jnp.float32)


def dot_nn(a, b):
    return jnp.dot(a, b, preferred_element_type=jnp.float32)


def lane_tiles(x):
    return [x[:, i : i + HD] for i in range(0, x.shape[1], HD)]


def row_reduce(op, final, pieces):
    tiles = [tile for piece in pieces for tile in lane_tiles(piece)]
    return final(functools.reduce(op, tiles), axis=1, keepdims=True)


TABLE_COUNTS, TABLE_TEXT, TABLE_CHOICE = 4, 6, 7


def video_kernel(kind, table, q, k_own, v_own, *rest):
    packed = {"earlier": rest[0], "later": rest[1], "above": rest[4], "below": rest[5]}
    relayed_k, relayed_v, text_k, text_v = rest[2], rest[3], rest[6], rest[7]
    out, k_all, v_all, bias_all = rest[-4:]
    tok = q.shape[0] // 2
    text = text_k.shape[0]
    scale = LOG2E / math.sqrt(HD)
    near = BLOCKS * tok
    dead = 2 * BLOCKS
    lane = lax.broadcasted_iota(jnp.int32, (8, tok), 1)
    lane_f = lane.astype(jnp.float32)

    def put(block, k, v, v_row):
        for i in range(STEP_HEADS):
            cols = pl.ds(i * HD, HD)
            for c in range(2):
                rows = pl.ds((c * BLOCKS + block) * tok, tok)
                k_all[i, rows, :] = k[pl.ds(c * tok, tok), cols]
                v_all[i, rows, :] = v[pl.ds(v_row + c * tok, tok), cols]

    def put_limits(block, tail):
        limits = tail[...].astype(jnp.float32)
        for c in range(2):
            bias_all[c * BLOCKS + block] = jnp.where(lane_f < limits[c : c + 1, :], 0.0, -jnp.inf)

    put(0, k_own, v_own, 0)
    for c in range(2):
        bias_all[c * BLOCKS] = jnp.where(lane < table[TABLE_COUNTS + c], 0.0, -jnp.inf)
    tail = (pl.ds(2 * tok, PAD_ROWS), pl.ds(0, HD))
    options = {1: ("earlier",), 2: ("later",), 3: ("above", "earlier"), 4: ("below", "later")}
    zeros = jnp.zeros((tok, HD), k_all.dtype)
    for block in range(1, BLOCKS):
        chosen = table[TABLE_CHOICE + 4 * kind + block - 1]
        for name in options[block]:

            @pl.when(chosen == SOURCES.index(name))
            def _(ref=packed[name], block=block):
                put(block, ref, ref, 2 * tok + PAD_ROWS)
                put_limits(block, ref.at[tail])

        @pl.when(chosen == SOURCES.index("relayed"))
        def _(block=block):
            put(block, relayed_k, relayed_v, 0)
            put_limits(block, relayed_k.at[tail])

        @pl.when(chosen < 0)
        def _(block=block):
            for c in range(2):
                bias_all[c * BLOCKS + block] = jnp.full((8, tok), -jnp.inf, jnp.float32)
                for i in range(STEP_HEADS):
                    rows = pl.ds((c * BLOCKS + block) * tok, tok)
                    k_all[i, rows, :] = zeros
                    v_all[i, rows, :] = zeros

    bias_all[dead] = jnp.full((8, tok), -jnp.inf, jnp.float32)
    for i in range(STEP_HEADS):
        k_all[i, pl.ds(dead * tok, tok), :] = zeros
        v_all[i, pl.ds(dead * tok, tok), :] = zeros

    text_lane = lax.broadcasted_iota(jnp.int32, (1, text), 1)
    text_bias = jnp.where(text_lane < table[TABLE_TEXT], 0.0, -jnp.inf)
    slot = lax.broadcasted_iota(jnp.int32, (tok, 1), 0)
    for i in range(STEP_HEADS):
        cols = pl.ds(i * HD, HD)
        for c in range(2):
            query = q[pl.ds(c * tok, tok), cols]
            fixed = pl.ds(c * near, near)
            fixed_bias = jnp.concatenate(
                [bias_all[c * BLOCKS + b][0:1] for b in range(BLOCKS)], axis=1
            )
            scores = [dot_nt(query, k_all[i, fixed, :]) + fixed_bias]
            values = [v_all[i, fixed, :]]
            for j in range(2):
                cell = table[2 * c + j]
                rows = pl.ds(pl.multiple_of(cell * tok, tok), tok)
                scores.append(dot_nt(query, k_all[i, rows, :]) + bias_all[cell][0:1])
                values.append(v_all[i, rows, :])
            scores.append(dot_nt(query, text_k[:, cols]) + text_bias)
            values.append(text_v[:, cols])
            top = row_reduce(jnp.maximum, jnp.max, scores)
            probs = [jnp.exp2((s - top) * scale) for s in scores]
            denom = row_reduce(jnp.add, jnp.sum, probs)
            acc = sum(dot_nn(p.astype(jnp.bfloat16), v) for p, v in zip(probs, values))
            valid = slot < table[TABLE_COUNTS + c]
            out[pl.ds(c * tok, tok), cols] = jnp.where(valid, acc / denom, 0.0).astype(out.dtype)


def video_call(kind, first, heads, table, q, k, v, near, text_k, text_v, carried):
    rows, width = q.shape
    text = text_k.shape[0]
    tok = rows // 2
    step = STEP_HEADS * HD
    base = first // STEP_HEADS
    whole = lambda h: (0, base + h)
    part = lambda h: (0, h)
    own_spec = pl.BlockSpec((rows, step), whole)
    part_spec = pl.BlockSpec((2 * rows + PAD_ROWS, step), part)
    whole_spec = pl.BlockSpec((2 * rows + PAD_ROWS, step), whole)
    text_spec = pl.BlockSpec((text, step), whole)
    in_specs = [pl.BlockSpec(memory_space=pltpu.SMEM), own_spec, own_spec, own_spec]
    in_specs += [part_spec] * 2
    in_specs += [pl.BlockSpec((rows + PAD_ROWS, step), part), pl.BlockSpec((rows, step), part)]
    in_specs += [whole_spec] * 2 + [text_spec] * 2
    operands = [table, q, k, v, *near, text_k, text_v]
    aliases = {}
    if carried is not None:
        aliases = {len(operands): 0}
        operands.append(carried)
        in_specs.append(pl.BlockSpec(memory_space=pl.ANY))
    cells = 2 * BLOCKS + 1
    keys = 7 * tok + text
    return pl.pallas_call(
        functools.partial(video_kernel, kind),
        grid=(heads // STEP_HEADS,),
        in_specs=in_specs,
        out_specs=own_spec,
        out_shape=jax.ShapeDtypeStruct((rows, width), q.dtype),
        scratch_shapes=[
            pltpu.VMEM((STEP_HEADS, cells * tok, HD), q.dtype),
            pltpu.VMEM((STEP_HEADS, cells * tok, HD), q.dtype),
            pltpu.VMEM((cells, 8, tok), jnp.float32),
        ],
        input_output_aliases=aliases,
        compiler_params=pltpu.CompilerParams(vmem_limit_bytes=VMEM_BYTES),
        cost_estimate=pl.CostEstimate(
            flops=heads * rows * keys * HD // 4,
            bytes_accessed=heads * rows * HD,
            transcendentals=0,
        ),
        name="video_attention",
    )(*operands)


STAT_SUMS = 32


def text_kernel(order, counts, q, k, v, keep, send, top, denom):
    step = pl.program_id(0)
    rows = k.shape[0]
    text = q.shape[0]
    half = text // 2
    share = text // order.shape[0]
    lane = lax.broadcasted_iota(jnp.int32, (text, HD), 1)

    @pl.when(step == 0)
    def _():
        top[...] = jnp.zeros_like(top)
        denom[...] = jnp.zeros_like(denom)

    @pl.when(step < HEADS // STEP_HEADS)
    def _():
        slot = lax.broadcasted_iota(jnp.int32, (1, rows // 2), 1)
        bias = jnp.concatenate(
            [jnp.where(slot < counts[c], 0.0, -jnp.inf) for c in range(2)], axis=1
        )
        for i in range(STEP_HEADS):
            cols = pl.ds(i * HD, HD)
            head = step * STEP_HEADS + i
            query = jnp.concatenate(
                [
                    q[pl.ds(pl.multiple_of(order[j] * share, share), share), cols]
                    for j in range(order.shape[0])
                ],
                axis=0,
            )
            s = dot_nt(query, k[:, cols]) * (1.0 / math.sqrt(HD)) + bias
            m = row_reduce(jnp.maximum, jnp.max, [s])
            w = jnp.exp(s - m)
            l = row_reduce(jnp.add, jnp.sum, [w])
            high = w.astype(jnp.bfloat16)
            low = (w - high.astype(jnp.float32)).astype(jnp.bfloat16)
            acc = dot_nn(high, v[:, cols]) + dot_nn(low, v[:, cols])
            top[...] = jnp.where(lane == head, m, top[...])
            denom[...] = jnp.where(lane == head + STAT_SUMS, l, denom[...])
            keep[:, cols] = acc[:half]
            send[:, cols] = acc[half:]

    @pl.when(step == HEADS // STEP_HEADS)
    def _():
        stats = top[...] + denom[...]
        keep[:, pl.ds(0, HD)] = stats[:half]
        send[:, pl.ds(0, HD)] = stats[half:]


def text_local(order, counts, q, k, v):
    text = q.shape[0]
    rows = k.shape[0]
    step = STEP_HEADS * HD
    last = HEADS // STEP_HEADS - 1
    smem = pl.BlockSpec(memory_space=pltpu.SMEM)
    q_spec = pl.BlockSpec((text, step), lambda h: (0, jnp.minimum(h, last)))
    k_spec = pl.BlockSpec((rows, step), lambda h: (0, jnp.minimum(h, last)))
    out_spec = pl.BlockSpec((text // 2, step), lambda h: (0, h))
    shape = jax.ShapeDtypeStruct((text // 2, HEADS * HD + step), jnp.float32)
    work = HEADS * text * rows
    return pl.pallas_call(
        text_kernel,
        grid=(last + 2,),
        in_specs=[smem, smem, q_spec, k_spec, k_spec],
        out_specs=[out_spec, out_spec],
        out_shape=[shape, shape],
        scratch_shapes=[pltpu.VMEM((text, HD), jnp.float32)] * 2,
        compiler_params=pltpu.CompilerParams(vmem_limit_bytes=VMEM_BYTES),
        cost_estimate=pl.CostEstimate(
            flops=work * HD // 4, bytes_accessed=text * HEADS * HD, transcendentals=0
        ),
        name="text_partials",
    )(order, counts, q, k, v)


def merge_kernel(finish, *refs):
    width = HEADS * HD
    stat_cols = pl.ds(width, HD)
    keep, got = refs[:2]
    mine = keep[:, stat_cols]
    theirs = got[:, stat_cols]
    lane = lax.broadcasted_iota(jnp.int32, mine.shape, 1)
    is_top = lane < STAT_SUMS
    top = jnp.maximum(mine, theirs)
    a = jnp.exp(jnp.where(is_top, mine - top, 0.0))
    b = jnp.exp(jnp.where(is_top, theirs - top, 0.0))
    sums = []
    for h in range(HEADS):
        at = slice(h, h + 1)
        to = slice(STAT_SUMS + h, STAT_SUMS + h + 1)
        sums.append(mine[:, to] * a[:, at] + theirs[:, to] * b[:, at])
    if finish:
        limit, out = refs[2:]
        share = out.shape[0]
        row = lax.broadcasted_iota(jnp.int32, (share, 1), 0)
        valid = row < limit[0]
        for h in range(HEADS):
            cols = pl.ds(h * HD, HD)
            at = slice(h, h + 1)
            acc = keep[:, cols] * a[:, at] + got[:, cols] * b[:, at]
            out[:, cols] = jnp.where(valid, acc / sums[h], 0.0).astype(out.dtype)
        return
    next_keep, next_send = refs[2:]
    half = next_keep.shape[0]
    stats = jnp.where(is_top, top, 0.0)
    for h in range(HEADS):
        cols = pl.ds(h * HD, HD)
        at = slice(h, h + 1)
        acc = keep[:, cols] * a[:, at] + got[:, cols] * b[:, at]
        stats = jnp.where(lane == STAT_SUMS + h, sums[h], stats)
        next_keep[:, cols] = acc[:half]
        next_send[:, cols] = acc[half:]
    next_keep[:, stat_cols] = stats[:half]
    next_send[:, stat_cols] = stats[half:]


def text_merge(keep, got):
    half = keep.shape[0] // 2
    shape = jax.ShapeDtypeStruct((half, (HEADS + 1) * HD), jnp.float32)
    return pl.pallas_call(
        functools.partial(merge_kernel, False),
        out_shape=[shape, shape],
        compiler_params=pltpu.CompilerParams(vmem_limit_bytes=VMEM_BYTES),
        name="text_merge",
    )(keep, got)


def text_finish(keep, got, limit):
    share = keep.shape[0]
    vmem = pl.BlockSpec(memory_space=pltpu.VMEM)
    return pl.pallas_call(
        functools.partial(merge_kernel, True),
        in_specs=[vmem, vmem, pl.BlockSpec(memory_space=pltpu.SMEM)],
        out_shape=jax.ShapeDtypeStruct((share, HEADS * HD), jnp.bfloat16),
        compiler_params=pltpu.CompilerParams(vmem_limit_bytes=VMEM_BYTES),
        name="text_finish",
    )(keep, got, limit)


def slot_order(n, position):
    bits = n.bit_length() - 1
    mirrored = [int(format(i, f"0{bits}b")[::-1], 2) for i in range(n)]
    return jnp.array(mirrored, jnp.int32) ^ position.astype(jnp.int32)


def text_plain(position, n, text_count, q, k, v, counts):
    text, width = q.shape
    share = text // n
    keys = k.reshape(-1, HEADS, HD)
    values = v.reshape(-1, HEADS, HD)
    slots = jnp.arange(k.shape[0] // counts.shape[0], dtype=jnp.int32)
    valid = (slots[None, :] < counts[:, None]).reshape(-1)
    scores = jnp.einsum(
        "qhd,khd->hqk", q.reshape(text, HEADS, HD), keys, preferred_element_type=jnp.float32
    ) * (1.0 / math.sqrt(HD))
    scores = jnp.where(valid[None, None, :], scores, -jnp.inf)
    top = lax.pmax(jnp.max(scores, axis=-1), "tiles")
    weights = jnp.exp(scores - top[..., None])
    denom = jnp.sum(weights, axis=-1).T
    numer = jnp.einsum(
        "hqk,khd->qhd", weights.astype(jnp.bfloat16), values, preferred_element_type=jnp.float32
    ).reshape(text, width)
    numer = lax.psum_scatter(numer, "tiles", scatter_dimension=0, tiled=True)
    denom = lax.psum_scatter(denom, "tiles", scatter_dimension=0, tiled=True)
    result = numer.reshape(share, HEADS, HD) / denom[:, :, None]
    row_ids = position * share + jnp.arange(share, dtype=jnp.int32)
    result = jnp.where((row_ids < text_count[0])[:, None, None], result, 0.0)
    return result.astype(jnp.bfloat16).reshape(share, width)


def make_table(window, counts, text_count, choices, position):
    columns = counts.shape[0]
    extra = (window % 3 != 0) | (window == 0)
    rank = jnp.cumsum(extra.astype(jnp.int32), axis=1) * extra
    codes = jnp.stack([jnp.sum(jnp.where(rank == j, window, 0), axis=1) for j in (1, 2)], axis=1)
    cells = codes + (codes >= 1)
    own = jnp.arange(columns, dtype=jnp.int32)[:, None]
    column = own + cells % 3 - 1
    inside = (column >= 0) & (column < columns)
    extra_cells = jnp.where(inside, column * BLOCKS + cells // 3, columns * BLOCKS)
    chosen = lax.dynamic_index_in_dim(jnp.array(choices, jnp.int32), position, 0, False)
    parts = [extra_cells.reshape(-1), counts, text_count, chosen]
    return jnp.concatenate([part.astype(jnp.int32) for part in parts])


def tie(value, *others):
    return lax.optimization_barrier((value, *others))[0]


def per_device(n, video_q, video_k, video_v, text_q, text_k, text_v, window, counts, text_count):
    rows, width = video_q.shape
    text = text_q.shape[0]
    position = lax.axis_index("tiles")
    plans = [plan_moves(n, kind) for kind in (False, True)]
    choices = [plans[0][2][d] + plans[1][2][d] for d in range(n)]
    sends_later = jnp.array(plans[0][1], jnp.int32)[position] == 1
    table = make_table(window, counts, text_count, choices, position)

    limits = jnp.concatenate([counts, jnp.zeros((PAD_ROWS - counts.shape[0],), jnp.int32)])
    limits = jnp.broadcast_to(limits.astype(jnp.bfloat16)[:, None], (PAD_ROWS, width))

    def pack(cols):
        return jnp.concatenate([video_k[:, cols], limits[:, cols], video_v[:, cols]], axis=0)

    starts = [sum(CHUNK_HEADS[:i]) for i in range(len(CHUNK_HEADS))]
    direct, outs = [], []

    def send(i, *before):
        cols = slice(starts[i] * HD, (starts[i] + CHUNK_HEADS[i]) * HD)
        mine = tie(pack(cols), *before)
        pairs = plans[DIVERTED[i]][0]
        direct.append([lax.ppermute(mine, "tiles", pairs[x]) for x in ("earlier", "later")])

    send(0)
    everything = pack(slice(0, width))
    sides = [lax.ppermute(everything, "tiles", plans[0][0][x]) for x in ("above", "below")]
    halving = text % (PAD_ROWS * n) == 0 and n & (n - 1) == 0
    stages = n.bit_length() - 1
    parts = []
    if halving:
        order = tie(slot_order(n, position), *sides)
        parts = [text_local(order, counts, text_q, video_k, video_v)]

    def exchanged(i):
        return lax.ppermute(parts[i][1], "tiles", [(d, d ^ (1 << i)) for d in range(n)])

    def merge(*before):
        i = len(parts) - 1
        if 0 <= i < stages - 1:
            parts.append(text_merge(tie(parts[i][0], *before), exchanged(i)))

    for i in range(len(CHUNK_HEADS)):
        pairs = plans[DIVERTED[i]][0]
        if i + 1 < len(CHUNK_HEADS):
            before = outs[-1:] + ([parts[-1][0]] if halving else [])
            send(i + 1, *direct[i], *before)
        up, down = direct[i]
        if i + 1 == len(CHUNK_HEADS):
            before = outs[-1:]
            if halving:
                limit = text_count - position.astype(jnp.int32) * (text // n)
                text_out = text_finish(parts[-1][0], exchanged(stages - 1), limit)
                before.append(text_out)
            up, down = tie(up, *before), tie(down, *before)
        relays = [
            lax.ppermute(jnp.where(sends_later, down[half], up[half]), "tiles", pairs["relayed"])
            for half in (slice(0, rows + PAD_ROWS), slice(rows + PAD_ROWS, None))
        ]
        merge(*relays)
        outs.append(
            video_call(
                int(DIVERTED[i]), starts[i], CHUNK_HEADS[i], table, video_q, video_k, video_v,
                [*direct[i], *relays, *sides], text_k, text_v, outs[-1] if outs else None,
            )
        )
        merge(outs[-1])
    if not halving:
        text_out = text_plain(position, n, text_count, text_q, video_k, video_v, counts)
    return (outs[-1], text_out)


def solution(mesh):
    tiles = mesh.shape["tiles"]
    return jax.shard_map(
        functools.partial(per_device, tiles),
        mesh=mesh,
        in_specs=(
            P(("groups", "tiles"), None),
            P(("groups", "tiles"), None),
            P(("groups", "tiles"), None),
            P("groups", None),
            P("groups", None),
            P("groups", None),
            P("tiles", None),
            P(("groups", "tiles")),
            P("groups"),
        ),
        out_specs=(P(("groups", "tiles"), None), P(("groups", "tiles"), None)),
        check_vma=False,
    )
```

time: 411 us -> 245 us (0.60); the launches traced: 404 us -> 242 us
  local copies, waits for them, and re-layouts: 119 us -> 12.2 us
  blocking collectives: 70.7 us -> 0 us
  Pallas kernels: 0 us -> 53.3 us
  matrix products: 43.2 us -> 0 us
  starting transfers between devices: 22.7 us -> 57.7 us
  waiting for transfers between devices: 116 us -> 98.7 us
  between operations: 14.9 us -> 2.38 us
    pmax x1 -> x0, blocking collectives: 70.7 us -> none  [per_device(): global_top = lax.pmax(local_top, 'tiles')]
    pallas_call x0 -> x9, Pallas kernels: none -> 53.3 us  [the longest x4 34.8 us: video_call(): pl.pallas_call(functools.partial(video_kernel, kind), grid=(heads // STEP...]
    dot_general x10 -> x0, matrix products: 43.2 us -> none  [the longest x2 21.1 us: one_tile(): jnp.einsum('hqk,khd->qhd', video_probs.astype(jnp.bfloat16), values_chose...]
    gather x6 -> x0, local copies, waits for them, and re-layouts: 36.6 us -> none  [the longest x2 17.8 us: one_tile(): keys_chosen = key_flat[flat_row].reshape(-1, HEADS, HD)]
    ppermute x12 -> x22, starting transfers between devices: 22.7 us -> 57.7 us  [the longest x8 25.6 us: send(): lax.ppermute(mine, 'tiles', pairs[x])]
    while x20 -> x0, local copies, waits for them, and re-layouts: 22.8 us -> none
    unnamed x30 -> x42, local copies, waits for them, and re-layouts: 28.2 us -> 10.5 us
    ppermute x12 -> x22, waiting for transfers between devices: 116 us -> 98.7 us  [the longest x4 37 us: exchanged(): lax.ppermute(parts[i][1], 'tiles', [(d, d ^ 1 << i) for d in range(n)])]
  transfers between devices with their start and end apart: 14 -> 22, of which waited for: 5 -> 7; matrix products, arithmetic and copies ran while one was open for 43% -> 5% of each run, Pallas kernels for 0% -> 19%
where the time goes in v2:
time: 245 us; the launch traced here: 242 us
  waiting for transfers between devices  98.7 us (40%)
  starting transfers between devices  57.7 us (24%)
  Pallas kernels  53.3 us (22%)
  other arithmetic  17.8 us (7%)
  local copies, waits for them, and re-layouts  12.2 us (5%)
    ppermute x4, waiting for transfers between devices, exchanged(): lax.ppermute(parts[i][1], 'tiles', [(d, d ^ 1 << i) for d in range(n)])  37 us
    pallas_call x4, Pallas kernels, video_call(): pl.pallas_call(functools.partial(video_kernel, kind), grid=(heads // STEP...  34.8 us
    ppermute x8, waiting for transfers between devices, per_device(): lax.ppermute(jnp.where(sends_later, down[half], up[half]), 'tiles', pairs...  34.6 us
    ppermute x8, waiting for transfers between devices, send(): lax.ppermute(mine, 'tiles', pairs[x])  27.1 us
    ppermute x8, starting transfers between devices, send(): lax.ppermute(mine, 'tiles', pairs[x])  25.6 us
    ppermute x8, starting transfers between devices, per_device(): lax.ppermute(jnp.where(sends_later, down[half], up[half]), 'tiles', pairs...  22.2 us
    unnamed x42, local copies, waits for them, and re-layouts  10.5 us
    pallas_call x1, Pallas kernels, text_local(): pl.pallas_call(text_kernel, grid=(last + 2,), in_specs=[smem, smem, q_spe...  9.74 us
  transfers between devices with their start and end apart: 22, of which 7 were waited for; matrix products, arithmetic and copies ran while one was open for 5% of the time, Pallas kernels for 19%

profile of v2, /device:TPU:24, one launch (start us, length us, event | category | flops | bytes accessed | tf_op | source)
XLA Modules:
  0.0 242.2 jit_solution(8282779869141162164)
XLA Ops:
  1.3 4.5 %pad_maximum_fusion = bf16[528,3072]{1,0:T(8,128)(2,1)} fusion(bf16[256,3072]{1,0:T(8,128)(2,1)} %v_own.7, bf16[256,3072]{1,0:T(8,128)(2,1)} %k_own.7, bf16[528]{0:T(1024)(128)(2,1)S(1)} %pad.15.clone), kind=kLoop, calls=%fused_computation | loop fusion | flops 9732096 | bytes 6390816 | tf_op jit(solution)/shard_map/concatenate | solution.py:442
  5.8 3.5 %collective-permute-start.2 = (bf16[528,3072]{1,0:T(8,128)(2,1)}, bf16[528,3072]{1,0:T(8,128)(2,1)}, u32[]{:S(2)}, u32[]{:S(2)}) collective-permute-start(bf16[528,3072]{1,0:T(8,128)(2,1)} %pad_maximum_fusion), channel_id=1, source_target_pairs={{0,1},{2,3},{4,5},{6,7},{8,9},{10,11},{12,13},{14,15},{16,17},{18,... | collective-permute-start | bytes 9732104 | tf_op jit(solution)/shard_map/ppermute | solution.py:455
  9.4 1.3 collective-permute-start.3
  10.7 1.2 pad_maximum_fusion.1
  11.9 1.9 collective-permute-start
  13.8 3.9 %collective-permute-start.1 = (bf16[528,1024]{1,0:T(8,128)(2,1)}, bf16[528,1024]{1,0:T(8,128)(2,1)}, u32[]{:S(2)}, u32[]{:S(2)}) collective-permute-start(bf16[528,1024]{1,0:T(8,128)(2,1)} %pad_maximum_fusion.1), channel_id=1, source_target_pairs={{0,12},{1,14},{4,0},{6,2},{7,3},{8,4},{9,5},{10,6},{11,7},{12,8},{... | collective-permute-start | bytes 3244040 | tf_op jit(solution)/shard_map/ppermute | solution.py:451
  17.9 1.4 copy-done.1
  19.3 1.4 copy-done.9
  20.7 9.7 %text_partials.1 = (f32[128,3328]{1,0:T(8,128)}, f32[128,3328]{1,0:T(8,128)}) custom-call(s32[16]{0:T(128)S(1)} %broadcast_xor_fusion.order, s32[2]{0:T(128)S(1)} %copy-done.16, bf16[256,3072]{1,0:T(8,128)(2,1)S(1)} %copy-done.9, bf16[256,3072]{1,0:T(8,128)(2,1)S(1)} %copy-done, bf16[256,3072]{1,0:T(8,128)(2,1)S(1)} %copy-done.1), custom_call_target="tpu_custom_call" | custom-call | flops 50331648 | bytes 786432 | tf_op jit(solution)/shard_map/text_partials/pallas_call | solution.py:300
  30.4 3.3 %collective-permute-start.8 = (f32[128,3328]{1,0:T(8,128)}, f32[128,3328]{1,0:T(8,128)}, u32[]{:S(2)}, u32[]{:S(2)}) collective-permute-start(f32[128,3328]{1,0:T(8,128)} %get-tuple-element.23), channel_id=1, source_target_pairs={{0,1},{1,0},{2,3},{3,2},{4,5},{5,4},{6,7},{7,6},{8,9},{9,8},{10,11... | collective-permute-start | bytes 5111816 | tf_op jit(solution)/shard_map/ppermute | solution.py:464
  34.9 27.1 %collective-permute-done.rest_0_ = bf16[528,1024]{1,0:T(8,128)(2,1)S(1)} collective-permute-done((bf16[528,1024]{1,0:T(8,128)(2,1)}, bf16[528,1024]{1,0:T(8,128)(2,1)S(1)}, u32[]{:S(2)}, u32[]{:S(2)}) %collective-permute-start) | collective-permute-done | bytes 1081376 | tf_op jit(solution)/shard_map/ppermute | solution.py:451
  62.0 1.2 slice_select_fusion
  63.3 1.9 collective-permute-start.6
  65.2 1.1 slice_select_fusion.1
  66.3 3.6 %collective-permute-start.7 = (bf16[256,1024]{1,0:T(8,128)(2,1)S(1)}, bf16[256,1024]{1,0:T(8,128)(2,1)S(1)}, u32[]{:S(2)}, u32[]{:S(2)}) collective-permute-start(bf16[256,1024]{1,0:T(8,128)(2,1)S(1)} %slice_select_fusion.1), channel_id=1, source_target_pairs={{0,3},{3,0},{4,7},{7,4},{8,11},{11,8},{12,15},{14,13},{15,12},{16,... | collective-permute-start | bytes 1572872 | tf_op jit(solution)/shard_map/ppermute | solution.py:485
  70.1 1.5 pad_maximum_fusion.3
  71.6 2.0 collective-permute-start.4
  73.7 3.9 %collective-permute-start.5 = (bf16[528,768]{1,0:T(8,128)(2,1)}, bf16[528,768]{1,0:T(8,128)(2,1)}, u32[]{:S(2)}, u32[]{:S(2)}) collective-permute-start(bf16[528,768]{1,0:T(8,128)(2,1)} %get-tuple-element.21), channel_id=1, source_target_pairs={{0,12},{1,14},{4,0},{6,2},{7,3},{8,4},{9,5},{10,6},{11,7},{12,8},{... | collective-permute-start | bytes 2433032 | tf_op jit(solution)/shard_map/ppermute | solution.py:451
  77.6 11.8 %collective-permute-done.7.rest_3_ = bf16[256,1024]{1,0:T(8,128)(2,1)S(1)} collective-permute-done((bf16[256,1024]{1,0:T(8,128)(2,1)S(1)}, bf16[256,1024]{1,0:T(8,128)(2,1)S(1)}, u32[]{:S(2)}, u32[]{:S(2)}) %collective-permute-start.7) | collective-permute-done | bytes 524320 | tf_op jit(solution)/shard_map/ppermute | solution.py:485
  90.2 3.8 %text_merge.3 = (f32[64,3200]{1,0:T(8,128)S(1)}, f32[64,3200]{1,0:T(8,128)}) custom-call(f32[128,3328]{1,0:T(8,128)S(1)} %copy-done.8, f32[128,3328]{1,0:T(8,128)} %collective-permute-done.8.refs_1_), custom_call_target="tpu_custom_call" | custom-call | tf_op jit(solution)/shard_map/text_merge/pallas_call | solution.py:359
  94.9 1.5 collective-permute-start.9
  98.5 1.4 copy-done.3
  100.9 11.1 %video_attention.4.rest_8_ = bf16[256,3072]{1,0:T(8,128)(2,1)} custom-call(s32[15]{0:T(128)S(1)} %pad_add_fusion.1.table, bf16[256,3072]{1,0:T(8,128)(2,1)S(1)} %copy-done.3, bf16[256,3072]{1,0:T(8,128)(2,1)} %k_own.7, bf16[256,3072]{1,0:T(8,128)(2,1)} %v_own.7, bf16[528,1024]{1,0:T(8,128)(2,1)S(1)} %collective-permute-done.rest_0_, ...), custom_call_target="tpu_custom_call" | custom-call | flops 75497472 | bytes 262144 | tf_op jit(solution)/shard_map/video_attention/pallas_call | solution.py:216
  112.0 3.3 %collective-permute-done.9.refs_1_ = f32[64,3200]{1,0:T(8,128)} collective-permute-done((f32[64,3200]{1,0:T(8,128)}, f32[64,3200]{1,0:T(8,128)}, u32[]{:S(2)}, u32[]{:S(2)}) %collective-permute-start.9) | collective-permute-done | bytes 819232 | tf_op jit(solution)/shard_map/ppermute | solution.py:464
  115.3 1.9 text_merge.4
  117.3 2.1 collective-permute-start.10
  119.4 3.9 %collective-permute-start.11 = (bf16[528,768]{1,0:T(8,128)(2,1)S(1)}, bf16[528,768]{1,0:T(8,128)(2,1)S(1)}, u32[]{:S(2)}, u32[]{:S(2)}) collective-permute-start(bf16[528,768]{1,0:T(8,128)(2,1)S(1)} %copy-done.17), channel_id=1, source_target_pairs={{0,12},{1,14},{4,0},{6,2},{7,3},{8,4},{9,5},{10,6},{11,7},{12,8},{... | collective-permute-start | bytes 2433032 | tf_op jit(solution)/shard_map/ppermute | solution.py:451
  123.3 1.2 slice_select_fusion.3
  124.5 3.6 %collective-permute-start.12 = (bf16[272,768]{1,0:T(8,128)(2,1)S(1)}, bf16[272,768]{1,0:T(8,128)(2,1)S(1)}, u32[]{:S(2)}, u32[]{:S(2)}) collective-permute-start(bf16[272,768]{1,0:T(8,128)(2,1)S(1)} %slice_select_fusion.3), channel_id=1, source_target_pairs={{0,3},{2,0},{3,1},{4,7},{7,4},{8,11},{11,8},{12,15},{14,13},{15,12... | collective-permute-start | bytes 1253384 | tf_op jit(solution)/shard_map/ppermute | solution.py:485
  128.4 1.3 slice_select_fusion.5
  129.7 1.9 collective-permute-start.13
  132.7 13.7 %collective-permute-done.13.rest_3_ = bf16[256,768]{1,0:T(8,128)(2,1)S(1)} collective-permute-done((bf16[256,768]{1,0:T(8,128)(2,1)S(1)}, bf16[256,768]{1,0:T(8,128)(2,1)S(1)}, u32[]{:S(2)}, u32[]{:S(2)}) %collective-permute-start.13) | collective-permute-done | bytes 393248 | tf_op jit(solution)/shard_map/ppermute | solution.py:485
  146.4 8.7 %video_attention.5.rest_8_ = bf16[256,3072]{1,0:T(8,128)(2,1)} custom-call(s32[15]{0:T(128)S(1)} %pad_add_fusion.1.table, bf16[256,3072]{1,0:T(8,128)(2,1)S(1)} %copy-done.4, bf16[256,3072]{1,0:T(8,128)(2,1)S(1)} %copy-done, bf16[256,3072]{1,0:T(8,128)(2,1)} %v_own.7, ...), custom_call_target="tpu_custom_call", output_to_operand_aliasing={{}: (12, {})} | custom-call | flops 56623104 | bytes 196608 | tf_op jit(solution)/shard_map/video_attention/pallas_call | solution.py:216
  155.1 17.0 %collective-permute-done.14.refs_1_ = f32[32,3200]{1,0:T(8,128)S(1)} collective-permute-done((f32[32,3200]{1,0:T(8,128)S(1)}, f32[32,3200]{1,0:T(8,128)S(1)}, u32[]{:S(2)}, u32[]{:S(2)}) %collective-permute-start.14) | collective-permute-done | bytes 409632 | tf_op jit(solution)/shard_map/ppermute | solution.py:464
  172.1 1.2 text_merge.5
  173.3 1.9 collective-permute-start.16
  175.2 5.9 %collective-permute-start.15 = (bf16[528,512]{1,0:T(8,128)(2,1)}, bf16[528,512]{1,0:T(8,128)(2,1)}, u32[]{:S(2)}, u32[]{:S(2)}) collective-permute-start(bf16[528,512]{1,0:T(8,128)(2,1)} %pad_maximum_fusion.4), channel_id=1, source_target_pairs={{2,6},{3,7},{4,8},{5,9},{6,10},{7,11},{8,12},{9,13},{10,14},{11,15... | collective-permute-start | bytes 1622024 | tf_op jit(solution)/shard_map/ppermute | solution.py:451
  182.0 1.9 collective-permute-start.17
  184.7 3.6 %collective-permute-start.18 = (bf16[256,768]{1,0:T(8,128)(2,1)}, bf16[256,768]{1,0:T(8,128)(2,1)}, u32[]{:S(2)}, u32[]{:S(2)}) collective-permute-start(bf16[256,768]{1,0:T(8,128)(2,1)} %slice_select_fusion.4), channel_id=1, source_target_pairs={{0,3},{2,0},{3,1},{4,7},{7,4},{8,11},{11,8},{12,15},{14,13},{15,12... | collective-permute-start | bytes 1179656 | tf_op jit(solution)/shard_map/ppermute | solution.py:485
  188.4 16.7 %collective-permute-done.19.refs_1_ = f32[16,3200]{1,0:T(8,128)} collective-permute-done((f32[16,3200]{1,0:T(8,128)}, f32[16,3200]{1,0:T(8,128)}, u32[]{:S(2)}, u32[]{:S(2)}) %collective-permute-start.19) | collective-permute-done | bytes 204832 | tf_op jit(solution)/shard_map/ppermute | solution.py:464
  206.0 1.9 text_finish.1
  207.9 1.4 copy-done.5
  209.3 1.1 copy-done.7
  210.5 8.6 %video_attention.6.rest_8_ = bf16[256,3072]{1,0:T(8,128)(2,1)} custom-call(s32[15]{0:T(128)S(1)} %pad_add_fusion.1.table, bf16[256,3072]{1,0:T(8,128)(2,1)S(1)} %copy-done.5, bf16[256,3072]{1,0:T(8,128)(2,1)S(1)} %copy-done, bf16[256,3072]{1,0:T(8,128)(2,1)} %v_own.7, ...), custom_call_target="tpu_custom_call", output_to_operand_aliasing={{}: (12, {})} | custom-call | flops 56623104 | bytes 196608 | tf_op jit(solution)/shard_map/video_attention/pallas_call | solution.py:216
  220.1 1.9 collective-permute-start.20
  223.0 3.6 %collective-permute-start.21 = (bf16[256,512]{1,0:T(8,128)(2,1)S(1)}, bf16[256,512]{1,0:T(8,128)(2,1)S(1)}, u32[]{:S(2)}, u32[]{:S(2)}) collective-permute-start(bf16[256,512]{1,0:T(8,128)(2,1)S(1)} %slice_select_fusion.7), channel_id=1, source_target_pairs={{0,3},{3,0},{4,7},{7,4},{8,11},{11,8},{12,15},{14,13},{15,12},{16,... | collective-permute-start | bytes 786440 | tf_op jit(solution)/shard_map/ppermute | solution.py:485
  226.7 9.1 %collective-permute-done.21.rest_3_ = bf16[256,512]{1,0:T(8,128)(2,1)S(1)} collective-permute-done((bf16[256,512]{1,0:T(8,128)(2,1)S(1)}, bf16[256,512]{1,0:T(8,128)(2,1)S(1)}, u32[]{:S(2)}, u32[]{:S(2)}) %collective-permute-start.21) | collective-permute-done | bytes 262176 | tf_op jit(solution)/shard_map/ppermute | solution.py:485
  235.8 6.4 %video_attention.7 = bf16[256,3072]{1,0:T(8,128)(2,1)} custom-call(s32[15]{0:T(128)S(1)} %pad_add_fusion.1.table, bf16[256,3072]{1,0:T(8,128)(2,1)S(1)} %copy-done.5, bf16[256,3072]{1,0:T(8,128)(2,1)S(1)} %copy-done, bf16[256,3072]{1,0:T(8,128)(2,1)} %v_own.7, bf16[528,512]{1,0:T(8,128)(2,1)} %collective-permute-done.15.rest_0_, ...), custom_call_target="tpu_custom_call", output_to_operand_aliasing={{}: (12, {})} | custom-call | flops 37748736 | bytes 131072 | tf_op jit(solution)/shard_map/video_attention/pallas_call | solution.py:216
  (84 shorter events, 11.6 us)
Async XLA Ops:
  5.8 4.9 %slice-start = ((bf16[256,3072]{1,0:T(8,128)(2,1)}), bf16[256,1024]{1,0:T(8,128)(2,1)S(1)}, s32[]{:S(2)}) async-start(bf16[256,3072]{1,0:T(8,128)(2,1)} %k_own.7), calls=%async_computation | async-start | bytes 1048576 | tf_op jit(solution)/shard_map/slice | solution.py:442
  5.8 4.9 %slice-start.2 = ((bf16[256,3072]{1,0:T(8,128)(2,1)}), bf16[256,1024]{1,0:T(8,128)(2,1)S(1)}, s32[]{:S(2)}) async-start(bf16[256,3072]{1,0:T(8,128)(2,1)} %v_own.7), calls=%async_computation.2 | async-start | bytes 1048576 | tf_op jit(solution)/shard_map/slice | solution.py:442
  5.8 12.0 %collective-permute-start.2 = (bf16[528,3072]{1,0:T(8,128)(2,1)}, bf16[528,3072]{1,0:T(8,128)(2,1)}, u32[]{:S(2)}, u32[]{:S(2)}) collective-permute-start(bf16[528,3072]{1,0:T(8,128)(2,1)} %pad_maximum_fusion), channel_id=1, source_target_pairs={{0,1},{2,3},{4,5},{6,7},{8,9},{10,11},{12,13},{14,15},{16,17},{18,... | collective-permute-start | bytes 9732104 | tf_op jit(solution)/shard_map/ppermute | solution.py:455
  9.4 8.5 %collective-permute-start.3 = (bf16[528,3072]{1,0:T(8,128)(2,1)}, bf16[528,3072]{1,0:T(8,128)(2,1)}, u32[]{:S(2)}, u32[]{:S(2)}) collective-permute-start(bf16[528,3072]{1,0:T(8,128)(2,1)} %pad_maximum_fusion), channel_id=1, source_target_pairs={{1,0},{3,2},{5,4},{7,6},{9,8},{11,10},{13,12},{15,14},{17,16},{19,... | collective-permute-start | bytes 9732104 | tf_op jit(solution)/shard_map/ppermute | solution.py:455
  10.6 7.1 %copy-start.20 = (s32[16]{0:T(128)S(1)}, s32[16]{0:T(128)}, u32[]{:S(2)}) copy-start(s32[16]{0:T(128)} %constant.67.clone) | copy-start | bytes 196
  10.7 7.2 %copy-start = (bf16[256,3072]{1,0:T(8,128)(2,1)S(1)}, bf16[256,3072]{1,0:T(8,128)(2,1)}, u32[]{:S(2)}) copy-start(bf16[256,3072]{1,0:T(8,128)(2,1)} %k_own.7) | copy-start | bytes 4718596
  10.7 7.2 %copy-start.16 = (s32[2]{0:T(128)S(1)}, s32[2]{0:T(128)}, u32[]{:S(2)}) copy-start(s32[2]{0:T(128)} %counts.1) | copy-start | bytes 28
  11.9 50.1 %collective-permute-start = (bf16[528,1024]{1,0:T(8,128)(2,1)}, bf16[528,1024]{1,0:T(8,128)(2,1)S(1)}, u32[]{:S(2)}, u32[]{:S(2)}) collective-permute-start(bf16[528,1024]{1,0:T(8,128)(2,1)} %pad_maximum_fusion.1), channel_id=1, source_target_pairs={{2,6},{3,7},{4,8},{5,9},{6,10},{7,11},{8,12},{9,13},{10,14},{11,15... | collective-permute-start | bytes 3244040 | tf_op jit(solution)/shard_map/ppermute | solution.py:451
  13.8 48.2 %collective-permute-start.1 = (bf16[528,1024]{1,0:T(8,128)(2,1)}, bf16[528,1024]{1,0:T(8,128)(2,1)}, u32[]{:S(2)}, u32[]{:S(2)}) collective-permute-start(bf16[528,1024]{1,0:T(8,128)(2,1)} %pad_maximum_fusion.1), channel_id=1, source_target_pairs={{0,12},{1,14},{4,0},{6,2},{7,3},{8,4},{9,5},{10,6},{11,7},{12,8},{... | collective-permute-start | bytes 3244040 | tf_op jit(solution)/shard_map/ppermute | solution.py:451
  17.8 15.9 %copy-start.19 = (s32[16]{0:T(128)S(1)}, s32[16]{0:T(128)}, u32[]{:S(2)}) copy-start(s32[16]{0:T(128)} %constant.65.clone) | copy-start | bytes 196
  17.9 1.4 copy-start.1
  19.3 1.4 copy-start.9
  30.4 59.8 %collective-permute-start.8 = (f32[128,3328]{1,0:T(8,128)}, f32[128,3328]{1,0:T(8,128)}, u32[]{:S(2)}, u32[]{:S(2)}) collective-permute-start(f32[128,3328]{1,0:T(8,128)} %get-tuple-element.23), channel_id=1, source_target_pairs={{0,1},{1,0},{2,3},{3,2},{4,5},{5,4},{6,7},{7,6},{8,9},{9,8},{10,11... | collective-permute-start | bytes 5111816 | tf_op jit(solution)/shard_map/ppermute | solution.py:464
  62.0 7.9 %copy-start.2 = (bf16[256,3072]{1,0:T(8,128)(2,1)S(1)}, bf16[256,3072]{1,0:T(8,128)(2,1)}, u32[]{:S(2)}) copy-start(bf16[256,3072]{1,0:T(8,128)(2,1)} %v_own.7) | copy-start | bytes 4718596
  63.3 26.1 %collective-permute-start.6 = (bf16[272,1024]{1,0:T(8,128)(2,1)S(1)}, bf16[272,1024]{1,0:T(8,128)(2,1)S(1)}, u32[]{:S(2)}, u32[]{:S(2)}) collective-permute-start(bf16[272,1024]{1,0:T(8,128)(2,1)S(1)} %slice_select_fusion), channel_id=1, source_target_pairs={{0,3},{3,0},{4,7},{7,4},{8,11},{11,8},{12,15},{14,13},{15,12},{16,... | collective-permute-start | bytes 1671176 | tf_op jit(solution)/shard_map/ppermute | solution.py:485
  66.3 23.1 %collective-permute-start.7 = (bf16[256,1024]{1,0:T(8,128)(2,1)S(1)}, bf16[256,1024]{1,0:T(8,128)(2,1)S(1)}, u32[]{:S(2)}, u32[]{:S(2)}) collective-permute-start(bf16[256,1024]{1,0:T(8,128)(2,1)S(1)} %slice_select_fusion.1), channel_id=1, source_target_pairs={{0,3},{3,0},{4,7},{7,4},{8,11},{11,8},{12,15},{14,13},{15,12},{16,... | collective-permute-start | bytes 1572872 | tf_op jit(solution)/shard_map/ppermute | solution.py:485
  70.1 20.1 %copy-start.8 = (f32[128,3328]{1,0:T(8,128)S(1)}, f32[128,3328]{1,0:T(8,128)}, u32[]{:S(2)}) copy-start(f32[128,3328]{1,0:T(8,128)} %get-tuple-element.22.refs_0_) | copy-start | bytes 5111812
  71.6 24.8 %copy-start.18 = (s32[2,6]{1,0:T(2,128)S(1)}, s32[2,6]{1,0:T(2,128)}, u32[]{:S(2)}) copy-start(s32[2,6]{1,0:T(2,128)} %param.18) | copy-start | bytes 148
  71.6 45.7 %collective-permute-start.4 = (bf16[528,768]{1,0:T(8,128)(2,1)}, bf16[528,768]{1,0:T(8,128)(2,1)}, u32[]{:S(2)}, u32[]{:S(2)}) collective-permute-start(bf16[528,768]{1,0:T(8,128)(2,1)} %get-tuple-element.21), channel_id=1, source_target_pairs={{2,6},{3,7},{4,8},{5,9},{6,10},{7,11},{8,12},{9,13},{10,14},{11,15... | collective-permute-start | bytes 2433032 | tf_op jit(solution)/shard_map/ppermute | solution.py:451
  73.7 43.6 %collective-permute-start.5 = (bf16[528,768]{1,0:T(8,128)(2,1)}, bf16[528,768]{1,0:T(8,128)(2,1)}, u32[]{:S(2)}, u32[]{:S(2)}) collective-permute-start(bf16[528,768]{1,0:T(8,128)(2,1)} %get-tuple-element.21), channel_id=1, source_target_pairs={{0,12},{1,14},{4,0},{6,2},{7,3},{8,4},{9,5},{10,6},{11,7},{12,8},{... | collective-permute-start | bytes 2433032 | tf_op jit(solution)/shard_map/ppermute | solution.py:451
  89.4 0.8 copy-start.12
  94.0 0.9 copy-start.10
  94.9 20.5 %collective-permute-start.9 = (f32[64,3200]{1,0:T(8,128)}, f32[64,3200]{1,0:T(8,128)}, u32[]{:S(2)}, u32[]{:S(2)}) collective-permute-start(f32[64,3200]{1,0:T(8,128)} %get-tuple-element.26), channel_id=1, source_target_pairs={{0,2},{1,3},{2,0},{3,1},{4,6},{5,7},{6,4},{7,5},{8,10},{9,11},{10,... | collective-permute-start | bytes 2457608 | tf_op jit(solution)/shard_map/ppermute | solution.py:464
  98.5 1.4 copy-start.3
  99.9 1.1 copy-start.13
  100.9 14.4 %copy-start.11 = (f32[64,3200]{1,0:T(8,128)S(1)}, f32[64,3200]{1,0:T(8,128)}, u32[]{:S(2)}) copy-start(f32[64,3200]{1,0:T(8,128)} %copy-done.10) | copy-start | bytes 2457604
  112.0 5.3 %copy-start.17 = (bf16[528,768]{1,0:T(8,128)(2,1)S(1)}, bf16[528,768]{1,0:T(8,128)(2,1)}, u32[]{:S(2)}) copy-start(bf16[528,768]{1,0:T(8,128)(2,1)} %get-tuple-element.28) | copy-start | bytes 2433028
  117.3 14.3 %slice-start.1 = ((bf16[256,3072]{1,0:T(8,128)(2,1)}), bf16[256,512]{1,0:T(8,128)(2,1)S(1)}, s32[]{:S(2)}) async-start(bf16[256,3072]{1,0:T(8,128)(2,1)} %k_own.7), calls=%async_computation.1 | async-start | bytes 524288 | tf_op jit(solution)/shard_map/slice | solution.py:442
  117.3 14.3 %slice-start.3 = ((bf16[256,3072]{1,0:T(8,128)(2,1)}), bf16[256,512]{1,0:T(8,128)(2,1)S(1)}, s32[]{:S(2)}) async-start(bf16[256,3072]{1,0:T(8,128)(2,1)} %v_own.7), calls=%async_computation.3 | async-start | bytes 524288 | tf_op jit(solution)/shard_map/slice | solution.py:442
  117.3 55.9 %collective-permute-start.10 = (bf16[528,768]{1,0:T(8,128)(2,1)S(1)}, bf16[528,768]{1,0:T(8,128)(2,1)S(1)}, u32[]{:S(2)}, u32[]{:S(2)}) collective-permute-start(bf16[528,768]{1,0:T(8,128)(2,1)S(1)} %copy-done.17), channel_id=1, source_target_pairs={{2,6},{3,7},{4,8},{5,9},{6,10},{7,11},{8,12},{9,13},{10,14},{11,15... | collective-permute-start | bytes 2433032 | tf_op jit(solution)/shard_map/ppermute | solution.py:451
  119.4 53.9 %collective-permute-start.11 = (bf16[528,768]{1,0:T(8,128)(2,1)S(1)}, bf16[528,768]{1,0:T(8,128)(2,1)S(1)}, u32[]{:S(2)}, u32[]{:S(2)}) collective-permute-start(bf16[528,768]{1,0:T(8,128)(2,1)S(1)} %copy-done.17), channel_id=1, source_target_pairs={{0,12},{1,14},{4,0},{6,2},{7,3},{8,4},{9,5},{10,6},{11,7},{12,8},{... | collective-permute-start | bytes 2433032 | tf_op jit(solution)/shard_map/ppermute | solution.py:451
  124.5 21.9 %collective-permute-start.12 = (bf16[272,768]{1,0:T(8,128)(2,1)S(1)}, bf16[272,768]{1,0:T(8,128)(2,1)S(1)}, u32[]{:S(2)}, u32[]{:S(2)}) collective-permute-start(bf16[272,768]{1,0:T(8,128)(2,1)S(1)} %slice_select_fusion.3), channel_id=1, source_target_pairs={{0,3},{2,0},{3,1},{4,7},{7,4},{8,11},{11,8},{12,15},{14,13},{15,12... | collective-permute-start | bytes 1253384 | tf_op jit(solution)/shard_map/ppermute | solution.py:485
  128.1 18.3 %copy-start.4 = (bf16[256,3072]{1,0:T(8,128)(2,1)S(1)}, bf16[256,3072]{1,0:T(8,128)(2,1)}, u32[]{:S(2)}) copy-start(bf16[256,3072]{1,0:T(8,128)(2,1)} %q.9) | copy-start | bytes 4718596
  128.1 44.0 %collective-permute-start.14 = (f32[32,3200]{1,0:T(8,128)S(1)}, f32[32,3200]{1,0:T(8,128)S(1)}, u32[]{:S(2)}, u32[]{:S(2)}) collective-permute-start(f32[32,3200]{1,0:T(8,128)S(1)} %get-tuple-element.30), channel_id=1, source_target_pairs={{0,4},{1,5},{2,6},{3,7},{4,0},{5,1},{6,2},{7,3},{8,12},{9,13},{10,... | collective-permute-start | bytes 1228808 | tf_op jit(solution)/shard_map/ppermute | solution.py:464
  129.7 16.6 %collective-permute-start.13 = (bf16[256,768]{1,0:T(8,128)(2,1)S(1)}, bf16[256,768]{1,0:T(8,128)(2,1)S(1)}, u32[]{:S(2)}, u32[]{:S(2)}) collective-permute-start(bf16[256,768]{1,0:T(8,128)(2,1)S(1)} %slice_select_fusion.5), channel_id=1, source_target_pairs={{0,3},{2,0},{3,1},{4,7},{7,4},{8,11},{11,8},{12,15},{14,13},{15,12... | collective-permute-start | bytes 1179656 | tf_op jit(solution)/shard_map/ppermute | solution.py:485
  173.2 11.4 %copy-start.14 = (f32[16,3200]{1,0:T(8,128)}, f32[16,3200]{1,0:T(8,128)S(1)}, u32[]{:S(2)}) copy-start(f32[16,3200]{1,0:T(8,128)S(1)} %get-tuple-element.31.refs_0_) | copy-start | bytes 614404
  173.3 10.6 %copy-start.6 = (bf16[528,768]{1,0:T(8,128)(2,1)}, bf16[528,768]{1,0:T(8,128)(2,1)S(1)}, u32[]{:S(2)}) copy-start(bf16[528,768]{1,0:T(8,128)(2,1)S(1)} %collective-permute-done.11.rest_1_) | copy-start | bytes 2433028
  173.3 45.8 %collective-permute-start.16 = (bf16[528,512]{1,0:T(8,128)(2,1)}, bf16[528,512]{1,0:T(8,128)(2,1)S(1)}, u32[]{:S(2)}, u32[]{:S(2)}) collective-permute-start(bf16[528,512]{1,0:T(8,128)(2,1)} %pad_maximum_fusion.4), channel_id=1, source_target_pairs={{0,12},{1,14},{4,0},{6,2},{7,3},{8,4},{9,5},{10,6},{11,7},{12,8},{... | collective-permute-start | bytes 1622024 | tf_op jit(solution)/shard_map/ppermute | solution.py:451
  175.2 43.9 %collective-permute-start.15 = (bf16[528,512]{1,0:T(8,128)(2,1)}, bf16[528,512]{1,0:T(8,128)(2,1)}, u32[]{:S(2)}, u32[]{:S(2)}) collective-permute-start(bf16[528,512]{1,0:T(8,128)(2,1)} %pad_maximum_fusion.4), channel_id=1, source_target_pairs={{2,6},{3,7},{4,8},{5,9},{6,10},{7,11},{8,12},{9,13},{10,14},{11,15... | collective-permute-start | bytes 1622024 | tf_op jit(solution)/shard_map/ppermute | solution.py:451
  182.0 25.9 %collective-permute-start.17 = (bf16[272,768]{1,0:T(8,128)(2,1)}, bf16[272,768]{1,0:T(8,128)(2,1)S(1)}, u32[]{:S(2)}, u32[]{:S(2)}) collective-permute-start(bf16[272,768]{1,0:T(8,128)(2,1)} %slice_select_fusion.2), channel_id=1, source_target_pairs={{0,3},{2,0},{3,1},{4,7},{7,4},{8,11},{11,8},{12,15},{14,13},{15,12... | collective-permute-start | bytes 1253384 | tf_op jit(solution)/shard_map/ppermute | solution.py:485
  184.7 23.2 %collective-permute-start.18 = (bf16[256,768]{1,0:T(8,128)(2,1)}, bf16[256,768]{1,0:T(8,128)(2,1)}, u32[]{:S(2)}, u32[]{:S(2)}) collective-permute-start(bf16[256,768]{1,0:T(8,128)(2,1)} %slice_select_fusion.4), channel_id=1, source_target_pairs={{0,3},{2,0},{3,1},{4,7},{7,4},{8,11},{11,8},{12,15},{14,13},{15,12... | collective-permute-start | bytes 1179656 | tf_op jit(solution)/shard_map/ppermute | solution.py:485
  188.3 16.8 %collective-permute-start.19 = (f32[16,3200]{1,0:T(8,128)}, f32[16,3200]{1,0:T(8,128)}, u32[]{:S(2)}, u32[]{:S(2)}) collective-permute-start(f32[16,3200]{1,0:T(8,128)} %get-tuple-element.33), channel_id=1, source_target_pairs={{0,8},{1,9},{2,10},{3,11},{4,12},{5,13},{6,14},{7,15},{8,0},{9,1},... | collective-permute-start | bytes 614408 | tf_op jit(solution)/shard_map/ppermute | solution.py:464
  205.1 0.9 copy-start.15
  207.9 1.4 copy-start.5
  209.3 1.1 copy-start.7
  220.1 15.7 %collective-permute-start.20 = (bf16[272,512]{1,0:T(8,128)(2,1)S(1)}, bf16[272,512]{1,0:T(8,128)(2,1)S(1)}, u32[]{:S(2)}, u32[]{:S(2)}) collective-permute-start(bf16[272,512]{1,0:T(8,128)(2,1)S(1)} %slice_select_fusion.6), channel_id=1, source_target_pairs={{0,3},{3,0},{4,7},{7,4},{8,11},{11,8},{12,15},{14,13},{15,12},{16,... | collective-permute-start | bytes 835592 | tf_op jit(solution)/shard_map/ppermute | solution.py:485
  223.0 12.8 %collective-permute-start.21 = (bf16[256,512]{1,0:T(8,128)(2,1)S(1)}, bf16[256,512]{1,0:T(8,128)(2,1)S(1)}, u32[]{:S(2)}, u32[]{:S(2)}) collective-permute-start(bf16[256,512]{1,0:T(8,128)(2,1)S(1)} %slice_select_fusion.7), channel_id=1, source_target_pairs={{0,3},{3,0},{4,7},{7,4},{8,11},{11,8},{12,15},{14,13},{15,12},{16,... | collective-permute-start | bytes 786440 | tf_op jit(solution)/shard_map/ppermute | solution.py:485

commit v3 on v2

--- a/solution.py
+++ b/solution.py
@@ -18,7 +18,7 @@
 PAD_ROWS = 16
 VMEM_BYTES = 48 * 1024 * 1024
 LOG2E = 1.4426950408889634
-SOURCES = ("own", "earlier", "later", "relayed", "above", "below")
+SOURCES = ("own", "earlier", "later", "relayed", "beside")
 
 
 def spot_shift(n):
@@ -35,32 +35,28 @@
     moves = {
         "earlier": {at(t - 1, r): at(t, r) for t in range(1, times) for r in range(NR)},
         "later": {at(t + 1, r): at(t, r) for t in range(last) for r in range(NR)},
-        "above": {at(t, r - 1): at(t, r) for t in range(times) for r in (1, 3)},
-        "below": {at(t, r + 1): at(t, r) for t in range(times) for r in (0, 2)},
+        "beside": {at(t, r): at(t, r ^ 1) for t in range(times) for r in range(NR)},
     }
     relay_earlier = {at(t + 1, 1): at(t, 2) for t in range(last)}
     relay_later = {at(t - 1, 2): at(t, 1) for t in range(1, times)}
+    moves["later"][at(0, 2)] = at(last, 2)
+    relay_later[at(last, 2)] = at(0, 1)
     if times == 4:
-        moves["later"][at(0, 2)] = at(3, 2)
-        relay_later[at(3, 2)] = at(0, 1)
         moves["later"][at(3, 3)] = at(3, 0)
         relay_later[at(3, 0)] = at(2, 3)
-        if diverted:
-            moves["earlier"][at(2, 2)] = at(0, 0)
-            relay_earlier[at(0, 0)] = at(3, 2)
-            moves["earlier"][at(2, 3)] = at(0, 1)
-            relay_earlier[at(0, 1)] = at(3, 3)
-            moves["earlier"][at(3, 1)] = at(3, 2)
-        else:
-            moves["earlier"][at(3, 1)] = at(0, 1)
-            relay_earlier[at(0, 1)] = at(3, 2)
+    if times == 4 and diverted:
+        moves["earlier"][at(2, 2)] = at(0, 0)
+        relay_earlier[at(0, 0)] = at(3, 2)
+        moves["earlier"][at(2, 3)] = at(0, 1)
+        relay_earlier[at(0, 1)] = at(3, 3)
+        moves["earlier"][at(3, 1)] = at(3, 2)
     else:
-        moves["above"][at(last, 1)] = at(last, 2)
-        moves["below"][at(0, 2)] = at(0, 1)
+        moves["earlier"][at(last, 1)] = at(0, 1)
+        relay_earlier[at(0, 1)] = at(last, 2)
     assert not set(relay_earlier) & set(relay_later)
     moves["relayed"] = {**relay_earlier, **relay_later}
     held = {"own": {d: d for d in range(n)}}
-    for name in ("earlier", "later", "above", "below"):
+    for name in ("earlier", "later", "beside"):
         held[name] = {dst: src for src, dst in moves[name].items()}
     held["relayed"] = {dst: held["earlier"].get(src) for src, dst in relay_earlier.items()}
     held["relayed"].update({dst: held["later"].get(src) for src, dst in relay_later.items()})
@@ -99,12 +95,12 @@
     return final(functools.reduce(op, tiles), axis=1, keepdims=True)
 
 
-TABLE_COUNTS, TABLE_TEXT, TABLE_CHOICE = 4, 6, 7
+TABLE_COUNTS, TABLE_BESIDE, TABLE_TEXT, TABLE_CHOICE = 4, 6, 8, 9
 
 
 def video_kernel(kind, table, q, k_own, v_own, *rest):
-    packed = {"earlier": rest[0], "later": rest[1], "above": rest[4], "below": rest[5]}
-    relayed_k, relayed_v, text_k, text_v = rest[2], rest[3], rest[6], rest[7]
+    packed = {"earlier": rest[0], "later": rest[1]}
+    relayed_k, relayed_v, beside_k, beside_v, text_k, text_v = rest[2:8]
     out, k_all, v_all, bias_all = rest[-4:]
     tok = q.shape[0] // 2
     text = text_k.shape[0]
@@ -127,11 +123,14 @@
         for c in range(2):
             bias_all[c * BLOCKS + block] = jnp.where(lane_f < limits[c : c + 1, :], 0.0, -jnp.inf)
 
+    def put_counts(block, at):
+        for c in range(2):
+            bias_all[c * BLOCKS + block] = jnp.where(lane < table[at + c], 0.0, -jnp.inf)
+
     put(0, k_own, v_own, 0)
-    for c in range(2):
-        bias_all[c * BLOCKS] = jnp.where(lane < table[TABLE_COUNTS + c], 0.0, -jnp.inf)
+    put_counts(0, TABLE_COUNTS)
     tail = (pl.ds(2 * tok, PAD_ROWS), pl.ds(0, HD))
-    options = {1: ("earlier",), 2: ("later",), 3: ("above", "earlier"), 4: ("below", "later")}
+    options = {1: ("earlier",), 2: ("later",), 3: ("earlier",), 4: ("later",)}
     zeros = jnp.zeros((tok, HD), k_all.dtype)
     for block in range(1, BLOCKS):
         chosen = table[TABLE_CHOICE + 4 * kind + block - 1]
@@ -146,6 +145,13 @@
         def _(block=block):
             put(block, relayed_k, relayed_v, 0)
             put_limits(block, relayed_k.at[tail])
+
+        if block > 2:
+
+            @pl.when(chosen == SOURCES.index("beside"))
+            def _(block=block):
+                put(block, beside_k, beside_v, 0)
+                put_counts(block, TABLE_BESIDE)
 
         @pl.when(chosen < 0)
         def _(block=block):
@@ -199,12 +205,11 @@
     part = lambda h: (0, h)
     own_spec = pl.BlockSpec((rows, step), whole)
     part_spec = pl.BlockSpec((2 * rows + PAD_ROWS, step), part)
-    whole_spec = pl.BlockSpec((2 * rows + PAD_ROWS, step), whole)
     text_spec = pl.BlockSpec((text, step), whole)
     in_specs = [pl.BlockSpec(memory_space=pltpu.SMEM), own_spec, own_spec, own_spec]
     in_specs += [part_spec] * 2
     in_specs += [pl.BlockSpec((rows + PAD_ROWS, step), part), pl.BlockSpec((rows, step), part)]
-    in_specs += [whole_spec] * 2 + [text_spec] * 2
+    in_specs += [own_spec] * 2 + [text_spec] * 2
     operands = [table, q, k, v, *near, text_k, text_v]
     aliases = {}
     if carried is not None:
@@ -236,14 +241,16 @@
 
 
 STAT_SUMS = 32
-
-
-def text_kernel(order, counts, q, k, v, keep, send, top, denom):
+PAIR_HEADS = HEADS // 2
+
+
+def text_kernel(order, counts, q, k, v, k_beside, v_beside, keep, send, top, denom):
     step = pl.program_id(0)
     rows = k.shape[0]
     text = q.shape[0]
     half = text // 2
-    share = text // order.shape[0]
+    places = order.shape[0] - 1
+    share = text // places
     lane = lax.broadcasted_iota(jnp.int32, (text, HD), 1)
 
     @pl.when(step == 0)
@@ -251,69 +258,78 @@
         top[...] = jnp.zeros_like(top)
         denom[...] = jnp.zeros_like(denom)
 
-    @pl.when(step < HEADS // STEP_HEADS)
+    @pl.when(step < PAIR_HEADS // STEP_HEADS)
     def _():
         slot = lax.broadcasted_iota(jnp.int32, (1, rows // 2), 1)
-        bias = jnp.concatenate(
-            [jnp.where(slot < counts[c], 0.0, -jnp.inf) for c in range(2)], axis=1
-        )
+        bias = [
+            jnp.concatenate(
+                [jnp.where(slot < counts[at + c], 0.0, -jnp.inf) for c in range(2)], axis=1
+            )
+            for at in (0, 2)
+        ]
         for i in range(STEP_HEADS):
             cols = pl.ds(i * HD, HD)
             head = step * STEP_HEADS + i
             query = jnp.concatenate(
                 [
                     q[pl.ds(pl.multiple_of(order[j] * share, share), share), cols]
-                    for j in range(order.shape[0])
+                    for j in range(places)
                 ],
                 axis=0,
             )
-            s = dot_nt(query, k[:, cols]) * (1.0 / math.sqrt(HD)) + bias
-            m = row_reduce(jnp.maximum, jnp.max, [s])
-            w = jnp.exp(s - m)
-            l = row_reduce(jnp.add, jnp.sum, [w])
-            high = w.astype(jnp.bfloat16)
-            low = (w - high.astype(jnp.float32)).astype(jnp.bfloat16)
-            acc = dot_nn(high, v[:, cols]) + dot_nn(low, v[:, cols])
+            scores = [
+                dot_nt(query, keys[:, cols]) * (1.0 / math.sqrt(HD)) + bound
+                for keys, bound in zip((k, k_beside), bias)
+            ]
+            m = row_reduce(jnp.maximum, jnp.max, scores)
+            weights = [jnp.exp(s - m) for s in scores]
+            l = row_reduce(jnp.add, jnp.sum, weights)
+            acc = 0.0
+            for w, values in zip(weights, (v, v_beside)):
+                high = w.astype(jnp.bfloat16)
+                low = (w - high.astype(jnp.float32)).astype(jnp.bfloat16)
+                acc = acc + dot_nn(high, values[:, cols]) + dot_nn(low, values[:, cols])
             top[...] = jnp.where(lane == head, m, top[...])
             denom[...] = jnp.where(lane == head + STAT_SUMS, l, denom[...])
             keep[:, cols] = acc[:half]
             send[:, cols] = acc[half:]
 
-    @pl.when(step == HEADS // STEP_HEADS)
+    @pl.when(step == PAIR_HEADS // STEP_HEADS)
     def _():
         stats = top[...] + denom[...]
         keep[:, pl.ds(0, HD)] = stats[:half]
         send[:, pl.ds(0, HD)] = stats[half:]
 
 
-def text_local(order, counts, q, k, v):
+def text_local(order, counts, q, k, v, k_beside, v_beside):
     text = q.shape[0]
     rows = k.shape[0]
     step = STEP_HEADS * HD
-    last = HEADS // STEP_HEADS - 1
-    smem = pl.BlockSpec(memory_space=pltpu.SMEM)
-    q_spec = pl.BlockSpec((text, step), lambda h: (0, jnp.minimum(h, last)))
-    k_spec = pl.BlockSpec((rows, step), lambda h: (0, jnp.minimum(h, last)))
-    out_spec = pl.BlockSpec((text // 2, step), lambda h: (0, h))
-    shape = jax.ShapeDtypeStruct((text // 2, HEADS * HD + step), jnp.float32)
-    work = HEADS * text * rows
+    last = PAIR_HEADS // STEP_HEADS - 1
+    at = lambda h, order, counts: (0, order[order.shape[0] - 1] + jnp.minimum(h, last))
+    k_spec = pl.BlockSpec((rows, step), at)
+    out_spec = pl.BlockSpec((text // 2, step), lambda h, order, counts: (0, h))
+    shape = jax.ShapeDtypeStruct((text // 2, PAIR_HEADS * HD + step), jnp.float32)
     return pl.pallas_call(
         text_kernel,
-        grid=(last + 2,),
-        in_specs=[smem, smem, q_spec, k_spec, k_spec],
-        out_specs=[out_spec, out_spec],
+        grid_spec=pltpu.PrefetchScalarGridSpec(
+            num_scalar_prefetch=2,
+            grid=(last + 2,),
+            in_specs=[pl.BlockSpec((text, step), at)] + [k_spec] * 4,
+            out_specs=[out_spec, out_spec],
+            scratch_shapes=[pltpu.VMEM((text, HD), jnp.float32)] * 2,
+        ),
         out_shape=[shape, shape],
-        scratch_shapes=[pltpu.VMEM((text, HD), jnp.float32)] * 2,
         compiler_params=pltpu.CompilerParams(vmem_limit_bytes=VMEM_BYTES),
         cost_estimate=pl.CostEstimate(
-            flops=work * HD // 4, bytes_accessed=text * HEADS * HD, transcendentals=0
+            flops=text * rows * HD, bytes_accessed=text * HEADS * HD, transcendentals=0
         ),
         name="text_partials",
-    )(order, counts, q, k, v)
+    )(order, counts, q, k, v, k_beside, v_beside)
 
 
 def merge_kernel(finish, *refs):
-    width = HEADS * HD
+    width = PAIR_HEADS * HD
     stat_cols = pl.ds(width, HD)
     keep, got = refs[:2]
     mine = keep[:, stat_cols]
@@ -323,39 +339,32 @@
     top = jnp.maximum(mine, theirs)
     a = jnp.exp(jnp.where(is_top, mine - top, 0.0))
     b = jnp.exp(jnp.where(is_top, theirs - top, 0.0))
-    sums = []
-    for h in range(HEADS):
+    first, second = refs[-2:]
+    half = first.shape[0]
+    stats = jnp.where(is_top, top, 0.0)
+    if finish:
+        limits = refs[2]
+        row = lax.broadcasted_iota(jnp.int32, (2 * half, 1), 0)
+        valid = row < jnp.where(row < half, limits[0], limits[1] + half)
+    for h in range(PAIR_HEADS):
+        cols = pl.ds(h * HD, HD)
         at = slice(h, h + 1)
         to = slice(STAT_SUMS + h, STAT_SUMS + h + 1)
-        sums.append(mine[:, to] * a[:, at] + theirs[:, to] * b[:, at])
-    if finish:
-        limit, out = refs[2:]
-        share = out.shape[0]
-        row = lax.broadcasted_iota(jnp.int32, (share, 1), 0)
-        valid = row < limit[0]
-        for h in range(HEADS):
-            cols = pl.ds(h * HD, HD)
-            at = slice(h, h + 1)
-            acc = keep[:, cols] * a[:, at] + got[:, cols] * b[:, at]
-            out[:, cols] = jnp.where(valid, acc / sums[h], 0.0).astype(out.dtype)
-        return
-    next_keep, next_send = refs[2:]
-    half = next_keep.shape[0]
-    stats = jnp.where(is_top, top, 0.0)
-    for h in range(HEADS):
-        cols = pl.ds(h * HD, HD)
-        at = slice(h, h + 1)
+        total = mine[:, to] * a[:, at] + theirs[:, to] * b[:, at]
         acc = keep[:, cols] * a[:, at] + got[:, cols] * b[:, at]
-        stats = jnp.where(lane == STAT_SUMS + h, sums[h], stats)
-        next_keep[:, cols] = acc[:half]
-        next_send[:, cols] = acc[half:]
-    next_keep[:, stat_cols] = stats[:half]
-    next_send[:, stat_cols] = stats[half:]
+        if finish:
+            acc = jnp.where(valid, acc / total, 0.0)
+        else:
+            stats = jnp.where(lane == STAT_SUMS + h, total, stats)
+        first[:, cols] = acc[:half].astype(first.dtype)
+        second[:, cols] = acc[half:].astype(second.dtype)
+    if not finish:
+        first[:, stat_cols] = stats[:half]
+        second[:, stat_cols] = stats[half:]
 
 
 def text_merge(keep, got):
-    half = keep.shape[0] // 2
-    shape = jax.ShapeDtypeStruct((half, (HEADS + 1) * HD), jnp.float32)
+    shape = jax.ShapeDtypeStruct((keep.shape[0] // 2, (PAIR_HEADS + 1) * HD), jnp.float32)
     return pl.pallas_call(
         functools.partial(merge_kernel, False),
         out_shape=[shape, shape],
@@ -364,22 +373,27 @@
     )(keep, got)
 
 
-def text_finish(keep, got, limit):
-    share = keep.shape[0]
+def text_finish(keep, got, limits):
+    shape = jax.ShapeDtypeStruct((keep.shape[0] // 2, PAIR_HEADS * HD), jnp.bfloat16)
     vmem = pl.BlockSpec(memory_space=pltpu.VMEM)
     return pl.pallas_call(
         functools.partial(merge_kernel, True),
         in_specs=[vmem, vmem, pl.BlockSpec(memory_space=pltpu.SMEM)],
-        out_shape=jax.ShapeDtypeStruct((share, HEADS * HD), jnp.bfloat16),
+        out_shape=[shape, shape],
         compiler_params=pltpu.CompilerParams(vmem_limit_bytes=VMEM_BYTES),
         name="text_finish",
-    )(keep, got, limit)
-
-
-def slot_order(n, position):
+    )(keep, got, limits)
+
+
+def text_order(n, position):
     bits = n.bit_length() - 1
-    mirrored = [int(format(i, f"0{bits}b")[::-1], 2) for i in range(n)]
-    return jnp.array(mirrored, jnp.int32) ^ position.astype(jnp.int32)
+    masks = [1 << b for b in (*range(1, bits), 0)]
+    owners = [
+        sum(mask for j, mask in enumerate(masks) if i >> (bits - 1 - j) & 1) for i in range(n)
+    ]
+    order = jnp.array(owners, jnp.int32) ^ position
+    first = position % 2 * (PAIR_HEADS // STEP_HEADS)
+    return jnp.concatenate([order, first[None]])
 
 
 def text_plain(position, n, text_count, q, k, v, counts):
@@ -407,7 +421,7 @@
     return result.astype(jnp.bfloat16).reshape(share, width)
 
 
-def make_table(window, counts, text_count, choices, position):
+def make_table(window, counts, counts_beside, text_count, choices, position):
     columns = counts.shape[0]
     extra = (window % 3 != 0) | (window == 0)
     rank = jnp.cumsum(extra.astype(jnp.int32), axis=1) * extra
@@ -418,7 +432,7 @@
     inside = (column >= 0) & (column < columns)
     extra_cells = jnp.where(inside, column * BLOCKS + cells // 3, columns * BLOCKS)
     chosen = lax.dynamic_index_in_dim(jnp.array(choices, jnp.int32), position, 0, False)
-    parts = [extra_cells.reshape(-1), counts, text_count, chosen]
+    parts = [extra_cells.reshape(-1), counts, counts_beside, text_count, chosen]
     return jnp.concatenate([part.astype(jnp.int32) for part in parts])
 
 
@@ -429,11 +443,10 @@
 def per_device(n, video_q, video_k, video_v, text_q, text_k, text_v, window, counts, text_count):
     rows, width = video_q.shape
     text = text_q.shape[0]
-    position = lax.axis_index("tiles")
+    position = lax.axis_index("tiles").astype(jnp.int32)
     plans = [plan_moves(n, kind) for kind in (False, True)]
     choices = [plans[0][2][d] + plans[1][2][d] for d in range(n)]
     sends_later = jnp.array(plans[0][1], jnp.int32)[position] == 1
-    table = make_table(window, counts, text_count, choices, position)
 
     limits = jnp.concatenate([counts, jnp.zeros((PAD_ROWS - counts.shape[0],), jnp.int32)])
     limits = jnp.broadcast_to(limits.astype(jnp.bfloat16)[:, None], (PAD_ROWS, width))
@@ -451,48 +464,56 @@
         direct.append([lax.ppermute(mine, "tiles", pairs[x]) for x in ("earlier", "later")])
 
     send(0)
-    everything = pack(slice(0, width))
-    sides = [lax.ppermute(everything, "tiles", plans[0][0][x]) for x in ("above", "below")]
+    beside = [
+        lax.ppermute(x, "tiles", plans[0][0]["beside"]) for x in (counts, video_k, video_v)
+    ]
+    send(1, *beside)
+    table = make_table(window, counts, beside[0], text_count, choices, position)
     halving = text % (PAD_ROWS * n) == 0 and n & (n - 1) == 0
     stages = n.bit_length() - 1
     parts = []
     if halving:
-        order = tie(slot_order(n, position), *sides)
-        parts = [text_local(order, counts, text_q, video_k, video_v)]
+        order = text_order(n, position)
+        both = jnp.concatenate([counts, beside[0]])
+        parts.append(text_local(order, both, text_q, video_k, video_v, *beside[1:]))
 
     def exchanged(i):
-        return lax.ppermute(parts[i][1], "tiles", [(d, d ^ (1 << i)) for d in range(n)])
+        return lax.ppermute(parts[i][1], "tiles", [(d, d ^ (2 << i)) for d in range(n)])
 
     def merge(*before):
         i = len(parts) - 1
-        if 0 <= i < stages - 1:
+        if 0 <= i < stages - 2:
             parts.append(text_merge(tie(parts[i][0], *before), exchanged(i)))
-
-    for i in range(len(CHUNK_HEADS)):
+        elif i == stages - 2:
+            share = text // n
+            limits = [text_count - place * share for place in (position, position ^ 1)]
+            limits = jnp.concatenate(limits)
+            parts.append(text_finish(tie(parts[i][0], *before), exchanged(i), limits))
+
+    count = len(CHUNK_HEADS)
+    for i in range(count):
         pairs = plans[DIVERTED[i]][0]
-        if i + 1 < len(CHUNK_HEADS):
-            before = outs[-1:] + ([parts[-1][0]] if halving else [])
-            send(i + 1, *direct[i], *before)
         up, down = direct[i]
-        if i + 1 == len(CHUNK_HEADS):
-            before = outs[-1:]
-            if halving:
-                limit = text_count - position.astype(jnp.int32) * (text // n)
-                text_out = text_finish(parts[-1][0], exchanged(stages - 1), limit)
-                before.append(text_out)
-            up, down = tie(up, *before), tie(down, *before)
+        before = [parts[0][0]] if halving and i == 0 else outs[-1:]
+        up, down = tie(up, *before), tie(down, *before)
         relays = [
             lax.ppermute(jnp.where(sends_later, down[half], up[half]), "tiles", pairs["relayed"])
             for half in (slice(0, rows + PAD_ROWS), slice(rows + PAD_ROWS, None))
         ]
+        if i + 2 < count:
+            send(i + 2, *direct[i])
         merge(*relays)
         outs.append(
             video_call(
                 int(DIVERTED[i]), starts[i], CHUNK_HEADS[i], table, video_q, video_k, video_v,
-                [*direct[i], *relays, *sides], text_k, text_v, outs[-1] if outs else None,
+                [*direct[i], *relays, *beside[1:]], text_k, text_v, outs[-1] if outs else None,
             )
         )
-        merge(outs[-1])
+    if halving:
+        mine, leave = parts[-1]
+        got = lax.ppermute(leave, "tiles", [(d, d ^ 1) for d in range(n)])
+        low, high = jnp.concatenate([mine, got], axis=1), jnp.concatenate([got, mine], axis=1)
+        text_out = jnp.where(position % 2 == 0, low, high)
     if not halving:
         text_out = text_plain(position, n, text_count, text_q, video_k, video_v, counts)
     return (outs[-1], text_out)

time: 245 us -> 233 us (0.951)
  Pallas kernels: 53.3 us -> 46.9 us
  waiting for transfers between devices: 98.7 us -> 102 us
  local copies, waits for them, and re-layouts: 12.2 us -> 9.03 us
  starting transfers between devices: 57.7 us -> 55 us
    ppermute x6 -> x7, waiting for transfers between devices: 37 us -> 11.6 us  [the longest x3 11.6 us: exchanged(): lax.ppermute(parts[i][1], 'tiles', [(d, d ^ 2 << i) for d in range(n)])]
    ppermute x8, waiting for transfers between devices: 27.1 us -> 48.5 us  [send(): lax.ppermute(mine, 'tiles', pairs[x])]
    ppermute x6 -> x7, starting transfers between devices: 9.95 us -> 0.89 us  [the longest x3 0.65 us: per_device(): lax.ppermute(x, 'tiles', plans[0][0]['beside'])]
    ppermute x8, waiting for transfers between devices: 34.6 us -> 41.7 us  [per_device(): lax.ppermute(jnp.where(sends_later, down[half], up[half]), 'tiles', pairs...]
    unnamed x42 -> x36, local copies, waits for them, and re-layouts: 10.5 us -> 4.02 us
    concatenate x4 -> x3, other arithmetic: 8.28 us -> 3.71 us  [pack(): jnp.concatenate([video_k[:, cols], limits[:, cols], video_v[:, cols]], ax...]
    pallas_call x3 -> x2, Pallas kernels: 6.91 us -> 3.1 us  [text_merge(): pl.pallas_call(functools.partial(merge_kernel, False), out_shape=[shape,...]
    ppermute x8, starting transfers between devices: 22.2 us -> 25.7 us  [per_device(): lax.ppermute(jnp.where(sends_later, down[half], up[half]), 'tiles', pairs...]
  transfers between devices with their start and end apart: 22 -> 23, of which waited for: 7 -> 9; matrix products, arithmetic and copies ran while one was open for 5% -> 9% of each run, Pallas kernels for 19% -> 18%
where the time goes in v3:
time: 233 us; the launch traced here: 231 us
  waiting for transfers between devices  102 us (44%)
  starting transfers between devices  55 us (24%)
  Pallas kernels  46.9 us (20%)
  other arithmetic  15.9 us (7%)
  local copies, waits for them, and re-layouts  9.03 us (4%)
  between operations  2.42 us (1%)
    ppermute x8, waiting for transfers between devices, send(): lax.ppermute(mine, 'tiles', pairs[x])  48.5 us
    ppermute x8, waiting for transfers between devices, per_device(): lax.ppermute(jnp.where(sends_later, down[half], up[half]), 'tiles', pairs...  41.7 us
    pallas_call x4, Pallas kernels, video_call(): pl.pallas_call(functools.partial(video_kernel, kind), grid=(heads // STEP...  34.5 us
    ppermute x8, starting transfers between devices, send(): lax.ppermute(mine, 'tiles', pairs[x])  28.4 us
    ppermute x8, starting transfers between devices, per_device(): lax.ppermute(jnp.where(sends_later, down[half], up[half]), 'tiles', pairs...  25.7 us
    ppermute x3, waiting for transfers between devices, exchanged(): lax.ppermute(parts[i][1], 'tiles', [(d, d ^ 2 << i) for d in range(n)])  11.6 us
    select_n x8, other arithmetic, per_device(): jnp.where(sends_later, down[half], up[half])  10.2 us
    pallas_call x1, Pallas kernels, text_local(): pl.pallas_call(text_kernel, grid_spec=pltpu.PrefetchScalarGridSpec(num_sc...  8.08 us
  transfers between devices with their start and end apart: 23, of which 9 were waited for; matrix products, arithmetic and copies ran while one was open for 9% of the time, Pallas kernels for 18%

profile of v3, /device:TPU:24, one launch (start us, length us, event | category | flops | bytes accessed | tf_op | source)
XLA Modules:
  0.0 231.1 jit_solution(3397302247105321525)
XLA Ops:
  1.9 1.1 slice.90
  3.1 1.2 slice.92
  4.3 1.2 pad_maximum_fusion
  5.5 2.3 %collective-permute-start.8 = (bf16[528,1024]{1,0:T(8,128)(2,1)}, bf16[528,1024]{1,0:T(8,128)(2,1)S(1)}, u32[]{:S(2)}, u32[]{:S(2)}) collective-permute-start(bf16[528,1024]{1,0:T(8,128)(2,1)} %pad_maximum_fusion), channel_id=1, source_target_pairs={{0,12},{1,14},{4,0},{6,2},{7,3},{8,4},{9,5},{10,6},{11,7},{12,8},{... | collective-permute-start | bytes 3244040 | tf_op jit(solution)/shard_map/ppermute | solution.py:464
  7.9 5.3 %collective-permute-start.7 = (bf16[528,1024]{1,0:T(8,128)(2,1)}, bf16[528,1024]{1,0:T(8,128)(2,1)}, u32[]{:S(2)}, u32[]{:S(2)}) collective-permute-start(bf16[528,1024]{1,0:T(8,128)(2,1)} %pad_maximum_fusion), channel_id=1, source_target_pairs={{2,6},{3,7},{4,8},{5,9},{6,10},{7,11},{8,12},{9,13},{10,14},{11,15... | collective-permute-start | bytes 3244040 | tf_op jit(solution)/shard_map/ppermute | solution.py:464
  14.9 1.5 pad_maximum_fusion.2
  16.5 1.9 collective-permute-start.4
  18.4 1.9 collective-permute-start.3
  20.4 8.1 %text_partials.1 = (f32[128,1792]{1,0:T(8,128)S(1)}, f32[128,1792]{1,0:T(8,128)S(1)}) custom-call(s32[17]{0:T(128)S(1)} %pad_add_fusion.1.order, s32[4]{0:T(128)S(1)} %pad_add_fusion.2.counts, bf16[256,3072]{1,0:T(8,128)(2,1)S(1)} %copy-done.7, bf16[256,3072]{1,0:T(8,128)(2,1)S(1)} %copy-done, bf16[256,3072]{1,0:T(8,128)(2,1)} %v_own.7, ...), custom_call_target="tpu_custom_call" | custom-call | flops 8388608 | bytes 786432 | tf_op jit(solution)/shard_map/text_partials/pallas_call | solution.py:313
  28.5 7.5 %collective-permute-done.8.rest_1_ = bf16[528,1024]{1,0:T(8,128)(2,1)S(1)} collective-permute-done((bf16[528,1024]{1,0:T(8,128)(2,1)}, bf16[528,1024]{1,0:T(8,128)(2,1)S(1)}, u32[]{:S(2)}, u32[]{:S(2)}) %collective-permute-start.8) | collective-permute-done | bytes 1081376 | tf_op jit(solution)/shard_map/ppermute | solution.py:464
  36.0 40.9 %collective-permute-done.7.rest_0_ = bf16[528,1024]{1,0:T(8,128)(2,1)} collective-permute-done((bf16[528,1024]{1,0:T(8,128)(2,1)}, bf16[528,1024]{1,0:T(8,128)(2,1)}, u32[]{:S(2)}, u32[]{:S(2)}) %collective-permute-start.7) | collective-permute-done | bytes 1081376 | tf_op jit(solution)/shard_map/ppermute | solution.py:464
  77.0 2.0 slice_select_fusion
  79.0 1.9 collective-permute-start.11
  80.9 1.9 slice_select_fusion.1
  82.8 3.6 %collective-permute-start.12 = (bf16[256,1024]{1,0:T(8,128)(2,1)}, bf16[256,1024]{1,0:T(8,128)(2,1)}, u32[]{:S(2)}, u32[]{:S(2)}) collective-permute-start(bf16[256,1024]{1,0:T(8,128)(2,1)} %slice_select_fusion.1), channel_id=1, source_target_pairs={{0,3},{3,0},{4,7},{7,4},{8,11},{11,8},{12,15},{14,13},{15,12},{16,... | collective-permute-start | bytes 1572872 | tf_op jit(solution)/shard_map/ppermute | solution.py:500
  88.4 18.8 %collective-permute-done.12.rest_3_ = bf16[256,1024]{1,0:T(8,128)(2,1)} collective-permute-done((bf16[256,1024]{1,0:T(8,128)(2,1)}, bf16[256,1024]{1,0:T(8,128)(2,1)}, u32[]{:S(2)}, u32[]{:S(2)}) %collective-permute-start.12) | collective-permute-done | bytes 524320 | tf_op jit(solution)/shard_map/ppermute | solution.py:500
  107.3 1.9 collective-permute-start.10
  109.2 1.9 collective-permute-start.9
  111.1 10.9 %video_attention.4.rest_8_ = bf16[256,3072]{1,0:T(8,128)(2,1)} custom-call(s32[17]{0:T(128)S(1)} %concatenate.33.table, bf16[256,3072]{1,0:T(8,128)(2,1)S(1)} %copy-done.2, bf16[256,3072]{1,0:T(8,128)(2,1)} %k_own.7, bf16[256,3072]{1,0:T(8,128)(2,1)} %v_own.7, bf16[528,1024]{1,0:T(8,128)(2,1)} %collective-permute-done.7.rest_0_, ...), custom_call_target="tpu_custom_call" | custom-call | flops 75497472 | bytes 262144 | tf_op jit(solution)/shard_map/video_attention/pallas_call | solution.py:221
  122.1 1.3 slice_select_fusion.3
  123.4 7.0 %collective-permute-start.13 = (bf16[272,768]{1,0:T(8,128)(2,1)S(1)}, bf16[272,768]{1,0:T(8,128)(2,1)S(1)}, u32[]{:S(2)}, u32[]{:S(2)}) collective-permute-start(bf16[272,768]{1,0:T(8,128)(2,1)S(1)} %slice_select_fusion.3), channel_id=1, source_target_pairs={{0,3},{2,0},{3,1},{4,7},{7,4},{8,11},{11,8},{12,15},{14,13},{15,12... | collective-permute-start | bytes 1253384 | tf_op jit(solution)/shard_map/ppermute | solution.py:500
  130.4 1.2 slice_select_fusion.5
  131.5 1.9 collective-permute-start.14
  133.5 1.0 slice.84
  134.5 1.0 pad_maximum_fusion.3
  135.4 1.9 collective-permute-start.6
  137.4 1.9 text_merge.2
  139.3 6.6 %collective-permute-done.14.rest_3_ = bf16[256,768]{1,0:T(8,128)(2,1)S(1)} collective-permute-done((bf16[256,768]{1,0:T(8,128)(2,1)S(1)}, bf16[256,768]{1,0:T(8,128)(2,1)S(1)}, u32[]{:S(2)}, u32[]{:S(2)}) %collective-permute-start.14) | collective-permute-done | bytes 393248 | tf_op jit(solution)/shard_map/ppermute | solution.py:500
  145.9 11.2 %collective-permute-start.5 = (bf16[528,512]{1,0:T(8,128)(2,1)}, bf16[528,512]{1,0:T(8,128)(2,1)}, u32[]{:S(2)}, u32[]{:S(2)}) collective-permute-start(bf16[528,512]{1,0:T(8,128)(2,1)} %pad_maximum_fusion.3), channel_id=1, source_target_pairs={{2,6},{3,7},{4,8},{5,9},{6,10},{7,11},{8,12},{9,13},{10,14},{11,15... | collective-permute-start | bytes 1622024 | tf_op jit(solution)/shard_map/ppermute | solution.py:464
  157.2 8.7 %video_attention.5.rest_8_ = bf16[256,3072]{1,0:T(8,128)(2,1)} custom-call(s32[17]{0:T(128)S(1)} %concatenate.33.table, bf16[256,3072]{1,0:T(8,128)(2,1)S(1)} %copy-done.2, bf16[256,3072]{1,0:T(8,128)(2,1)S(1)} %copy-done.1, bf16[256,3072]{1,0:T(8,128)(2,1)} %v_own.7, ...), custom_call_target="tpu_custom_call", output_to_operand_aliasing={{}: (12, {})} | custom-call | flops 56623104 | bytes 196608 | tf_op jit(solution)/shard_map/video_attention/pallas_call | solution.py:221
  166.8 3.0 %collective-permute-start.15 = (bf16[272,768]{1,0:T(8,128)(2,1)}, bf16[272,768]{1,0:T(8,128)(2,1)}, u32[]{:S(2)}, u32[]{:S(2)}) collective-permute-start(bf16[272,768]{1,0:T(8,128)(2,1)} %slice_select_fusion.2), channel_id=1, source_target_pairs={{0,3},{2,0},{3,1},{4,7},{7,4},{8,11},{11,8},{12,15},{14,13},{15,12... | collective-permute-start | bytes 1253384 | tf_op jit(solution)/shard_map/ppermute | solution.py:500
  170.6 2.7 %collective-permute-start.16 = (bf16[256,768]{1,0:T(8,128)(2,1)}, bf16[256,768]{1,0:T(8,128)(2,1)S(1)}, u32[]{:S(2)}, u32[]{:S(2)}) collective-permute-start(bf16[256,768]{1,0:T(8,128)(2,1)} %slice_select_fusion.4), channel_id=1, source_target_pairs={{0,3},{2,0},{3,1},{4,7},{7,4},{8,11},{11,8},{12,15},{14,13},{15,12... | collective-permute-start | bytes 1179656 | tf_op jit(solution)/shard_map/ppermute | solution.py:500
  173.3 6.4 %collective-permute-done.20.refs_1_ = f32[64,1664]{1,0:T(8,128)S(1)} collective-permute-done((f32[64,1664]{1,0:T(8,128)S(1)}, f32[64,1664]{1,0:T(8,128)S(1)}, u32[]{:S(2)}, u32[]{:S(2)}) %collective-permute-start.20) | collective-permute-done | bytes 426016 | tf_op jit(solution)/shard_map/ppermute | solution.py:481
  179.8 1.1 text_merge.3
  181.7 6.6 %collective-permute-done.16.rest_3_ = bf16[256,768]{1,0:T(8,128)(2,1)S(1)} collective-permute-done((bf16[256,768]{1,0:T(8,128)(2,1)}, bf16[256,768]{1,0:T(8,128)(2,1)S(1)}, u32[]{:S(2)}, u32[]{:S(2)}) %collective-permute-start.16) | collective-permute-done | bytes 393248 | tf_op jit(solution)/shard_map/ppermute | solution.py:500
  188.3 5.2 %collective-permute-done.21.refs_1_ = f32[32,1664]{1,0:T(8,128)} collective-permute-done((f32[32,1664]{1,0:T(8,128)}, f32[32,1664]{1,0:T(8,128)}, u32[]{:S(2)}, u32[]{:S(2)}) %collective-permute-start.21) | collective-permute-done | bytes 213024 | tf_op jit(solution)/shard_map/ppermute | solution.py:481
  193.6 0.9 copy-done.11
  194.5 1.2 text_finish.1
  195.8 1.1 copy-done.4
  197.0 1.1 copy-done.6
  198.1 8.6 %video_attention.6.rest_8_ = bf16[256,3072]{1,0:T(8,128)(2,1)} custom-call(s32[17]{0:T(128)S(1)} %concatenate.33.table, bf16[256,3072]{1,0:T(8,128)(2,1)S(1)} %copy-done.2, bf16[256,3072]{1,0:T(8,128)(2,1)S(1)} %copy-done.1, bf16[256,3072]{1,0:T(8,128)(2,1)} %v_own.7, bf16[528,768]{1,0:T(8,128)(2,1)S(1)} %copy-done.6, ...), custom_call_target="tpu_custom_call", output_to_operand_aliasing={{}: (12, {})} | custom-call | flops 56623104 | bytes 196608 | tf_op jit(solution)/shard_map/video_attention/pallas_call | solution.py:221
  206.7 1.1 slice_select_fusion.6
  207.8 1.1 slice_select_fusion.7
  208.9 1.9 collective-permute-start.18
  210.8 3.6 %collective-permute-start.17 = (bf16[272,512]{1,0:T(8,128)(2,1)S(1)}, bf16[272,512]{1,0:T(8,128)(2,1)S(1)}, u32[]{:S(2)}, u32[]{:S(2)}) collective-permute-start(bf16[272,512]{1,0:T(8,128)(2,1)S(1)} %slice_select_fusion.6), channel_id=1, source_target_pairs={{0,3},{3,0},{4,7},{7,4},{8,11},{11,8},{12,15},{14,13},{15,12},{16,... | collective-permute-start | bytes 835592 | tf_op jit(solution)/shard_map/ppermute | solution.py:500
  215.1 3.7 %collective-permute-done.18.rest_3_ = bf16[256,512]{1,0:T(8,128)(2,1)S(1)} collective-permute-done((bf16[256,512]{1,0:T(8,128)(2,1)S(1)}, bf16[256,512]{1,0:T(8,128)(2,1)S(1)}, u32[]{:S(2)}, u32[]{:S(2)}) %collective-permute-start.18) | collective-permute-done | bytes 262176 | tf_op jit(solution)/shard_map/ppermute | solution.py:500
  218.8 6.0 %collective-permute-done.17.rest_2_ = bf16[272,512]{1,0:T(8,128)(2,1)S(1)} collective-permute-done((bf16[272,512]{1,0:T(8,128)(2,1)S(1)}, bf16[272,512]{1,0:T(8,128)(2,1)S(1)}, u32[]{:S(2)}, u32[]{:S(2)}) %collective-permute-start.17) | collective-permute-done | bytes 278560 | tf_op jit(solution)/shard_map/ppermute | solution.py:500
  224.8 6.3 %video_attention.7 = bf16[256,3072]{1,0:T(8,128)(2,1)} custom-call(s32[17]{0:T(128)S(1)} %concatenate.33.table, bf16[256,3072]{1,0:T(8,128)(2,1)S(1)} %copy-done.2, bf16[256,3072]{1,0:T(8,128)(2,1)S(1)} %copy-done.1, bf16[256,3072]{1,0:T(8,128)(2,1)} %v_own.7, bf16[528,512]{1,0:T(8,128)(2,1)} %collective-permute-done.5.rest_0_, ...), custom_call_target="tpu_custom_call", output_to_operand_aliasing={{}: (12, {})} | custom-call | flops 37748736 | bytes 131072 | tf_op jit(solution)/shard_map/video_attention/pallas_call | solution.py:221
  (79 shorter events, 7.2 us)
Async XLA Ops:
  0.6 15.9 %collective-permute-start.1 = (bf16[256,3072]{1,0:T(8,128)(2,1)}, bf16[256,3072]{1,0:T(8,128)(2,1)}, u32[]{:S(2)}, u32[]{:S(2)}) collective-permute-start(bf16[256,3072]{1,0:T(8,128)(2,1)} %k_own.7), channel_id=1, source_target_pairs={{0,1},{1,0},{2,3},{3,2},{4,5},{5,4},{6,7},{7,6},{8,9},{9,8},{10,11... | collective-permute-start | bytes 4718600 | tf_op jit(solution)/shard_map/ppermute | solution.py:468
  0.7 15.8 %collective-permute-start.2 = (bf16[256,3072]{1,0:T(8,128)(2,1)}, bf16[256,3072]{1,0:T(8,128)(2,1)}, u32[]{:S(2)}, u32[]{:S(2)}) collective-permute-start(bf16[256,3072]{1,0:T(8,128)(2,1)} %v_own.7), channel_id=1, source_target_pairs={{0,1},{1,0},{2,3},{3,2},{4,5},{5,4},{6,7},{7,6},{8,9},{9,8},{10,11... | collective-permute-start | bytes 4718600 | tf_op jit(solution)/shard_map/ppermute | solution.py:468
  1.2 15.2 %collective-permute-start = (s32[2]{0:T(128)}, s32[2]{0:T(128)S(1)}, u32[]{:S(2)}, u32[]{:S(2)}) collective-permute-start(s32[2]{0:T(128)} %param.19), channel_id=1, source_target_pairs={{0,1},{1,0},{2,3},{3,2},{4,5},{5,4},{6,7},{7,6},{8,9},{9,8},{10,11... | collective-permute-start | bytes 32 | tf_op jit(solution)/shard_map/ppermute | solution.py:468
  3.0 10.2 %copy-start.14 = (s32[2,6]{1,0:T(2,128)S(1)}, s32[2,6]{1,0:T(2,128)}, u32[]{:S(2)}) copy-start(s32[2,6]{1,0:T(2,128)} %param.18) | copy-start | bytes 148
  3.0 10.2 %copy-start.17 = (s32[16]{0:T(128)S(1)}, s32[16]{0:T(128)}, u32[]{:S(2)}) copy-start(s32[16]{0:T(128)} %constant.81.clone) | copy-start | bytes 196
  3.0 10.4 %copy-start.16 = (s32[16]{0:T(128)S(1)}, s32[16]{0:T(128)}, u32[]{:S(2)}) copy-start(s32[16]{0:T(128)} %constant.79.clone) | copy-start | bytes 196
  3.1 11.7 %copy-start = (bf16[256,3072]{1,0:T(8,128)(2,1)S(1)}, bf16[256,3072]{1,0:T(8,128)(2,1)}, u32[]{:S(2)}) copy-start(bf16[256,3072]{1,0:T(8,128)(2,1)} %k_own.7) | copy-start | bytes 4718596
  5.5 30.5 %collective-permute-start.8 = (bf16[528,1024]{1,0:T(8,128)(2,1)}, bf16[528,1024]{1,0:T(8,128)(2,1)S(1)}, u32[]{:S(2)}, u32[]{:S(2)}) collective-permute-start(bf16[528,1024]{1,0:T(8,128)(2,1)} %pad_maximum_fusion), channel_id=1, source_target_pairs={{0,12},{1,14},{4,0},{6,2},{7,3},{8,4},{9,5},{10,6},{11,7},{12,8},{... | collective-permute-start | bytes 3244040 | tf_op jit(solution)/shard_map/ppermute | solution.py:464
  7.9 69.1 %collective-permute-start.7 = (bf16[528,1024]{1,0:T(8,128)(2,1)}, bf16[528,1024]{1,0:T(8,128)(2,1)}, u32[]{:S(2)}, u32[]{:S(2)}) collective-permute-start(bf16[528,1024]{1,0:T(8,128)(2,1)} %pad_maximum_fusion), channel_id=1, source_target_pairs={{2,6},{3,7},{4,8},{5,9},{6,10},{7,11},{8,12},{9,13},{10,14},{11,15... | collective-permute-start | bytes 3244040 | tf_op jit(solution)/shard_map/ppermute | solution.py:464
  13.4 1.4 copy-start.13
  14.9 1.5 copy-start.15
  14.9 5.5 %copy-start.7 = (bf16[256,3072]{1,0:T(8,128)(2,1)S(1)}, bf16[256,3072]{1,0:T(8,128)(2,1)}, u32[]{:S(2)}) copy-start(bf16[256,3072]{1,0:T(8,128)(2,1)} %q.5) | copy-start | bytes 4718596
  16.5 105.5 %collective-permute-start.4 = (bf16[528,768]{1,0:T(8,128)(2,1)}, bf16[528,768]{1,0:T(8,128)(2,1)}, u32[]{:S(2)}, u32[]{:S(2)}) collective-permute-start(bf16[528,768]{1,0:T(8,128)(2,1)} %get-tuple-element.24), channel_id=1, source_target_pairs={{0,12},{1,14},{4,0},{6,2},{7,3},{8,4},{9,5},{10,6},{11,7},{12,8},{... | collective-permute-start | bytes 2433032 | tf_op jit(solution)/shard_map/ppermute | solution.py:464
  18.4 103.6 %collective-permute-start.3 = (bf16[528,768]{1,0:T(8,128)(2,1)}, bf16[528,768]{1,0:T(8,128)(2,1)}, u32[]{:S(2)}, u32[]{:S(2)}) collective-permute-start(bf16[528,768]{1,0:T(8,128)(2,1)} %get-tuple-element.24), channel_id=1, source_target_pairs={{2,6},{3,7},{4,8},{5,9},{6,10},{7,11},{8,12},{9,13},{10,14},{11,15... | collective-permute-start | bytes 2433032 | tf_op jit(solution)/shard_map/ppermute | solution.py:464
  28.5 54.3 %copy-start.8 = (f32[128,1792]{1,0:T(8,128)}, f32[128,1792]{1,0:T(8,128)S(1)}, u32[]{:S(2)}) copy-start(f32[128,1792]{1,0:T(8,128)S(1)} %get-tuple-element.36.refs_0_) | copy-start | bytes 2752516
  28.5 58.0 %copy-start.12 = (f32[128,1792]{1,0:T(8,128)}, f32[128,1792]{1,0:T(8,128)S(1)}, u32[]{:S(2)}) copy-start(f32[128,1792]{1,0:T(8,128)S(1)} %get-tuple-element.37) | copy-start | bytes 2752516
  77.0 34.2 %copy-start.2 = (bf16[256,3072]{1,0:T(8,128)(2,1)S(1)}, bf16[256,3072]{1,0:T(8,128)(2,1)}, u32[]{:S(2)}) copy-start(bf16[256,3072]{1,0:T(8,128)(2,1)} %q.9) | copy-start | bytes 4718596
  79.0 30.2 %collective-permute-start.11 = (bf16[272,1024]{1,0:T(8,128)(2,1)}, bf16[272,1024]{1,0:T(8,128)(2,1)S(1)}, u32[]{:S(2)}, u32[]{:S(2)}) collective-permute-start(bf16[272,1024]{1,0:T(8,128)(2,1)} %slice_select_fusion), channel_id=1, source_target_pairs={{0,3},{3,0},{4,7},{7,4},{8,11},{11,8},{12,15},{14,13},{15,12},{16,... | collective-permute-start | bytes 1671176 | tf_op jit(solution)/shard_map/ppermute | solution.py:500
  82.8 24.5 %collective-permute-start.12 = (bf16[256,1024]{1,0:T(8,128)(2,1)}, bf16[256,1024]{1,0:T(8,128)(2,1)}, u32[]{:S(2)}, u32[]{:S(2)}) collective-permute-start(bf16[256,1024]{1,0:T(8,128)(2,1)} %slice_select_fusion.1), channel_id=1, source_target_pairs={{0,3},{3,0},{4,7},{7,4},{8,11},{11,8},{12,15},{14,13},{15,12},{16,... | collective-permute-start | bytes 1572872 | tf_op jit(solution)/shard_map/ppermute | solution.py:500
  86.9 48.5 %collective-permute-start.19 = (f32[128,1792]{1,0:T(8,128)}, f32[128,1792]{1,0:T(8,128)}, u32[]{:S(2)}, u32[]{:S(2)}) collective-permute-start(f32[128,1792]{1,0:T(8,128)} %copy-done.12), channel_id=1, source_target_pairs={{0,2},{1,3},{2,0},{3,1},{4,6},{5,7},{6,4},{7,5},{8,10},{9,11},{10,... | collective-permute-start | bytes 2752520 | tf_op jit(solution)/shard_map/ppermute | solution.py:481
  107.3 58.6 %collective-permute-start.10 = (bf16[528,768]{1,0:T(8,128)(2,1)}, bf16[528,768]{1,0:T(8,128)(2,1)S(1)}, u32[]{:S(2)}, u32[]{:S(2)}) collective-permute-start(bf16[528,768]{1,0:T(8,128)(2,1)} %get-tuple-element.26), channel_id=1, source_target_pairs={{0,12},{1,14},{4,0},{6,2},{7,3},{8,4},{9,5},{10,6},{11,7},{12,8},{... | collective-permute-start | bytes 2433032 | tf_op jit(solution)/shard_map/ppermute | solution.py:464
  109.2 56.7 %collective-permute-start.9 = (bf16[528,768]{1,0:T(8,128)(2,1)}, bf16[528,768]{1,0:T(8,128)(2,1)S(1)}, u32[]{:S(2)}, u32[]{:S(2)}) collective-permute-start(bf16[528,768]{1,0:T(8,128)(2,1)} %get-tuple-element.26), channel_id=1, source_target_pairs={{2,6},{3,7},{4,8},{5,9},{6,10},{7,11},{8,12},{9,13},{10,14},{11,15... | collective-permute-start | bytes 2433032 | tf_op jit(solution)/shard_map/ppermute | solution.py:464
  122.1 11.4 %copy-start.1 = (bf16[256,3072]{1,0:T(8,128)(2,1)S(1)}, bf16[256,3072]{1,0:T(8,128)(2,1)}, u32[]{:S(2)}) copy-start(bf16[256,3072]{1,0:T(8,128)(2,1)} %k_own.7) | copy-start | bytes 4718596
  123.4 14.0 %copy-start.9 = (f32[128,1792]{1,0:T(8,128)S(1)}, f32[128,1792]{1,0:T(8,128)}, u32[]{:S(2)}) copy-start(f32[128,1792]{1,0:T(8,128)} %copy-done.8) | copy-start | bytes 2752516
  123.4 33.7 %collective-permute-start.13 = (bf16[272,768]{1,0:T(8,128)(2,1)S(1)}, bf16[272,768]{1,0:T(8,128)(2,1)S(1)}, u32[]{:S(2)}, u32[]{:S(2)}) collective-permute-start(bf16[272,768]{1,0:T(8,128)(2,1)S(1)} %slice_select_fusion.3), channel_id=1, source_target_pairs={{0,3},{2,0},{3,1},{4,7},{7,4},{8,11},{11,8},{12,15},{14,13},{15,12... | collective-permute-start | bytes 1253384 | tf_op jit(solution)/shard_map/ppermute | solution.py:500
  131.5 14.4 %collective-permute-start.14 = (bf16[256,768]{1,0:T(8,128)(2,1)S(1)}, bf16[256,768]{1,0:T(8,128)(2,1)S(1)}, u32[]{:S(2)}, u32[]{:S(2)}) collective-permute-start(bf16[256,768]{1,0:T(8,128)(2,1)S(1)} %slice_select_fusion.5), channel_id=1, source_target_pairs={{0,3},{2,0},{3,1},{4,7},{7,4},{8,11},{11,8},{12,15},{14,13},{15,12... | collective-permute-start | bytes 1179656 | tf_op jit(solution)/shard_map/ppermute | solution.py:500
  135.4 71.3 %collective-permute-start.6 = (bf16[528,512]{1,0:T(8,128)(2,1)}, bf16[528,512]{1,0:T(8,128)(2,1)}, u32[]{:S(2)}, u32[]{:S(2)}) collective-permute-start(bf16[528,512]{1,0:T(8,128)(2,1)} %pad_maximum_fusion.3), channel_id=1, source_target_pairs={{0,12},{1,14},{4,0},{6,2},{7,3},{8,4},{9,5},{10,6},{11,7},{12,8},{... | collective-permute-start | bytes 1622024 | tf_op jit(solution)/shard_map/ppermute | solution.py:464
  145.9 60.8 %collective-permute-start.5 = (bf16[528,512]{1,0:T(8,128)(2,1)}, bf16[528,512]{1,0:T(8,128)(2,1)}, u32[]{:S(2)}, u32[]{:S(2)}) collective-permute-start(bf16[528,512]{1,0:T(8,128)(2,1)} %pad_maximum_fusion.3), channel_id=1, source_target_pairs={{2,6},{3,7},{4,8},{5,9},{6,10},{7,11},{8,12},{9,13},{10,14},{11,15... | collective-permute-start | bytes 1622024 | tf_op jit(solution)/shard_map/ppermute | solution.py:464
  157.1 22.6 %collective-permute-start.20 = (f32[64,1664]{1,0:T(8,128)S(1)}, f32[64,1664]{1,0:T(8,128)S(1)}, u32[]{:S(2)}, u32[]{:S(2)}) collective-permute-start(f32[64,1664]{1,0:T(8,128)S(1)} %get-tuple-element.40), channel_id=1, source_target_pairs={{0,4},{1,5},{2,6},{3,7},{4,0},{5,1},{6,2},{7,3},{8,12},{9,13},{10,... | collective-permute-start | bytes 1277960 | tf_op jit(solution)/shard_map/ppermute | solution.py:481
  165.9 15.1 %copy-start.3 = (bf16[528,768]{1,0:T(8,128)(2,1)}, bf16[528,768]{1,0:T(8,128)(2,1)S(1)}, u32[]{:S(2)}) copy-start(bf16[528,768]{1,0:T(8,128)(2,1)S(1)} %collective-permute-done.10.rest_1_) | copy-start | bytes 2433028
  165.9 15.0 %copy-start.5 = (bf16[528,768]{1,0:T(8,128)(2,1)}, bf16[528,768]{1,0:T(8,128)(2,1)S(1)}, u32[]{:S(2)}) copy-start(bf16[528,768]{1,0:T(8,128)(2,1)S(1)} %collective-permute-done.9.rest_0_) | copy-start | bytes 2433028
  166.8 21.5 %collective-permute-start.15 = (bf16[272,768]{1,0:T(8,128)(2,1)}, bf16[272,768]{1,0:T(8,128)(2,1)}, u32[]{:S(2)}, u32[]{:S(2)}) collective-permute-start(bf16[272,768]{1,0:T(8,128)(2,1)} %slice_select_fusion.2), channel_id=1, source_target_pairs={{0,3},{2,0},{3,1},{4,7},{7,4},{8,11},{11,8},{12,15},{14,13},{15,12... | collective-permute-start | bytes 1253384 | tf_op jit(solution)/shard_map/ppermute | solution.py:500
  170.6 17.7 %collective-permute-start.16 = (bf16[256,768]{1,0:T(8,128)(2,1)}, bf16[256,768]{1,0:T(8,128)(2,1)S(1)}, u32[]{:S(2)}, u32[]{:S(2)}) collective-permute-start(bf16[256,768]{1,0:T(8,128)(2,1)} %slice_select_fusion.4), channel_id=1, source_target_pairs={{0,3},{2,0},{3,1},{4,7},{7,4},{8,11},{11,8},{12,15},{14,13},{15,12... | collective-permute-start | bytes 1179656 | tf_op jit(solution)/shard_map/ppermute | solution.py:500
  180.9 0.7 copy-start.10
  181.6 11.9 %collective-permute-start.21 = (f32[32,1664]{1,0:T(8,128)}, f32[32,1664]{1,0:T(8,128)}, u32[]{:S(2)}, u32[]{:S(2)}) collective-permute-start(f32[32,1664]{1,0:T(8,128)} %get-tuple-element.43), channel_id=1, source_target_pairs={{0,8},{1,9},{2,10},{3,11},{4,12},{5,13},{6,14},{7,15},{8,0},{9,1},... | collective-permute-start | bytes 638984 | tf_op jit(solution)/shard_map/ppermute | solution.py:481
  193.6 0.9 copy-start.11
  195.7 18.7 %collective-permute-start.22 = (bf16[16,1536]{1,0:T(8,128)(2,1)S(1)}, bf16[16,1536]{1,0:T(8,128)(2,1)S(1)}, u32[]{:S(2)}, u32[]{:S(2)}) collective-permute-start(bf16[16,1536]{1,0:T(8,128)(2,1)S(1)} %get-tuple-element.45), channel_id=1, source_target_pairs={{0,1},{1,0},{2,3},{3,2},{4,5},{5,4},{6,7},{7,6},{8,9},{9,8},{10,11... | collective-permute-start | bytes 147464 | tf_op jit(solution)/shard_map/ppermute | solution.py:514
  195.8 1.1 copy-start.4
  197.0 1.1 copy-start.6
  208.9 9.9 %collective-permute-start.18 = (bf16[256,512]{1,0:T(8,128)(2,1)S(1)}, bf16[256,512]{1,0:T(8,128)(2,1)S(1)}, u32[]{:S(2)}, u32[]{:S(2)}) collective-permute-start(bf16[256,512]{1,0:T(8,128)(2,1)S(1)} %slice_select_fusion.7), channel_id=1, source_target_pairs={{0,3},{3,0},{4,7},{7,4},{8,11},{11,8},{12,15},{14,13},{15,12},{16,... | collective-permute-start | bytes 786440 | tf_op jit(solution)/shard_map/ppermute | solution.py:500
  210.8 14.0 %collective-permute-start.17 = (bf16[272,512]{1,0:T(8,128)(2,1)S(1)}, bf16[272,512]{1,0:T(8,128)(2,1)S(1)}, u32[]{:S(2)}, u32[]{:S(2)}) collective-permute-start(bf16[272,512]{1,0:T(8,128)(2,1)S(1)} %slice_select_fusion.6), channel_id=1, source_target_pairs={{0,3},{3,0},{4,7},{7,4},{8,11},{11,8},{12,15},{14,13},{15,12},{16,... | collective-permute-start | bytes 835592 | tf_op jit(solution)/shard_map/ppermute | solution.py:500

commit v4 on v3

--- a/solution.py
+++ b/solution.py
@@ -14,7 +14,6 @@
 BLOCKS = 5
 STEP_HEADS = 2
 CHUNK_HEADS = (8, 6, 6, 4)
-DIVERTED = (False, True, True, False)
 PAD_ROWS = 16
 VMEM_BYTES = 48 * 1024 * 1024
 LOG2E = 1.4426950408889634
@@ -25,7 +24,7 @@
     return n // 2 + NR + NR // 2
 
 
-def plan_moves(n, diverted):
+def plan_moves(n):
     shift, times = spot_shift(n), n // NR
     last = times - 1
 
@@ -41,18 +40,8 @@
     relay_later = {at(t - 1, 2): at(t, 1) for t in range(1, times)}
     moves["later"][at(0, 2)] = at(last, 2)
     relay_later[at(last, 2)] = at(0, 1)
-    if times == 4:
-        moves["later"][at(3, 3)] = at(3, 0)
-        relay_later[at(3, 0)] = at(2, 3)
-    if times == 4 and diverted:
-        moves["earlier"][at(2, 2)] = at(0, 0)
-        relay_earlier[at(0, 0)] = at(3, 2)
-        moves["earlier"][at(2, 3)] = at(0, 1)
-        relay_earlier[at(0, 1)] = at(3, 3)
-        moves["earlier"][at(3, 1)] = at(3, 2)
-    else:
-        moves["earlier"][at(last, 1)] = at(0, 1)
-        relay_earlier[at(0, 1)] = at(last, 2)
+    moves["earlier"][at(last, 1)] = at(0, 1)
+    relay_earlier[at(0, 1)] = at(last, 2)
     assert not set(relay_earlier) & set(relay_later)
     moves["relayed"] = {**relay_earlier, **relay_later}
     held = {"own": {d: d for d in range(n)}}
@@ -98,7 +87,7 @@
 TABLE_COUNTS, TABLE_BESIDE, TABLE_TEXT, TABLE_CHOICE = 4, 6, 8, 9
 
 
-def video_kernel(kind, table, q, k_own, v_own, *rest):
+def video_kernel(table, q, k_own, v_own, *rest):
     packed = {"earlier": rest[0], "later": rest[1]}
     relayed_k, relayed_v, beside_k, beside_v, text_k, text_v = rest[2:8]
     out, k_all, v_all, bias_all = rest[-4:]
@@ -133,7 +122,7 @@
     options = {1: ("earlier",), 2: ("later",), 3: ("earlier",), 4: ("later",)}
     zeros = jnp.zeros((tok, HD), k_all.dtype)
     for block in range(1, BLOCKS):
-        chosen = table[TABLE_CHOICE + 4 * kind + block - 1]
+        chosen = table[TABLE_CHOICE + block - 1]
         for name in options[block]:
 
             @pl.when(chosen == SOURCES.index(name))
@@ -195,7 +184,7 @@
             out[pl.ds(c * tok, tok), cols] = jnp.where(valid, acc / denom, 0.0).astype(out.dtype)
 
 
-def video_call(kind, first, heads, table, q, k, v, near, text_k, text_v, carried):
+def video_call(first, heads, table, q, k, v, near, text_k, text_v, carried):
     rows, width = q.shape
     text = text_k.shape[0]
     tok = rows // 2
@@ -219,7 +208,7 @@
     cells = 2 * BLOCKS + 1
     keys = 7 * tok + text
     return pl.pallas_call(
-        functools.partial(video_kernel, kind),
+        video_kernel,
         grid=(heads // STEP_HEADS,),
         in_specs=in_specs,
         out_specs=own_spec,
@@ -444,9 +433,8 @@
     rows, width = video_q.shape
     text = text_q.shape[0]
     position = lax.axis_index("tiles").astype(jnp.int32)
-    plans = [plan_moves(n, kind) for kind in (False, True)]
-    choices = [plans[0][2][d] + plans[1][2][d] for d in range(n)]
-    sends_later = jnp.array(plans[0][1], jnp.int32)[position] == 1
+    pairs, relays_later, choices = plan_moves(n)
+    sends_later = jnp.array(relays_later, jnp.int32)[position] == 1
 
     limits = jnp.concatenate([counts, jnp.zeros((PAD_ROWS - counts.shape[0],), jnp.int32)])
     limits = jnp.broadcast_to(limits.astype(jnp.bfloat16)[:, None], (PAD_ROWS, width))
@@ -460,12 +448,11 @@
     def send(i, *before):
         cols = slice(starts[i] * HD, (starts[i] + CHUNK_HEADS[i]) * HD)
         mine = tie(pack(cols), *before)
-        pairs = plans[DIVERTED[i]][0]
         direct.append([lax.ppermute(mine, "tiles", pairs[x]) for x in ("earlier", "later")])
 
     send(0)
     beside = [
-        lax.ppermute(x, "tiles", plans[0][0]["beside"]) for x in (counts, video_k, video_v)
+        lax.ppermute(x, "tiles", pairs["beside"]) for x in (counts, video_k, video_v)
     ]
     send(1, *beside)
     table = make_table(window, counts, beside[0], text_count, choices, position)
@@ -490,11 +477,11 @@
             limits = jnp.concatenate(limits)
             parts.append(text_finish(tie(parts[i][0], *before), exchanged(i), limits))
 
+    merge()
     count = len(CHUNK_HEADS)
     for i in range(count):
-        pairs = plans[DIVERTED[i]][0]
         up, down = direct[i]
-        before = [parts[0][0]] if halving and i == 0 else outs[-1:]
+        before = [parts[-1][0]] if halving and i == 0 else outs[-1:]
         up, down = tie(up, *before), tie(down, *before)
         relays = [
             lax.ppermute(jnp.where(sends_later, down[half], up[half]), "tiles", pairs["relayed"])
@@ -502,10 +489,11 @@
         ]
         if i + 2 < count:
             send(i + 2, *direct[i])
-        merge(*relays)
+        if i:
+            merge(*relays)
         outs.append(
             video_call(
-                int(DIVERTED[i]), starts[i], CHUNK_HEADS[i], table, video_q, video_k, video_v,
+                starts[i], CHUNK_HEADS[i], table, video_q, video_k, video_v,
                 [*direct[i], *relays, *beside[1:]], text_k, text_v, outs[-1] if outs else None,
             )
         )

time: 233 us -> 209 us (0.90)
  waiting for transfers between devices: 102 us -> 76.9 us
  starting transfers between devices: 55 us -> 52.5 us
  local copies, waits for them, and re-layouts: 9.03 us -> 11.4 us
    ppermute x8, waiting for transfers between devices: 41.7 us -> 6.88 us  [per_device(): lax.ppermute(jnp.where(sends_later, down[half], up[half]), 'tiles', pairs...]
    ppermute x3, waiting for transfers between devices: 11.6 us -> 36.5 us  [exchanged(): lax.ppermute(parts[i][1], 'tiles', [(d, d ^ 2 << i) for d in range(n)])]
    ppermute x8, waiting for transfers between devices: 48.5 us -> 33.5 us  [send(): lax.ppermute(mine, 'tiles', pairs[x])]
    ppermute x8, starting transfers between devices: 25.7 us -> 22.5 us  [per_device(): lax.ppermute(jnp.where(sends_later, down[half], up[half]), 'tiles', pairs...]
    unnamed x36 -> x42, local copies, waits for them, and re-layouts: 4.02 us -> 6.41 us
  transfers between devices with their start and end apart: 23 -> 23, of which waited for: 9 -> 9; matrix products, arithmetic and copies ran while one was open for 9% -> 10% of each run, Pallas kernels for 18% -> 20%
where the time goes in v4:
time: 209 us; the launch traced here: 207 us
  waiting for transfers between devices  76.9 us (37%)
  starting transfers between devices  52.5 us (25%)
  Pallas kernels  47.5 us (23%)
  other arithmetic  15.9 us (8%)
  local copies, waits for them, and re-layouts  11.4 us (5%)
  between operations  2.38 us (1%)
    ppermute x3, waiting for transfers between devices, exchanged(): lax.ppermute(parts[i][1], 'tiles', [(d, d ^ 2 << i) for d in range(n)])  36.5 us
    pallas_call x4, Pallas kernels, video_call(): pl.pallas_call(video_kernel, grid=(heads // STEP_HEADS,), in_specs=in_spe...  34.5 us
    ppermute x8, waiting for transfers between devices, send(): lax.ppermute(mine, 'tiles', pairs[x])  33.5 us
    ppermute x8, starting transfers between devices, send(): lax.ppermute(mine, 'tiles', pairs[x])  28.1 us
    ppermute x8, starting transfers between devices, per_device(): lax.ppermute(jnp.where(sends_later, down[half], up[half]), 'tiles', pairs...  22.5 us
    select_n x8, other arithmetic, per_device(): jnp.where(sends_later, down[half], up[half])  10.2 us
    pallas_call x1, Pallas kernels, text_local(): pl.pallas_call(text_kernel, grid_spec=pltpu.PrefetchScalarGridSpec(num_sc...  8.72 us
    ppermute x8, waiting for transfers between devices, per_device(): lax.ppermute(jnp.where(sends_later, down[half], up[half]), 'tiles', pairs...  6.88 us
  transfers between devices with their start and end apart: 23, of which 9 were waited for; matrix products, arithmetic and copies ran while one was open for 10% of the time, Pallas kernels for 20%

profile of v4, /device:TPU:24, one launch (start us, length us, event | category | flops | bytes accessed | tf_op | source)
XLA Modules:
  0.0 206.7 jit_solution(9009953209162797190)
XLA Ops:
  1.9 1.1 slice.90
  3.1 1.2 slice.92
  4.3 1.2 pad_maximum_fusion
  5.5 2.3 %collective-permute-start.8 = (bf16[528,1024]{1,0:T(8,128)(2,1)}, bf16[528,1024]{1,0:T(8,128)(2,1)S(1)}, u32[]{:S(2)}, u32[]{:S(2)}) collective-permute-start(bf16[528,1024]{1,0:T(8,128)(2,1)} %pad_maximum_fusion), channel_id=1, source_target_pairs={{0,12},{1,13},{4,0},{6,2},{7,3},{8,4},{9,5},{10,6},{11,7},{12,8},{... | collective-permute-start | bytes 3244040 | tf_op jit(solution)/shard_map/ppermute | solution.py:451
  7.9 5.3 %collective-permute-start.7 = (bf16[528,1024]{1,0:T(8,128)(2,1)}, bf16[528,1024]{1,0:T(8,128)(2,1)}, u32[]{:S(2)}, u32[]{:S(2)}) collective-permute-start(bf16[528,1024]{1,0:T(8,128)(2,1)} %pad_maximum_fusion), channel_id=1, source_target_pairs={{2,6},{3,7},{4,8},{5,9},{6,10},{7,11},{8,12},{9,13},{10,14},{11,15... | collective-permute-start | bytes 3244040 | tf_op jit(solution)/shard_map/ppermute | solution.py:451
  13.4 1.4 copy-done.7
  14.8 8.7 %text_partials.1 = (f32[128,1792]{1,0:T(8,128)S(1)}, f32[128,1792]{1,0:T(8,128)}) custom-call(s32[17]{0:T(128)S(1)} %pad_add_fusion.1.order, s32[4]{0:T(128)S(1)} %pad_add_fusion.2.counts, bf16[256,3072]{1,0:T(8,128)(2,1)S(1)} %copy-done.7, bf16[256,3072]{1,0:T(8,128)(2,1)S(1)} %copy-done, bf16[256,3072]{1,0:T(8,128)(2,1)} %v_own.7, ...), custom_call_target="tpu_custom_call" | custom-call | flops 8388608 | bytes 786432 | tf_op jit(solution)/shard_map/text_partials/pallas_call | solution.py:302
  26.1 1.6 pad_maximum_fusion.2
  27.7 2.1 %collective-permute-start.4 = (bf16[528,768]{1,0:T(8,128)(2,1)}, bf16[528,768]{1,0:T(8,128)(2,1)}, u32[]{:S(2)}, u32[]{:S(2)}) collective-permute-start(bf16[528,768]{1,0:T(8,128)(2,1)} %get-tuple-element.23), channel_id=1, source_target_pairs={{0,12},{1,13},{4,0},{6,2},{7,3},{8,4},{9,5},{10,6},{11,7},{12,8},{... | collective-permute-start | bytes 2433032 | tf_op jit(solution)/shard_map/ppermute | solution.py:451
  29.8 5.5 %collective-permute-start.3 = (bf16[528,768]{1,0:T(8,128)(2,1)}, bf16[528,768]{1,0:T(8,128)(2,1)}, u32[]{:S(2)}, u32[]{:S(2)}) collective-permute-start(bf16[528,768]{1,0:T(8,128)(2,1)} %get-tuple-element.23), channel_id=1, source_target_pairs={{2,6},{3,7},{4,8},{5,9},{6,10},{7,11},{8,12},{9,13},{10,14},{11,15... | collective-permute-start | bytes 2433032 | tf_op jit(solution)/shard_map/ppermute | solution.py:451
  35.3 11.6 %collective-permute-done.11.refs_1_ = f32[128,1792]{1,0:T(8,128)} collective-permute-done((f32[128,1792]{1,0:T(8,128)}, f32[128,1792]{1,0:T(8,128)}, u32[]{:S(2)}, u32[]{:S(2)}) %collective-permute-start.11) | collective-permute-done | bytes 917536 | tf_op jit(solution)/shard_map/ppermute | solution.py:468
  47.0 1.9 text_merge.2
  48.9 27.5 %collective-permute-done.7.rest_0_ = bf16[528,1024]{1,0:T(8,128)(2,1)} collective-permute-done((bf16[528,1024]{1,0:T(8,128)(2,1)}, bf16[528,1024]{1,0:T(8,128)(2,1)}, u32[]{:S(2)}, u32[]{:S(2)}) %collective-permute-start.7) | collective-permute-done | bytes 1081376 | tf_op jit(solution)/shard_map/ppermute | solution.py:451
  76.4 2.0 slice_select_fusion.1
  78.5 1.9 collective-permute-start.13
  80.4 1.9 slice_select_fusion
  82.3 3.6 %collective-permute-start.12 = (bf16[272,1024]{1,0:T(8,128)(2,1)}, bf16[272,1024]{1,0:T(8,128)(2,1)S(1)}, u32[]{:S(2)}, u32[]{:S(2)}) collective-permute-start(bf16[272,1024]{1,0:T(8,128)(2,1)} %slice_select_fusion), channel_id=1, source_target_pairs={{0,3},{3,0},{4,7},{7,4},{8,11},{11,8},{12,15},{15,12},{16,19},{19,... | collective-permute-start | bytes 1671176 | tf_op jit(solution)/shard_map/ppermute | solution.py:487
  87.8 2.4 %collective-permute-start.10 = (bf16[528,768]{1,0:T(8,128)(2,1)}, bf16[528,768]{1,0:T(8,128)(2,1)S(1)}, u32[]{:S(2)}, u32[]{:S(2)}) collective-permute-start(bf16[528,768]{1,0:T(8,128)(2,1)} %get-tuple-element.25), channel_id=1, source_target_pairs={{0,12},{1,13},{4,0},{6,2},{7,3},{8,4},{9,5},{10,6},{11,7},{12,8},{... | collective-permute-start | bytes 2433032 | tf_op jit(solution)/shard_map/ppermute | solution.py:451
  90.2 5.2 %collective-permute-start.9 = (bf16[528,768]{1,0:T(8,128)(2,1)}, bf16[528,768]{1,0:T(8,128)(2,1)S(1)}, u32[]{:S(2)}, u32[]{:S(2)}) collective-permute-start(bf16[528,768]{1,0:T(8,128)(2,1)} %get-tuple-element.25), channel_id=1, source_target_pairs={{2,6},{3,7},{4,8},{5,9},{6,10},{7,11},{8,12},{9,13},{10,14},{11,15... | collective-permute-start | bytes 2433032 | tf_op jit(solution)/shard_map/ppermute | solution.py:451
  95.5 10.9 %video_attention.4.rest_8_ = bf16[256,3072]{1,0:T(8,128)(2,1)} custom-call(s32[13]{0:T(128)S(1)} %concatenate.33.table, bf16[256,3072]{1,0:T(8,128)(2,1)S(1)} %copy-done.2, bf16[256,3072]{1,0:T(8,128)(2,1)} %k_own.7, bf16[256,3072]{1,0:T(8,128)(2,1)} %v_own.7, bf16[528,1024]{1,0:T(8,128)(2,1)} %collective-permute-done.7.rest_0_, ...), custom_call_target="tpu_custom_call" | custom-call | flops 75497472 | bytes 262144 | tf_op jit(solution)/shard_map/video_attention/pallas_call | solution.py:210
  106.4 4.7 %collective-permute-done.3.rest_0_ = bf16[528,768]{1,0:T(8,128)(2,1)} collective-permute-done((bf16[528,768]{1,0:T(8,128)(2,1)}, bf16[528,768]{1,0:T(8,128)(2,1)}, u32[]{:S(2)}, u32[]{:S(2)}) %collective-permute-start.3) | collective-permute-done | bytes 811040 | tf_op jit(solution)/shard_map/ppermute | solution.py:451
  111.2 1.2 slice_select_fusion.3
  112.3 2.1 collective-permute-start.14
  114.4 1.2 slice_select_fusion.5
  115.6 3.6 %collective-permute-start.15 = (bf16[256,768]{1,0:T(8,128)(2,1)S(1)}, bf16[256,768]{1,0:T(8,128)(2,1)S(1)}, u32[]{:S(2)}, u32[]{:S(2)}) collective-permute-start(bf16[256,768]{1,0:T(8,128)(2,1)S(1)} %slice_select_fusion.5), channel_id=1, source_target_pairs={{0,3},{3,0},{4,7},{7,4},{8,11},{11,8},{12,15},{15,12},{16,19},{19,... | collective-permute-start | bytes 1179656 | tf_op jit(solution)/shard_map/ppermute | solution.py:487
  119.3 1.0 slice.84
  121.2 2.4 %collective-permute-start.6 = (bf16[528,512]{1,0:T(8,128)(2,1)}, bf16[528,512]{1,0:T(8,128)(2,1)}, u32[]{:S(2)}, u32[]{:S(2)}) collective-permute-start(bf16[528,512]{1,0:T(8,128)(2,1)} %pad_maximum_fusion.3), channel_id=1, source_target_pairs={{0,12},{1,13},{4,0},{6,2},{7,3},{8,4},{9,5},{10,6},{11,7},{12,8},{... | collective-permute-start | bytes 1622024 | tf_op jit(solution)/shard_map/ppermute | solution.py:451
  123.6 2.4 %collective-permute-done.15.rest_3_ = bf16[256,768]{1,0:T(8,128)(2,1)S(1)} collective-permute-done((bf16[256,768]{1,0:T(8,128)(2,1)S(1)}, bf16[256,768]{1,0:T(8,128)(2,1)S(1)}, u32[]{:S(2)}, u32[]{:S(2)}) %collective-permute-start.15) | collective-permute-done | bytes 393248 | tf_op jit(solution)/shard_map/ppermute | solution.py:487
  126.0 2.8 %collective-permute-start.5 = (bf16[528,512]{1,0:T(8,128)(2,1)}, bf16[528,512]{1,0:T(8,128)(2,1)}, u32[]{:S(2)}, u32[]{:S(2)}) collective-permute-start(bf16[528,512]{1,0:T(8,128)(2,1)} %pad_maximum_fusion.3), channel_id=1, source_target_pairs={{2,6},{3,7},{4,8},{5,9},{6,10},{7,11},{8,12},{9,13},{10,14},{11,15... | collective-permute-start | bytes 1622024 | tf_op jit(solution)/shard_map/ppermute | solution.py:451
  128.9 1.2 collective-permute-start.20
  130.1 8.6 %video_attention.5.rest_8_ = bf16[256,3072]{1,0:T(8,128)(2,1)} custom-call(s32[13]{0:T(128)S(1)} %concatenate.33.table, bf16[256,3072]{1,0:T(8,128)(2,1)S(1)} %copy-done.2, bf16[256,3072]{1,0:T(8,128)(2,1)S(1)} %copy-done.1, bf16[256,3072]{1,0:T(8,128)(2,1)} %v_own.7, ...), custom_call_target="tpu_custom_call", output_to_operand_aliasing={{}: (12, {})} | custom-call | flops 56623104 | bytes 196608 | tf_op jit(solution)/shard_map/video_attention/pallas_call | solution.py:210
  138.7 1.3 collective-permute-done.9.rest_0_
  141.0 1.9 collective-permute-start.16
  143.7 3.8 %collective-permute-start.17 = (bf16[256,768]{1,0:T(8,128)(2,1)}, bf16[256,768]{1,0:T(8,128)(2,1)S(1)}, u32[]{:S(2)}, u32[]{:S(2)}) collective-permute-start(bf16[256,768]{1,0:T(8,128)(2,1)} %slice_select_fusion.4), channel_id=1, source_target_pairs={{0,3},{3,0},{4,7},{7,4},{8,11},{11,8},{12,15},{15,12},{16,19},{19,... | collective-permute-start | bytes 1179656 | tf_op jit(solution)/shard_map/ppermute | solution.py:487
  147.5 13.1 %collective-permute-done.20.refs_1_ = f32[64,1664]{1,0:T(8,128)S(1)} collective-permute-done((f32[64,1664]{1,0:T(8,128)S(1)}, f32[64,1664]{1,0:T(8,128)S(1)}, u32[]{:S(2)}, u32[]{:S(2)}) %collective-permute-start.20) | collective-permute-done | bytes 426016 | tf_op jit(solution)/shard_map/ppermute | solution.py:468
  160.6 1.1 text_merge.3
  162.5 11.8 %collective-permute-done.21.refs_1_ = f32[32,1664]{1,0:T(8,128)} collective-permute-done((f32[32,1664]{1,0:T(8,128)}, f32[32,1664]{1,0:T(8,128)}, u32[]{:S(2)}, u32[]{:S(2)}) %collective-permute-start.21) | collective-permute-done | bytes 213024 | tf_op jit(solution)/shard_map/ppermute | solution.py:468
  175.3 1.2 text_finish.1
  176.6 1.1 copy-done.4
  177.8 1.1 copy-done.6
  178.9 8.6 %video_attention.6.rest_8_ = bf16[256,3072]{1,0:T(8,128)(2,1)} custom-call(s32[13]{0:T(128)S(1)} %concatenate.33.table, bf16[256,3072]{1,0:T(8,128)(2,1)S(1)} %copy-done.2, bf16[256,3072]{1,0:T(8,128)(2,1)S(1)} %copy-done.1, bf16[256,3072]{1,0:T(8,128)(2,1)} %v_own.7, bf16[528,768]{1,0:T(8,128)(2,1)S(1)} %copy-done.6, ...), custom_call_target="tpu_custom_call", output_to_operand_aliasing={{}: (12, {})} | custom-call | flops 56623104 | bytes 196608 | tf_op jit(solution)/shard_map/video_attention/pallas_call | solution.py:210
  187.5 1.1 slice_select_fusion.6
  188.6 1.1 slice_select_fusion.7
  189.7 1.9 collective-permute-start.19
  191.6 3.6 %collective-permute-start.18 = (bf16[272,512]{1,0:T(8,128)(2,1)S(1)}, bf16[272,512]{1,0:T(8,128)(2,1)S(1)}, u32[]{:S(2)}, u32[]{:S(2)}) collective-permute-start(bf16[272,512]{1,0:T(8,128)(2,1)S(1)} %slice_select_fusion.6), channel_id=1, source_target_pairs={{0,3},{3,0},{4,7},{7,4},{8,11},{11,8},{12,15},{15,12},{16,19},{19,... | collective-permute-start | bytes 835592 | tf_op jit(solution)/shard_map/ppermute | solution.py:487
  195.9 1.4 collective-permute-done.19.rest_3_
  197.3 3.0 %collective-permute-done.18.rest_2_ = bf16[272,512]{1,0:T(8,128)(2,1)S(1)} collective-permute-done((bf16[272,512]{1,0:T(8,128)(2,1)S(1)}, bf16[272,512]{1,0:T(8,128)(2,1)S(1)}, u32[]{:S(2)}, u32[]{:S(2)}) %collective-permute-start.18) | collective-permute-done | bytes 278560 | tf_op jit(solution)/shard_map/ppermute | solution.py:487
  200.3 6.3 %video_attention.7 = bf16[256,3072]{1,0:T(8,128)(2,1)} custom-call(s32[13]{0:T(128)S(1)} %concatenate.33.table, bf16[256,3072]{1,0:T(8,128)(2,1)S(1)} %copy-done.2, bf16[256,3072]{1,0:T(8,128)(2,1)S(1)} %copy-done.1, bf16[256,3072]{1,0:T(8,128)(2,1)} %v_own.7, bf16[528,512]{1,0:T(8,128)(2,1)} %collective-permute-done.5.rest_0_, ...), custom_call_target="tpu_custom_call", output_to_operand_aliasing={{}: (12, {})} | custom-call | flops 37748736 | bytes 131072 | tf_op jit(solution)/shard_map/video_attention/pallas_call | solution.py:210
  (85 shorter events, 10.0 us)
Async XLA Ops:
  0.6 12.7 %collective-permute-start.1 = (bf16[256,3072]{1,0:T(8,128)(2,1)}, bf16[256,3072]{1,0:T(8,128)(2,1)}, u32[]{:S(2)}, u32[]{:S(2)}) collective-permute-start(bf16[256,3072]{1,0:T(8,128)(2,1)} %k_own.7), channel_id=1, source_target_pairs={{0,1},{1,0},{2,3},{3,2},{4,5},{5,4},{6,7},{7,6},{8,9},{9,8},{10,11... | collective-permute-start | bytes 4718600 | tf_op jit(solution)/shard_map/ppermute | solution.py:455
  0.7 12.7 %collective-permute-start.2 = (bf16[256,3072]{1,0:T(8,128)(2,1)}, bf16[256,3072]{1,0:T(8,128)(2,1)}, u32[]{:S(2)}, u32[]{:S(2)}) collective-permute-start(bf16[256,3072]{1,0:T(8,128)(2,1)} %v_own.7), channel_id=1, source_target_pairs={{0,1},{1,0},{2,3},{3,2},{4,5},{5,4},{6,7},{7,6},{8,9},{9,8},{10,11... | collective-permute-start | bytes 4718600 | tf_op jit(solution)/shard_map/ppermute | solution.py:455
  1.2 12.1 %collective-permute-start = (s32[2]{0:T(128)}, s32[2]{0:T(128)S(1)}, u32[]{:S(2)}, u32[]{:S(2)}) collective-permute-start(s32[2]{0:T(128)} %param.19), channel_id=1, source_target_pairs={{0,1},{1,0},{2,3},{3,2},{4,5},{5,4},{6,7},{7,6},{8,9},{9,8},{10,11... | collective-permute-start | bytes 32 | tf_op jit(solution)/shard_map/ppermute | solution.py:455
  3.0 10.1 %copy-start.20 = (s32[16]{0:T(128)S(1)}, s32[16]{0:T(128)}, u32[]{:S(2)}) copy-start(s32[16]{0:T(128)} %constant.81.clone) | copy-start | bytes 196
  3.0 10.2 %copy-start.18 = (s32[2]{0:T(128)S(1)}, s32[2]{0:T(128)}, u32[]{:S(2)}) copy-start(s32[2]{0:T(128)} %param.19) | copy-start | bytes 28
  3.0 10.3 %copy-start = (bf16[256,3072]{1,0:T(8,128)(2,1)S(1)}, bf16[256,3072]{1,0:T(8,128)(2,1)}, u32[]{:S(2)}) copy-start(bf16[256,3072]{1,0:T(8,128)(2,1)} %k_own.7) | copy-start | bytes 4718596
  5.5 43.4 %collective-permute-start.8 = (bf16[528,1024]{1,0:T(8,128)(2,1)}, bf16[528,1024]{1,0:T(8,128)(2,1)S(1)}, u32[]{:S(2)}, u32[]{:S(2)}) collective-permute-start(bf16[528,1024]{1,0:T(8,128)(2,1)} %pad_maximum_fusion), channel_id=1, source_target_pairs={{0,12},{1,13},{4,0},{6,2},{7,3},{8,4},{9,5},{10,6},{11,7},{12,8},{... | collective-permute-start | bytes 3244040 | tf_op jit(solution)/shard_map/ppermute | solution.py:451
  7.9 68.5 %collective-permute-start.7 = (bf16[528,1024]{1,0:T(8,128)(2,1)}, bf16[528,1024]{1,0:T(8,128)(2,1)}, u32[]{:S(2)}, u32[]{:S(2)}) collective-permute-start(bf16[528,1024]{1,0:T(8,128)(2,1)} %pad_maximum_fusion), channel_id=1, source_target_pairs={{2,6},{3,7},{4,8},{5,9},{6,10},{7,11},{8,12},{9,13},{10,14},{11,15... | collective-permute-start | bytes 3244040 | tf_op jit(solution)/shard_map/ppermute | solution.py:451
  13.3 11.2 %copy-start.17 = (s32[2,6]{1,0:T(2,128)S(1)}, s32[2,6]{1,0:T(2,128)}, u32[]{:S(2)}) copy-start(s32[2,6]{1,0:T(2,128)} %param.18) | copy-start | bytes 148
  13.3 11.4 %copy-start.19 = (s32[16]{0:T(128)S(1)}, s32[16]{0:T(128)}, u32[]{:S(2)}) copy-start(s32[16]{0:T(128)} %constant.79.clone) | copy-start | bytes 196
  13.4 1.4 copy-start.7
  23.5 0.9 copy-start.8
  24.4 22.5 %collective-permute-start.11 = (f32[128,1792]{1,0:T(8,128)}, f32[128,1792]{1,0:T(8,128)}, u32[]{:S(2)}, u32[]{:S(2)}) collective-permute-start(f32[128,1792]{1,0:T(8,128)} %get-tuple-element.27), channel_id=1, source_target_pairs={{0,2},{1,3},{2,0},{3,1},{4,6},{5,7},{6,4},{7,5},{8,10},{9,11},{10,... | collective-permute-start | bytes 2752520 | tf_op jit(solution)/shard_map/ppermute | solution.py:468
  24.6 1.4 copy-start.16
  26.1 20.8 %copy-start.9 = (f32[128,1792]{1,0:T(8,128)S(1)}, f32[128,1792]{1,0:T(8,128)}, u32[]{:S(2)}) copy-start(f32[128,1792]{1,0:T(8,128)} %copy-done.8) | copy-start | bytes 2752516
  27.7 78.8 %collective-permute-start.4 = (bf16[528,768]{1,0:T(8,128)(2,1)}, bf16[528,768]{1,0:T(8,128)(2,1)}, u32[]{:S(2)}, u32[]{:S(2)}) collective-permute-start(bf16[528,768]{1,0:T(8,128)(2,1)} %get-tuple-element.23), channel_id=1, source_target_pairs={{0,12},{1,13},{4,0},{6,2},{7,3},{8,4},{9,5},{10,6},{11,7},{12,8},{... | collective-permute-start | bytes 2433032 | tf_op jit(solution)/shard_map/ppermute | solution.py:451
  29.8 81.3 %collective-permute-start.3 = (bf16[528,768]{1,0:T(8,128)(2,1)}, bf16[528,768]{1,0:T(8,128)(2,1)}, u32[]{:S(2)}, u32[]{:S(2)}) collective-permute-start(bf16[528,768]{1,0:T(8,128)(2,1)} %get-tuple-element.23), channel_id=1, source_target_pairs={{2,6},{3,7},{4,8},{5,9},{6,10},{7,11},{8,12},{9,13},{10,14},{11,15... | collective-permute-start | bytes 2433032 | tf_op jit(solution)/shard_map/ppermute | solution.py:451
  48.9 33.4 %copy-start.10 = (f32[64,1664]{1,0:T(8,128)}, f32[64,1664]{1,0:T(8,128)S(1)}, u32[]{:S(2)}) copy-start(f32[64,1664]{1,0:T(8,128)S(1)} %get-tuple-element.37.refs_0_) | copy-start | bytes 1277956
  48.9 33.4 %copy-start.14 = (f32[64,1664]{1,0:T(8,128)}, f32[64,1664]{1,0:T(8,128)S(1)}, u32[]{:S(2)}) copy-start(f32[64,1664]{1,0:T(8,128)S(1)} %get-tuple-element.38) | copy-start | bytes 1277956
  76.4 19.1 %copy-start.2 = (bf16[256,3072]{1,0:T(8,128)(2,1)S(1)}, bf16[256,3072]{1,0:T(8,128)(2,1)}, u32[]{:S(2)}) copy-start(bf16[256,3072]{1,0:T(8,128)(2,1)} %q.9) | copy-start | bytes 4718596
  78.5 11.8 %collective-permute-start.13 = (bf16[256,1024]{1,0:T(8,128)(2,1)}, bf16[256,1024]{1,0:T(8,128)(2,1)}, u32[]{:S(2)}, u32[]{:S(2)}) collective-permute-start(bf16[256,1024]{1,0:T(8,128)(2,1)} %slice_select_fusion.1), channel_id=1, source_target_pairs={{0,3},{3,0},{4,7},{7,4},{8,11},{11,8},{12,15},{15,12},{16,19},{19,... | collective-permute-start | bytes 1572872 | tf_op jit(solution)/shard_map/ppermute | solution.py:487
  82.3 13.2 %collective-permute-start.12 = (bf16[272,1024]{1,0:T(8,128)(2,1)}, bf16[272,1024]{1,0:T(8,128)(2,1)S(1)}, u32[]{:S(2)}, u32[]{:S(2)}) collective-permute-start(bf16[272,1024]{1,0:T(8,128)(2,1)} %slice_select_fusion), channel_id=1, source_target_pairs={{0,3},{3,0},{4,7},{7,4},{8,11},{11,8},{12,15},{15,12},{16,19},{19,... | collective-permute-start | bytes 1671176 | tf_op jit(solution)/shard_map/ppermute | solution.py:487
  87.8 50.9 %collective-permute-start.10 = (bf16[528,768]{1,0:T(8,128)(2,1)}, bf16[528,768]{1,0:T(8,128)(2,1)S(1)}, u32[]{:S(2)}, u32[]{:S(2)}) collective-permute-start(bf16[528,768]{1,0:T(8,128)(2,1)} %get-tuple-element.25), channel_id=1, source_target_pairs={{0,12},{1,13},{4,0},{6,2},{7,3},{8,4},{9,5},{10,6},{11,7},{12,8},{... | collective-permute-start | bytes 2433032 | tf_op jit(solution)/shard_map/ppermute | solution.py:451
  90.2 49.8 %collective-permute-start.9 = (bf16[528,768]{1,0:T(8,128)(2,1)}, bf16[528,768]{1,0:T(8,128)(2,1)S(1)}, u32[]{:S(2)}, u32[]{:S(2)}) collective-permute-start(bf16[528,768]{1,0:T(8,128)(2,1)} %get-tuple-element.25), channel_id=1, source_target_pairs={{2,6},{3,7},{4,8},{5,9},{6,10},{7,11},{8,12},{9,13},{10,14},{11,15... | collective-permute-start | bytes 2433032 | tf_op jit(solution)/shard_map/ppermute | solution.py:451
  106.4 12.8 %copy-start.1 = (bf16[256,3072]{1,0:T(8,128)(2,1)S(1)}, bf16[256,3072]{1,0:T(8,128)(2,1)}, u32[]{:S(2)}) copy-start(bf16[256,3072]{1,0:T(8,128)(2,1)} %k_own.7) | copy-start | bytes 4718596
  112.3 16.5 %copy-start.15 = (f32[64,1664]{1,0:T(8,128)S(1)}, f32[64,1664]{1,0:T(8,128)}, u32[]{:S(2)}) copy-start(f32[64,1664]{1,0:T(8,128)} %copy-done.14) | copy-start | bytes 1277956
  112.3 16.5 %collective-permute-start.14 = (bf16[272,768]{1,0:T(8,128)(2,1)S(1)}, bf16[272,768]{1,0:T(8,128)(2,1)S(1)}, u32[]{:S(2)}, u32[]{:S(2)}) collective-permute-start(bf16[272,768]{1,0:T(8,128)(2,1)S(1)} %slice_select_fusion.3), channel_id=1, source_target_pairs={{0,3},{3,0},{4,7},{7,4},{8,11},{11,8},{12,15},{15,12},{16,19},{19,... | collective-permute-start | bytes 1253384 | tf_op jit(solution)/shard_map/ppermute | solution.py:487
  115.6 10.5 %collective-permute-start.15 = (bf16[256,768]{1,0:T(8,128)(2,1)S(1)}, bf16[256,768]{1,0:T(8,128)(2,1)S(1)}, u32[]{:S(2)}, u32[]{:S(2)}) collective-permute-start(bf16[256,768]{1,0:T(8,128)(2,1)S(1)} %slice_select_fusion.5), channel_id=1, source_target_pairs={{0,3},{3,0},{4,7},{7,4},{8,11},{11,8},{12,15},{15,12},{16,19},{19,... | collective-permute-start | bytes 1179656 | tf_op jit(solution)/shard_map/ppermute | solution.py:487
  121.2 66.3 %collective-permute-start.6 = (bf16[528,512]{1,0:T(8,128)(2,1)}, bf16[528,512]{1,0:T(8,128)(2,1)}, u32[]{:S(2)}, u32[]{:S(2)}) collective-permute-start(bf16[528,512]{1,0:T(8,128)(2,1)} %pad_maximum_fusion.3), channel_id=1, source_target_pairs={{0,12},{1,13},{4,0},{6,2},{7,3},{8,4},{9,5},{10,6},{11,7},{12,8},{... | collective-permute-start | bytes 1622024 | tf_op jit(solution)/shard_map/ppermute | solution.py:451
  126.0 61.5 %collective-permute-start.5 = (bf16[528,512]{1,0:T(8,128)(2,1)}, bf16[528,512]{1,0:T(8,128)(2,1)}, u32[]{:S(2)}, u32[]{:S(2)}) collective-permute-start(bf16[528,512]{1,0:T(8,128)(2,1)} %pad_maximum_fusion.3), channel_id=1, source_target_pairs={{2,6},{3,7},{4,8},{5,9},{6,10},{7,11},{8,12},{9,13},{10,14},{11,15... | collective-permute-start | bytes 1622024 | tf_op jit(solution)/shard_map/ppermute | solution.py:451
  128.9 31.7 %collective-permute-start.20 = (f32[64,1664]{1,0:T(8,128)S(1)}, f32[64,1664]{1,0:T(8,128)S(1)}, u32[]{:S(2)}, u32[]{:S(2)}) collective-permute-start(f32[64,1664]{1,0:T(8,128)S(1)} %copy-done.15), channel_id=1, source_target_pairs={{0,4},{1,5},{2,6},{3,7},{4,0},{5,1},{6,2},{7,3},{8,12},{9,13},{10,... | collective-permute-start | bytes 1277960 | tf_op jit(solution)/shard_map/ppermute | solution.py:468
  138.7 21.9 %copy-start.11 = (f32[64,1664]{1,0:T(8,128)S(1)}, f32[64,1664]{1,0:T(8,128)}, u32[]{:S(2)}) copy-start(f32[64,1664]{1,0:T(8,128)} %copy-done.10) | copy-start | bytes 1277956
  138.7 23.1 %copy-start.3 = (bf16[528,768]{1,0:T(8,128)(2,1)}, bf16[528,768]{1,0:T(8,128)(2,1)S(1)}, u32[]{:S(2)}) copy-start(bf16[528,768]{1,0:T(8,128)(2,1)S(1)} %collective-permute-done.10.rest_1_) | copy-start | bytes 2433028
  140.0 21.7 %copy-start.5 = (bf16[528,768]{1,0:T(8,128)(2,1)}, bf16[528,768]{1,0:T(8,128)(2,1)S(1)}, u32[]{:S(2)}) copy-start(bf16[528,768]{1,0:T(8,128)(2,1)S(1)} %collective-permute-done.9.rest_0_) | copy-start | bytes 2433028
  141.0 21.6 %collective-permute-start.16 = (bf16[272,768]{1,0:T(8,128)(2,1)}, bf16[272,768]{1,0:T(8,128)(2,1)}, u32[]{:S(2)}, u32[]{:S(2)}) collective-permute-start(bf16[272,768]{1,0:T(8,128)(2,1)} %slice_select_fusion.2), channel_id=1, source_target_pairs={{0,3},{3,0},{4,7},{7,4},{8,11},{11,8},{12,15},{15,12},{16,19},{19,... | collective-permute-start | bytes 1253384 | tf_op jit(solution)/shard_map/ppermute | solution.py:487
  143.7 18.8 %collective-permute-start.17 = (bf16[256,768]{1,0:T(8,128)(2,1)}, bf16[256,768]{1,0:T(8,128)(2,1)S(1)}, u32[]{:S(2)}, u32[]{:S(2)}) collective-permute-start(bf16[256,768]{1,0:T(8,128)(2,1)} %slice_select_fusion.4), channel_id=1, source_target_pairs={{0,3},{3,0},{4,7},{7,4},{8,11},{11,8},{12,15},{15,12},{16,19},{19,... | collective-permute-start | bytes 1179656 | tf_op jit(solution)/shard_map/ppermute | solution.py:487
  161.8 0.7 copy-start.12
  162.4 11.9 %collective-permute-start.21 = (f32[32,1664]{1,0:T(8,128)}, f32[32,1664]{1,0:T(8,128)}, u32[]{:S(2)}, u32[]{:S(2)}) collective-permute-start(f32[32,1664]{1,0:T(8,128)} %get-tuple-element.41), channel_id=1, source_target_pairs={{0,8},{1,9},{2,10},{3,11},{4,12},{5,13},{6,14},{7,15},{8,0},{9,1},... | collective-permute-start | bytes 638984 | tf_op jit(solution)/shard_map/ppermute | solution.py:468
  174.3 0.9 copy-start.13
  176.5 18.7 %collective-permute-start.22 = (bf16[16,1536]{1,0:T(8,128)(2,1)S(1)}, bf16[16,1536]{1,0:T(8,128)(2,1)S(1)}, u32[]{:S(2)}, u32[]{:S(2)}) collective-permute-start(bf16[16,1536]{1,0:T(8,128)(2,1)S(1)} %get-tuple-element.43), channel_id=1, source_target_pairs={{0,1},{1,0},{2,3},{3,2},{4,5},{5,4},{6,7},{7,6},{8,9},{9,8},{10,11... | collective-permute-start | bytes 147464 | tf_op jit(solution)/shard_map/ppermute | solution.py:502
  176.6 1.1 copy-start.4
  177.8 1.1 copy-start.6
  189.7 7.7 %collective-permute-start.19 = (bf16[256,512]{1,0:T(8,128)(2,1)S(1)}, bf16[256,512]{1,0:T(8,128)(2,1)S(1)}, u32[]{:S(2)}, u32[]{:S(2)}) collective-permute-start(bf16[256,512]{1,0:T(8,128)(2,1)S(1)} %slice_select_fusion.7), channel_id=1, source_target_pairs={{0,3},{3,0},{4,7},{7,4},{8,11},{11,8},{12,15},{15,12},{16,19},{19,... | collective-permute-start | bytes 786440 | tf_op jit(solution)/shard_map/ppermute | solution.py:487
  191.6 8.7 %collective-permute-start.18 = (bf16[272,512]{1,0:T(8,128)(2,1)S(1)}, bf16[272,512]{1,0:T(8,128)(2,1)S(1)}, u32[]{:S(2)}, u32[]{:S(2)}) collective-permute-start(bf16[272,512]{1,0:T(8,128)(2,1)S(1)} %slice_select_fusion.6), channel_id=1, source_target_pairs={{0,3},{3,0},{4,7},{7,4},{8,11},{11,8},{12,15},{15,12},{16,19},{19,... | collective-permute-start | bytes 835592 | tf_op jit(solution)/shard_map/ppermute | solution.py:487

commit v5 on v4

--- a/solution.py
+++ b/solution.py
@@ -13,7 +13,7 @@
 NR = 4
 BLOCKS = 5
 STEP_HEADS = 2
-CHUNK_HEADS = (8, 6, 6, 4)
+CHUNK_HEADS = (4, 6, 8, 6)
 PAD_ROWS = 16
 VMEM_BYTES = 48 * 1024 * 1024
 LOG2E = 1.4426950408889634
@@ -65,6 +65,71 @@
         assert len(set(move.values())) == len(move)
     pairs = {name: sorted(move.items()) for name, move in moves.items()}
     return pairs, [int(d in relay_later) for d in range(n)], choice
+
+
+def pack_kernel(start, counts, k, v, out, limits, sems):
+    rows, width = k.shape[0], out.shape[1]
+    cols = pl.ds(start, width)
+    copies = [
+        pltpu.make_async_copy(k.at[:, cols], out.at[pl.ds(0, rows)], sems.at[0]),
+        pltpu.make_async_copy(v.at[:, cols], out.at[pl.ds(rows + PAD_ROWS, rows)], sems.at[1]),
+        pltpu.make_async_copy(limits, out.at[pl.ds(rows, PAD_ROWS)], sems.at[2]),
+    ]
+    copies[0].start()
+    copies[1].start()
+    row = lax.broadcasted_iota(jnp.int32, limits.shape, 0)
+    value = jnp.where(row == 0, counts[0], jnp.where(row == 1, counts[1], 0))
+    limits[...] = value.astype(jnp.float32).astype(limits.dtype)
+    copies[2].start()
+    for copy in copies:
+        copy.wait()
+
+
+def pack(start, width, counts, k, v):
+    rows = k.shape[0]
+    anywhere = pl.BlockSpec(memory_space=pl.ANY)
+    return pl.pallas_call(
+        functools.partial(pack_kernel, start),
+        in_specs=[pl.BlockSpec(memory_space=pltpu.SMEM), anywhere, anywhere],
+        out_specs=anywhere,
+        out_shape=jax.ShapeDtypeStruct((2 * rows + PAD_ROWS, width), k.dtype),
+        scratch_shapes=[pltpu.VMEM((PAD_ROWS, width), k.dtype), pltpu.SemaphoreType.DMA((3,))],
+        compiler_params=pltpu.CompilerParams(vmem_limit_bytes=VMEM_BYTES),
+        name="pack_chunk",
+    )(counts, k, v)
+
+
+def choose_kernel(second, a, b, first_out, last_out, sems):
+    rows = first_out.shape[0]
+
+    def move(ref):
+        copies = [
+            pltpu.make_async_copy(ref.at[pl.ds(0, rows)], first_out, sems.at[0]),
+            pltpu.make_async_copy(ref.at[pl.ds(rows, last_out.shape[0])], last_out, sems.at[1]),
+        ]
+        for copy in copies:
+            copy.start()
+        for copy in copies:
+            copy.wait()
+
+    pl.when(second[0] == 0)(lambda: move(a))
+    pl.when(second[0] != 0)(lambda: move(b))
+
+
+def choose(second, a, b, rows):
+    anywhere = pl.BlockSpec(memory_space=pl.ANY)
+    shapes = [
+        jax.ShapeDtypeStruct((part, a.shape[1]), a.dtype) for part in (rows, a.shape[0] - rows)
+    ]
+    return pl.pallas_call(
+        choose_kernel,
+        in_specs=[pl.BlockSpec(memory_space=pltpu.SMEM), anywhere, anywhere],
+        out_specs=[anywhere, anywhere],
+        out_shape=shapes,
+        scratch_shapes=[pltpu.SemaphoreType.DMA((2,))],
+        compiler_params=pltpu.CompilerParams(vmem_limit_bytes=VMEM_BYTES),
+        name="choose_relayed",
+    )(second, a, b)
 
 
 def dot_nt(a, b):
@@ -434,20 +499,14 @@
     text = text_q.shape[0]
     position = lax.axis_index("tiles").astype(jnp.int32)
     pairs, relays_later, choices = plan_moves(n)
-    sends_later = jnp.array(relays_later, jnp.int32)[position] == 1
-
-    limits = jnp.concatenate([counts, jnp.zeros((PAD_ROWS - counts.shape[0],), jnp.int32)])
-    limits = jnp.broadcast_to(limits.astype(jnp.bfloat16)[:, None], (PAD_ROWS, width))
-
-    def pack(cols):
-        return jnp.concatenate([video_k[:, cols], limits[:, cols], video_v[:, cols]], axis=0)
+    sends_later = jnp.array(relays_later, jnp.int32)[position][None]
 
     starts = [sum(CHUNK_HEADS[:i]) for i in range(len(CHUNK_HEADS))]
     direct, outs = [], []
 
     def send(i, *before):
-        cols = slice(starts[i] * HD, (starts[i] + CHUNK_HEADS[i]) * HD)
-        mine = tie(pack(cols), *before)
+        chunk = pack(starts[i] * HD, CHUNK_HEADS[i] * HD, counts, video_k, video_v)
+        mine = tie(chunk, *before)
         direct.append([lax.ppermute(mine, "tiles", pairs[x]) for x in ("earlier", "later")])
 
     send(0)
@@ -477,20 +536,18 @@
             limits = jnp.concatenate(limits)
             parts.append(text_finish(tie(parts[i][0], *before), exchanged(i), limits))
 
-    merge()
     count = len(CHUNK_HEADS)
     for i in range(count):
         up, down = direct[i]
-        before = [parts[-1][0]] if halving and i == 0 else outs[-1:]
+        before = outs[-1:] + ([parts[-1][0]] if halving else [])
         up, down = tie(up, *before), tie(down, *before)
         relays = [
-            lax.ppermute(jnp.where(sends_later, down[half], up[half]), "tiles", pairs["relayed"])
-            for half in (slice(0, rows + PAD_ROWS), slice(rows + PAD_ROWS, None))
+            lax.ppermute(half, "tiles", pairs["relayed"])
+            for half in choose(sends_later, up, down, rows + PAD_ROWS)
         ]
         if i + 2 < count:
             send(i + 2, *direct[i])
-        if i:
-            merge(*relays)
+        merge(*relays)
         outs.append(
             video_call(
                 starts[i], CHUNK_HEADS[i], table, video_q, video_k, video_v,

time: 209 us -> 257 us (1.23)
  Pallas kernels: 47.5 us -> 124 us
  other arithmetic: 15.9 us -> 2.15 us
  waiting for transfers between devices: 76.9 us -> 64.1 us
    pallas_call x0 -> x8, Pallas kernels: none -> 77.5 us  [the longest x4 72.4 us: choose(): pl.pallas_call(choose_kernel, in_specs=[pl.BlockSpec(memory_space=pltpu.S...]
    ppermute x8, waiting for transfers between devices: 6.88 us -> 27 us  [per_device(): lax.ppermute(half, 'tiles', pairs['relayed'])]
    ppermute x3, waiting for transfers between devices: 36.5 us -> 18.8 us  [exchanged(): lax.ppermute(parts[i][1], 'tiles', [(d, d ^ 2 << i) for d in range(n)])]
    ppermute x8, waiting for transfers between devices: 33.5 us -> 16.7 us  [send(): lax.ppermute(mine, 'tiles', pairs[x])]
    select_n x8 -> x0, other arithmetic: 10.2 us -> none  [per_device(): jnp.where(sends_later, down[half], up[half])]
    concatenate x3 -> x0, other arithmetic: 3.75 us -> none  [pack(): jnp.concatenate([video_k[:, cols], limits[:, cols], video_v[:, cols]], ax...]
    slice x6 -> x0, local copies, waits for them, and re-layouts: 3.37 us -> none  [the longest x3 2.22 us: pack(): video_v[:, cols]]
    unnamed x42 -> x38, local copies, waits for them, and re-layouts: 6.41 us -> 8.05 us
  transfers between devices with their start and end apart: 23 -> 23, of which waited for: 9 -> 7; matrix products, arithmetic and copies ran while one was open for 10% -> 2% of each run, Pallas kernels for 20% -> 35%
where the time goes in v5:
time: 257 us; the launch traced here: 256 us
  Pallas kernels  124 us (48%)
  waiting for transfers between devices  64.1 us (25%)
  starting transfers between devices  54.2 us (21%)
  local copies, waits for them, and re-layouts  9.74 us (4%)
    pallas_call x4, Pallas kernels, choose(): pl.pallas_call(choose_kernel, in_specs=[pl.BlockSpec(memory_space=pltpu.S...  72.4 us
    pallas_call x4, Pallas kernels, video_call(): pl.pallas_call(video_kernel, grid=(heads // STEP_HEADS,), in_specs=in_spe...  34.7 us
    ppermute x8, starting transfers between devices, send(): lax.ppermute(mine, 'tiles', pairs[x])  28.8 us
    ppermute x8, waiting for transfers between devices, per_device(): lax.ppermute(half, 'tiles', pairs['relayed'])  27 us
    ppermute x8, starting transfers between devices, per_device(): lax.ppermute(half, 'tiles', pairs['relayed'])  22.2 us
    ppermute x3, waiting for transfers between devices, exchanged(): lax.ppermute(parts[i][1], 'tiles', [(d, d ^ 2 << i) for d in range(n)])  18.8 us
    ppermute x8, waiting for transfers between devices, send(): lax.ppermute(mine, 'tiles', pairs[x])  16.7 us
    pallas_call x1, Pallas kernels, text_local(): pl.pallas_call(text_kernel, grid_spec=pltpu.PrefetchScalarGridSpec(num_sc...  8.08 us
  transfers between devices with their start and end apart: 23, of which 7 were waited for; matrix products, arithmetic and copies ran while one was open for 2% of the time, Pallas kernels for 35%

profile of v5, /device:TPU:24, one launch (start us, length us, event | category | flops | bytes accessed | tf_op | source)
XLA Modules:
  0.0 256.2 jit_solution(15576789008593570452)
XLA Ops:
  1.3 1.4 copy-done
  2.7 1.4 copy-done.3
  4.1 0.7 copy-done.14
  4.8 1.4 pack_chunk.7
  6.1 1.9 collective-permute-start.7
  8.1 3.9 %collective-permute-start.8 = (bf16[528,512]{1,0:T(8,128)(2,1)}, bf16[528,512]{1,0:T(8,128)(2,1)}, u32[]{:S(2)}, u32[]{:S(2)}) collective-permute-start(bf16[528,512]{1,0:T(8,128)(2,1)} %pack_chunk.7), channel_id=1, source_target_pairs={{0,12},{1,13},{4,0},{6,2},{7,3},{8,4},{9,5},{10,6},{11,7},{12,8},{... | collective-permute-start | bytes 1622024 | tf_op jit(solution)/shard_map/ppermute | solution.py:510
  12.2 1.5 copy-done.9
  13.7 8.1 %text_partials.1 = (f32[128,1792]{1,0:T(8,128)S(1)}, f32[128,1792]{1,0:T(8,128)S(1)}) custom-call(s32[17]{0:T(128)S(1)} %pad_add_fusion.1.order, s32[4]{0:T(128)S(1)} %pad_add_fusion.2.counts, bf16[256,3072]{1,0:T(8,128)(2,1)S(1)} %copy-done.9, bf16[256,3072]{1,0:T(8,128)(2,1)S(1)} %copy-done.1, bf16[256,3072]{1,0:T(8,128)(2,1)} %v_own.7, ...), custom_call_target="tpu_custom_call" | custom-call | flops 8388608 | bytes 786432 | tf_op jit(solution)/shard_map/text_partials/pallas_call | solution.py:367
  21.8 2.4 collective-permute-start.13
  24.2 1.4 pack_chunk.5
  25.7 1.9 collective-permute-start.4
  27.6 5.7 %collective-permute-start.3 = (bf16[528,768]{1,0:T(8,128)(2,1)}, bf16[528,768]{1,0:T(8,128)(2,1)}, u32[]{:S(2)}, u32[]{:S(2)}) collective-permute-start(bf16[528,768]{1,0:T(8,128)(2,1)} %pack_chunk.5), channel_id=1, source_target_pairs={{2,6},{3,7},{4,8},{5,9},{6,10},{7,11},{8,12},{9,13},{10,14},{11,15... | collective-permute-start | bytes 2433032 | tf_op jit(solution)/shard_map/ppermute | solution.py:510
  33.4 0.7 pack_chunk.6
  34.1 1.0 copy-done.10
  35.1 0.6 dynamic_slice.8.second
  35.7 16.7 %collective-permute-done.7.a.rest_0_ = bf16[528,512]{1,0:T(8,128)(2,1)} collective-permute-done((bf16[528,512]{1,0:T(8,128)(2,1)}, bf16[528,512]{1,0:T(8,128)(2,1)}, u32[]{:S(2)}, u32[]{:S(2)}) %collective-permute-start.7) | collective-permute-done | bytes 540704 | tf_op jit(solution)/shard_map/ppermute | solution.py:510
  52.4 9.7 %choose_relayed.4 = (bf16[272,512]{1,0:T(8,128)(2,1)S(1)}, bf16[256,512]{1,0:T(8,128)(2,1)}) custom-call(s32[1]{0:T(128)} %dynamic_slice.8.second, bf16[528,512]{1,0:T(8,128)(2,1)} %collective-permute-done.7.a.rest_0_, bf16[528,512]{1,0:T(8,128)(2,1)} %collective-permute-done.8.b.rest_1_), custom_call_target="tpu_custom_call" | custom-call | tf_op jit(solution)/shard_map/choose_relayed/pallas_call | solution.py:124
  62.1 1.9 collective-permute-start.11
  64.0 3.6 %collective-permute-start.12 = (bf16[256,512]{1,0:T(8,128)(2,1)}, bf16[256,512]{1,0:T(8,128)(2,1)S(1)}, u32[]{:S(2)}, u32[]{:S(2)}) collective-permute-start(bf16[256,512]{1,0:T(8,128)(2,1)} %get-tuple-element.39), channel_id=1, source_target_pairs={{0,3},{3,0},{4,7},{7,4},{8,11},{11,8},{12,15},{15,12},{16,19},{19,... | collective-permute-start | bytes 786440 | tf_op jit(solution)/shard_map/ppermute | solution.py:545
  68.0 4.7 %collective-permute-done.12.rest_3_ = bf16[256,512]{1,0:T(8,128)(2,1)S(1)} collective-permute-done((bf16[256,512]{1,0:T(8,128)(2,1)}, bf16[256,512]{1,0:T(8,128)(2,1)S(1)}, u32[]{:S(2)}, u32[]{:S(2)}) %collective-permute-start.12) | collective-permute-done | bytes 262176 | tf_op jit(solution)/shard_map/ppermute | solution.py:545
  72.8 2.3 collective-permute-start.10
  75.2 5.3 %collective-permute-start.9 = (bf16[528,1024]{1,0:T(8,128)(2,1)}, bf16[528,1024]{1,0:T(8,128)(2,1)}, u32[]{:S(2)}, u32[]{:S(2)}) collective-permute-start(bf16[528,1024]{1,0:T(8,128)(2,1)} %copy-done.10), channel_id=1, source_target_pairs={{2,6},{3,7},{4,8},{5,9},{6,10},{7,11},{8,12},{9,13},{10,14},{11,15... | collective-permute-start | bytes 3244040 | tf_op jit(solution)/shard_map/ppermute | solution.py:510
  81.4 0.7 dynamic-slice_bitcast_fusion
  82.2 1.4 copy-done.6
  83.6 6.4 %video_attention.4.rest_8_ = bf16[256,3072]{1,0:T(8,128)(2,1)} custom-call(s32[13]{0:T(128)S(1)} %concatenate.18.table, bf16[256,3072]{1,0:T(8,128)(2,1)S(1)} %copy-done.6, bf16[256,3072]{1,0:T(8,128)(2,1)S(1)} %copy-done.1, bf16[256,3072]{1,0:T(8,128)(2,1)} %v_own.7, bf16[528,512]{1,0:T(8,128)(2,1)} %collective-permute-done.7.a.rest_0_, ...), custom_call_target="tpu_custom_call" | custom-call | flops 37748736 | bytes 131072 | tf_op jit(solution)/shard_map/video_attention/pallas_call | solution.py:275
  90.0 2.1 text_merge.2
  92.1 1.8 choose_relayed.5
  93.9 1.9 collective-permute-start.14
  95.8 3.6 %collective-permute-start.15 = (bf16[256,768]{1,0:T(8,128)(2,1)S(1)}, bf16[256,768]{1,0:T(8,128)(2,1)S(1)}, u32[]{:S(2)}, u32[]{:S(2)}) collective-permute-start(bf16[256,768]{1,0:T(8,128)(2,1)S(1)} %get-tuple-element.46), channel_id=1, source_target_pairs={{0,3},{3,0},{4,7},{7,4},{8,11},{11,8},{12,15},{15,12},{16,19},{19,... | collective-permute-start | bytes 1179656 | tf_op jit(solution)/shard_map/ppermute | solution.py:545
  99.6 1.5 pack_chunk.4
  101.1 6.3 %collective-permute-done.15.rest_3_ = bf16[256,768]{1,0:T(8,128)(2,1)S(1)} collective-permute-done((bf16[256,768]{1,0:T(8,128)(2,1)S(1)}, bf16[256,768]{1,0:T(8,128)(2,1)S(1)}, u32[]{:S(2)}, u32[]{:S(2)}) %collective-permute-start.15) | collective-permute-done | bytes 393248 | tf_op jit(solution)/shard_map/ppermute | solution.py:545
  107.5 1.9 collective-permute-start.6
  109.4 5.7 %collective-permute-start.5 = (bf16[528,768]{1,0:T(8,128)(2,1)}, bf16[528,768]{1,0:T(8,128)(2,1)}, u32[]{:S(2)}, u32[]{:S(2)}) collective-permute-start(bf16[528,768]{1,0:T(8,128)(2,1)} %pack_chunk.4), channel_id=1, source_target_pairs={{2,6},{3,7},{4,8},{5,9},{6,10},{7,11},{8,12},{9,13},{10,14},{11,15... | collective-permute-start | bytes 2433032 | tf_op jit(solution)/shard_map/ppermute | solution.py:510
  115.1 8.7 %video_attention.5.rest_8_ = bf16[256,3072]{1,0:T(8,128)(2,1)} custom-call(s32[13]{0:T(128)S(1)} %concatenate.18.table, bf16[256,3072]{1,0:T(8,128)(2,1)S(1)} %copy-done.7, bf16[256,3072]{1,0:T(8,128)(2,1)S(1)} %copy-done.1, bf16[256,3072]{1,0:T(8,128)(2,1)} %v_own.7, ...), custom_call_target="tpu_custom_call", output_to_operand_aliasing={{}: (12, {})} | custom-call | flops 56623104 | bytes 196608 | tf_op jit(solution)/shard_map/video_attention/pallas_call | solution.py:275
  123.8 18.8 %collective-permute-done.16.refs_1_ = f32[64,1664]{1,0:T(8,128)S(1)} collective-permute-done((f32[64,1664]{1,0:T(8,128)S(1)}, f32[64,1664]{1,0:T(8,128)S(1)}, u32[]{:S(2)}, u32[]{:S(2)}) %collective-permute-start.16) | collective-permute-done | bytes 426016 | tf_op jit(solution)/shard_map/ppermute | solution.py:527
  143.0 34.5 %choose_relayed.6 = (bf16[272,1024]{1,0:T(8,128)(2,1)}, bf16[256,1024]{1,0:T(8,128)(2,1)}) custom-call(s32[1]{0:T(128)} %dynamic_slice.8.second, bf16[528,1024]{1,0:T(8,128)(2,1)} %collective-permute-done.9.a.rest_0_, bf16[528,1024]{1,0:T(8,128)(2,1)} %collective-permute-done.10.b.rest_1_), custom_call_target="tpu_custom_call" | custom-call | tf_op jit(solution)/shard_map/choose_relayed/pallas_call | solution.py:124
  177.5 1.9 collective-permute-start.17
  179.5 3.6 %collective-permute-start.18 = (bf16[256,1024]{1,0:T(8,128)(2,1)}, bf16[256,1024]{1,0:T(8,128)(2,1)S(1)}, u32[]{:S(2)}, u32[]{:S(2)}) collective-permute-start(bf16[256,1024]{1,0:T(8,128)(2,1)} %get-tuple-element.53), channel_id=1, source_target_pairs={{0,3},{3,0},{4,7},{7,4},{8,11},{11,8},{12,15},{15,12},{16,19},{19,... | collective-permute-start | bytes 1572872 | tf_op jit(solution)/shard_map/ppermute | solution.py:545
  183.3 10.9 %collective-permute-done.18.rest_3_ = bf16[256,1024]{1,0:T(8,128)(2,1)S(1)} collective-permute-done((bf16[256,1024]{1,0:T(8,128)(2,1)}, bf16[256,1024]{1,0:T(8,128)(2,1)S(1)}, u32[]{:S(2)}, u32[]{:S(2)}) %collective-permute-start.18) | collective-permute-done | bytes 524320 | tf_op jit(solution)/shard_map/ppermute | solution.py:545
  194.2 1.5 text_finish.1
  196.3 11.0 %video_attention.6.rest_8_ = bf16[256,3072]{1,0:T(8,128)(2,1)} custom-call(s32[13]{0:T(128)S(1)} %concatenate.18.table, bf16[256,3072]{1,0:T(8,128)(2,1)S(1)} %copy-done.8, bf16[256,3072]{1,0:T(8,128)(2,1)} %k_own.7, bf16[256,3072]{1,0:T(8,128)(2,1)} %v_own.7, bf16[528,1024]{1,0:T(8,128)(2,1)} %collective-permute-done.9.a.rest_0_, ...), custom_call_target="tpu_custom_call", output_to_operand_aliasing={{}: (12, {})} | custom-call | flops 75497472 | bytes 262144 | tf_op jit(solution)/shard_map/video_attention/pallas_call | solution.py:275
  207.3 26.4 %choose_relayed.7 = (bf16[272,768]{1,0:T(8,128)(2,1)}, bf16[256,768]{1,0:T(8,128)(2,1)}) custom-call(s32[1]{0:T(128)} %dynamic_slice.8.second, bf16[528,768]{1,0:T(8,128)(2,1)} %collective-permute-done.5.a.rest_0_, bf16[528,768]{1,0:T(8,128)(2,1)} %collective-permute-done.6.b.rest_1_), custom_call_target="tpu_custom_call" | custom-call | tf_op jit(solution)/shard_map/choose_relayed/pallas_call | solution.py:124
  233.7 1.9 collective-permute-start.20
  235.7 3.6 %collective-permute-start.21 = (bf16[256,768]{1,0:T(8,128)(2,1)}, bf16[256,768]{1,0:T(8,128)(2,1)S(1)}, u32[]{:S(2)}, u32[]{:S(2)}) collective-permute-start(bf16[256,768]{1,0:T(8,128)(2,1)} %get-tuple-element.60), channel_id=1, source_target_pairs={{0,3},{3,0},{4,7},{7,4},{8,11},{11,8},{12,15},{15,12},{16,19},{19,... | collective-permute-start | bytes 1179656 | tf_op jit(solution)/shard_map/ppermute | solution.py:545
  239.4 1.6 collective-permute-done.22
  241.0 1.5 maximum_select_fusion
  242.5 5.0 %collective-permute-done.21.rest_3_ = bf16[256,768]{1,0:T(8,128)(2,1)S(1)} collective-permute-done((bf16[256,768]{1,0:T(8,128)(2,1)}, bf16[256,768]{1,0:T(8,128)(2,1)S(1)}, u32[]{:S(2)}, u32[]{:S(2)}) %collective-permute-start.21) | collective-permute-done | bytes 393248 | tf_op jit(solution)/shard_map/ppermute | solution.py:545
  247.5 8.7 %video_attention.7 = bf16[256,3072]{1,0:T(8,128)(2,1)} custom-call(s32[13]{0:T(128)S(1)} %concatenate.18.table, bf16[256,3072]{1,0:T(8,128)(2,1)S(1)} %copy-done.8, bf16[256,3072]{1,0:T(8,128)(2,1)S(1)} %copy-done.2, bf16[256,3072]{1,0:T(8,128)(2,1)} %v_own.7, bf16[528,768]{1,0:T(8,128)(2,1)} %collective-permute-done.5.a.rest_0_, ...), custom_call_target="tpu_custom_call", output_to_operand_aliasing={{}: (12, {})} | custom-call | flops 56623104 | bytes 196608 | tf_op jit(solution)/shard_map/video_attention/pallas_call | solution.py:275
  (69 shorter events, 3.0 us)
Async XLA Ops:
  0.6 11.4 %copy-start.18 = (s32[16]{0:T(128)S(1)}, s32[16]{0:T(128)}, u32[]{:S(2)}) copy-start(s32[16]{0:T(128)} %constant.76.clone) | copy-start | bytes 196
  0.6 11.6 %collective-permute-start.1 = (bf16[256,3072]{1,0:T(8,128)(2,1)}, bf16[256,3072]{1,0:T(8,128)(2,1)}, u32[]{:S(2)}, u32[]{:S(2)}) collective-permute-start(bf16[256,3072]{1,0:T(8,128)(2,1)} %k_own.7), channel_id=1, source_target_pairs={{0,1},{1,0},{2,3},{3,2},{4,5},{5,4},{6,7},{7,6},{8,9},{9,8},{10,11... | collective-permute-start | bytes 4718600 | tf_op jit(solution)/shard_map/ppermute | solution.py:514
  0.7 11.5 %collective-permute-start.2 = (bf16[256,3072]{1,0:T(8,128)(2,1)}, bf16[256,3072]{1,0:T(8,128)(2,1)}, u32[]{:S(2)}, u32[]{:S(2)}) collective-permute-start(bf16[256,3072]{1,0:T(8,128)(2,1)} %v_own.7), channel_id=1, source_target_pairs={{0,1},{1,0},{2,3},{3,2},{4,5},{5,4},{6,7},{7,6},{8,9},{9,8},{10,11... | collective-permute-start | bytes 4718600 | tf_op jit(solution)/shard_map/ppermute | solution.py:514
  1.2 10.9 %collective-permute-start = (s32[2]{0:T(128)}, s32[2]{0:T(128)S(1)}, u32[]{:S(2)}, u32[]{:S(2)}) collective-permute-start(s32[2]{0:T(128)} %counts.7), channel_id=1, source_target_pairs={{0,1},{1,0},{2,3},{3,2},{4,5},{5,4},{6,7},{7,6},{8,9},{9,8},{10,11... | collective-permute-start | bytes 32 | tf_op jit(solution)/shard_map/ppermute | solution.py:514
  1.3 1.4 copy-start
  2.7 1.4 copy-start.3
  4.1 0.7 copy-start.14
  4.8 7.3 %copy-start.15 = (s32[2]{0:T(128)S(1)}, s32[2]{0:T(128)}, u32[]{:S(2)}) copy-start(s32[2]{0:T(128)} %counts.7) | copy-start | bytes 28
  4.8 7.4 %copy-start.1 = (bf16[256,3072]{1,0:T(8,128)(2,1)S(1)}, bf16[256,3072]{1,0:T(8,128)(2,1)}, u32[]{:S(2)}) copy-start(bf16[256,3072]{1,0:T(8,128)(2,1)} %k_own.7) | copy-start | bytes 4718596
  6.1 46.3 %collective-permute-start.7 = (bf16[528,512]{1,0:T(8,128)(2,1)}, bf16[528,512]{1,0:T(8,128)(2,1)}, u32[]{:S(2)}, u32[]{:S(2)}) collective-permute-start(bf16[528,512]{1,0:T(8,128)(2,1)} %pack_chunk.7), channel_id=1, source_target_pairs={{2,6},{3,7},{4,8},{5,9},{6,10},{7,11},{8,12},{9,13},{10,14},{11,15... | collective-permute-start | bytes 1622024 | tf_op jit(solution)/shard_map/ppermute | solution.py:510
  8.1 44.3 %collective-permute-start.8 = (bf16[528,512]{1,0:T(8,128)(2,1)}, bf16[528,512]{1,0:T(8,128)(2,1)}, u32[]{:S(2)}, u32[]{:S(2)}) collective-permute-start(bf16[528,512]{1,0:T(8,128)(2,1)} %pack_chunk.7), channel_id=1, source_target_pairs={{0,12},{1,13},{4,0},{6,2},{7,3},{8,4},{9,5},{10,6},{11,7},{12,8},{... | collective-permute-start | bytes 1622024 | tf_op jit(solution)/shard_map/ppermute | solution.py:510
  12.2 12.0 %copy-start.4 = (bf16[256,3072]{1,0:T(8,128)(2,1)S(1)}, bf16[256,3072]{1,0:T(8,128)(2,1)}, u32[]{:S(2)}) copy-start(bf16[256,3072]{1,0:T(8,128)(2,1)} %v_own.7) | copy-start | bytes 4718596
  12.2 1.5 copy-start.9
  21.8 3.8 %copy-start.11 = (f32[128,1792]{1,0:T(8,128)}, f32[128,1792]{1,0:T(8,128)S(1)}, u32[]{:S(2)}) copy-start(f32[128,1792]{1,0:T(8,128)S(1)} %get-tuple-element.40.refs_0_) | copy-start | bytes 2752516
  21.8 68.2 %collective-permute-start.13 = (f32[128,1792]{1,0:T(8,128)S(1)}, f32[128,1792]{1,0:T(8,128)}, u32[]{:S(2)}, u32[]{:S(2)}) collective-permute-start(f32[128,1792]{1,0:T(8,128)S(1)} %get-tuple-element.41), channel_id=1, source_target_pairs={{0,2},{1,3},{2,0},{3,1},{4,6},{5,7},{6,4},{7,5},{8,10},{9,11},{10,... | collective-permute-start | bytes 2752520 | tf_op jit(solution)/shard_map/ppermute | solution.py:527
  25.7 9.4 %copy-start.17 = (s32[16]{0:T(128)S(1)}, s32[16]{0:T(128)}, u32[]{:S(2)}) copy-start(s32[16]{0:T(128)} %constant.74.clone) | copy-start | bytes 196
  25.7 42.0 %copy-start.16 = (s32[2,6]{1,0:T(2,128)S(1)}, s32[2,6]{1,0:T(2,128)}, u32[]{:S(2)}) copy-start(s32[2,6]{1,0:T(2,128)} %param.18) | copy-start | bytes 148
  25.7 66.4 %collective-permute-start.4 = (bf16[528,768]{1,0:T(8,128)(2,1)}, bf16[528,768]{1,0:T(8,128)(2,1)}, u32[]{:S(2)}, u32[]{:S(2)}) collective-permute-start(bf16[528,768]{1,0:T(8,128)(2,1)} %pack_chunk.5), channel_id=1, source_target_pairs={{0,12},{1,13},{4,0},{6,2},{7,3},{8,4},{9,5},{10,6},{11,7},{12,8},{... | collective-permute-start | bytes 2433032 | tf_op jit(solution)/shard_map/ppermute | solution.py:510
  27.6 64.4 %collective-permute-start.3 = (bf16[528,768]{1,0:T(8,128)(2,1)}, bf16[528,768]{1,0:T(8,128)(2,1)}, u32[]{:S(2)}, u32[]{:S(2)}) collective-permute-start(bf16[528,768]{1,0:T(8,128)(2,1)} %pack_chunk.5), channel_id=1, source_target_pairs={{2,6},{3,7},{4,8},{5,9},{6,10},{7,11},{8,12},{9,13},{10,14},{11,15... | collective-permute-start | bytes 2433032 | tf_op jit(solution)/shard_map/ppermute | solution.py:510
  34.1 1.0 copy-start.10
  62.1 13.0 %collective-permute-start.11 = (bf16[272,512]{1,0:T(8,128)(2,1)S(1)}, bf16[272,512]{1,0:T(8,128)(2,1)S(1)}, u32[]{:S(2)}, u32[]{:S(2)}) collective-permute-start(bf16[272,512]{1,0:T(8,128)(2,1)S(1)} %get-tuple-element.38), channel_id=1, source_target_pairs={{0,3},{3,0},{4,7},{7,4},{8,11},{11,8},{12,15},{15,12},{16,19},{19,... | collective-permute-start | bytes 835592 | tf_op jit(solution)/shard_map/ppermute | solution.py:545
  64.0 8.7 %collective-permute-start.12 = (bf16[256,512]{1,0:T(8,128)(2,1)}, bf16[256,512]{1,0:T(8,128)(2,1)S(1)}, u32[]{:S(2)}, u32[]{:S(2)}) collective-permute-start(bf16[256,512]{1,0:T(8,128)(2,1)} %get-tuple-element.39), channel_id=1, source_target_pairs={{0,3},{3,0},{4,7},{7,4},{8,11},{11,8},{12,15},{15,12},{16,19},{19,... | collective-permute-start | bytes 786440 | tf_op jit(solution)/shard_map/ppermute | solution.py:545
  72.8 70.2 %collective-permute-start.10 = (bf16[528,1024]{1,0:T(8,128)(2,1)}, bf16[528,1024]{1,0:T(8,128)(2,1)}, u32[]{:S(2)}, u32[]{:S(2)}) collective-permute-start(bf16[528,1024]{1,0:T(8,128)(2,1)} %copy-done.10), channel_id=1, source_target_pairs={{0,12},{1,13},{4,0},{6,2},{7,3},{8,4},{9,5},{10,6},{11,7},{12,8},{... | collective-permute-start | bytes 3244040 | tf_op jit(solution)/shard_map/ppermute | solution.py:510
  75.2 67.8 %collective-permute-start.9 = (bf16[528,1024]{1,0:T(8,128)(2,1)}, bf16[528,1024]{1,0:T(8,128)(2,1)}, u32[]{:S(2)}, u32[]{:S(2)}) collective-permute-start(bf16[528,1024]{1,0:T(8,128)(2,1)} %copy-done.10), channel_id=1, source_target_pairs={{2,6},{3,7},{4,8},{5,9},{6,10},{7,11},{8,12},{9,13},{10,14},{11,15... | collective-permute-start | bytes 3244040 | tf_op jit(solution)/shard_map/ppermute | solution.py:510
  82.2 1.4 copy-start.6
  83.6 6.4 %copy-start.12 = (f32[128,1792]{1,0:T(8,128)S(1)}, f32[128,1792]{1,0:T(8,128)}, u32[]{:S(2)}) copy-start(f32[128,1792]{1,0:T(8,128)} %copy-done.11) | copy-start | bytes 2752516
  90.0 9.6 %copy-start.5 = (bf16[256,3072]{1,0:T(8,128)(2,1)S(1)}, bf16[256,3072]{1,0:T(8,128)(2,1)}, u32[]{:S(2)}) copy-start(bf16[256,3072]{1,0:T(8,128)(2,1)} %v_own.7) | copy-start | bytes 4718596
  93.9 15.5 %collective-permute-start.14 = (bf16[272,768]{1,0:T(8,128)(2,1)S(1)}, bf16[272,768]{1,0:T(8,128)(2,1)S(1)}, u32[]{:S(2)}, u32[]{:S(2)}) collective-permute-start(bf16[272,768]{1,0:T(8,128)(2,1)S(1)} %get-tuple-element.45), channel_id=1, source_target_pairs={{0,3},{3,0},{4,7},{7,4},{8,11},{11,8},{12,15},{15,12},{16,19},{19,... | collective-permute-start | bytes 1253384 | tf_op jit(solution)/shard_map/ppermute | solution.py:545
  95.8 11.6 %collective-permute-start.15 = (bf16[256,768]{1,0:T(8,128)(2,1)S(1)}, bf16[256,768]{1,0:T(8,128)(2,1)S(1)}, u32[]{:S(2)}, u32[]{:S(2)}) collective-permute-start(bf16[256,768]{1,0:T(8,128)(2,1)S(1)} %get-tuple-element.46), channel_id=1, source_target_pairs={{0,3},{3,0},{4,7},{7,4},{8,11},{11,8},{12,15},{15,12},{16,19},{19,... | collective-permute-start | bytes 1179656 | tf_op jit(solution)/shard_map/ppermute | solution.py:545
  99.5 15.7 %copy-start.7 = (bf16[256,3072]{1,0:T(8,128)(2,1)S(1)}, bf16[256,3072]{1,0:T(8,128)(2,1)}, u32[]{:S(2)}) copy-start(bf16[256,3072]{1,0:T(8,128)(2,1)} %q.9) | copy-start | bytes 4718596
  99.5 43.1 %collective-permute-start.16 = (f32[64,1664]{1,0:T(8,128)S(1)}, f32[64,1664]{1,0:T(8,128)S(1)}, u32[]{:S(2)}, u32[]{:S(2)}) collective-permute-start(f32[64,1664]{1,0:T(8,128)S(1)} %get-tuple-element.48), channel_id=1, source_target_pairs={{0,4},{1,5},{2,6},{3,7},{4,0},{5,1},{6,2},{7,3},{8,12},{9,13},{10,... | collective-permute-start | bytes 1277960 | tf_op jit(solution)/shard_map/ppermute | solution.py:527
  107.5 99.8 %collective-permute-start.6 = (bf16[528,768]{1,0:T(8,128)(2,1)}, bf16[528,768]{1,0:T(8,128)(2,1)}, u32[]{:S(2)}, u32[]{:S(2)}) collective-permute-start(bf16[528,768]{1,0:T(8,128)(2,1)} %pack_chunk.4), channel_id=1, source_target_pairs={{0,12},{1,13},{4,0},{6,2},{7,3},{8,4},{9,5},{10,6},{11,7},{12,8},{... | collective-permute-start | bytes 2433032 | tf_op jit(solution)/shard_map/ppermute | solution.py:510
  109.4 97.9 %collective-permute-start.5 = (bf16[528,768]{1,0:T(8,128)(2,1)}, bf16[528,768]{1,0:T(8,128)(2,1)}, u32[]{:S(2)}, u32[]{:S(2)}) collective-permute-start(bf16[528,768]{1,0:T(8,128)(2,1)} %pack_chunk.4), channel_id=1, source_target_pairs={{2,6},{3,7},{4,8},{5,9},{6,10},{7,11},{8,12},{9,13},{10,14},{11,15... | collective-permute-start | bytes 2433032 | tf_op jit(solution)/shard_map/ppermute | solution.py:510
  123.8 72.5 %copy-start.8 = (bf16[256,3072]{1,0:T(8,128)(2,1)S(1)}, bf16[256,3072]{1,0:T(8,128)(2,1)}, u32[]{:S(2)}) copy-start(bf16[256,3072]{1,0:T(8,128)(2,1)} %q.9) | copy-start | bytes 4718596
  177.5 16.7 %collective-permute-start.17 = (bf16[272,1024]{1,0:T(8,128)(2,1)}, bf16[272,1024]{1,0:T(8,128)(2,1)S(1)}, u32[]{:S(2)}, u32[]{:S(2)}) collective-permute-start(bf16[272,1024]{1,0:T(8,128)(2,1)} %get-tuple-element.52), channel_id=1, source_target_pairs={{0,3},{3,0},{4,7},{7,4},{8,11},{11,8},{12,15},{15,12},{16,19},{19,... | collective-permute-start | bytes 1671176 | tf_op jit(solution)/shard_map/ppermute | solution.py:545
  179.5 14.8 %collective-permute-start.18 = (bf16[256,1024]{1,0:T(8,128)(2,1)}, bf16[256,1024]{1,0:T(8,128)(2,1)S(1)}, u32[]{:S(2)}, u32[]{:S(2)}) collective-permute-start(bf16[256,1024]{1,0:T(8,128)(2,1)} %get-tuple-element.53), channel_id=1, source_target_pairs={{0,3},{3,0},{4,7},{7,4},{8,11},{11,8},{12,15},{15,12},{16,19},{19,... | collective-permute-start | bytes 1572872 | tf_op jit(solution)/shard_map/ppermute | solution.py:545
  183.1 11.1 %collective-permute-start.19 = (f32[32,1664]{1,0:T(8,128)S(1)}, f32[32,1664]{1,0:T(8,128)S(1)}, u32[]{:S(2)}, u32[]{:S(2)}) collective-permute-start(f32[32,1664]{1,0:T(8,128)S(1)} %get-tuple-element.55), channel_id=1, source_target_pairs={{0,8},{1,9},{2,10},{3,11},{4,12},{5,13},{6,14},{7,15},{8,0},{9,1},... | collective-permute-start | bytes 638984 | tf_op jit(solution)/shard_map/ppermute | solution.py:527
  195.7 0.6 copy-start.13
  207.3 40.3 %copy-start.2 = (bf16[256,3072]{1,0:T(8,128)(2,1)S(1)}, bf16[256,3072]{1,0:T(8,128)(2,1)}, u32[]{:S(2)}) copy-start(bf16[256,3072]{1,0:T(8,128)(2,1)} %k_own.7) | copy-start | bytes 4718596
  233.7 13.8 %collective-permute-start.20 = (bf16[272,768]{1,0:T(8,128)(2,1)}, bf16[272,768]{1,0:T(8,128)(2,1)}, u32[]{:S(2)}, u32[]{:S(2)}) collective-permute-start(bf16[272,768]{1,0:T(8,128)(2,1)} %get-tuple-element.59), channel_id=1, source_target_pairs={{0,3},{3,0},{4,7},{7,4},{8,11},{11,8},{12,15},{15,12},{16,19},{19,... | collective-permute-start | bytes 1253384 | tf_op jit(solution)/shard_map/ppermute | solution.py:545
  235.7 11.9 %collective-permute-start.21 = (bf16[256,768]{1,0:T(8,128)(2,1)}, bf16[256,768]{1,0:T(8,128)(2,1)S(1)}, u32[]{:S(2)}, u32[]{:S(2)}) collective-permute-start(bf16[256,768]{1,0:T(8,128)(2,1)} %get-tuple-element.60), channel_id=1, source_target_pairs={{0,3},{3,0},{4,7},{7,4},{8,11},{11,8},{12,15},{15,12},{16,19},{19,... | collective-permute-start | bytes 1179656 | tf_op jit(solution)/shard_map/ppermute | solution.py:545
  239.3 1.6 collective-permute-start.22

commit v6 on v5

--- a/solution.py
+++ b/solution.py
@@ -13,7 +13,7 @@
 NR = 4
 BLOCKS = 5
 STEP_HEADS = 2
-CHUNK_HEADS = (4, 6, 8, 6)
+CHUNK_HEADS = (6, 8, 6, 4)
 PAD_ROWS = 16
 VMEM_BYTES = 48 * 1024 * 1024
 LOG2E = 1.4426950408889634
@@ -124,7 +124,7 @@
     return pl.pallas_call(
         choose_kernel,
         in_specs=[pl.BlockSpec(memory_space=pltpu.SMEM), anywhere, anywhere],
-        out_specs=[anywhere, anywhere],
+        out_specs=[pl.BlockSpec(memory_space=pltpu.VMEM)] * 2,
         out_shape=shapes,
         scratch_shapes=[pltpu.SemaphoreType.DMA((2,))],
         compiler_params=pltpu.CompilerParams(vmem_limit_bytes=VMEM_BYTES),

time: 257 us -> 210 us (0.82)
  Pallas kernels: 124 us -> 62.7 us
  waiting for transfers between devices: 64.1 us -> 75.9 us
  local copies, waits for them, and re-layouts: 9.74 us -> 12.5 us
    pallas_call x4, Pallas kernels: 72.4 us -> 9.24 us  [choose(): pl.pallas_call(choose_kernel, in_specs=[pl.BlockSpec(memory_space=pltpu.S...]
    ppermute x8, waiting for transfers between devices: 16.7 us -> 38.8 us  [send(): lax.ppermute(mine, 'tiles', pairs[x])]
    ppermute x3, waiting for transfers between devices: 18.8 us -> 12.3 us  [exchanged(): lax.ppermute(parts[i][1], 'tiles', [(d, d ^ 2 << i) for d in range(n)])]
    unnamed x38 -> x44, local copies, waits for them, and re-layouts: 8.05 us -> 10.1 us
  transfers between devices with their start and end apart: 23 -> 23, of which waited for: 7 -> 8; matrix products, arithmetic and copies ran while one was open for 2% -> 2% of each run, Pallas kernels for 35% -> 27%
where the time goes in v6:
time: 210 us; the launch traced here: 208 us
  waiting for transfers between devices  75.9 us (36%)
  Pallas kernels  62.7 us (30%)
  starting transfers between devices  52.4 us (25%)
  local copies, waits for them, and re-layouts  12.5 us (6%)
  other arithmetic  2.8 us (1%)
    ppermute x8, waiting for transfers between devices, send(): lax.ppermute(mine, 'tiles', pairs[x])  38.8 us
    pallas_call x4, Pallas kernels, video_call(): pl.pallas_call(video_kernel, grid=(heads // STEP_HEADS,), in_specs=in_spe...  34.8 us
    ppermute x8, starting transfers between devices, send(): lax.ppermute(mine, 'tiles', pairs[x])  28.8 us
    ppermute x8, waiting for transfers between devices, per_device(): lax.ppermute(half, 'tiles', pairs['relayed'])  24.8 us
    ppermute x8, starting transfers between devices, per_device(): lax.ppermute(half, 'tiles', pairs['relayed'])  22.4 us
    ppermute x3, waiting for transfers between devices, exchanged(): lax.ppermute(parts[i][1], 'tiles', [(d, d ^ 2 << i) for d in range(n)])  12.3 us
    unnamed x44, local copies, waits for them, and re-layouts  10.1 us
    pallas_call x4, Pallas kernels, choose(): pl.pallas_call(choose_kernel, in_specs=[pl.BlockSpec(memory_space=pltpu.S...  9.24 us
  transfers between devices with their start and end apart: 23, of which 8 were waited for; matrix products, arithmetic and copies ran while one was open for 2% of the time, Pallas kernels for 27%

profile of v6, /device:TPU:24, one launch (start us, length us, event | category | flops | bytes accessed | tf_op | source)
XLA Modules:
  0.0 208.1 jit_solution(10986952495494841677)
XLA Ops:
  1.2 1.4 copy-done
  2.6 1.4 copy-done.3
  4.0 1.7 pack_chunk.7
  5.7 1.9 collective-permute-start.7
  7.7 3.9 %collective-permute-start.8 = (bf16[528,768]{1,0:T(8,128)(2,1)}, bf16[528,768]{1,0:T(8,128)(2,1)}, u32[]{:S(2)}, u32[]{:S(2)}) collective-permute-start(bf16[528,768]{1,0:T(8,128)(2,1)} %pack_chunk.7), channel_id=1, source_target_pairs={{0,12},{1,13},{4,0},{6,2},{7,3},{8,4},{9,5},{10,6},{11,7},{12,8},{... | collective-permute-start | bytes 2433032 | tf_op jit(solution)/shard_map/ppermute | solution.py:510
  11.7 0.9 pack_chunk.5
  12.7 1.0 copy-done.11
  13.7 3.3 %collective-permute-start.4 = (bf16[528,1024]{1,0:T(8,128)(2,1)}, bf16[528,1024]{1,0:T(8,128)(2,1)}, u32[]{:S(2)}, u32[]{:S(2)}) collective-permute-start(bf16[528,1024]{1,0:T(8,128)(2,1)} %copy-done.11), channel_id=1, source_target_pairs={{0,12},{1,13},{4,0},{6,2},{7,3},{8,4},{9,5},{10,6},{11,7},{12,8},{... | collective-permute-start | bytes 3244040 | tf_op jit(solution)/shard_map/ppermute | solution.py:510
  17.0 4.4 %collective-permute-start.3 = (bf16[528,1024]{1,0:T(8,128)(2,1)}, bf16[528,1024]{1,0:T(8,128)(2,1)}, u32[]{:S(2)}, u32[]{:S(2)}) collective-permute-start(bf16[528,1024]{1,0:T(8,128)(2,1)} %copy-done.11), channel_id=1, source_target_pairs={{2,6},{3,7},{4,8},{5,9},{6,10},{7,11},{8,12},{9,13},{10,14},{11,15... | collective-permute-start | bytes 3244040 | tf_op jit(solution)/shard_map/ppermute | solution.py:510
  22.2 1.4 copy-done.10
  23.6 8.7 %text_partials.1 = (f32[128,1792]{1,0:T(8,128)S(1)}, f32[128,1792]{1,0:T(8,128)}) custom-call(s32[17]{0:T(128)S(1)} %pad_add_fusion.1.order, s32[4]{0:T(128)S(1)} %pad_add_fusion.2.counts, bf16[256,3072]{1,0:T(8,128)(2,1)S(1)} %copy-done.10, bf16[256,3072]{1,0:T(8,128)(2,1)S(1)} %copy-done.1, bf16[256,3072]{1,0:T(8,128)(2,1)} %v_own.7, ...), custom_call_target="tpu_custom_call" | custom-call | flops 8388608 | bytes 786432 | tf_op jit(solution)/shard_map/text_partials/pallas_call | solution.py:367
  32.3 1.0 copy-done.12
  34.0 35.4 %collective-permute-done.7.a.rest_0_ = bf16[528,768]{1,0:T(8,128)(2,1)} collective-permute-done((bf16[528,768]{1,0:T(8,128)(2,1)}, bf16[528,768]{1,0:T(8,128)(2,1)}, u32[]{:S(2)}, u32[]{:S(2)}) %collective-permute-start.7) | collective-permute-done | bytes 811040 | tf_op jit(solution)/shard_map/ppermute | solution.py:510
  69.4 2.7 %choose_relayed.4 = (bf16[272,768]{1,0:T(8,128)(2,1)}, bf16[256,768]{1,0:T(8,128)(2,1)}) custom-call(s32[1]{0:T(128)} %dynamic_slice.8.second, bf16[528,768]{1,0:T(8,128)(2,1)} %collective-permute-done.7.a.rest_0_, bf16[528,768]{1,0:T(8,128)(2,1)} %collective-permute-done.8.b.rest_1_), custom_call_target="tpu_custom_call" | custom-call | tf_op jit(solution)/shard_map/choose_relayed/pallas_call | solution.py:124
  72.2 1.9 collective-permute-start.11
  74.1 3.6 %collective-permute-start.12 = (bf16[256,768]{1,0:T(8,128)(2,1)}, bf16[256,768]{1,0:T(8,128)(2,1)S(1)}, u32[]{:S(2)}, u32[]{:S(2)}) collective-permute-start(bf16[256,768]{1,0:T(8,128)(2,1)} %get-tuple-element.39), channel_id=1, source_target_pairs={{0,3},{3,0},{4,7},{7,4},{8,11},{11,8},{12,15},{15,12},{16,19},{19,... | collective-permute-start | bytes 1179656 | tf_op jit(solution)/shard_map/ppermute | solution.py:545
  77.8 0.8 pack_chunk.6
  78.6 0.9 copy-done.14
  81.4 4.5 %collective-permute-done.12.rest_3_ = bf16[256,768]{1,0:T(8,128)(2,1)S(1)} collective-permute-done((bf16[256,768]{1,0:T(8,128)(2,1)}, bf16[256,768]{1,0:T(8,128)(2,1)S(1)}, u32[]{:S(2)}, u32[]{:S(2)}) %collective-permute-start.12) | collective-permute-done | bytes 393248 | tf_op jit(solution)/shard_map/ppermute | solution.py:545
  85.9 2.3 %collective-permute-start.10 = (bf16[528,768]{1,0:T(8,128)(2,1)}, bf16[528,768]{1,0:T(8,128)(2,1)}, u32[]{:S(2)}, u32[]{:S(2)}) collective-permute-start(bf16[528,768]{1,0:T(8,128)(2,1)} %copy-done.14), channel_id=1, source_target_pairs={{0,12},{1,13},{4,0},{6,2},{7,3},{8,4},{9,5},{10,6},{11,7},{12,8},{... | collective-permute-start | bytes 2433032 | tf_op jit(solution)/shard_map/ppermute | solution.py:510
  88.3 5.3 %collective-permute-start.9 = (bf16[528,768]{1,0:T(8,128)(2,1)}, bf16[528,768]{1,0:T(8,128)(2,1)}, u32[]{:S(2)}, u32[]{:S(2)}) collective-permute-start(bf16[528,768]{1,0:T(8,128)(2,1)} %copy-done.14), channel_id=1, source_target_pairs={{2,6},{3,7},{4,8},{5,9},{6,10},{7,11},{8,12},{9,13},{10,14},{11,15... | collective-permute-start | bytes 2433032 | tf_op jit(solution)/shard_map/ppermute | solution.py:510
  94.4 1.4 copy-done.7
  95.8 8.7 %video_attention.4.rest_8_ = bf16[256,3072]{1,0:T(8,128)(2,1)} custom-call(s32[13]{0:T(128)S(1)} %concatenate.18.table, bf16[256,3072]{1,0:T(8,128)(2,1)S(1)} %copy-done.7, bf16[256,3072]{1,0:T(8,128)(2,1)S(1)} %copy-done.1, bf16[256,3072]{1,0:T(8,128)(2,1)} %v_own.7, bf16[528,768]{1,0:T(8,128)(2,1)} %collective-permute-done.7.a.rest_0_, ...), custom_call_target="tpu_custom_call" | custom-call | flops 56623104 | bytes 196608 | tf_op jit(solution)/shard_map/video_attention/pallas_call | solution.py:275
  104.5 2.1 text_merge.2
  106.6 3.4 %collective-permute-done.3.a.rest_0_ = bf16[528,1024]{1,0:T(8,128)(2,1)} collective-permute-done((bf16[528,1024]{1,0:T(8,128)(2,1)}, bf16[528,1024]{1,0:T(8,128)(2,1)}, u32[]{:S(2)}, u32[]{:S(2)}) %collective-permute-start.3) | collective-permute-done | bytes 1081376 | tf_op jit(solution)/shard_map/ppermute | solution.py:510
  110.0 1.9 choose_relayed.5
  111.9 1.9 collective-permute-start.14
  113.8 3.6 %collective-permute-start.15 = (bf16[256,1024]{1,0:T(8,128)(2,1)S(1)}, bf16[256,1024]{1,0:T(8,128)(2,1)S(1)}, u32[]{:S(2)}, u32[]{:S(2)}) collective-permute-start(bf16[256,1024]{1,0:T(8,128)(2,1)S(1)} %get-tuple-element.46), channel_id=1, source_target_pairs={{0,3},{3,0},{4,7},{7,4},{8,11},{11,8},{12,15},{15,12},{16,19},{19,... | collective-permute-start | bytes 1572872 | tf_op jit(solution)/shard_map/ppermute | solution.py:545
  118.0 1.5 pack_chunk.4
  119.5 8.9 %collective-permute-done.15.rest_3_ = bf16[256,1024]{1,0:T(8,128)(2,1)S(1)} collective-permute-done((bf16[256,1024]{1,0:T(8,128)(2,1)S(1)}, bf16[256,1024]{1,0:T(8,128)(2,1)S(1)}, u32[]{:S(2)}, u32[]{:S(2)}) %collective-permute-start.15) | collective-permute-done | bytes 524320 | tf_op jit(solution)/shard_map/ppermute | solution.py:545
  128.4 2.3 %collective-permute-start.6 = (bf16[528,512]{1,0:T(8,128)(2,1)}, bf16[528,512]{1,0:T(8,128)(2,1)}, u32[]{:S(2)}, u32[]{:S(2)}) collective-permute-start(bf16[528,512]{1,0:T(8,128)(2,1)} %pack_chunk.4), channel_id=1, source_target_pairs={{0,12},{1,13},{4,0},{6,2},{7,3},{8,4},{9,5},{10,6},{11,7},{12,8},{... | collective-permute-start | bytes 1622024 | tf_op jit(solution)/shard_map/ppermute | solution.py:510
  130.7 5.3 %collective-permute-start.5 = (bf16[528,512]{1,0:T(8,128)(2,1)}, bf16[528,512]{1,0:T(8,128)(2,1)}, u32[]{:S(2)}, u32[]{:S(2)}) collective-permute-start(bf16[528,512]{1,0:T(8,128)(2,1)} %pack_chunk.4), channel_id=1, source_target_pairs={{2,6},{3,7},{4,8},{5,9},{6,10},{7,11},{8,12},{9,13},{10,14},{11,15... | collective-permute-start | bytes 1622024 | tf_op jit(solution)/shard_map/ppermute | solution.py:510
  136.0 11.9 %collective-permute-done.16.refs_1_ = f32[64,1664]{1,0:T(8,128)S(1)} collective-permute-done((f32[64,1664]{1,0:T(8,128)S(1)}, f32[64,1664]{1,0:T(8,128)S(1)}, u32[]{:S(2)}, u32[]{:S(2)}) %collective-permute-start.16) | collective-permute-done | bytes 426016 | tf_op jit(solution)/shard_map/ppermute | solution.py:527
  148.0 1.1 text_merge.3
  149.1 11.1 %video_attention.5.rest_8_ = bf16[256,3072]{1,0:T(8,128)(2,1)} custom-call(s32[13]{0:T(128)S(1)} %concatenate.18.table, bf16[256,3072]{1,0:T(8,128)(2,1)S(1)} %copy-done.8, bf16[256,3072]{1,0:T(8,128)(2,1)} %k_own.7, bf16[256,3072]{1,0:T(8,128)(2,1)} %v_own.7, bf16[528,1024]{1,0:T(8,128)(2,1)} %collective-permute-done.3.a.rest_0_, ...), custom_call_target="tpu_custom_call", output_to_operand_aliasing={{}: (12, {})} | custom-call | flops 75497472 | bytes 262144 | tf_op jit(solution)/shard_map/video_attention/pallas_call | solution.py:275
  160.2 2.8 %choose_relayed.6 = (bf16[272,768]{1,0:T(8,128)(2,1)}, bf16[256,768]{1,0:T(8,128)(2,1)}) custom-call(s32[1]{0:T(128)} %dynamic_slice.8.second, bf16[528,768]{1,0:T(8,128)(2,1)} %collective-permute-done.9.a.rest_0_, bf16[528,768]{1,0:T(8,128)(2,1)} %collective-permute-done.10.b.rest_1_), custom_call_target="tpu_custom_call" | custom-call | tf_op jit(solution)/shard_map/choose_relayed/pallas_call | solution.py:124
  163.1 1.9 collective-permute-start.17
  165.0 3.8 %collective-permute-start.18 = (bf16[256,768]{1,0:T(8,128)(2,1)}, bf16[256,768]{1,0:T(8,128)(2,1)S(1)}, u32[]{:S(2)}, u32[]{:S(2)}) collective-permute-start(bf16[256,768]{1,0:T(8,128)(2,1)} %get-tuple-element.53), channel_id=1, source_target_pairs={{0,3},{3,0},{4,7},{7,4},{8,11},{11,8},{12,15},{15,12},{16,19},{19,... | collective-permute-start | bytes 1179656 | tf_op jit(solution)/shard_map/ppermute | solution.py:545
  169.0 7.9 %collective-permute-done.18.rest_3_ = bf16[256,768]{1,0:T(8,128)(2,1)S(1)} collective-permute-done((bf16[256,768]{1,0:T(8,128)(2,1)}, bf16[256,768]{1,0:T(8,128)(2,1)S(1)}, u32[]{:S(2)}, u32[]{:S(2)}) %collective-permute-start.18) | collective-permute-done | bytes 393248 | tf_op jit(solution)/shard_map/ppermute | solution.py:545
  177.2 0.9 copy-done.16
  178.1 1.9 text_finish.1
  180.6 8.7 %video_attention.6.rest_8_ = bf16[256,3072]{1,0:T(8,128)(2,1)} custom-call(s32[13]{0:T(128)S(1)} %concatenate.18.table, bf16[256,3072]{1,0:T(8,128)(2,1)S(1)} %copy-done.9, bf16[256,3072]{1,0:T(8,128)(2,1)S(1)} %copy-done.2, bf16[256,3072]{1,0:T(8,128)(2,1)} %v_own.7, ...), custom_call_target="tpu_custom_call", output_to_operand_aliasing={{}: (12, {})} | custom-call | flops 56623104 | bytes 196608 | tf_op jit(solution)/shard_map/video_attention/pallas_call | solution.py:275
  189.3 1.7 choose_relayed.7
  191.1 1.9 collective-permute-start.20
  193.0 3.6 %collective-permute-start.21 = (bf16[256,512]{1,0:T(8,128)(2,1)S(1)}, bf16[256,512]{1,0:T(8,128)(2,1)S(1)}, u32[]{:S(2)}, u32[]{:S(2)}) collective-permute-start(bf16[256,512]{1,0:T(8,128)(2,1)S(1)} %get-tuple-element.60), channel_id=1, source_target_pairs={{0,3},{3,0},{4,7},{7,4},{8,11},{11,8},{12,15},{15,12},{16,19},{19,... | collective-permute-start | bytes 786440 | tf_op jit(solution)/shard_map/ppermute | solution.py:545
  196.7 1.5 maximum_select_fusion
  198.2 3.5 %collective-permute-done.21.rest_3_ = bf16[256,512]{1,0:T(8,128)(2,1)S(1)} collective-permute-done((bf16[256,512]{1,0:T(8,128)(2,1)S(1)}, bf16[256,512]{1,0:T(8,128)(2,1)S(1)}, u32[]{:S(2)}, u32[]{:S(2)}) %collective-permute-start.21) | collective-permute-done | bytes 262176 | tf_op jit(solution)/shard_map/ppermute | solution.py:545
  201.8 6.3 %video_attention.7 = bf16[256,3072]{1,0:T(8,128)(2,1)} custom-call(s32[13]{0:T(128)S(1)} %concatenate.18.table, bf16[256,3072]{1,0:T(8,128)(2,1)S(1)} %copy-done.9, bf16[256,3072]{1,0:T(8,128)(2,1)S(1)} %copy-done.2, bf16[256,3072]{1,0:T(8,128)(2,1)} %v_own.7, bf16[528,512]{1,0:T(8,128)(2,1)} %collective-permute-done.5.a.rest_0_, ...), custom_call_target="tpu_custom_call", output_to_operand_aliasing={{}: (12, {})} | custom-call | flops 37748736 | bytes 131072 | tf_op jit(solution)/shard_map/video_attention/pallas_call | solution.py:275
  (75 shorter events, 6.0 us)
Async XLA Ops:
  0.6 13.0 %collective-permute-start.1 = (bf16[256,3072]{1,0:T(8,128)(2,1)}, bf16[256,3072]{1,0:T(8,128)(2,1)}, u32[]{:S(2)}, u32[]{:S(2)}) collective-permute-start(bf16[256,3072]{1,0:T(8,128)(2,1)} %k_own.7), channel_id=1, source_target_pairs={{0,1},{1,0},{2,3},{3,2},{4,5},{5,4},{6,7},{7,6},{8,9},{9,8},{10,11... | collective-permute-start | bytes 4718600 | tf_op jit(solution)/shard_map/ppermute | solution.py:514
  0.7 13.0 %collective-permute-start.2 = (bf16[256,3072]{1,0:T(8,128)(2,1)}, bf16[256,3072]{1,0:T(8,128)(2,1)}, u32[]{:S(2)}, u32[]{:S(2)}) collective-permute-start(bf16[256,3072]{1,0:T(8,128)(2,1)} %v_own.7), channel_id=1, source_target_pairs={{0,1},{1,0},{2,3},{3,2},{4,5},{5,4},{6,7},{7,6},{8,9},{9,8},{10,11... | collective-permute-start | bytes 4718600 | tf_op jit(solution)/shard_map/ppermute | solution.py:514
  1.2 1.4 copy-start
  2.6 1.4 copy-start.3
  4.0 7.7 %copy-start.1 = (bf16[256,3072]{1,0:T(8,128)(2,1)S(1)}, bf16[256,3072]{1,0:T(8,128)(2,1)}, u32[]{:S(2)}) copy-start(bf16[256,3072]{1,0:T(8,128)(2,1)} %k_own.7) | copy-start | bytes 4718596
  4.0 7.7 %copy-start.4 = (bf16[256,3072]{1,0:T(8,128)(2,1)S(1)}, bf16[256,3072]{1,0:T(8,128)(2,1)}, u32[]{:S(2)}) copy-start(bf16[256,3072]{1,0:T(8,128)(2,1)} %v_own.7) | copy-start | bytes 4718596
  5.7 63.7 %collective-permute-start.7 = (bf16[528,768]{1,0:T(8,128)(2,1)}, bf16[528,768]{1,0:T(8,128)(2,1)}, u32[]{:S(2)}, u32[]{:S(2)}) collective-permute-start(bf16[528,768]{1,0:T(8,128)(2,1)} %pack_chunk.7), channel_id=1, source_target_pairs={{2,6},{3,7},{4,8},{5,9},{6,10},{7,11},{8,12},{9,13},{10,14},{11,15... | collective-permute-start | bytes 2433032 | tf_op jit(solution)/shard_map/ppermute | solution.py:510
  7.7 61.8 %collective-permute-start.8 = (bf16[528,768]{1,0:T(8,128)(2,1)}, bf16[528,768]{1,0:T(8,128)(2,1)}, u32[]{:S(2)}, u32[]{:S(2)}) collective-permute-start(bf16[528,768]{1,0:T(8,128)(2,1)} %pack_chunk.7), channel_id=1, source_target_pairs={{0,12},{1,13},{4,0},{6,2},{7,3},{8,4},{9,5},{10,6},{11,7},{12,8},{... | collective-permute-start | bytes 2433032 | tf_op jit(solution)/shard_map/ppermute | solution.py:510
  11.6 2.1 collective-permute-start
  11.7 2.0 copy-start.21
  12.7 1.0 copy-start.11
  13.7 92.9 %collective-permute-start.4 = (bf16[528,1024]{1,0:T(8,128)(2,1)}, bf16[528,1024]{1,0:T(8,128)(2,1)}, u32[]{:S(2)}, u32[]{:S(2)}) collective-permute-start(bf16[528,1024]{1,0:T(8,128)(2,1)} %copy-done.11), channel_id=1, source_target_pairs={{0,12},{1,13},{4,0},{6,2},{7,3},{8,4},{9,5},{10,6},{11,7},{12,8},{... | collective-permute-start | bytes 3244040 | tf_op jit(solution)/shard_map/ppermute | solution.py:510
  17.0 93.0 %collective-permute-start.3 = (bf16[528,1024]{1,0:T(8,128)(2,1)}, bf16[528,1024]{1,0:T(8,128)(2,1)}, u32[]{:S(2)}, u32[]{:S(2)}) collective-permute-start(bf16[528,1024]{1,0:T(8,128)(2,1)} %copy-done.11), channel_id=1, source_target_pairs={{2,6},{3,7},{4,8},{5,9},{6,10},{7,11},{8,12},{9,13},{10,14},{11,15... | collective-permute-start | bytes 3244040 | tf_op jit(solution)/shard_map/ppermute | solution.py:510
  22.2 1.4 copy-start.10
  23.6 9.7 %copy-start.20 = (s32[16]{0:T(128)S(1)}, s32[16]{0:T(128)}, u32[]{:S(2)}) copy-start(s32[16]{0:T(128)} %constant.74.clone) | copy-start | bytes 196
  32.3 1.0 copy-start.12
  33.3 44.4 %copy-start.19 = (s32[2,6]{1,0:T(2,128)S(1)}, s32[2,6]{1,0:T(2,128)}, u32[]{:S(2)}) copy-start(s32[2,6]{1,0:T(2,128)} %param.18) | copy-start | bytes 148
  33.3 44.5 %copy-start.5 = (bf16[256,3072]{1,0:T(8,128)(2,1)S(1)}, bf16[256,3072]{1,0:T(8,128)(2,1)}, u32[]{:S(2)}) copy-start(bf16[256,3072]{1,0:T(8,128)(2,1)} %v_own.7) | copy-start | bytes 4718596
  33.3 71.2 %collective-permute-start.13 = (f32[128,1792]{1,0:T(8,128)}, f32[128,1792]{1,0:T(8,128)}, u32[]{:S(2)}, u32[]{:S(2)}) collective-permute-start(f32[128,1792]{1,0:T(8,128)} %get-tuple-element.41), channel_id=1, source_target_pairs={{0,2},{1,3},{2,0},{3,1},{4,6},{5,7},{6,4},{7,5},{8,10},{9,11},{10,... | collective-permute-start | bytes 2752520 | tf_op jit(solution)/shard_map/ppermute | solution.py:527
  72.2 16.1 %collective-permute-start.11 = (bf16[272,768]{1,0:T(8,128)(2,1)}, bf16[272,768]{1,0:T(8,128)(2,1)}, u32[]{:S(2)}, u32[]{:S(2)}) collective-permute-start(bf16[272,768]{1,0:T(8,128)(2,1)} %get-tuple-element.38), channel_id=1, source_target_pairs={{0,3},{3,0},{4,7},{7,4},{8,11},{11,8},{12,15},{15,12},{16,19},{19,... | collective-permute-start | bytes 1253384 | tf_op jit(solution)/shard_map/ppermute | solution.py:545
  74.1 11.9 %collective-permute-start.12 = (bf16[256,768]{1,0:T(8,128)(2,1)}, bf16[256,768]{1,0:T(8,128)(2,1)S(1)}, u32[]{:S(2)}, u32[]{:S(2)}) collective-permute-start(bf16[256,768]{1,0:T(8,128)(2,1)} %get-tuple-element.39), channel_id=1, source_target_pairs={{0,3},{3,0},{4,7},{7,4},{8,11},{11,8},{12,15},{15,12},{16,19},{19,... | collective-permute-start | bytes 1179656 | tf_op jit(solution)/shard_map/ppermute | solution.py:545
  78.6 0.9 copy-start.14
  85.9 74.2 %collective-permute-start.10 = (bf16[528,768]{1,0:T(8,128)(2,1)}, bf16[528,768]{1,0:T(8,128)(2,1)}, u32[]{:S(2)}, u32[]{:S(2)}) collective-permute-start(bf16[528,768]{1,0:T(8,128)(2,1)} %copy-done.14), channel_id=1, source_target_pairs={{0,12},{1,13},{4,0},{6,2},{7,3},{8,4},{9,5},{10,6},{11,7},{12,8},{... | collective-permute-start | bytes 2433032 | tf_op jit(solution)/shard_map/ppermute | solution.py:510
  88.3 71.9 %collective-permute-start.9 = (bf16[528,768]{1,0:T(8,128)(2,1)}, bf16[528,768]{1,0:T(8,128)(2,1)}, u32[]{:S(2)}, u32[]{:S(2)}) collective-permute-start(bf16[528,768]{1,0:T(8,128)(2,1)} %copy-done.14), channel_id=1, source_target_pairs={{2,6},{3,7},{4,8},{5,9},{6,10},{7,11},{8,12},{9,13},{10,14},{11,15... | collective-permute-start | bytes 2433032 | tf_op jit(solution)/shard_map/ppermute | solution.py:510
  94.4 1.4 copy-start.7
  95.8 8.7 %copy-start.13 = (f32[128,1792]{1,0:T(8,128)S(1)}, f32[128,1792]{1,0:T(8,128)}, u32[]{:S(2)}) copy-start(f32[128,1792]{1,0:T(8,128)} %copy-done.12) | copy-start | bytes 2752516
  104.5 13.5 %copy-start.6 = (bf16[256,3072]{1,0:T(8,128)(2,1)S(1)}, bf16[256,3072]{1,0:T(8,128)(2,1)}, u32[]{:S(2)}) copy-start(bf16[256,3072]{1,0:T(8,128)(2,1)} %v_own.7) | copy-start | bytes 4718596
  111.9 18.8 %collective-permute-start.14 = (bf16[272,1024]{1,0:T(8,128)(2,1)S(1)}, bf16[272,1024]{1,0:T(8,128)(2,1)S(1)}, u32[]{:S(2)}, u32[]{:S(2)}) collective-permute-start(bf16[272,1024]{1,0:T(8,128)(2,1)S(1)} %get-tuple-element.45), channel_id=1, source_target_pairs={{0,3},{3,0},{4,7},{7,4},{8,11},{11,8},{12,15},{15,12},{16,19},{19,... | collective-permute-start | bytes 1671176 | tf_op jit(solution)/shard_map/ppermute | solution.py:545
  113.8 14.5 %collective-permute-start.15 = (bf16[256,1024]{1,0:T(8,128)(2,1)S(1)}, bf16[256,1024]{1,0:T(8,128)(2,1)S(1)}, u32[]{:S(2)}, u32[]{:S(2)}) collective-permute-start(bf16[256,1024]{1,0:T(8,128)(2,1)S(1)} %get-tuple-element.46), channel_id=1, source_target_pairs={{0,3},{3,0},{4,7},{7,4},{8,11},{11,8},{12,15},{15,12},{16,19},{19,... | collective-permute-start | bytes 1572872 | tf_op jit(solution)/shard_map/ppermute | solution.py:545
  117.5 31.6 %copy-start.8 = (bf16[256,3072]{1,0:T(8,128)(2,1)S(1)}, bf16[256,3072]{1,0:T(8,128)(2,1)}, u32[]{:S(2)}) copy-start(bf16[256,3072]{1,0:T(8,128)(2,1)} %q.9) | copy-start | bytes 4718596
  117.5 30.5 %collective-permute-start.16 = (f32[64,1664]{1,0:T(8,128)S(1)}, f32[64,1664]{1,0:T(8,128)S(1)}, u32[]{:S(2)}, u32[]{:S(2)}) collective-permute-start(f32[64,1664]{1,0:T(8,128)S(1)} %get-tuple-element.48), channel_id=1, source_target_pairs={{0,4},{1,5},{2,6},{3,7},{4,0},{5,1},{6,2},{7,3},{8,12},{9,13},{10,... | collective-permute-start | bytes 1277960 | tf_op jit(solution)/shard_map/ppermute | solution.py:527
  128.4 61.0 %collective-permute-start.6 = (bf16[528,512]{1,0:T(8,128)(2,1)}, bf16[528,512]{1,0:T(8,128)(2,1)}, u32[]{:S(2)}, u32[]{:S(2)}) collective-permute-start(bf16[528,512]{1,0:T(8,128)(2,1)} %pack_chunk.4), channel_id=1, source_target_pairs={{0,12},{1,13},{4,0},{6,2},{7,3},{8,4},{9,5},{10,6},{11,7},{12,8},{... | collective-permute-start | bytes 1622024 | tf_op jit(solution)/shard_map/ppermute | solution.py:510
  130.7 58.6 %collective-permute-start.5 = (bf16[528,512]{1,0:T(8,128)(2,1)}, bf16[528,512]{1,0:T(8,128)(2,1)}, u32[]{:S(2)}, u32[]{:S(2)}) collective-permute-start(bf16[528,512]{1,0:T(8,128)(2,1)} %pack_chunk.4), channel_id=1, source_target_pairs={{2,6},{3,7},{4,8},{5,9},{6,10},{7,11},{8,12},{9,13},{10,14},{11,15... | collective-permute-start | bytes 1622024 | tf_op jit(solution)/shard_map/ppermute | solution.py:510
  149.1 11.1 %copy-start.15 = (f32[32,1664]{1,0:T(8,128)}, f32[32,1664]{1,0:T(8,128)S(1)}, u32[]{:S(2)}) copy-start(f32[32,1664]{1,0:T(8,128)S(1)} %get-tuple-element.54.refs_0_) | copy-start | bytes 638980
  149.1 31.5 %copy-start.9 = (bf16[256,3072]{1,0:T(8,128)(2,1)S(1)}, bf16[256,3072]{1,0:T(8,128)(2,1)}, u32[]{:S(2)}) copy-start(bf16[256,3072]{1,0:T(8,128)(2,1)} %q.9) | copy-start | bytes 4718596
  160.2 20.4 %copy-start.2 = (bf16[256,3072]{1,0:T(8,128)(2,1)S(1)}, bf16[256,3072]{1,0:T(8,128)(2,1)}, u32[]{:S(2)}) copy-start(bf16[256,3072]{1,0:T(8,128)(2,1)} %k_own.7) | copy-start | bytes 4718596
  163.1 13.8 %collective-permute-start.17 = (bf16[272,768]{1,0:T(8,128)(2,1)}, bf16[272,768]{1,0:T(8,128)(2,1)}, u32[]{:S(2)}, u32[]{:S(2)}) collective-permute-start(bf16[272,768]{1,0:T(8,128)(2,1)} %get-tuple-element.52), channel_id=1, source_target_pairs={{0,3},{3,0},{4,7},{7,4},{8,11},{11,8},{12,15},{15,12},{16,19},{19,... | collective-permute-start | bytes 1253384 | tf_op jit(solution)/shard_map/ppermute | solution.py:545
  165.0 11.9 %collective-permute-start.18 = (bf16[256,768]{1,0:T(8,128)(2,1)}, bf16[256,768]{1,0:T(8,128)(2,1)S(1)}, u32[]{:S(2)}, u32[]{:S(2)}) collective-permute-start(bf16[256,768]{1,0:T(8,128)(2,1)} %get-tuple-element.53), channel_id=1, source_target_pairs={{0,3},{3,0},{4,7},{7,4},{8,11},{11,8},{12,15},{15,12},{16,19},{19,... | collective-permute-start | bytes 1179656 | tf_op jit(solution)/shard_map/ppermute | solution.py:545
  168.8 8.4 %collective-permute-start.19 = (f32[32,1664]{1,0:T(8,128)}, f32[32,1664]{1,0:T(8,128)}, u32[]{:S(2)}, u32[]{:S(2)}) collective-permute-start(f32[32,1664]{1,0:T(8,128)} %get-tuple-element.55), channel_id=1, source_target_pairs={{0,8},{1,9},{2,10},{3,11},{4,12},{5,13},{6,14},{7,15},{8,0},{9,1},... | collective-permute-start | bytes 638984 | tf_op jit(solution)/shard_map/ppermute | solution.py:527
  177.2 0.9 copy-start.16
  180.0 0.6 copy-start.17
  180.6 16.1 %collective-permute-start.22 = (bf16[16,1536]{1,0:T(8,128)(2,1)}, bf16[16,1536]{1,0:T(8,128)(2,1)}, u32[]{:S(2)}, u32[]{:S(2)}) collective-permute-start(bf16[16,1536]{1,0:T(8,128)(2,1)} %get-tuple-element.61), channel_id=1, source_target_pairs={{0,1},{1,0},{2,3},{3,2},{4,5},{5,4},{6,7},{7,6},{8,9},{9,8},{10,11... | collective-permute-start | bytes 147464 | tf_op jit(solution)/shard_map/ppermute | solution.py:559
  180.6 16.1 %copy-start.18 = (bf16[16,1536]{1,0:T(8,128)(2,1)S(1)}, bf16[16,1536]{1,0:T(8,128)(2,1)}, u32[]{:S(2)}) copy-start(bf16[16,1536]{1,0:T(8,128)(2,1)} %copy-done.17) | copy-start | bytes 147460
  191.1 10.7 %collective-permute-start.20 = (bf16[272,512]{1,0:T(8,128)(2,1)S(1)}, bf16[272,512]{1,0:T(8,128)(2,1)S(1)}, u32[]{:S(2)}, u32[]{:S(2)}) collective-permute-start(bf16[272,512]{1,0:T(8,128)(2,1)S(1)} %get-tuple-element.59), channel_id=1, source_target_pairs={{0,3},{3,0},{4,7},{7,4},{8,11},{11,8},{12,15},{15,12},{16,19},{19,... | collective-permute-start | bytes 835592 | tf_op jit(solution)/shard_map/ppermute | solution.py:545
  193.0 8.7 %collective-permute-start.21 = (bf16[256,512]{1,0:T(8,128)(2,1)S(1)}, bf16[256,512]{1,0:T(8,128)(2,1)S(1)}, u32[]{:S(2)}, u32[]{:S(2)}) collective-permute-start(bf16[256,512]{1,0:T(8,128)(2,1)S(1)} %get-tuple-element.60), channel_id=1, source_target_pairs={{0,3},{3,0},{4,7},{7,4},{8,11},{11,8},{12,15},{15,12},{16,19},{19,... | collective-permute-start | bytes 786440 | tf_op jit(solution)/shard_map/ppermute | solution.py:545

commit v7 on v6

--- a/solution.py
+++ b/solution.py
@@ -13,7 +13,7 @@
 NR = 4
 BLOCKS = 5
 STEP_HEADS = 2
-CHUNK_HEADS = (6, 8, 6, 4)
+CHUNK_HEADS = (8, 6, 6, 4)
 PAD_ROWS = 16
 VMEM_BYTES = 48 * 1024 * 1024
 LOG2E = 1.4426950408889634
@@ -513,7 +513,6 @@
     beside = [
         lax.ppermute(x, "tiles", pairs["beside"]) for x in (counts, video_k, video_v)
     ]
-    send(1, *beside)
     table = make_table(window, counts, beside[0], text_count, choices, position)
     halving = text % (PAD_ROWS * n) == 0 and n & (n - 1) == 0
     stages = n.bit_length() - 1
@@ -538,22 +537,24 @@
 
     count = len(CHUNK_HEADS)
     for i in range(count):
-        up, down = direct[i]
         before = outs[-1:] + ([parts[-1][0]] if halving else [])
-        up, down = tie(up, *before), tie(down, *before)
+        if i + 1 < count:
+            send(i + 1, *direct[i], *before)
+        up, down = tie(direct[i][0], *before), tie(direct[i][1], *before)
         relays = [
             lax.ppermute(half, "tiles", pairs["relayed"])
             for half in choose(sends_later, up, down, rows + PAD_ROWS)
         ]
-        if i + 2 < count:
-            send(i + 2, *direct[i])
-        merge(*relays)
         outs.append(
             video_call(
                 starts[i], CHUNK_HEADS[i], table, video_q, video_k, video_v,
                 [*direct[i], *relays, *beside[1:]], text_k, text_v, outs[-1] if outs else None,
             )
         )
+        if i < 2:
+            merge(*relays)
+        if i == 1:
+            merge(outs[0])
     if halving:
         mine, leave = parts[-1]
         got = lax.ppermute(leave, "tiles", [(d, d ^ 1) for d in range(n)])

time: 210 us -> 220 us (1.048)
  waiting for transfers between devices: 75.9 us -> 83.4 us
    ppermute x3, waiting for transfers between devices: 12.3 us -> 25.2 us  [exchanged(): lax.ppermute(parts[i][1], 'tiles', [(d, d ^ 2 << i) for d in range(n)])]
    ppermute x8, waiting for transfers between devices: 38.8 us -> 29 us  [send(): lax.ppermute(mine, 'tiles', pairs[x])]
    ppermute x8, waiting for transfers between devices: 24.8 us -> 28 us  [per_device(): lax.ppermute(half, 'tiles', pairs['relayed'])]
    unnamed x44 -> x42, local copies, waits for them, and re-layouts: 10.1 us -> 8.12 us
  transfers between devices with their start and end apart: 23 -> 23, of which waited for: 8 -> 7; matrix products, arithmetic and copies ran while one was open for 2% -> 2% of each run, Pallas kernels for 27% -> 27%
where the time goes in v7:
time: 220 us; the launch traced here: 217 us
  waiting for transfers between devices  83.4 us (38%)
  Pallas kernels  64.1 us (29%)
  starting transfers between devices  54.5 us (25%)
  local copies, waits for them, and re-layouts  10.5 us (5%)
  other arithmetic  2.8 us (1%)
    pallas_call x4, Pallas kernels, video_call(): pl.pallas_call(video_kernel, grid=(heads // STEP_HEADS,), in_specs=in_spe...  34.6 us
    ppermute x8, waiting for transfers between devices, send(): lax.ppermute(mine, 'tiles', pairs[x])  29 us
    ppermute x8, starting transfers between devices, send(): lax.ppermute(mine, 'tiles', pairs[x])  29 us
    ppermute x8, waiting for transfers between devices, per_device(): lax.ppermute(half, 'tiles', pairs['relayed'])  28 us
    ppermute x3, waiting for transfers between devices, exchanged(): lax.ppermute(parts[i][1], 'tiles', [(d, d ^ 2 << i) for d in range(n)])  25.2 us
    ppermute x8, starting transfers between devices, per_device(): lax.ppermute(half, 'tiles', pairs['relayed'])  22.3 us
    pallas_call x4, Pallas kernels, choose(): pl.pallas_call(choose_kernel, in_specs=[pl.BlockSpec(memory_space=pltpu.S...  9.05 us
    pallas_call x1, Pallas kernels, text_local(): pl.pallas_call(text_kernel, grid_spec=pltpu.PrefetchScalarGridSpec(num_sc...  8.69 us
  transfers between devices with their start and end apart: 23, of which 7 were waited for; matrix products, arithmetic and copies ran while one was open for 2% of the time, Pallas kernels for 27%

profile of v7, /device:TPU:24, one launch (start us, length us, event | category | flops | bytes accessed | tf_op | source)
XLA Modules:
  0.0 217.0 jit_solution(16008927002314491295)
XLA Ops:
  1.2 1.4 copy-done
  2.6 1.4 copy-done.3
  4.0 1.8 pack_chunk.7
  5.8 1.9 collective-permute-start.1
  7.8 3.9 %collective-permute-start.2 = (bf16[528,1024]{1,0:T(8,128)(2,1)}, bf16[528,1024]{1,0:T(8,128)(2,1)}, u32[]{:S(2)}, u32[]{:S(2)}) collective-permute-start(bf16[528,1024]{1,0:T(8,128)(2,1)} %pack_chunk.7), channel_id=1, source_target_pairs={{0,12},{1,13},{4,0},{6,2},{7,3},{8,4},{9,5},{10,6},{11,7},{12,8},{... | collective-permute-start | bytes 3244040 | tf_op jit(solution)/shard_map/ppermute | solution.py:510
  11.9 1.1 collective-permute-done
  13.0 0.7 pad_add_fusion.2.counts
  13.8 1.5 copy-done.9
  15.3 8.7 %text_partials.1 = (f32[128,1792]{1,0:T(8,128)S(1)}, f32[128,1792]{1,0:T(8,128)}) custom-call(s32[17]{0:T(128)S(1)} %pad_add_fusion.1.order, s32[4]{0:T(128)S(1)} %pad_add_fusion.2.counts, bf16[256,3072]{1,0:T(8,128)(2,1)S(1)} %copy-done.9, bf16[256,3072]{1,0:T(8,128)(2,1)S(1)} %copy-done.1, bf16[256,3072]{1,0:T(8,128)(2,1)} %v_own.7, ...), custom_call_target="tpu_custom_call" | custom-call | flops 8388608 | bytes 786432 | tf_op jit(solution)/shard_map/text_partials/pallas_call | solution.py:367
  24.0 2.5 %collective-permute-start.9 = (f32[128,1792]{1,0:T(8,128)}, f32[128,1792]{1,0:T(8,128)}, u32[]{:S(2)}, u32[]{:S(2)}) collective-permute-start(f32[128,1792]{1,0:T(8,128)} %get-tuple-element.39), channel_id=1, source_target_pairs={{0,2},{1,3},{2,0},{3,1},{4,6},{5,7},{6,4},{7,5},{8,10},{9,11},{10,... | collective-permute-start | bytes 2752520 | tf_op jit(solution)/shard_map/ppermute | solution.py:526
  26.5 1.6 pack_chunk.6
  28.0 29.0 %collective-permute-done.1.a.rest_0_ = bf16[528,1024]{1,0:T(8,128)(2,1)} collective-permute-done((bf16[528,1024]{1,0:T(8,128)(2,1)}, bf16[528,1024]{1,0:T(8,128)(2,1)}, u32[]{:S(2)}, u32[]{:S(2)}) %collective-permute-start.1) | collective-permute-done | bytes 1081376 | tf_op jit(solution)/shard_map/ppermute | solution.py:510
  57.1 2.5 %collective-permute-start.6 = (bf16[528,768]{1,0:T(8,128)(2,1)}, bf16[528,768]{1,0:T(8,128)(2,1)}, u32[]{:S(2)}, u32[]{:S(2)}) collective-permute-start(bf16[528,768]{1,0:T(8,128)(2,1)} %pack_chunk.6), channel_id=1, source_target_pairs={{0,12},{1,13},{4,0},{6,2},{7,3},{8,4},{9,5},{10,6},{11,7},{12,8},{... | collective-permute-start | bytes 2433032 | tf_op jit(solution)/shard_map/ppermute | solution.py:510
  59.6 5.3 %collective-permute-start.5 = (bf16[528,768]{1,0:T(8,128)(2,1)}, bf16[528,768]{1,0:T(8,128)(2,1)}, u32[]{:S(2)}, u32[]{:S(2)}) collective-permute-start(bf16[528,768]{1,0:T(8,128)(2,1)} %pack_chunk.6), channel_id=1, source_target_pairs={{2,6},{3,7},{4,8},{5,9},{6,10},{7,11},{8,12},{9,13},{10,14},{11,15... | collective-permute-start | bytes 2433032 | tf_op jit(solution)/shard_map/ppermute | solution.py:510
  64.9 1.7 pack_chunk.5
  67.4 2.7 %choose_relayed.4 = (bf16[272,1024]{1,0:T(8,128)(2,1)S(1)}, bf16[256,1024]{1,0:T(8,128)(2,1)}) custom-call(s32[1]{0:T(128)} %dynamic_slice.8.second, bf16[528,1024]{1,0:T(8,128)(2,1)} %collective-permute-done.1.a.rest_0_, bf16[528,1024]{1,0:T(8,128)(2,1)} %collective-permute-done.2.b.rest_1_), custom_call_target="tpu_custom_call" | custom-call | tf_op jit(solution)/shard_map/choose_relayed/pallas_call | solution.py:124
  70.2 1.9 collective-permute-start.7
  72.1 3.6 %collective-permute-start.8 = (bf16[256,1024]{1,0:T(8,128)(2,1)}, bf16[256,1024]{1,0:T(8,128)(2,1)S(1)}, u32[]{:S(2)}, u32[]{:S(2)}) collective-permute-start(bf16[256,1024]{1,0:T(8,128)(2,1)} %get-tuple-element.37), channel_id=1, source_target_pairs={{0,3},{3,0},{4,7},{7,4},{8,11},{11,8},{12,15},{15,12},{16,19},{19,... | collective-permute-start | bytes 1572872 | tf_op jit(solution)/shard_map/ppermute | solution.py:545
  77.5 0.7 concatenate.18.table
  78.3 8.3 %collective-permute-done.8.rest_3_ = bf16[256,1024]{1,0:T(8,128)(2,1)S(1)} collective-permute-done((bf16[256,1024]{1,0:T(8,128)(2,1)}, bf16[256,1024]{1,0:T(8,128)(2,1)S(1)}, u32[]{:S(2)}, u32[]{:S(2)}) %collective-permute-start.8) | collective-permute-done | bytes 524320 | tf_op jit(solution)/shard_map/ppermute | solution.py:545
  86.6 10.9 %video_attention.4.rest_8_ = bf16[256,3072]{1,0:T(8,128)(2,1)} custom-call(s32[13]{0:T(128)S(1)} %concatenate.18.table, bf16[256,3072]{1,0:T(8,128)(2,1)S(1)} %copy-done.6, bf16[256,3072]{1,0:T(8,128)(2,1)} %k_own.7, bf16[256,3072]{1,0:T(8,128)(2,1)} %v_own.7, bf16[528,1024]{1,0:T(8,128)(2,1)} %collective-permute-done.1.a.rest_0_, ...), custom_call_target="tpu_custom_call" | custom-call | flops 75497472 | bytes 262144 | tf_op jit(solution)/shard_map/video_attention/pallas_call | solution.py:275
  97.6 2.1 text_merge.2
  99.7 2.1 collective-permute-start.11
  101.8 5.7 %collective-permute-start.10 = (bf16[528,768]{1,0:T(8,128)(2,1)}, bf16[528,768]{1,0:T(8,128)(2,1)}, u32[]{:S(2)}, u32[]{:S(2)}) collective-permute-start(bf16[528,768]{1,0:T(8,128)(2,1)} %pack_chunk.5), channel_id=1, source_target_pairs={{2,6},{3,7},{4,8},{5,9},{6,10},{7,11},{8,12},{9,13},{10,14},{11,15... | collective-permute-start | bytes 2433032 | tf_op jit(solution)/shard_map/ppermute | solution.py:510
  107.6 1.8 choose_relayed.5
  109.4 1.9 collective-permute-start.12
  111.3 3.6 %collective-permute-start.13 = (bf16[256,768]{1,0:T(8,128)(2,1)S(1)}, bf16[256,768]{1,0:T(8,128)(2,1)S(1)}, u32[]{:S(2)}, u32[]{:S(2)}) collective-permute-start(bf16[256,768]{1,0:T(8,128)(2,1)S(1)} %get-tuple-element.45), channel_id=1, source_target_pairs={{0,3},{3,0},{4,7},{7,4},{8,11},{11,8},{12,15},{15,12},{16,19},{19,... | collective-permute-start | bytes 1179656 | tf_op jit(solution)/shard_map/ppermute | solution.py:545
  115.0 8.0 %collective-permute-done.13.rest_3_ = bf16[256,768]{1,0:T(8,128)(2,1)S(1)} collective-permute-done((bf16[256,768]{1,0:T(8,128)(2,1)S(1)}, bf16[256,768]{1,0:T(8,128)(2,1)S(1)}, u32[]{:S(2)}, u32[]{:S(2)}) %collective-permute-start.13) | collective-permute-done | bytes 393248 | tf_op jit(solution)/shard_map/ppermute | solution.py:545
  123.0 25.2 %collective-permute-done.14.refs_1_ = f32[64,1664]{1,0:T(8,128)S(1)} collective-permute-done((f32[64,1664]{1,0:T(8,128)S(1)}, f32[64,1664]{1,0:T(8,128)S(1)}, u32[]{:S(2)}, u32[]{:S(2)}) %collective-permute-start.14) | collective-permute-done | bytes 426016 | tf_op jit(solution)/shard_map/ppermute | solution.py:526
  148.2 1.1 text_merge.3
  150.1 1.5 pack_chunk.4
  151.7 1.4 copy-done.7
  153.1 1.0 copy-done.13
  154.1 8.7 %video_attention.5.rest_8_ = bf16[256,3072]{1,0:T(8,128)(2,1)} custom-call(s32[13]{0:T(128)S(1)} %concatenate.18.table, bf16[256,3072]{1,0:T(8,128)(2,1)S(1)} %copy-done.7, bf16[256,3072]{1,0:T(8,128)(2,1)S(1)} %copy-done.2, bf16[256,3072]{1,0:T(8,128)(2,1)} %v_own.7, ...), custom_call_target="tpu_custom_call", output_to_operand_aliasing={{}: (12, {})} | custom-call | flops 56623104 | bytes 196608 | tf_op jit(solution)/shard_map/video_attention/pallas_call | solution.py:275
  162.8 2.0 text_finish.1
  165.4 1.9 collective-permute-start.17
  167.3 5.7 %collective-permute-start.16 = (bf16[528,512]{1,0:T(8,128)(2,1)}, bf16[528,512]{1,0:T(8,128)(2,1)}, u32[]{:S(2)}, u32[]{:S(2)}) collective-permute-start(bf16[528,512]{1,0:T(8,128)(2,1)} %pack_chunk.4), channel_id=1, source_target_pairs={{2,6},{3,7},{4,8},{5,9},{6,10},{7,11},{8,12},{9,13},{10,14},{11,15... | collective-permute-start | bytes 1622024 | tf_op jit(solution)/shard_map/ppermute | solution.py:510
  173.0 2.8 %choose_relayed.6 = (bf16[272,768]{1,0:T(8,128)(2,1)}, bf16[256,768]{1,0:T(8,128)(2,1)}) custom-call(s32[1]{0:T(128)} %dynamic_slice.8.second, bf16[528,768]{1,0:T(8,128)(2,1)} %collective-permute-done.10.a.rest_0_, bf16[528,768]{1,0:T(8,128)(2,1)} %collective-permute-done.11.b.rest_1_), custom_call_target="tpu_custom_call" | custom-call | tf_op jit(solution)/shard_map/choose_relayed/pallas_call | solution.py:124
  175.8 1.9 collective-permute-start.18
  177.7 3.6 %collective-permute-start.19 = (bf16[256,768]{1,0:T(8,128)(2,1)}, bf16[256,768]{1,0:T(8,128)(2,1)S(1)}, u32[]{:S(2)}, u32[]{:S(2)}) collective-permute-start(bf16[256,768]{1,0:T(8,128)(2,1)} %get-tuple-element.56), channel_id=1, source_target_pairs={{0,3},{3,0},{4,7},{7,4},{8,11},{11,8},{12,15},{15,12},{16,19},{19,... | collective-permute-start | bytes 1179656 | tf_op jit(solution)/shard_map/ppermute | solution.py:545
  181.5 8.1 %collective-permute-done.19.rest_3_ = bf16[256,768]{1,0:T(8,128)(2,1)S(1)} collective-permute-done((bf16[256,768]{1,0:T(8,128)(2,1)}, bf16[256,768]{1,0:T(8,128)(2,1)S(1)}, u32[]{:S(2)}, u32[]{:S(2)}) %collective-permute-start.19) | collective-permute-done | bytes 393248 | tf_op jit(solution)/shard_map/ppermute | solution.py:545
  189.6 8.7 %video_attention.6.rest_8_ = bf16[256,3072]{1,0:T(8,128)(2,1)} custom-call(s32[13]{0:T(128)S(1)} %concatenate.18.table, bf16[256,3072]{1,0:T(8,128)(2,1)S(1)} %copy-done.8, bf16[256,3072]{1,0:T(8,128)(2,1)S(1)} %copy-done.2, bf16[256,3072]{1,0:T(8,128)(2,1)} %v_own.7, ...), custom_call_target="tpu_custom_call", output_to_operand_aliasing={{}: (12, {})} | custom-call | flops 56623104 | bytes 196608 | tf_op jit(solution)/shard_map/video_attention/pallas_call | solution.py:275
  198.3 1.7 choose_relayed.7
  200.0 1.9 collective-permute-start.20
  201.9 3.6 %collective-permute-start.21 = (bf16[256,512]{1,0:T(8,128)(2,1)S(1)}, bf16[256,512]{1,0:T(8,128)(2,1)S(1)}, u32[]{:S(2)}, u32[]{:S(2)}) collective-permute-start(bf16[256,512]{1,0:T(8,128)(2,1)S(1)} %get-tuple-element.60), channel_id=1, source_target_pairs={{0,3},{3,0},{4,7},{7,4},{8,11},{11,8},{12,15},{15,12},{16,19},{19,... | collective-permute-start | bytes 786440 | tf_op jit(solution)/shard_map/ppermute | solution.py:545
  205.6 1.5 maximum_select_fusion
  207.2 3.5 %collective-permute-done.21.rest_3_ = bf16[256,512]{1,0:T(8,128)(2,1)S(1)} collective-permute-done((bf16[256,512]{1,0:T(8,128)(2,1)S(1)}, bf16[256,512]{1,0:T(8,128)(2,1)S(1)}, u32[]{:S(2)}, u32[]{:S(2)}) %collective-permute-start.21) | collective-permute-done | bytes 262176 | tf_op jit(solution)/shard_map/ppermute | solution.py:545
  210.7 6.3 %video_attention.7 = bf16[256,3072]{1,0:T(8,128)(2,1)} custom-call(s32[13]{0:T(128)S(1)} %concatenate.18.table, bf16[256,3072]{1,0:T(8,128)(2,1)S(1)} %copy-done.8, bf16[256,3072]{1,0:T(8,128)(2,1)S(1)} %copy-done.2, bf16[256,3072]{1,0:T(8,128)(2,1)} %v_own.7, bf16[528,512]{1,0:T(8,128)(2,1)} %collective-permute-done.16.a.rest_0_, ...), custom_call_target="tpu_custom_call", output_to_operand_aliasing={{}: (12, {})} | custom-call | flops 37748736 | bytes 131072 | tf_op jit(solution)/shard_map/video_attention/pallas_call | solution.py:275
  (73 shorter events, 4.4 us)
Async XLA Ops:
  0.6 11.2 %copy-start.20 = (s32[16]{0:T(128)S(1)}, s32[16]{0:T(128)}, u32[]{:S(2)}) copy-start(s32[16]{0:T(128)} %constant.76.clone) | copy-start | bytes 196
  0.6 13.1 %collective-permute-start.3 = (bf16[256,3072]{1,0:T(8,128)(2,1)}, bf16[256,3072]{1,0:T(8,128)(2,1)}, u32[]{:S(2)}, u32[]{:S(2)}) collective-permute-start(bf16[256,3072]{1,0:T(8,128)(2,1)} %k_own.7), channel_id=1, source_target_pairs={{0,1},{1,0},{2,3},{3,2},{4,5},{5,4},{6,7},{7,6},{8,9},{9,8},{10,11... | collective-permute-start | bytes 4718600 | tf_op jit(solution)/shard_map/ppermute | solution.py:514
  0.7 13.0 %collective-permute-start.4 = (bf16[256,3072]{1,0:T(8,128)(2,1)}, bf16[256,3072]{1,0:T(8,128)(2,1)}, u32[]{:S(2)}, u32[]{:S(2)}) collective-permute-start(bf16[256,3072]{1,0:T(8,128)(2,1)} %v_own.7), channel_id=1, source_target_pairs={{0,1},{1,0},{2,3},{3,2},{4,5},{5,4},{6,7},{7,6},{8,9},{9,8},{10,11... | collective-permute-start | bytes 4718600 | tf_op jit(solution)/shard_map/ppermute | solution.py:514
  1.2 1.4 copy-start
  2.6 1.4 copy-start.3
  4.0 9.7 %copy-start.1 = (bf16[256,3072]{1,0:T(8,128)(2,1)S(1)}, bf16[256,3072]{1,0:T(8,128)(2,1)}, u32[]{:S(2)}) copy-start(bf16[256,3072]{1,0:T(8,128)(2,1)} %k_own.7) | copy-start | bytes 4718596
  5.8 51.2 %collective-permute-start.1 = (bf16[528,1024]{1,0:T(8,128)(2,1)}, bf16[528,1024]{1,0:T(8,128)(2,1)}, u32[]{:S(2)}, u32[]{:S(2)}) collective-permute-start(bf16[528,1024]{1,0:T(8,128)(2,1)} %pack_chunk.7), channel_id=1, source_target_pairs={{2,6},{3,7},{4,8},{5,9},{6,10},{7,11},{8,12},{9,13},{10,14},{11,15... | collective-permute-start | bytes 3244040 | tf_op jit(solution)/shard_map/ppermute | solution.py:510
  7.8 49.3 %collective-permute-start.2 = (bf16[528,1024]{1,0:T(8,128)(2,1)}, bf16[528,1024]{1,0:T(8,128)(2,1)}, u32[]{:S(2)}, u32[]{:S(2)}) collective-permute-start(bf16[528,1024]{1,0:T(8,128)(2,1)} %pack_chunk.7), channel_id=1, source_target_pairs={{0,12},{1,13},{4,0},{6,2},{7,3},{8,4},{9,5},{10,6},{11,7},{12,8},{... | collective-permute-start | bytes 3244040 | tf_op jit(solution)/shard_map/ppermute | solution.py:510
  11.7 1.3 collective-permute-start
  13.7 12.7 %copy-start.4 = (bf16[256,3072]{1,0:T(8,128)(2,1)S(1)}, bf16[256,3072]{1,0:T(8,128)(2,1)}, u32[]{:S(2)}) copy-start(bf16[256,3072]{1,0:T(8,128)(2,1)} %v_own.7) | copy-start | bytes 4718596
  13.8 1.5 copy-start.9
  24.0 4.1 %copy-start.10 = (f32[128,1792]{1,0:T(8,128)}, f32[128,1792]{1,0:T(8,128)S(1)}, u32[]{:S(2)}) copy-start(f32[128,1792]{1,0:T(8,128)S(1)} %get-tuple-element.38.refs_0_) | copy-start | bytes 2752516
  24.0 73.6 %collective-permute-start.9 = (f32[128,1792]{1,0:T(8,128)}, f32[128,1792]{1,0:T(8,128)}, u32[]{:S(2)}, u32[]{:S(2)}) collective-permute-start(f32[128,1792]{1,0:T(8,128)} %get-tuple-element.39), channel_id=1, source_target_pairs={{0,2},{1,3},{2,0},{3,1},{4,6},{5,7},{6,4},{7,5},{8,10},{9,11},{10,... | collective-permute-start | bytes 2752520 | tf_op jit(solution)/shard_map/ppermute | solution.py:526
  57.1 9.5 %copy-start.18 = (s32[2,6]{1,0:T(2,128)S(1)}, s32[2,6]{1,0:T(2,128)}, u32[]{:S(2)}) copy-start(s32[2,6]{1,0:T(2,128)} %param.18) | copy-start | bytes 148
  57.1 9.7 %copy-start.19 = (s32[16]{0:T(128)S(1)}, s32[16]{0:T(128)}, u32[]{:S(2)}) copy-start(s32[16]{0:T(128)} %constant.74.clone) | copy-start | bytes 196
  57.1 42.6 %collective-permute-start.6 = (bf16[528,768]{1,0:T(8,128)(2,1)}, bf16[528,768]{1,0:T(8,128)(2,1)}, u32[]{:S(2)}, u32[]{:S(2)}) collective-permute-start(bf16[528,768]{1,0:T(8,128)(2,1)} %pack_chunk.6), channel_id=1, source_target_pairs={{0,12},{1,13},{4,0},{6,2},{7,3},{8,4},{9,5},{10,6},{11,7},{12,8},{... | collective-permute-start | bytes 2433032 | tf_op jit(solution)/shard_map/ppermute | solution.py:510
  59.6 40.1 %collective-permute-start.5 = (bf16[528,768]{1,0:T(8,128)(2,1)}, bf16[528,768]{1,0:T(8,128)(2,1)}, u32[]{:S(2)}, u32[]{:S(2)}) collective-permute-start(bf16[528,768]{1,0:T(8,128)(2,1)} %pack_chunk.6), channel_id=1, source_target_pairs={{2,6},{3,7},{4,8},{5,9},{6,10},{7,11},{8,12},{9,13},{10,14},{11,15... | collective-permute-start | bytes 2433032 | tf_op jit(solution)/shard_map/ppermute | solution.py:510
  66.5 20.1 %copy-start.6 = (bf16[256,3072]{1,0:T(8,128)(2,1)S(1)}, bf16[256,3072]{1,0:T(8,128)(2,1)}, u32[]{:S(2)}) copy-start(bf16[256,3072]{1,0:T(8,128)(2,1)} %q.9) | copy-start | bytes 4718596
  70.2 16.5 %collective-permute-start.7 = (bf16[272,1024]{1,0:T(8,128)(2,1)S(1)}, bf16[272,1024]{1,0:T(8,128)(2,1)S(1)}, u32[]{:S(2)}, u32[]{:S(2)}) collective-permute-start(bf16[272,1024]{1,0:T(8,128)(2,1)S(1)} %get-tuple-element.36), channel_id=1, source_target_pairs={{0,3},{3,0},{4,7},{7,4},{8,11},{11,8},{12,15},{15,12},{16,19},{19,... | collective-permute-start | bytes 1671176 | tf_op jit(solution)/shard_map/ppermute | solution.py:545
  72.1 14.5 %collective-permute-start.8 = (bf16[256,1024]{1,0:T(8,128)(2,1)}, bf16[256,1024]{1,0:T(8,128)(2,1)S(1)}, u32[]{:S(2)}, u32[]{:S(2)}) collective-permute-start(bf16[256,1024]{1,0:T(8,128)(2,1)} %get-tuple-element.37), channel_id=1, source_target_pairs={{0,3},{3,0},{4,7},{7,4},{8,11},{11,8},{12,15},{15,12},{16,19},{19,... | collective-permute-start | bytes 1572872 | tf_op jit(solution)/shard_map/ppermute | solution.py:545
  78.3 19.3 %copy-start.11 = (f32[128,1792]{1,0:T(8,128)S(1)}, f32[128,1792]{1,0:T(8,128)}, u32[]{:S(2)}) copy-start(f32[128,1792]{1,0:T(8,128)} %copy-done.10) | copy-start | bytes 2752516
  97.6 52.5 %copy-start.5 = (bf16[256,3072]{1,0:T(8,128)(2,1)S(1)}, bf16[256,3072]{1,0:T(8,128)(2,1)}, u32[]{:S(2)}) copy-start(bf16[256,3072]{1,0:T(8,128)(2,1)} %v_own.7) | copy-start | bytes 4718596
  99.7 50.4 %copy-start.2 = (bf16[256,3072]{1,0:T(8,128)(2,1)S(1)}, bf16[256,3072]{1,0:T(8,128)(2,1)}, u32[]{:S(2)}) copy-start(bf16[256,3072]{1,0:T(8,128)(2,1)} %k_own.7) | copy-start | bytes 4718596
  99.7 65.7 %collective-permute-start.11 = (bf16[528,768]{1,0:T(8,128)(2,1)}, bf16[528,768]{1,0:T(8,128)(2,1)}, u32[]{:S(2)}, u32[]{:S(2)}) collective-permute-start(bf16[528,768]{1,0:T(8,128)(2,1)} %pack_chunk.5), channel_id=1, source_target_pairs={{0,12},{1,13},{4,0},{6,2},{7,3},{8,4},{9,5},{10,6},{11,7},{12,8},{... | collective-permute-start | bytes 2433032 | tf_op jit(solution)/shard_map/ppermute | solution.py:510
  101.8 63.6 %collective-permute-start.10 = (bf16[528,768]{1,0:T(8,128)(2,1)}, bf16[528,768]{1,0:T(8,128)(2,1)}, u32[]{:S(2)}, u32[]{:S(2)}) collective-permute-start(bf16[528,768]{1,0:T(8,128)(2,1)} %pack_chunk.5), channel_id=1, source_target_pairs={{2,6},{3,7},{4,8},{5,9},{6,10},{7,11},{8,12},{9,13},{10,14},{11,15... | collective-permute-start | bytes 2433032 | tf_op jit(solution)/shard_map/ppermute | solution.py:510
  107.5 40.7 %collective-permute-start.14 = (f32[64,1664]{1,0:T(8,128)S(1)}, f32[64,1664]{1,0:T(8,128)S(1)}, u32[]{:S(2)}, u32[]{:S(2)}) collective-permute-start(f32[64,1664]{1,0:T(8,128)S(1)} %get-tuple-element.47), channel_id=1, source_target_pairs={{0,4},{1,5},{2,6},{3,7},{4,0},{5,1},{6,2},{7,3},{8,12},{9,13},{10,... | collective-permute-start | bytes 1277960 | tf_op jit(solution)/shard_map/ppermute | solution.py:526
  109.4 13.6 %collective-permute-start.12 = (bf16[272,768]{1,0:T(8,128)(2,1)S(1)}, bf16[272,768]{1,0:T(8,128)(2,1)S(1)}, u32[]{:S(2)}, u32[]{:S(2)}) collective-permute-start(bf16[272,768]{1,0:T(8,128)(2,1)S(1)} %get-tuple-element.44), channel_id=1, source_target_pairs={{0,3},{3,0},{4,7},{7,4},{8,11},{11,8},{12,15},{15,12},{16,19},{19,... | collective-permute-start | bytes 1253384 | tf_op jit(solution)/shard_map/ppermute | solution.py:545
  111.3 11.6 %collective-permute-start.13 = (bf16[256,768]{1,0:T(8,128)(2,1)S(1)}, bf16[256,768]{1,0:T(8,128)(2,1)S(1)}, u32[]{:S(2)}, u32[]{:S(2)}) collective-permute-start(bf16[256,768]{1,0:T(8,128)(2,1)S(1)} %get-tuple-element.45), channel_id=1, source_target_pairs={{0,3},{3,0},{4,7},{7,4},{8,11},{11,8},{12,15},{15,12},{16,19},{19,... | collective-permute-start | bytes 1179656 | tf_op jit(solution)/shard_map/ppermute | solution.py:545
  123.0 26.4 %copy-start.12 = (bf16[272,768]{1,0:T(8,128)(2,1)}, bf16[272,768]{1,0:T(8,128)(2,1)S(1)}, u32[]{:S(2)}) copy-start(bf16[272,768]{1,0:T(8,128)(2,1)S(1)} %collective-permute-done.12.rest_2_) | copy-start | bytes 1253380
  149.4 0.7 copy-start.14
  150.1 12.7 %collective-permute-start.15 = (f32[32,1664]{1,0:T(8,128)}, f32[32,1664]{1,0:T(8,128)}, u32[]{:S(2)}, u32[]{:S(2)}) collective-permute-start(f32[32,1664]{1,0:T(8,128)} %get-tuple-element.50), channel_id=1, source_target_pairs={{0,8},{1,9},{2,10},{3,11},{4,12},{5,13},{6,14},{7,15},{8,0},{9,1},... | collective-permute-start | bytes 638984 | tf_op jit(solution)/shard_map/ppermute | solution.py:526
  151.7 1.4 copy-start.7
  153.1 1.0 copy-start.13
  154.1 8.7 %copy-start.15 = (f32[32,1664]{1,0:T(8,128)S(1)}, f32[32,1664]{1,0:T(8,128)}, u32[]{:S(2)}) copy-start(f32[32,1664]{1,0:T(8,128)} %copy-done.14) | copy-start | bytes 638980
  162.8 26.8 %copy-start.8 = (bf16[256,3072]{1,0:T(8,128)(2,1)S(1)}, bf16[256,3072]{1,0:T(8,128)(2,1)}, u32[]{:S(2)}) copy-start(bf16[256,3072]{1,0:T(8,128)(2,1)} %q.9) | copy-start | bytes 4718596
  164.7 0.6 copy-start.16
  165.4 32.9 %collective-permute-start.17 = (bf16[528,512]{1,0:T(8,128)(2,1)}, bf16[528,512]{1,0:T(8,128)(2,1)}, u32[]{:S(2)}, u32[]{:S(2)}) collective-permute-start(bf16[528,512]{1,0:T(8,128)(2,1)} %pack_chunk.4), channel_id=1, source_target_pairs={{0,12},{1,13},{4,0},{6,2},{7,3},{8,4},{9,5},{10,6},{11,7},{12,8},{... | collective-permute-start | bytes 1622024 | tf_op jit(solution)/shard_map/ppermute | solution.py:510
  167.3 31.0 %collective-permute-start.16 = (bf16[528,512]{1,0:T(8,128)(2,1)}, bf16[528,512]{1,0:T(8,128)(2,1)}, u32[]{:S(2)}, u32[]{:S(2)}) collective-permute-start(bf16[528,512]{1,0:T(8,128)(2,1)} %pack_chunk.4), channel_id=1, source_target_pairs={{2,6},{3,7},{4,8},{5,9},{6,10},{7,11},{8,12},{9,13},{10,14},{11,15... | collective-permute-start | bytes 1622024 | tf_op jit(solution)/shard_map/ppermute | solution.py:510
  175.8 13.8 %collective-permute-start.18 = (bf16[272,768]{1,0:T(8,128)(2,1)}, bf16[272,768]{1,0:T(8,128)(2,1)}, u32[]{:S(2)}, u32[]{:S(2)}) collective-permute-start(bf16[272,768]{1,0:T(8,128)(2,1)} %get-tuple-element.55), channel_id=1, source_target_pairs={{0,3},{3,0},{4,7},{7,4},{8,11},{11,8},{12,15},{15,12},{16,19},{19,... | collective-permute-start | bytes 1253384 | tf_op jit(solution)/shard_map/ppermute | solution.py:545
  177.7 11.9 %collective-permute-start.19 = (bf16[256,768]{1,0:T(8,128)(2,1)}, bf16[256,768]{1,0:T(8,128)(2,1)S(1)}, u32[]{:S(2)}, u32[]{:S(2)}) collective-permute-start(bf16[256,768]{1,0:T(8,128)(2,1)} %get-tuple-element.56), channel_id=1, source_target_pairs={{0,3},{3,0},{4,7},{7,4},{8,11},{11,8},{12,15},{15,12},{16,19},{19,... | collective-permute-start | bytes 1179656 | tf_op jit(solution)/shard_map/ppermute | solution.py:545
  181.4 24.2 %collective-permute-start.22 = (bf16[16,1536]{1,0:T(8,128)(2,1)}, bf16[16,1536]{1,0:T(8,128)(2,1)}, u32[]{:S(2)}, u32[]{:S(2)}) collective-permute-start(bf16[16,1536]{1,0:T(8,128)(2,1)} %get-tuple-element.61), channel_id=1, source_target_pairs={{0,1},{1,0},{2,3},{3,2},{4,5},{5,4},{6,7},{7,6},{8,9},{9,8},{10,11... | collective-permute-start | bytes 147464 | tf_op jit(solution)/shard_map/ppermute | solution.py:560
  181.4 24.2 %copy-start.17 = (bf16[16,1536]{1,0:T(8,128)(2,1)S(1)}, bf16[16,1536]{1,0:T(8,128)(2,1)}, u32[]{:S(2)}) copy-start(bf16[16,1536]{1,0:T(8,128)(2,1)} %copy-done.16) | copy-start | bytes 147460
  200.0 10.7 %collective-permute-start.20 = (bf16[272,512]{1,0:T(8,128)(2,1)S(1)}, bf16[272,512]{1,0:T(8,128)(2,1)S(1)}, u32[]{:S(2)}, u32[]{:S(2)}) collective-permute-start(bf16[272,512]{1,0:T(8,128)(2,1)S(1)} %get-tuple-element.59), channel_id=1, source_target_pairs={{0,3},{3,0},{4,7},{7,4},{8,11},{11,8},{12,15},{15,12},{16,19},{19,... | collective-permute-start | bytes 835592 | tf_op jit(solution)/shard_map/ppermute | solution.py:545
  201.9 8.7 %collective-permute-start.21 = (bf16[256,512]{1,0:T(8,128)(2,1)S(1)}, bf16[256,512]{1,0:T(8,128)(2,1)S(1)}, u32[]{:S(2)}, u32[]{:S(2)}) collective-permute-start(bf16[256,512]{1,0:T(8,128)(2,1)S(1)} %get-tuple-element.60), channel_id=1, source_target_pairs={{0,3},{3,0},{4,7},{7,4},{8,11},{11,8},{12,15},{15,12},{16,19},{19,... | collective-permute-start | bytes 786440 | tf_op jit(solution)/shard_map/ppermute | solution.py:545

commit v8 on v7

--- a/solution.py
+++ b/solution.py
@@ -13,7 +13,7 @@
 NR = 4
 BLOCKS = 5
 STEP_HEADS = 2
-CHUNK_HEADS = (8, 6, 6, 4)
+CHUNK_HEADS = (12, 8, 4)
 PAD_ROWS = 16
 VMEM_BYTES = 48 * 1024 * 1024
 LOG2E = 1.4426950408889634
@@ -535,12 +535,16 @@
             limits = jnp.concatenate(limits)
             parts.append(text_finish(tie(parts[i][0], *before), exchanged(i), limits))
 
+    for _ in range(stages - 1):
+        merge()
     count = len(CHUNK_HEADS)
     for i in range(count):
-        before = outs[-1:] + ([parts[-1][0]] if halving else [])
+        before = outs[i - 1 : i] + ([parts[-1][0]] if halving and i == 0 else [])
         if i + 1 < count:
             send(i + 1, *direct[i], *before)
-        up, down = tie(direct[i][0], *before), tie(direct[i][1], *before)
+        up, down = direct[i]
+        if i + 1 < count:
+            up, down = tie(up, *before), tie(down, *before)
         relays = [
             lax.ppermute(half, "tiles", pairs["relayed"])
             for half in choose(sends_later, up, down, rows + PAD_ROWS)
@@ -551,10 +555,6 @@
                 [*direct[i], *relays, *beside[1:]], text_k, text_v, outs[-1] if outs else None,
             )
         )
-        if i < 2:
-            merge(*relays)
-        if i == 1:
-            merge(outs[0])
     if halving:
         mine, leave = parts[-1]
         got = lax.ppermute(leave, "tiles", [(d, d ^ 1) for d in range(n)])

time: 220 us -> 213 us (0.968)
  waiting for transfers between devices: 83.4 us -> 108 us
  starting transfers between devices: 54.5 us -> 38.7 us
  Pallas kernels: 64.1 us -> 54.6 us
  local copies, waits for them, and re-layouts: 10.5 us -> 7.53 us
    ppermute x3, waiting for transfers between devices: 25.2 us -> 78.2 us  [exchanged(): lax.ppermute(parts[i][1], 'tiles', [(d, d ^ 2 << i) for d in range(n)])]
    ppermute x8 -> x6, waiting for transfers between devices: 28 us -> 14.2 us  [per_device(): lax.ppermute(half, 'tiles', pairs['relayed'])]
    ppermute x8 -> x6, waiting for transfers between devices: 29 us -> 15.6 us  [send(): lax.ppermute(mine, 'tiles', pairs[x])]
    ppermute x8 -> x6, starting transfers between devices: 29 us -> 21.1 us  [send(): lax.ppermute(mine, 'tiles', pairs[x])]
    ppermute x8 -> x6, starting transfers between devices: 22.3 us -> 16.7 us  [per_device(): lax.ppermute(half, 'tiles', pairs['relayed'])]
    pallas_call x4 -> x3, Pallas kernels: 6.56 us -> 3.78 us  [pack(): pl.pallas_call(functools.partial(pack_kernel, start), in_specs=[pl.BlockS...]
    ppermute x3, starting transfers between devices: 2.54 us -> 0.14 us  [exchanged(): lax.ppermute(parts[i][1], 'tiles', [(d, d ^ 2 << i) for d in range(n)])]
    unnamed x42 -> x28, local copies, waits for them, and re-layouts: 8.12 us -> 5.89 us
  transfers between devices with their start and end apart: 23 -> 19, of which waited for: 7 -> 6; matrix products, arithmetic and copies ran while one was open for 2% -> 1% of each run, Pallas kernels for 27% -> 23%
where the time goes in v8:
time: 213 us; the launch traced here: 212 us
  waiting for transfers between devices  108 us (51%)
  Pallas kernels  54.6 us (26%)
  starting transfers between devices  38.7 us (18%)
  local copies, waits for them, and re-layouts  7.53 us (4%)
    ppermute x3, waiting for transfers between devices, exchanged(): lax.ppermute(parts[i][1], 'tiles', [(d, d ^ 2 << i) for d in range(n)])  78.2 us
    pallas_call x3, Pallas kernels, video_call(): pl.pallas_call(video_kernel, grid=(heads // STEP_HEADS,), in_specs=in_spe...  32.8 us
    ppermute x6, starting transfers between devices, send(): lax.ppermute(mine, 'tiles', pairs[x])  21.1 us
    ppermute x6, starting transfers between devices, per_device(): lax.ppermute(half, 'tiles', pairs['relayed'])  16.7 us
    ppermute x6, waiting for transfers between devices, send(): lax.ppermute(mine, 'tiles', pairs[x])  15.6 us
    ppermute x6, waiting for transfers between devices, per_device(): lax.ppermute(half, 'tiles', pairs['relayed'])  14.2 us
    pallas_call x1, Pallas kernels, text_local(): pl.pallas_call(text_kernel, grid_spec=pltpu.PrefetchScalarGridSpec(num_sc...  8.08 us
    pallas_call x3, Pallas kernels, choose(): pl.pallas_call(choose_kernel, in_specs=[pl.BlockSpec(memory_space=pltpu.S...  6.84 us
  transfers between devices with their start and end apart: 19, of which 6 were waited for; matrix products, arithmetic and copies ran while one was open for 1% of the time, Pallas kernels for 23%

profile of v8, /device:TPU:24, one launch (start us, length us, event | category | flops | bytes accessed | tf_op | source)
XLA Modules:
  0.0 211.8 jit_solution(691424489435856723)
XLA Ops:
  0.7 0.5 collective-permute-start.4
  1.2 0.1 collective-permute-start
  1.3 1.4 copy-done
  2.7 1.4 copy-done.3
  4.1 0.7 copy-done.9
  4.8 1.7 pack_chunk.5
  6.5 2.4 %collective-permute-start.2 = (bf16[528,1536]{1,0:T(8,128)(2,1)}, bf16[528,1536]{1,0:T(8,128)(2,1)}, u32[]{:S(2)}, u32[]{:S(2)}) collective-permute-start(bf16[528,1536]{1,0:T(8,128)(2,1)} %pack_chunk.5), channel_id=1, source_target_pairs={{0,12},{1,13},{4,0},{6,2},{7,3},{8,4},{9,5},{10,6},{11,7},{12,8},{... | collective-permute-start | bytes 4866056 | tf_op jit(solution)/shard_map/ppermute | solution.py:510
  8.9 5.3 %collective-permute-start.1 = (bf16[528,1536]{1,0:T(8,128)(2,1)}, bf16[528,1536]{1,0:T(8,128)(2,1)}, u32[]{:S(2)}, u32[]{:S(2)}) collective-permute-start(bf16[528,1536]{1,0:T(8,128)(2,1)} %pack_chunk.5), channel_id=1, source_target_pairs={{2,6},{3,7},{4,8},{5,9},{6,10},{7,11},{8,12},{9,13},{10,14},{11,15... | collective-permute-start | bytes 4866056 | tf_op jit(solution)/shard_map/ppermute | solution.py:510
  14.2 0.1 pad_add_fusion.1.order
  14.4 8.1 %text_partials.1 = (f32[128,1792]{1,0:T(8,128)S(1)}, f32[128,1792]{1,0:T(8,128)S(1)}) custom-call(s32[17]{0:T(128)S(1)} %pad_add_fusion.1.order, s32[4]{0:T(128)S(1)} %pad_add_fusion.2.counts, bf16[256,3072]{1,0:T(8,128)(2,1)S(1)} %copy-done.7, bf16[256,3072]{1,0:T(8,128)(2,1)S(1)} %copy-done.1, bf16[256,3072]{1,0:T(8,128)(2,1)} %v_own.5, ...), custom_call_target="tpu_custom_call" | custom-call | flops 8388608 | bytes 786432 | tf_op jit(solution)/shard_map/text_partials/pallas_call | solution.py:367
  22.6 23.1 %collective-permute-done.5.refs_1_ = f32[128,1792]{1,0:T(8,128)S(1)} collective-permute-done((f32[128,1792]{1,0:T(8,128)S(1)}, f32[128,1792]{1,0:T(8,128)S(1)}, u32[]{:S(2)}, u32[]{:S(2)}) %collective-permute-start.5) | collective-permute-done | bytes 917536 | tf_op jit(solution)/shard_map/ppermute | solution.py:526
  45.7 0.8 text_merge.2
  46.5 45.6 %collective-permute-done.6.refs_1_ = f32[64,1664]{1,0:T(8,128)S(1)} collective-permute-done((f32[64,1664]{1,0:T(8,128)S(1)}, f32[64,1664]{1,0:T(8,128)S(1)}, u32[]{:S(2)}, u32[]{:S(2)}) %collective-permute-start.6) | collective-permute-done | bytes 426016 | tf_op jit(solution)/shard_map/ppermute | solution.py:526
  92.1 1.1 text_merge.3
  93.2 0.7 pack_chunk.4
  94.0 1.0 copy-done.8
  95.7 9.5 %collective-permute-done.7.refs_1_ = f32[32,1664]{1,0:T(8,128)} collective-permute-done((f32[32,1664]{1,0:T(8,128)}, f32[32,1664]{1,0:T(8,128)}, u32[]{:S(2)}, u32[]{:S(2)}) %collective-permute-start.7) | collective-permute-done | bytes 213024 | tf_op jit(solution)/shard_map/ppermute | solution.py:526
  105.1 1.2 text_finish.1
  106.4 1.9 collective-permute-start.9
  108.3 5.7 %collective-permute-start.8 = (bf16[528,1024]{1,0:T(8,128)(2,1)}, bf16[528,1024]{1,0:T(8,128)(2,1)}, u32[]{:S(2)}, u32[]{:S(2)}) collective-permute-start(bf16[528,1024]{1,0:T(8,128)(2,1)} %copy-done.8), channel_id=1, source_target_pairs={{2,6},{3,7},{4,8},{5,9},{6,10},{7,11},{8,12},{9,13},{10,14},{11,15... | collective-permute-start | bytes 3244040 | tf_op jit(solution)/shard_map/ppermute | solution.py:510
  114.1 0.6 dynamic_slice.8.second
  114.7 3.2 %choose_relayed.3 = (bf16[272,1536]{1,0:T(8,128)(2,1)}, bf16[256,1536]{1,0:T(8,128)(2,1)}) custom-call(s32[1]{0:T(128)} %dynamic_slice.8.second, bf16[528,1536]{1,0:T(8,128)(2,1)} %collective-permute-done.1.a.rest_0_, bf16[528,1536]{1,0:T(8,128)(2,1)} %collective-permute-done.2.b.rest_1_), custom_call_target="tpu_custom_call" | custom-call | tf_op jit(solution)/shard_map/choose_relayed/pallas_call | solution.py:124
  117.9 1.9 collective-permute-start.10
  119.9 3.6 %collective-permute-start.11 = (bf16[256,1536]{1,0:T(8,128)(2,1)}, bf16[256,1536]{1,0:T(8,128)(2,1)}, u32[]{:S(2)}, u32[]{:S(2)}) collective-permute-start(bf16[256,1536]{1,0:T(8,128)(2,1)} %get-tuple-element.33), channel_id=1, source_target_pairs={{0,3},{3,0},{4,7},{7,4},{8,11},{11,8},{12,15},{15,12},{16,19},{19,... | collective-permute-start | bytes 2359304 | tf_op jit(solution)/shard_map/ppermute | solution.py:549
  123.5 1.4 pack_chunk.3
  124.9 0.2 reduce_window_sum.11
  125.1 0.1 fusion
  125.3 0.1 copy.16
  125.3 0.1 stack.14
  125.4 0.1 add.47
  125.5 0.7 dynamic-slice_bitcast_fusion
  126.2 0.1 concatenate.18.table
  126.3 14.2 %collective-permute-done.11.rest_3_ = bf16[256,1536]{1,0:T(8,128)(2,1)} collective-permute-done((bf16[256,1536]{1,0:T(8,128)(2,1)}, bf16[256,1536]{1,0:T(8,128)(2,1)}, u32[]{:S(2)}, u32[]{:S(2)}) %collective-permute-start.11) | collective-permute-done | bytes 786464 | tf_op jit(solution)/shard_map/ppermute | solution.py:549
  140.5 1.4 copy-done.5
  141.9 15.4 %video_attention.3.rest_8_ = bf16[256,3072]{1,0:T(8,128)(2,1)} custom-call(s32[13]{0:T(128)S(1)} %concatenate.18.table, bf16[256,3072]{1,0:T(8,128)(2,1)S(1)} %copy-done.5, bf16[256,3072]{1,0:T(8,128)(2,1)S(1)} %copy-done.1, bf16[256,3072]{1,0:T(8,128)(2,1)} %v_own.5, bf16[528,1536]{1,0:T(8,128)(2,1)} %collective-permute-done.1.a.rest_0_, ...), custom_call_target="tpu_custom_call" | custom-call | flops 113246208 | bytes 393216 | tf_op jit(solution)/shard_map/video_attention/pallas_call | solution.py:275
  157.4 2.1 %collective-permute-done.8.a.rest_0_ = bf16[528,1024]{1,0:T(8,128)(2,1)} collective-permute-done((bf16[528,1024]{1,0:T(8,128)(2,1)}, bf16[528,1024]{1,0:T(8,128)(2,1)}, u32[]{:S(2)}, u32[]{:S(2)}) %collective-permute-start.8) | collective-permute-done | bytes 1081376 | tf_op jit(solution)/shard_map/ppermute | solution.py:510
  159.5 2.1 collective-permute-start.12
  161.6 3.7 %collective-permute-start.13 = (bf16[528,512]{1,0:T(8,128)(2,1)}, bf16[528,512]{1,0:T(8,128)(2,1)S(1)}, u32[]{:S(2)}, u32[]{:S(2)}) collective-permute-start(bf16[528,512]{1,0:T(8,128)(2,1)} %pack_chunk.3), channel_id=1, source_target_pairs={{0,12},{1,13},{4,0},{6,2},{7,3},{8,4},{9,5},{10,6},{11,7},{12,8},{... | collective-permute-start | bytes 1622024 | tf_op jit(solution)/shard_map/ppermute | solution.py:510
  165.3 2.9 %choose_relayed.5 = (bf16[272,1024]{1,0:T(8,128)(2,1)}, bf16[256,1024]{1,0:T(8,128)(2,1)}) custom-call(s32[1]{0:T(128)} %dynamic_slice.8.second, bf16[528,1024]{1,0:T(8,128)(2,1)} %collective-permute-done.8.a.rest_0_, bf16[528,1024]{1,0:T(8,128)(2,1)} %collective-permute-done.9.b.rest_1_), custom_call_target="tpu_custom_call" | custom-call | tf_op jit(solution)/shard_map/choose_relayed/pallas_call | solution.py:124
  168.2 1.9 collective-permute-start.16
  170.1 3.6 %collective-permute-start.17 = (bf16[256,1024]{1,0:T(8,128)(2,1)}, bf16[256,1024]{1,0:T(8,128)(2,1)}, u32[]{:S(2)}, u32[]{:S(2)}) collective-permute-start(bf16[256,1024]{1,0:T(8,128)(2,1)} %get-tuple-element.40), channel_id=1, source_target_pairs={{0,3},{3,0},{4,7},{7,4},{8,11},{11,8},{12,15},{15,12},{16,19},{19,... | collective-permute-start | bytes 1572872 | tf_op jit(solution)/shard_map/ppermute | solution.py:549
  173.9 13.5 %collective-permute-done.12.a.rest_0_ = bf16[528,512]{1,0:T(8,128)(2,1)S(1)} collective-permute-done((bf16[528,512]{1,0:T(8,128)(2,1)}, bf16[528,512]{1,0:T(8,128)(2,1)S(1)}, u32[]{:S(2)}, u32[]{:S(2)}) %collective-permute-start.12) | collective-permute-done | bytes 540704 | tf_op jit(solution)/shard_map/ppermute | solution.py:510
  187.4 0.7 choose_relayed.4
  188.1 1.9 collective-permute-start.14
  190.0 3.6 %collective-permute-start.15 = (bf16[256,512]{1,0:T(8,128)(2,1)S(1)}, bf16[256,512]{1,0:T(8,128)(2,1)S(1)}, u32[]{:S(2)}, u32[]{:S(2)}) collective-permute-start(bf16[256,512]{1,0:T(8,128)(2,1)S(1)} %get-tuple-element.36), channel_id=1, source_target_pairs={{0,3},{3,0},{4,7},{7,4},{8,11},{11,8},{12,15},{15,12},{16,19},{19,... | collective-permute-start | bytes 786440 | tf_op jit(solution)/shard_map/ppermute | solution.py:549
  193.7 0.7 maximum_select_fusion
  194.4 11.1 %video_attention.4.rest_8_ = bf16[256,3072]{1,0:T(8,128)(2,1)} custom-call(s32[13]{0:T(128)S(1)} %concatenate.18.table, bf16[256,3072]{1,0:T(8,128)(2,1)S(1)} %copy-done.6, bf16[256,3072]{1,0:T(8,128)(2,1)} %k_own.5, bf16[256,3072]{1,0:T(8,128)(2,1)} %v_own.5, bf16[528,1024]{1,0:T(8,128)(2,1)} %collective-permute-done.8.a.rest_0_, ...), custom_call_target="tpu_custom_call", output_to_operand_aliasing={{}: (12, {})} | custom-call | flops 75497472 | bytes 262144 | tf_op jit(solution)/shard_map/video_attention/pallas_call | solution.py:275
  205.5 6.3 %video_attention.5 = bf16[256,3072]{1,0:T(8,128)(2,1)} custom-call(s32[13]{0:T(128)S(1)} %concatenate.18.table, bf16[256,3072]{1,0:T(8,128)(2,1)S(1)} %copy-done.6, bf16[256,3072]{1,0:T(8,128)(2,1)S(1)} %copy-done.2, bf16[256,3072]{1,0:T(8,128)(2,1)} %v_own.5, ...), custom_call_target="tpu_custom_call", output_to_operand_aliasing={{}: (12, {})} | custom-call | flops 37748736 | bytes 131072 | tf_op jit(solution)/shard_map/video_attention/pallas_call | solution.py:275
  (48 shorter events, 0.6 us)
Async XLA Ops:
  0.6 13.5 %copy-start.13 = (s32[16]{0:T(128)S(1)}, s32[16]{0:T(128)}, u32[]{:S(2)}) copy-start(s32[16]{0:T(128)} %constant.76.clone) | copy-start | bytes 196
  0.6 13.7 %collective-permute-start.3 = (bf16[256,3072]{1,0:T(8,128)(2,1)}, bf16[256,3072]{1,0:T(8,128)(2,1)}, u32[]{:S(2)}, u32[]{:S(2)}) collective-permute-start(bf16[256,3072]{1,0:T(8,128)(2,1)} %k_own.5), channel_id=1, source_target_pairs={{0,1},{1,0},{2,3},{3,2},{4,5},{5,4},{6,7},{7,6},{8,9},{9,8},{10,11... | collective-permute-start | bytes 4718600 | tf_op jit(solution)/shard_map/ppermute | solution.py:514
  0.7 13.6 %collective-permute-start.4 = (bf16[256,3072]{1,0:T(8,128)(2,1)}, bf16[256,3072]{1,0:T(8,128)(2,1)}, u32[]{:S(2)}, u32[]{:S(2)}) collective-permute-start(bf16[256,3072]{1,0:T(8,128)(2,1)} %v_own.5), channel_id=1, source_target_pairs={{0,1},{1,0},{2,3},{3,2},{4,5},{5,4},{6,7},{7,6},{8,9},{9,8},{10,11... | collective-permute-start | bytes 4718600 | tf_op jit(solution)/shard_map/ppermute | solution.py:514
  1.2 13.1 %collective-permute-start = (s32[2]{0:T(128)}, s32[2]{0:T(128)S(1)}, u32[]{:S(2)}, u32[]{:S(2)}) collective-permute-start(s32[2]{0:T(128)} %counts.5), channel_id=1, source_target_pairs={{0,1},{1,0},{2,3},{3,2},{4,5},{5,4},{6,7},{7,6},{8,9},{9,8},{10,11... | collective-permute-start | bytes 32 | tf_op jit(solution)/shard_map/ppermute | solution.py:514
  1.3 1.4 copy-start
  2.7 1.4 copy-start.3
  4.1 0.7 copy-start.9
  4.8 9.5 %copy-start.10 = (s32[2]{0:T(128)S(1)}, s32[2]{0:T(128)}, u32[]{:S(2)}) copy-start(s32[2]{0:T(128)} %counts.5) | copy-start | bytes 28
  4.8 9.6 %copy-start.1 = (bf16[256,3072]{1,0:T(8,128)(2,1)S(1)}, bf16[256,3072]{1,0:T(8,128)(2,1)}, u32[]{:S(2)}) copy-start(bf16[256,3072]{1,0:T(8,128)(2,1)} %k_own.5) | copy-start | bytes 4718596
  4.8 9.6 %copy-start.7 = (bf16[256,3072]{1,0:T(8,128)(2,1)S(1)}, bf16[256,3072]{1,0:T(8,128)(2,1)}, u32[]{:S(2)}) copy-start(bf16[256,3072]{1,0:T(8,128)(2,1)} %q.4) | copy-start | bytes 4718596
  6.5 99.9 %collective-permute-start.2 = (bf16[528,1536]{1,0:T(8,128)(2,1)}, bf16[528,1536]{1,0:T(8,128)(2,1)}, u32[]{:S(2)}, u32[]{:S(2)}) collective-permute-start(bf16[528,1536]{1,0:T(8,128)(2,1)} %pack_chunk.5), channel_id=1, source_target_pairs={{0,12},{1,13},{4,0},{6,2},{7,3},{8,4},{9,5},{10,6},{11,7},{12,8},{... | collective-permute-start | bytes 4866056 | tf_op jit(solution)/shard_map/ppermute | solution.py:510
  8.9 97.5 %collective-permute-start.1 = (bf16[528,1536]{1,0:T(8,128)(2,1)}, bf16[528,1536]{1,0:T(8,128)(2,1)}, u32[]{:S(2)}, u32[]{:S(2)}) collective-permute-start(bf16[528,1536]{1,0:T(8,128)(2,1)} %pack_chunk.5), channel_id=1, source_target_pairs={{2,6},{3,7},{4,8},{5,9},{6,10},{7,11},{8,12},{9,13},{10,14},{11,15... | collective-permute-start | bytes 4866056 | tf_op jit(solution)/shard_map/ppermute | solution.py:510
  22.5 70.8 %copy-start.4 = (bf16[256,3072]{1,0:T(8,128)(2,1)S(1)}, bf16[256,3072]{1,0:T(8,128)(2,1)}, u32[]{:S(2)}) copy-start(bf16[256,3072]{1,0:T(8,128)(2,1)} %v_own.5) | copy-start | bytes 4718596
  22.5 23.2 %collective-permute-start.5 = (f32[128,1792]{1,0:T(8,128)S(1)}, f32[128,1792]{1,0:T(8,128)S(1)}, u32[]{:S(2)}, u32[]{:S(2)}) collective-permute-start(f32[128,1792]{1,0:T(8,128)S(1)} %get-tuple-element.23), channel_id=1, source_target_pairs={{0,2},{1,3},{2,0},{3,1},{4,6},{5,7},{6,4},{7,5},{8,10},{9,11},{10,... | collective-permute-start | bytes 2752520 | tf_op jit(solution)/shard_map/ppermute | solution.py:526
  46.5 45.6 %collective-permute-start.6 = (f32[64,1664]{1,0:T(8,128)S(1)}, f32[64,1664]{1,0:T(8,128)S(1)}, u32[]{:S(2)}, u32[]{:S(2)}) collective-permute-start(f32[64,1664]{1,0:T(8,128)S(1)} %get-tuple-element.25), channel_id=1, source_target_pairs={{0,4},{1,5},{2,6},{3,7},{4,0},{5,1},{6,2},{7,3},{8,12},{9,13},{10,... | collective-permute-start | bytes 1277960 | tf_op jit(solution)/shard_map/ppermute | solution.py:526
  93.2 11.9 %collective-permute-start.7 = (f32[32,1664]{1,0:T(8,128)}, f32[32,1664]{1,0:T(8,128)}, u32[]{:S(2)}, u32[]{:S(2)}) collective-permute-start(f32[32,1664]{1,0:T(8,128)} %get-tuple-element.27), channel_id=1, source_target_pairs={{0,8},{1,9},{2,10},{3,11},{4,12},{5,13},{6,14},{7,15},{8,0},{9,1},... | collective-permute-start | bytes 638984 | tf_op jit(solution)/shard_map/ppermute | solution.py:526
  93.2 20.8 %copy-start.12 = (s32[16]{0:T(128)S(1)}, s32[16]{0:T(128)}, u32[]{:S(2)}) copy-start(s32[16]{0:T(128)} %constant.74.clone) | copy-start | bytes 196
  93.9 1.0 copy-start.8
  106.4 50.9 %collective-permute-start.9 = (bf16[528,1024]{1,0:T(8,128)(2,1)}, bf16[528,1024]{1,0:T(8,128)(2,1)}, u32[]{:S(2)}, u32[]{:S(2)}) collective-permute-start(bf16[528,1024]{1,0:T(8,128)(2,1)} %copy-done.8), channel_id=1, source_target_pairs={{0,12},{1,13},{4,0},{6,2},{7,3},{8,4},{9,5},{10,6},{11,7},{12,8},{... | collective-permute-start | bytes 3244040 | tf_op jit(solution)/shard_map/ppermute | solution.py:510
  108.3 51.1 %collective-permute-start.8 = (bf16[528,1024]{1,0:T(8,128)(2,1)}, bf16[528,1024]{1,0:T(8,128)(2,1)}, u32[]{:S(2)}, u32[]{:S(2)}) collective-permute-start(bf16[528,1024]{1,0:T(8,128)(2,1)} %copy-done.8), channel_id=1, source_target_pairs={{2,6},{3,7},{4,8},{5,9},{6,10},{7,11},{8,12},{9,13},{10,14},{11,15... | collective-permute-start | bytes 3244040 | tf_op jit(solution)/shard_map/ppermute | solution.py:510
  117.9 22.6 %collective-permute-start.10 = (bf16[272,1536]{1,0:T(8,128)(2,1)}, bf16[272,1536]{1,0:T(8,128)(2,1)}, u32[]{:S(2)}, u32[]{:S(2)}) collective-permute-start(bf16[272,1536]{1,0:T(8,128)(2,1)} %get-tuple-element.32), channel_id=1, source_target_pairs={{0,3},{3,0},{4,7},{7,4},{8,11},{11,8},{12,15},{15,12},{16,19},{19,... | collective-permute-start | bytes 2506760 | tf_op jit(solution)/shard_map/ppermute | solution.py:549
  119.8 5.0 %copy-start.11 = (s32[2,6]{1,0:T(2,128)S(1)}, s32[2,6]{1,0:T(2,128)}, u32[]{:S(2)}) copy-start(s32[2,6]{1,0:T(2,128)} %param.18) | copy-start | bytes 148
  119.9 20.6 %collective-permute-start.11 = (bf16[256,1536]{1,0:T(8,128)(2,1)}, bf16[256,1536]{1,0:T(8,128)(2,1)}, u32[]{:S(2)}, u32[]{:S(2)}) collective-permute-start(bf16[256,1536]{1,0:T(8,128)(2,1)} %get-tuple-element.33), channel_id=1, source_target_pairs={{0,3},{3,0},{4,7},{7,4},{8,11},{11,8},{12,15},{15,12},{16,19},{19,... | collective-permute-start | bytes 2359304 | tf_op jit(solution)/shard_map/ppermute | solution.py:549
  140.5 1.4 copy-start.5
  157.3 37.0 %copy-start.6 = (bf16[256,3072]{1,0:T(8,128)(2,1)S(1)}, bf16[256,3072]{1,0:T(8,128)(2,1)}, u32[]{:S(2)}) copy-start(bf16[256,3072]{1,0:T(8,128)(2,1)} %q.7) | copy-start | bytes 4718596
  159.5 27.9 %collective-permute-start.12 = (bf16[528,512]{1,0:T(8,128)(2,1)}, bf16[528,512]{1,0:T(8,128)(2,1)S(1)}, u32[]{:S(2)}, u32[]{:S(2)}) collective-permute-start(bf16[528,512]{1,0:T(8,128)(2,1)} %pack_chunk.3), channel_id=1, source_target_pairs={{2,6},{3,7},{4,8},{5,9},{6,10},{7,11},{8,12},{9,13},{10,14},{11,15... | collective-permute-start | bytes 1622024 | tf_op jit(solution)/shard_map/ppermute | solution.py:510
  161.6 25.8 %collective-permute-start.13 = (bf16[528,512]{1,0:T(8,128)(2,1)}, bf16[528,512]{1,0:T(8,128)(2,1)S(1)}, u32[]{:S(2)}, u32[]{:S(2)}) collective-permute-start(bf16[528,512]{1,0:T(8,128)(2,1)} %pack_chunk.3), channel_id=1, source_target_pairs={{0,12},{1,13},{4,0},{6,2},{7,3},{8,4},{9,5},{10,6},{11,7},{12,8},{... | collective-permute-start | bytes 1622024 | tf_op jit(solution)/shard_map/ppermute | solution.py:510
  168.2 26.2 %collective-permute-start.16 = (bf16[272,1024]{1,0:T(8,128)(2,1)}, bf16[272,1024]{1,0:T(8,128)(2,1)S(1)}, u32[]{:S(2)}, u32[]{:S(2)}) collective-permute-start(bf16[272,1024]{1,0:T(8,128)(2,1)} %get-tuple-element.39), channel_id=1, source_target_pairs={{0,3},{3,0},{4,7},{7,4},{8,11},{11,8},{12,15},{15,12},{16,19},{19,... | collective-permute-start | bytes 1671176 | tf_op jit(solution)/shard_map/ppermute | solution.py:549
  170.1 24.2 %collective-permute-start.17 = (bf16[256,1024]{1,0:T(8,128)(2,1)}, bf16[256,1024]{1,0:T(8,128)(2,1)}, u32[]{:S(2)}, u32[]{:S(2)}) collective-permute-start(bf16[256,1024]{1,0:T(8,128)(2,1)} %get-tuple-element.40), channel_id=1, source_target_pairs={{0,3},{3,0},{4,7},{7,4},{8,11},{11,8},{12,15},{15,12},{16,19},{19,... | collective-permute-start | bytes 1572872 | tf_op jit(solution)/shard_map/ppermute | solution.py:549
  173.8 19.9 %collective-permute-start.18 = (bf16[16,1536]{1,0:T(8,128)(2,1)S(1)}, bf16[16,1536]{1,0:T(8,128)(2,1)S(1)}, u32[]{:S(2)}, u32[]{:S(2)}) collective-permute-start(bf16[16,1536]{1,0:T(8,128)(2,1)S(1)} %get-tuple-element.41), channel_id=1, source_target_pairs={{0,1},{1,0},{2,3},{3,2},{4,5},{5,4},{6,7},{7,6},{8,9},{9,8},{10,11... | collective-permute-start | bytes 147464 | tf_op jit(solution)/shard_map/ppermute | solution.py:560
  188.1 17.4 %collective-permute-start.14 = (bf16[272,512]{1,0:T(8,128)(2,1)S(1)}, bf16[272,512]{1,0:T(8,128)(2,1)S(1)}, u32[]{:S(2)}, u32[]{:S(2)}) collective-permute-start(bf16[272,512]{1,0:T(8,128)(2,1)S(1)} %get-tuple-element.35), channel_id=1, source_target_pairs={{0,3},{3,0},{4,7},{7,4},{8,11},{11,8},{12,15},{15,12},{16,19},{19,... | collective-permute-start | bytes 835592 | tf_op jit(solution)/shard_map/ppermute | solution.py:549
  190.0 15.4 %collective-permute-start.15 = (bf16[256,512]{1,0:T(8,128)(2,1)S(1)}, bf16[256,512]{1,0:T(8,128)(2,1)S(1)}, u32[]{:S(2)}, u32[]{:S(2)}) collective-permute-start(bf16[256,512]{1,0:T(8,128)(2,1)S(1)} %get-tuple-element.36), channel_id=1, source_target_pairs={{0,3},{3,0},{4,7},{7,4},{8,11},{11,8},{12,15},{15,12},{16,19},{19,... | collective-permute-start | bytes 786440 | tf_op jit(solution)/shard_map/ppermute | solution.py:549
  194.4 11.1 %copy-start.2 = (bf16[256,3072]{1,0:T(8,128)(2,1)S(1)}, bf16[256,3072]{1,0:T(8,128)(2,1)}, u32[]{:S(2)}) copy-start(bf16[256,3072]{1,0:T(8,128)(2,1)} %k_own.5) | copy-start | bytes 4718596

commit v9 on v8

--- a/solution.py
+++ b/solution.py
@@ -535,16 +535,13 @@
             limits = jnp.concatenate(limits)
             parts.append(text_finish(tie(parts[i][0], *before), exchanged(i), limits))
 
-    for _ in range(stages - 1):
-        merge()
+    merge()
     count = len(CHUNK_HEADS)
     for i in range(count):
         before = outs[i - 1 : i] + ([parts[-1][0]] if halving and i == 0 else [])
         if i + 1 < count:
             send(i + 1, *direct[i], *before)
-        up, down = direct[i]
-        if i + 1 < count:
-            up, down = tie(up, *before), tie(down, *before)
+        up, down = tie(direct[i][0], *before), tie(direct[i][1], *before)
         relays = [
             lax.ppermute(half, "tiles", pairs["relayed"])
             for half in choose(sends_later, up, down, rows + PAD_ROWS)
@@ -555,6 +552,10 @@
                 [*direct[i], *relays, *beside[1:]], text_k, text_v, outs[-1] if outs else None,
             )
         )
+        if i == 0:
+            merge(outs[0])
+        elif i == 1:
+            merge(outs[1])
     if halving:
         mine, leave = parts[-1]
         got = lax.ppermute(leave, "tiles", [(d, d ^ 1) for d in range(n)])

time: 213 us -> 201 us (0.944)
  waiting for transfers between devices: 108 us -> 85.3 us
  Pallas kernels: 54.6 us -> 58.3 us
  local copies, waits for them, and re-layouts: 7.53 us -> 10.6 us
  starting transfers between devices: 38.7 us -> 41.4 us
    ppermute x3, waiting for transfers between devices: 78.2 us -> 32.9 us  [exchanged(): lax.ppermute(parts[i][1], 'tiles', [(d, d ^ 2 << i) for d in range(n)])]
    ppermute x6, waiting for transfers between devices: 15.6 us -> 32.7 us  [send(): lax.ppermute(mine, 'tiles', pairs[x])]
    ppermute x6, waiting for transfers between devices: 14.2 us -> 18.6 us  [per_device(): lax.ppermute(half, 'tiles', pairs['relayed'])]
    ppermute x3, starting transfers between devices: 0.14 us -> 2.76 us  [exchanged(): lax.ppermute(parts[i][1], 'tiles', [(d, d ^ 2 << i) for d in range(n)])]
    unnamed x28 -> x34, local copies, waits for them, and re-layouts: 5.89 us -> 8.33 us
  transfers between devices with their start and end apart: 19 -> 19, of which waited for: 6 -> 7; matrix products, arithmetic and copies ran while one was open for 1% -> 2% of each run, Pallas kernels for 23% -> 26%
where the time goes in v9:
time: 201 us; the launch traced here: 199 us
  waiting for transfers between devices  85.3 us (42%)
  Pallas kernels  58.3 us (29%)
  starting transfers between devices  41.4 us (21%)
  local copies, waits for them, and re-layouts  10.6 us (5%)
    pallas_call x3, Pallas kernels, video_call(): pl.pallas_call(video_kernel, grid=(heads // STEP_HEADS,), in_specs=in_spe...  32.9 us
    ppermute x3, waiting for transfers between devices, exchanged(): lax.ppermute(parts[i][1], 'tiles', [(d, d ^ 2 << i) for d in range(n)])  32.9 us
    ppermute x6, waiting for transfers between devices, send(): lax.ppermute(mine, 'tiles', pairs[x])  32.7 us
    ppermute x6, starting transfers between devices, send(): lax.ppermute(mine, 'tiles', pairs[x])  21.1 us
    ppermute x6, waiting for transfers between devices, per_device(): lax.ppermute(half, 'tiles', pairs['relayed'])  18.6 us
    ppermute x6, starting transfers between devices, per_device(): lax.ppermute(half, 'tiles', pairs['relayed'])  16.8 us
    unnamed x34, local copies, waits for them, and re-layouts  8.33 us
    pallas_call x1, Pallas kernels, text_local(): pl.pallas_call(text_kernel, grid_spec=pltpu.PrefetchScalarGridSpec(num_sc...  8.07 us
  transfers between devices with their start and end apart: 19, of which 7 were waited for; matrix products, arithmetic and copies ran while one was open for 2% of the time, Pallas kernels for 26%

profile of v9, /device:TPU:24, one launch (start us, length us, event | category | flops | bytes accessed | tf_op | source)
XLA Modules:
  0.0 199.2 jit_solution(8932573146500386073)
XLA Ops:
  0.7 0.5 collective-permute-start.4
  1.2 1.4 copy-done
  2.6 1.4 copy-done.3
  4.0 2.0 pack_chunk.5
  6.0 1.9 collective-permute-start.1
  8.0 3.9 %collective-permute-start.2 = (bf16[528,1536]{1,0:T(8,128)(2,1)}, bf16[528,1536]{1,0:T(8,128)(2,1)}, u32[]{:S(2)}, u32[]{:S(2)}) collective-permute-start(bf16[528,1536]{1,0:T(8,128)(2,1)} %pack_chunk.5), channel_id=1, source_target_pairs={{0,12},{1,13},{4,0},{6,2},{7,3},{8,4},{9,5},{10,6},{11,7},{12,8},{... | collective-permute-start | bytes 4866056 | tf_op jit(solution)/shard_map/ppermute | solution.py:510
  12.1 1.1 collective-permute-done
  13.2 0.7 pad_add_fusion.2.counts
  14.0 1.1 copy-done.13
  15.1 1.4 copy-done.9
  16.5 8.1 %text_partials.1 = (f32[128,1792]{1,0:T(8,128)S(1)}, f32[128,1792]{1,0:T(8,128)S(1)}) custom-call(s32[17]{0:T(128)S(1)} %pad_add_fusion.1.order, s32[4]{0:T(128)S(1)} %pad_add_fusion.2.counts, bf16[256,3072]{1,0:T(8,128)(2,1)S(1)} %copy-done.9, bf16[256,3072]{1,0:T(8,128)(2,1)S(1)} %copy-done.1, bf16[256,3072]{1,0:T(8,128)(2,1)} %v_own.5, ...), custom_call_target="tpu_custom_call" | custom-call | flops 8388608 | bytes 786432 | tf_op jit(solution)/shard_map/text_partials/pallas_call | solution.py:367
  24.6 2.7 %collective-permute-start.5 = (f32[128,1792]{1,0:T(8,128)S(1)}, f32[128,1792]{1,0:T(8,128)S(1)}, u32[]{:S(2)}, u32[]{:S(2)}) collective-permute-start(f32[128,1792]{1,0:T(8,128)S(1)} %get-tuple-element.27), channel_id=1, source_target_pairs={{0,2},{1,3},{2,0},{3,1},{4,6},{5,7},{6,4},{7,5},{8,10},{9,11},{10,... | collective-permute-start | bytes 2752520 | tf_op jit(solution)/shard_map/ppermute | solution.py:526
  27.3 1.7 pack_chunk.4
  29.0 19.0 %collective-permute-done.5.refs_1_ = f32[128,1792]{1,0:T(8,128)S(1)} collective-permute-done((f32[128,1792]{1,0:T(8,128)S(1)}, f32[128,1792]{1,0:T(8,128)S(1)}, u32[]{:S(2)}, u32[]{:S(2)}) %collective-permute-start.5) | collective-permute-done | bytes 917536 | tf_op jit(solution)/shard_map/ppermute | solution.py:526
  48.0 0.8 text_merge.2
  48.8 0.8 copy-done.10
  49.5 0.8 copy-done.12
  50.3 30.1 %collective-permute-done.1.a.rest_0_ = bf16[528,1536]{1,0:T(8,128)(2,1)} collective-permute-done((bf16[528,1536]{1,0:T(8,128)(2,1)}, bf16[528,1536]{1,0:T(8,128)(2,1)}, u32[]{:S(2)}, u32[]{:S(2)}) %collective-permute-start.1) | collective-permute-done | bytes 1622048 | tf_op jit(solution)/shard_map/ppermute | solution.py:510
  80.4 2.3 %collective-permute-start.7 = (bf16[528,1024]{1,0:T(8,128)(2,1)}, bf16[528,1024]{1,0:T(8,128)(2,1)}, u32[]{:S(2)}, u32[]{:S(2)}) collective-permute-start(bf16[528,1024]{1,0:T(8,128)(2,1)} %pack_chunk.4), channel_id=1, source_target_pairs={{0,12},{1,13},{4,0},{6,2},{7,3},{8,4},{9,5},{10,6},{11,7},{12,8},{... | collective-permute-start | bytes 3244040 | tf_op jit(solution)/shard_map/ppermute | solution.py:510
  82.8 5.3 %collective-permute-start.6 = (bf16[528,1024]{1,0:T(8,128)(2,1)}, bf16[528,1024]{1,0:T(8,128)(2,1)}, u32[]{:S(2)}, u32[]{:S(2)}) collective-permute-start(bf16[528,1024]{1,0:T(8,128)(2,1)} %pack_chunk.4), channel_id=1, source_target_pairs={{2,6},{3,7},{4,8},{5,9},{6,10},{7,11},{8,12},{9,13},{10,14},{11,15... | collective-permute-start | bytes 3244040 | tf_op jit(solution)/shard_map/ppermute | solution.py:510
  88.1 0.6 dynamic_slice.8.second
  88.7 3.4 %choose_relayed.3 = (bf16[272,1536]{1,0:T(8,128)(2,1)}, bf16[256,1536]{1,0:T(8,128)(2,1)}) custom-call(s32[1]{0:T(128)} %dynamic_slice.8.second, bf16[528,1536]{1,0:T(8,128)(2,1)} %collective-permute-done.1.a.rest_0_, bf16[528,1536]{1,0:T(8,128)(2,1)} %collective-permute-done.2.b.rest_1_), custom_call_target="tpu_custom_call" | custom-call | tf_op jit(solution)/shard_map/choose_relayed/pallas_call | solution.py:124
  92.1 1.9 collective-permute-start.8
  94.0 3.6 %collective-permute-start.9 = (bf16[256,1536]{1,0:T(8,128)(2,1)}, bf16[256,1536]{1,0:T(8,128)(2,1)}, u32[]{:S(2)}, u32[]{:S(2)}) collective-permute-start(bf16[256,1536]{1,0:T(8,128)(2,1)} %get-tuple-element.33), channel_id=1, source_target_pairs={{0,3},{3,0},{4,7},{7,4},{8,11},{11,8},{12,15},{15,12},{16,19},{19,... | collective-permute-start | bytes 2359304 | tf_op jit(solution)/shard_map/ppermute | solution.py:546
  97.7 0.2 reduce_window_sum.11
  97.9 0.1 fusion
  99.1 0.7 dynamic-slice_bitcast_fusion
  99.8 0.7 concatenate.18.table
  100.5 14.2 %collective-permute-done.9.rest_3_ = bf16[256,1536]{1,0:T(8,128)(2,1)} collective-permute-done((bf16[256,1536]{1,0:T(8,128)(2,1)}, bf16[256,1536]{1,0:T(8,128)(2,1)}, u32[]{:S(2)}, u32[]{:S(2)}) %collective-permute-start.9) | collective-permute-done | bytes 786464 | tf_op jit(solution)/shard_map/ppermute | solution.py:546
  114.7 15.4 %video_attention.3.rest_8_ = bf16[256,3072]{1,0:T(8,128)(2,1)} custom-call(s32[13]{0:T(128)S(1)} %concatenate.18.table, bf16[256,3072]{1,0:T(8,128)(2,1)S(1)} %copy-done.6, bf16[256,3072]{1,0:T(8,128)(2,1)S(1)} %copy-done.1, bf16[256,3072]{1,0:T(8,128)(2,1)} %v_own.5, bf16[528,1536]{1,0:T(8,128)(2,1)} %collective-permute-done.1.a.rest_0_, ...), custom_call_target="tpu_custom_call" | custom-call | flops 113246208 | bytes 393216 | tf_op jit(solution)/shard_map/video_attention/pallas_call | solution.py:275
  130.1 2.6 %collective-permute-done.6.a.rest_0_ = bf16[528,1024]{1,0:T(8,128)(2,1)} collective-permute-done((bf16[528,1024]{1,0:T(8,128)(2,1)}, bf16[528,1024]{1,0:T(8,128)(2,1)}, u32[]{:S(2)}, u32[]{:S(2)}) %collective-permute-start.6) | collective-permute-done | bytes 1081376 | tf_op jit(solution)/shard_map/ppermute | solution.py:510
  132.7 2.9 %choose_relayed.4 = (bf16[272,1024]{1,0:T(8,128)(2,1)}, bf16[256,1024]{1,0:T(8,128)(2,1)}) custom-call(s32[1]{0:T(128)} %dynamic_slice.8.second, bf16[528,1024]{1,0:T(8,128)(2,1)} %collective-permute-done.6.a.rest_0_, bf16[528,1024]{1,0:T(8,128)(2,1)} %collective-permute-done.7.b.rest_1_), custom_call_target="tpu_custom_call" | custom-call | tf_op jit(solution)/shard_map/choose_relayed/pallas_call | solution.py:124
  135.6 1.9 collective-permute-start.12
  137.6 3.8 %collective-permute-start.13 = (bf16[256,1024]{1,0:T(8,128)(2,1)}, bf16[256,1024]{1,0:T(8,128)(2,1)}, u32[]{:S(2)}, u32[]{:S(2)}) collective-permute-start(bf16[256,1024]{1,0:T(8,128)(2,1)} %get-tuple-element.38), channel_id=1, source_target_pairs={{0,3},{3,0},{4,7},{7,4},{8,11},{11,8},{12,15},{15,12},{16,19},{19,... | collective-permute-start | bytes 1572872 | tf_op jit(solution)/shard_map/ppermute | solution.py:546
  141.3 1.5 pack_chunk.3
  142.9 2.4 %collective-permute-start.11 = (bf16[528,512]{1,0:T(8,128)(2,1)}, bf16[528,512]{1,0:T(8,128)(2,1)}, u32[]{:S(2)}, u32[]{:S(2)}) collective-permute-start(bf16[528,512]{1,0:T(8,128)(2,1)} %pack_chunk.3), channel_id=1, source_target_pairs={{0,12},{1,13},{4,0},{6,2},{7,3},{8,4},{9,5},{10,6},{11,7},{12,8},{... | collective-permute-start | bytes 1622024 | tf_op jit(solution)/shard_map/ppermute | solution.py:510
  145.2 5.3 %collective-permute-start.10 = (bf16[528,512]{1,0:T(8,128)(2,1)}, bf16[528,512]{1,0:T(8,128)(2,1)}, u32[]{:S(2)}, u32[]{:S(2)}) collective-permute-start(bf16[528,512]{1,0:T(8,128)(2,1)} %pack_chunk.3), channel_id=1, source_target_pairs={{2,6},{3,7},{4,8},{5,9},{6,10},{7,11},{8,12},{9,13},{10,14},{11,15... | collective-permute-start | bytes 1622024 | tf_op jit(solution)/shard_map/ppermute | solution.py:510
  150.5 2.1 %text_merge.3 = (f32[32,1664]{1,0:T(8,128)S(1)}, f32[32,1664]{1,0:T(8,128)}) custom-call(f32[64,1664]{1,0:T(8,128)S(1)} %copy-done.11, f32[64,1664]{1,0:T(8,128)} %collective-permute-done.16.refs_1_), custom_call_target="tpu_custom_call" | custom-call | tf_op jit(solution)/shard_map/text_merge/pallas_call | solution.py:422
  152.8 1.4 copy-done.7
  154.2 11.1 %video_attention.4.rest_8_ = bf16[256,3072]{1,0:T(8,128)(2,1)} custom-call(s32[13]{0:T(128)S(1)} %concatenate.18.table, bf16[256,3072]{1,0:T(8,128)(2,1)S(1)} %copy-done.7, bf16[256,3072]{1,0:T(8,128)(2,1)} %k_own.5, bf16[256,3072]{1,0:T(8,128)(2,1)} %v_own.5, bf16[528,1024]{1,0:T(8,128)(2,1)} %collective-permute-done.6.a.rest_0_, ...), custom_call_target="tpu_custom_call", output_to_operand_aliasing={{}: (12, {})} | custom-call | flops 75497472 | bytes 262144 | tf_op jit(solution)/shard_map/video_attention/pallas_call | solution.py:275
  165.3 13.8 %collective-permute-done.17.refs_1_ = f32[32,1664]{1,0:T(8,128)} collective-permute-done((f32[32,1664]{1,0:T(8,128)}, f32[32,1664]{1,0:T(8,128)}, u32[]{:S(2)}, u32[]{:S(2)}) %collective-permute-start.17) | collective-permute-done | bytes 213024 | tf_op jit(solution)/shard_map/ppermute | solution.py:526
  179.1 1.2 text_finish.1
  180.5 1.7 choose_relayed.5
  182.2 1.9 collective-permute-start.14
  184.1 3.6 %collective-permute-start.15 = (bf16[256,512]{1,0:T(8,128)(2,1)S(1)}, bf16[256,512]{1,0:T(8,128)(2,1)S(1)}, u32[]{:S(2)}, u32[]{:S(2)}) collective-permute-start(bf16[256,512]{1,0:T(8,128)(2,1)S(1)} %get-tuple-element.42), channel_id=1, source_target_pairs={{0,3},{3,0},{4,7},{7,4},{8,11},{11,8},{12,15},{15,12},{16,19},{19,... | collective-permute-start | bytes 786440 | tf_op jit(solution)/shard_map/ppermute | solution.py:546
  187.8 0.7 maximum_select_fusion
  188.4 4.4 %collective-permute-done.15.rest_3_ = bf16[256,512]{1,0:T(8,128)(2,1)S(1)} collective-permute-done((bf16[256,512]{1,0:T(8,128)(2,1)S(1)}, bf16[256,512]{1,0:T(8,128)(2,1)S(1)}, u32[]{:S(2)}, u32[]{:S(2)}) %collective-permute-start.15) | collective-permute-done | bytes 262176 | tf_op jit(solution)/shard_map/ppermute | solution.py:546
  192.9 6.4 %video_attention.5 = bf16[256,3072]{1,0:T(8,128)(2,1)} custom-call(s32[13]{0:T(128)S(1)} %concatenate.18.table, bf16[256,3072]{1,0:T(8,128)(2,1)S(1)} %copy-done.8, bf16[256,3072]{1,0:T(8,128)(2,1)S(1)} %copy-done.2, bf16[256,3072]{1,0:T(8,128)(2,1)} %v_own.5, bf16[528,512]{1,0:T(8,128)(2,1)} %collective-permute-done.10.a.rest_0_, ...), custom_call_target="tpu_custom_call", output_to_operand_aliasing={{}: (12, {})} | custom-call | flops 37748736 | bytes 131072 | tf_op jit(solution)/shard_map/video_attention/pallas_call | solution.py:275
  (54 shorter events, 0.9 us)
Async XLA Ops:
  0.6 11.4 %copy-start.16 = (s32[16]{0:T(128)S(1)}, s32[16]{0:T(128)}, u32[]{:S(2)}) copy-start(s32[16]{0:T(128)} %constant.76.clone) | copy-start | bytes 196
  0.6 13.3 %collective-permute-start.3 = (bf16[256,3072]{1,0:T(8,128)(2,1)}, bf16[256,3072]{1,0:T(8,128)(2,1)S(1)}, u32[]{:S(2)}, u32[]{:S(2)}) collective-permute-start(bf16[256,3072]{1,0:T(8,128)(2,1)} %k_own.5), channel_id=1, source_target_pairs={{0,1},{1,0},{2,3},{3,2},{4,5},{5,4},{6,7},{7,6},{8,9},{9,8},{10,11... | collective-permute-start | bytes 4718600 | tf_op jit(solution)/shard_map/ppermute | solution.py:514
  0.7 13.2 %collective-permute-start.4 = (bf16[256,3072]{1,0:T(8,128)(2,1)}, bf16[256,3072]{1,0:T(8,128)(2,1)}, u32[]{:S(2)}, u32[]{:S(2)}) collective-permute-start(bf16[256,3072]{1,0:T(8,128)(2,1)} %v_own.5), channel_id=1, source_target_pairs={{0,1},{1,0},{2,3},{3,2},{4,5},{5,4},{6,7},{7,6},{8,9},{9,8},{10,11... | collective-permute-start | bytes 4718600 | tf_op jit(solution)/shard_map/ppermute | solution.py:514
  1.2 1.4 copy-start
  2.6 1.4 copy-start.3
  4.0 11.1 %copy-start.1 = (bf16[256,3072]{1,0:T(8,128)(2,1)S(1)}, bf16[256,3072]{1,0:T(8,128)(2,1)}, u32[]{:S(2)}) copy-start(bf16[256,3072]{1,0:T(8,128)(2,1)} %k_own.5) | copy-start | bytes 4718596
  6.0 74.4 %collective-permute-start.1 = (bf16[528,1536]{1,0:T(8,128)(2,1)}, bf16[528,1536]{1,0:T(8,128)(2,1)}, u32[]{:S(2)}, u32[]{:S(2)}) collective-permute-start(bf16[528,1536]{1,0:T(8,128)(2,1)} %pack_chunk.5), channel_id=1, source_target_pairs={{2,6},{3,7},{4,8},{5,9},{6,10},{7,11},{8,12},{9,13},{10,14},{11,15... | collective-permute-start | bytes 4866056 | tf_op jit(solution)/shard_map/ppermute | solution.py:510
  8.0 72.5 %collective-permute-start.2 = (bf16[528,1536]{1,0:T(8,128)(2,1)}, bf16[528,1536]{1,0:T(8,128)(2,1)}, u32[]{:S(2)}, u32[]{:S(2)}) collective-permute-start(bf16[528,1536]{1,0:T(8,128)(2,1)} %pack_chunk.5), channel_id=1, source_target_pairs={{0,12},{1,13},{4,0},{6,2},{7,3},{8,4},{9,5},{10,6},{11,7},{12,8},{... | collective-permute-start | bytes 4866056 | tf_op jit(solution)/shard_map/ppermute | solution.py:510
  11.9 1.3 collective-permute-start
  13.9 13.3 %copy-start.4 = (bf16[256,3072]{1,0:T(8,128)(2,1)S(1)}, bf16[256,3072]{1,0:T(8,128)(2,1)}, u32[]{:S(2)}) copy-start(bf16[256,3072]{1,0:T(8,128)(2,1)} %v_own.5) | copy-start | bytes 4718596
  13.9 1.1 copy-start.13
  15.1 1.4 copy-start.9
  24.6 23.4 %collective-permute-start.5 = (f32[128,1792]{1,0:T(8,128)S(1)}, f32[128,1792]{1,0:T(8,128)S(1)}, u32[]{:S(2)}, u32[]{:S(2)}) collective-permute-start(f32[128,1792]{1,0:T(8,128)S(1)} %get-tuple-element.27), channel_id=1, source_target_pairs={{0,2},{1,3},{2,0},{3,1},{4,6},{5,7},{6,4},{7,5},{8,10},{9,11},{10,... | collective-permute-start | bytes 2752520 | tf_op jit(solution)/shard_map/ppermute | solution.py:526
  29.0 59.1 %copy-start.15 = (s32[16]{0:T(128)S(1)}, s32[16]{0:T(128)}, u32[]{:S(2)}) copy-start(s32[16]{0:T(128)} %constant.74.clone) | copy-start | bytes 196
  48.8 0.8 copy-start.10
  49.5 0.8 copy-start.12
  80.4 49.7 %collective-permute-start.7 = (bf16[528,1024]{1,0:T(8,128)(2,1)}, bf16[528,1024]{1,0:T(8,128)(2,1)}, u32[]{:S(2)}, u32[]{:S(2)}) collective-permute-start(bf16[528,1024]{1,0:T(8,128)(2,1)} %pack_chunk.4), channel_id=1, source_target_pairs={{0,12},{1,13},{4,0},{6,2},{7,3},{8,4},{9,5},{10,6},{11,7},{12,8},{... | collective-permute-start | bytes 3244040 | tf_op jit(solution)/shard_map/ppermute | solution.py:510
  82.8 49.9 %collective-permute-start.6 = (bf16[528,1024]{1,0:T(8,128)(2,1)}, bf16[528,1024]{1,0:T(8,128)(2,1)}, u32[]{:S(2)}, u32[]{:S(2)}) collective-permute-start(bf16[528,1024]{1,0:T(8,128)(2,1)} %pack_chunk.4), channel_id=1, source_target_pairs={{2,6},{3,7},{4,8},{5,9},{6,10},{7,11},{8,12},{9,13},{10,14},{11,15... | collective-permute-start | bytes 3244040 | tf_op jit(solution)/shard_map/ppermute | solution.py:510
  88.7 9.0 %copy-start.14 = (s32[2,6]{1,0:T(2,128)S(1)}, s32[2,6]{1,0:T(2,128)}, u32[]{:S(2)}) copy-start(s32[2,6]{1,0:T(2,128)} %param.18) | copy-start | bytes 148
  88.7 26.0 %copy-start.6 = (bf16[256,3072]{1,0:T(8,128)(2,1)S(1)}, bf16[256,3072]{1,0:T(8,128)(2,1)}, u32[]{:S(2)}) copy-start(bf16[256,3072]{1,0:T(8,128)(2,1)} %q.7) | copy-start | bytes 4718596
  92.1 22.6 %collective-permute-start.8 = (bf16[272,1536]{1,0:T(8,128)(2,1)}, bf16[272,1536]{1,0:T(8,128)(2,1)}, u32[]{:S(2)}, u32[]{:S(2)}) collective-permute-start(bf16[272,1536]{1,0:T(8,128)(2,1)} %get-tuple-element.32), channel_id=1, source_target_pairs={{0,3},{3,0},{4,7},{7,4},{8,11},{11,8},{12,15},{15,12},{16,19},{19,... | collective-permute-start | bytes 2506760 | tf_op jit(solution)/shard_map/ppermute | solution.py:546
  94.0 20.6 %collective-permute-start.9 = (bf16[256,1536]{1,0:T(8,128)(2,1)}, bf16[256,1536]{1,0:T(8,128)(2,1)}, u32[]{:S(2)}, u32[]{:S(2)}) collective-permute-start(bf16[256,1536]{1,0:T(8,128)(2,1)} %get-tuple-element.33), channel_id=1, source_target_pairs={{0,3},{3,0},{4,7},{7,4},{8,11},{11,8},{12,15},{15,12},{16,19},{19,... | collective-permute-start | bytes 2359304 | tf_op jit(solution)/shard_map/ppermute | solution.py:546
  99.0 51.5 %collective-permute-start.16 = (f32[64,1664]{1,0:T(8,128)}, f32[64,1664]{1,0:T(8,128)}, u32[]{:S(2)}, u32[]{:S(2)}) collective-permute-start(f32[64,1664]{1,0:T(8,128)} %copy-done.12), channel_id=1, source_target_pairs={{0,4},{1,5},{2,6},{3,7},{4,0},{5,1},{6,2},{7,3},{8,12},{9,13},{10,... | collective-permute-start | bytes 1277960 | tf_op jit(solution)/shard_map/ppermute | solution.py:526
  130.1 11.2 %copy-start.5 = (bf16[256,3072]{1,0:T(8,128)(2,1)S(1)}, bf16[256,3072]{1,0:T(8,128)(2,1)}, u32[]{:S(2)}) copy-start(bf16[256,3072]{1,0:T(8,128)(2,1)} %v_own.5) | copy-start | bytes 4718596
  135.6 17.2 %collective-permute-start.12 = (bf16[272,1024]{1,0:T(8,128)(2,1)}, bf16[272,1024]{1,0:T(8,128)(2,1)}, u32[]{:S(2)}, u32[]{:S(2)}) collective-permute-start(bf16[272,1024]{1,0:T(8,128)(2,1)} %get-tuple-element.37), channel_id=1, source_target_pairs={{0,3},{3,0},{4,7},{7,4},{8,11},{11,8},{12,15},{15,12},{16,19},{19,... | collective-permute-start | bytes 1671176 | tf_op jit(solution)/shard_map/ppermute | solution.py:546
  137.5 13.0 %copy-start.11 = (f32[64,1664]{1,0:T(8,128)S(1)}, f32[64,1664]{1,0:T(8,128)}, u32[]{:S(2)}) copy-start(f32[64,1664]{1,0:T(8,128)} %copy-done.10) | copy-start | bytes 1277956
  137.6 15.2 %collective-permute-start.13 = (bf16[256,1024]{1,0:T(8,128)(2,1)}, bf16[256,1024]{1,0:T(8,128)(2,1)}, u32[]{:S(2)}, u32[]{:S(2)}) collective-permute-start(bf16[256,1024]{1,0:T(8,128)(2,1)} %get-tuple-element.38), channel_id=1, source_target_pairs={{0,3},{3,0},{4,7},{7,4},{8,11},{11,8},{12,15},{15,12},{16,19},{19,... | collective-permute-start | bytes 1572872 | tf_op jit(solution)/shard_map/ppermute | solution.py:546
  142.9 37.6 %collective-permute-start.11 = (bf16[528,512]{1,0:T(8,128)(2,1)}, bf16[528,512]{1,0:T(8,128)(2,1)}, u32[]{:S(2)}, u32[]{:S(2)}) collective-permute-start(bf16[528,512]{1,0:T(8,128)(2,1)} %pack_chunk.3), channel_id=1, source_target_pairs={{0,12},{1,13},{4,0},{6,2},{7,3},{8,4},{9,5},{10,6},{11,7},{12,8},{... | collective-permute-start | bytes 1622024 | tf_op jit(solution)/shard_map/ppermute | solution.py:510
  145.2 35.2 %collective-permute-start.10 = (bf16[528,512]{1,0:T(8,128)(2,1)}, bf16[528,512]{1,0:T(8,128)(2,1)}, u32[]{:S(2)}, u32[]{:S(2)}) collective-permute-start(bf16[528,512]{1,0:T(8,128)(2,1)} %pack_chunk.3), channel_id=1, source_target_pairs={{2,6},{3,7},{4,8},{5,9},{6,10},{7,11},{8,12},{9,13},{10,14},{11,15... | collective-permute-start | bytes 1622024 | tf_op jit(solution)/shard_map/ppermute | solution.py:510
  152.7 26.4 %collective-permute-start.17 = (f32[32,1664]{1,0:T(8,128)}, f32[32,1664]{1,0:T(8,128)}, u32[]{:S(2)}, u32[]{:S(2)}) collective-permute-start(f32[32,1664]{1,0:T(8,128)} %get-tuple-element.47), channel_id=1, source_target_pairs={{0,8},{1,9},{2,10},{3,11},{4,12},{5,13},{6,14},{7,15},{8,0},{9,1},... | collective-permute-start | bytes 638984 | tf_op jit(solution)/shard_map/ppermute | solution.py:526
  152.8 1.4 copy-start.7
  154.2 38.7 %copy-start.8 = (bf16[256,3072]{1,0:T(8,128)(2,1)S(1)}, bf16[256,3072]{1,0:T(8,128)(2,1)}, u32[]{:S(2)}) copy-start(bf16[256,3072]{1,0:T(8,128)(2,1)} %q.7) | copy-start | bytes 4718596
  165.3 27.6 %copy-start.2 = (bf16[256,3072]{1,0:T(8,128)(2,1)S(1)}, bf16[256,3072]{1,0:T(8,128)(2,1)}, u32[]{:S(2)}) copy-start(bf16[256,3072]{1,0:T(8,128)(2,1)} %k_own.5) | copy-start | bytes 4718596
  180.4 7.4 %collective-permute-start.18 = (bf16[16,1536]{1,0:T(8,128)(2,1)S(1)}, bf16[16,1536]{1,0:T(8,128)(2,1)S(1)}, u32[]{:S(2)}, u32[]{:S(2)}) collective-permute-start(bf16[16,1536]{1,0:T(8,128)(2,1)S(1)} %get-tuple-element.49), channel_id=1, source_target_pairs={{0,1},{1,0},{2,3},{3,2},{4,5},{5,4},{6,7},{7,6},{8,9},{9,8},{10,11... | collective-permute-start | bytes 147464 | tf_op jit(solution)/shard_map/ppermute | solution.py:561
  182.2 10.7 %collective-permute-start.14 = (bf16[272,512]{1,0:T(8,128)(2,1)S(1)}, bf16[272,512]{1,0:T(8,128)(2,1)S(1)}, u32[]{:S(2)}, u32[]{:S(2)}) collective-permute-start(bf16[272,512]{1,0:T(8,128)(2,1)S(1)} %get-tuple-element.41), channel_id=1, source_target_pairs={{0,3},{3,0},{4,7},{7,4},{8,11},{11,8},{12,15},{15,12},{16,19},{19,... | collective-permute-start | bytes 835592 | tf_op jit(solution)/shard_map/ppermute | solution.py:546
  184.1 8.7 %collective-permute-start.15 = (bf16[256,512]{1,0:T(8,128)(2,1)S(1)}, bf16[256,512]{1,0:T(8,128)(2,1)S(1)}, u32[]{:S(2)}, u32[]{:S(2)}) collective-permute-start(bf16[256,512]{1,0:T(8,128)(2,1)S(1)} %get-tuple-element.42), channel_id=1, source_target_pairs={{0,3},{3,0},{4,7},{7,4},{8,11},{11,8},{12,15},{15,12},{16,19},{19,... | collective-permute-start | bytes 786440 | tf_op jit(solution)/shard_map/ppermute | solution.py:546

commit v10 on v9

--- a/solution.py
+++ b/solution.py
@@ -13,7 +13,7 @@
 NR = 4
 BLOCKS = 5
 STEP_HEADS = 2
-CHUNK_HEADS = (12, 8, 4)
+CHUNK_HEADS = (10, 8, 6)
 PAD_ROWS = 16
 VMEM_BYTES = 48 * 1024 * 1024
 LOG2E = 1.4426950408889634
@@ -538,7 +538,7 @@
     merge()
     count = len(CHUNK_HEADS)
     for i in range(count):
-        before = outs[i - 1 : i] + ([parts[-1][0]] if halving and i == 0 else [])
+        before = outs[i - 1 : i] + ([parts[-1][0]] if halving and i < 2 else [])
         if i + 1 < count:
             send(i + 1, *direct[i], *before)
         up, down = tie(direct[i][0], *before), tie(direct[i][1], *before)
@@ -554,8 +554,8 @@
         )
         if i == 0:
             merge(outs[0])
-        elif i == 1:
-            merge(outs[1])
+        elif i + 1 == count:
+            merge(*relays)
     if halving:
         mine, leave = parts[-1]
         got = lax.ppermute(leave, "tiles", [(d, d ^ 1) for d in range(n)])

time: 201 us -> 211 us (1.050)
  local copies, waits for them, and re-layouts: 10.6 us -> 15.9 us
  waiting for transfers between devices: 85.3 us -> 90.6 us
  Pallas kernels: 58.3 us -> 55.6 us
    ppermute x6, waiting for transfers between devices: 18.6 us -> 29.1 us  [per_device(): lax.ppermute(half, 'tiles', pairs['relayed'])]
    ppermute x6, waiting for transfers between devices: 32.7 us -> 26.2 us  [send(): lax.ppermute(mine, 'tiles', pairs[x])]
    unnamed x34 -> x52, local copies, waits for them, and re-layouts: 8.33 us -> 14.3 us
    ppermute x3, waiting for transfers between devices: 32.9 us -> 35.2 us  [exchanged(): lax.ppermute(parts[i][1], 'tiles', [(d, d ^ 2 << i) for d in range(n)])]
  transfers between devices with their start and end apart: 19 -> 19, of which waited for: 7 -> 8; matrix products, arithmetic and copies ran while one was open for 2% -> 1% of each run, Pallas kernels for 26% -> 25%
where the time goes in v10:
time: 211 us; the launch traced here: 207 us
  waiting for transfers between devices  90.6 us (43%)
  Pallas kernels  55.6 us (26%)
  starting transfers between devices  41.5 us (20%)
  local copies, waits for them, and re-layouts  15.9 us (8%)
  other arithmetic  2.14 us (1%)
    ppermute x3, waiting for transfers between devices, exchanged(): lax.ppermute(parts[i][1], 'tiles', [(d, d ^ 2 << i) for d in range(n)])  35.2 us
    pallas_call x3, Pallas kernels, video_call(): pl.pallas_call(video_kernel, grid=(heads // STEP_HEADS,), in_specs=in_spe...  32.9 us
    ppermute x6, waiting for transfers between devices, per_device(): lax.ppermute(half, 'tiles', pairs['relayed'])  29.1 us
    ppermute x6, waiting for transfers between devices, send(): lax.ppermute(mine, 'tiles', pairs[x])  26.2 us
    ppermute x6, starting transfers between devices, send(): lax.ppermute(mine, 'tiles', pairs[x])  21.1 us
    ppermute x6, starting transfers between devices, per_device(): lax.ppermute(half, 'tiles', pairs['relayed'])  16.9 us
    unnamed x52, local copies, waits for them, and re-layouts  14.3 us
    pallas_call x1, Pallas kernels, text_local(): pl.pallas_call(text_kernel, grid_spec=pltpu.PrefetchScalarGridSpec(num_sc...  8.08 us
  transfers between devices with their start and end apart: 19, of which 8 were waited for; matrix products, arithmetic and copies ran while one was open for 1% of the time, Pallas kernels for 25%

profile of v10, /device:TPU:24, one launch (start us, length us, event | category | flops | bytes accessed | tf_op | source)
XLA Modules:
  0.0 207.3 jit_solution(17307909758355730351)
XLA Ops:
  1.3 1.4 copy-done
  2.7 1.4 copy-done.3
  4.1 0.7 copy-done.20
  4.8 1.6 pack_chunk.5
  6.4 1.9 collective-permute-start.1
  8.3 3.9 %collective-permute-start.2 = (bf16[528,1280]{1,0:T(8,128)(2,1)}, bf16[528,1280]{1,0:T(8,128)(2,1)}, u32[]{:S(2)}, u32[]{:S(2)}) collective-permute-start(bf16[528,1280]{1,0:T(8,128)(2,1)} %pack_chunk.5), channel_id=1, source_target_pairs={{0,12},{1,13},{4,0},{6,2},{7,3},{8,4},{9,5},{10,6},{11,7},{12,8},{... | collective-permute-start | bytes 4055048 | tf_op jit(solution)/shard_map/ppermute | solution.py:510
  12.5 1.5 copy-done.11
  14.0 8.1 %text_partials.1 = (f32[128,1792]{1,0:T(8,128)S(1)}, f32[128,1792]{1,0:T(8,128)S(1)}) custom-call(s32[17]{0:T(128)S(1)} %pad_add_fusion.1.order, s32[4]{0:T(128)S(1)} %pad_add_fusion.2.counts, bf16[256,3072]{1,0:T(8,128)(2,1)S(1)} %copy-done.11, bf16[256,3072]{1,0:T(8,128)(2,1)S(1)} %copy-done.1, bf16[256,3072]{1,0:T(8,128)(2,1)} %v_own.5, ...), custom_call_target="tpu_custom_call" | custom-call | flops 8388608 | bytes 786432 | tf_op jit(solution)/shard_map/text_partials/pallas_call | solution.py:367
  22.1 2.7 %collective-permute-start.5 = (f32[128,1792]{1,0:T(8,128)S(1)}, f32[128,1792]{1,0:T(8,128)S(1)}, u32[]{:S(2)}, u32[]{:S(2)}) collective-permute-start(f32[128,1792]{1,0:T(8,128)S(1)} %get-tuple-element.27), channel_id=1, source_target_pairs={{0,2},{1,3},{2,0},{3,1},{4,6},{5,7},{6,4},{7,5},{8,10},{9,11},{10,... | collective-permute-start | bytes 2752520 | tf_op jit(solution)/shard_map/ppermute | solution.py:526
  24.8 1.6 pack_chunk.4
  26.4 18.8 %collective-permute-done.5.refs_1_ = f32[128,1792]{1,0:T(8,128)S(1)} collective-permute-done((f32[128,1792]{1,0:T(8,128)S(1)}, f32[128,1792]{1,0:T(8,128)S(1)}, u32[]{:S(2)}, u32[]{:S(2)}) %collective-permute-start.5) | collective-permute-done | bytes 917536 | tf_op jit(solution)/shard_map/ppermute | solution.py:526
  45.2 0.8 text_merge.2
  46.0 0.8 copy-done.14
  46.7 0.8 copy-done.22
  47.5 22.0 %collective-permute-done.1.a.rest_0_ = bf16[528,1280]{1,0:T(8,128)(2,1)} collective-permute-done((bf16[528,1280]{1,0:T(8,128)(2,1)}, bf16[528,1280]{1,0:T(8,128)(2,1)}, u32[]{:S(2)}, u32[]{:S(2)}) %collective-permute-start.1) | collective-permute-done | bytes 1351712 | tf_op jit(solution)/shard_map/ppermute | solution.py:510
  69.6 2.3 %collective-permute-start.7 = (bf16[528,1024]{1,0:T(8,128)(2,1)}, bf16[528,1024]{1,0:T(8,128)(2,1)}, u32[]{:S(2)}, u32[]{:S(2)}) collective-permute-start(bf16[528,1024]{1,0:T(8,128)(2,1)} %pack_chunk.4), channel_id=1, source_target_pairs={{0,12},{1,13},{4,0},{6,2},{7,3},{8,4},{9,5},{10,6},{11,7},{12,8},{... | collective-permute-start | bytes 3244040 | tf_op jit(solution)/shard_map/ppermute | solution.py:510
  71.9 5.3 %collective-permute-start.6 = (bf16[528,1024]{1,0:T(8,128)(2,1)}, bf16[528,1024]{1,0:T(8,128)(2,1)}, u32[]{:S(2)}, u32[]{:S(2)}) collective-permute-start(bf16[528,1024]{1,0:T(8,128)(2,1)} %pack_chunk.4), channel_id=1, source_target_pairs={{2,6},{3,7},{4,8},{5,9},{6,10},{7,11},{8,12},{9,13},{10,14},{11,15... | collective-permute-start | bytes 3244040 | tf_op jit(solution)/shard_map/ppermute | solution.py:510
  77.8 3.1 %choose_relayed.3 = (bf16[272,1280]{1,0:T(8,128)(2,1)}, bf16[256,1280]{1,0:T(8,128)(2,1)}) custom-call(s32[1]{0:T(128)} %dynamic_slice.8.second, bf16[528,1280]{1,0:T(8,128)(2,1)} %collective-permute-done.1.a.rest_0_, bf16[528,1280]{1,0:T(8,128)(2,1)} %collective-permute-done.2.b.rest_1_), custom_call_target="tpu_custom_call" | custom-call | tf_op jit(solution)/shard_map/choose_relayed/pallas_call | solution.py:124
  80.9 1.9 collective-permute-start.8
  82.8 3.6 %collective-permute-start.9 = (bf16[256,1280]{1,0:T(8,128)(2,1)}, bf16[256,1280]{1,0:T(8,128)(2,1)}, u32[]{:S(2)}, u32[]{:S(2)}) collective-permute-start(bf16[256,1280]{1,0:T(8,128)(2,1)} %get-tuple-element.33), channel_id=1, source_target_pairs={{0,3},{3,0},{4,7},{7,4},{8,11},{11,8},{12,15},{15,12},{16,19},{19,... | collective-permute-start | bytes 1966088 | tf_op jit(solution)/shard_map/ppermute | solution.py:546
  86.5 0.7 pack_chunk.3
  87.2 0.9 copy-done.12
  89.4 0.7 dynamic-slice_bitcast_fusion
  90.2 10.4 %collective-permute-done.9.rest_3_ = bf16[256,1280]{1,0:T(8,128)(2,1)} collective-permute-done((bf16[256,1280]{1,0:T(8,128)(2,1)}, bf16[256,1280]{1,0:T(8,128)(2,1)}, u32[]{:S(2)}, u32[]{:S(2)}) %collective-permute-start.9) | collective-permute-done | bytes 655392 | tf_op jit(solution)/shard_map/ppermute | solution.py:546
  100.6 1.4 copy-done.5
  102.0 13.3 %video_attention.3.rest_8_ = bf16[256,3072]{1,0:T(8,128)(2,1)} custom-call(s32[13]{0:T(128)S(1)} %concatenate.18.table, bf16[256,3072]{1,0:T(8,128)(2,1)S(1)} %copy-done.5, bf16[256,3072]{1,0:T(8,128)(2,1)} %k_own.5, bf16[256,3072]{1,0:T(8,128)(2,1)} %v_own.5, bf16[528,1280]{1,0:T(8,128)(2,1)} %collective-permute-done.1.a.rest_0_, ...), custom_call_target="tpu_custom_call" | custom-call | flops 94371840 | bytes 327680 | tf_op jit(solution)/shard_map/video_attention/pallas_call | solution.py:275
  115.3 15.9 %collective-permute-done.10.refs_1_ = f32[64,1664]{1,0:T(8,128)S(1)} collective-permute-done((f32[64,1664]{1,0:T(8,128)}, f32[64,1664]{1,0:T(8,128)S(1)}, u32[]{:S(2)}, u32[]{:S(2)}) %collective-permute-start.10) | collective-permute-done | bytes 426016 | tf_op jit(solution)/shard_map/ppermute | solution.py:526
  131.2 1.1 text_merge.3
  132.3 0.7 copy-done.16
  133.0 1.9 collective-permute-start.12
  135.0 5.7 %collective-permute-start.11 = (bf16[528,768]{1,0:T(8,128)(2,1)S(1)}, bf16[528,768]{1,0:T(8,128)(2,1)S(1)}, u32[]{:S(2)}, u32[]{:S(2)}) collective-permute-start(bf16[528,768]{1,0:T(8,128)(2,1)S(1)} %copy-done.13), channel_id=1, source_target_pairs={{2,6},{3,7},{4,8},{5,9},{6,10},{7,11},{8,12},{9,13},{10,14},{11,15... | collective-permute-start | bytes 2433032 | tf_op jit(solution)/shard_map/ppermute | solution.py:510
  140.7 1.9 choose_relayed.4
  142.6 1.9 collective-permute-start.13
  144.5 3.6 %collective-permute-start.14 = (bf16[256,1024]{1,0:T(8,128)(2,1)S(1)}, bf16[256,1024]{1,0:T(8,128)(2,1)S(1)}, u32[]{:S(2)}, u32[]{:S(2)}) collective-permute-start(bf16[256,1024]{1,0:T(8,128)(2,1)S(1)} %get-tuple-element.41), channel_id=1, source_target_pairs={{0,3},{3,0},{4,7},{7,4},{8,11},{11,8},{12,15},{15,12},{16,19},{19,... | collective-permute-start | bytes 1572872 | tf_op jit(solution)/shard_map/ppermute | solution.py:546
  148.2 10.9 %collective-permute-done.14.rest_3_ = bf16[256,1024]{1,0:T(8,128)(2,1)S(1)} collective-permute-done((bf16[256,1024]{1,0:T(8,128)(2,1)S(1)}, bf16[256,1024]{1,0:T(8,128)(2,1)S(1)}, u32[]{:S(2)}, u32[]{:S(2)}) %collective-permute-start.14) | collective-permute-done | bytes 524320 | tf_op jit(solution)/shard_map/ppermute | solution.py:546
  159.1 11.0 %video_attention.4.rest_8_ = bf16[256,3072]{1,0:T(8,128)(2,1)} custom-call(s32[13]{0:T(128)S(1)} %concatenate.18.table, bf16[256,3072]{1,0:T(8,128)(2,1)S(1)} %copy-done.6, bf16[256,3072]{1,0:T(8,128)(2,1)} %k_own.5, bf16[256,3072]{1,0:T(8,128)(2,1)} %v_own.5, bf16[528,1024]{1,0:T(8,128)(2,1)} %collective-permute-done.6.a.rest_0_, ...), custom_call_target="tpu_custom_call", output_to_operand_aliasing={{}: (12, {})} | custom-call | flops 75497472 | bytes 262144 | tf_op jit(solution)/shard_map/video_attention/pallas_call | solution.py:275
  170.0 4.1 %collective-permute-done.11.a.rest_0_ = bf16[528,768]{1,0:T(8,128)(2,1)S(1)} collective-permute-done((bf16[528,768]{1,0:T(8,128)(2,1)S(1)}, bf16[528,768]{1,0:T(8,128)(2,1)S(1)}, u32[]{:S(2)}, u32[]{:S(2)}) %collective-permute-start.11) | collective-permute-done | bytes 811040 | tf_op jit(solution)/shard_map/ppermute | solution.py:510
  174.2 2.0 choose_relayed.5
  176.2 0.9 copy-done.7
  177.1 1.9 collective-permute-start.15
  179.0 3.8 %collective-permute-start.16 = (bf16[256,768]{1,0:T(8,128)(2,1)}, bf16[256,768]{1,0:T(8,128)(2,1)S(1)}, u32[]{:S(2)}, u32[]{:S(2)}) collective-permute-start(bf16[256,768]{1,0:T(8,128)(2,1)} %get-tuple-element.45), channel_id=1, source_target_pairs={{0,3},{3,0},{4,7},{7,4},{8,11},{11,8},{12,15},{15,12},{16,19},{19,... | collective-permute-start | bytes 1179656 | tf_op jit(solution)/shard_map/ppermute | solution.py:546
  183.0 7.9 %collective-permute-done.16.rest_3_ = bf16[256,768]{1,0:T(8,128)(2,1)S(1)} collective-permute-done((bf16[256,768]{1,0:T(8,128)(2,1)}, bf16[256,768]{1,0:T(8,128)(2,1)S(1)}, u32[]{:S(2)}, u32[]{:S(2)}) %collective-permute-start.16) | collective-permute-done | bytes 393248 | tf_op jit(solution)/shard_map/ppermute | solution.py:546
  191.4 0.9 copy-done.17
  192.4 1.9 text_finish.1
  194.9 1.1 copy-done.8
  196.0 1.1 copy-done.10
  197.1 8.6 %video_attention.5 = bf16[256,3072]{1,0:T(8,128)(2,1)} custom-call(s32[13]{0:T(128)S(1)} %concatenate.18.table, bf16[256,3072]{1,0:T(8,128)(2,1)S(1)} %copy-done.6, bf16[256,3072]{1,0:T(8,128)(2,1)S(1)} %copy-done.2, bf16[256,3072]{1,0:T(8,128)(2,1)} %v_own.5, bf16[528,768]{1,0:T(8,128)(2,1)S(1)} %copy-done.10, ...), custom_call_target="tpu_custom_call", output_to_operand_aliasing={{}: (12, {})} | custom-call | flops 56623104 | bytes 196608 | tf_op jit(solution)/shard_map/video_attention/pallas_call | solution.py:275
  205.8 1.5 maximum_select_fusion
  (72 shorter events, 3.6 us)
Async XLA Ops:
  0.6 11.6 %copy-start.25 = (s32[16]{0:T(128)S(1)}, s32[16]{0:T(128)}, u32[]{:S(2)}) copy-start(s32[16]{0:T(128)} %constant.76.clone) | copy-start | bytes 196
  0.6 11.8 %collective-permute-start.3 = (bf16[256,3072]{1,0:T(8,128)(2,1)}, bf16[256,3072]{1,0:T(8,128)(2,1)}, u32[]{:S(2)}, u32[]{:S(2)}) collective-permute-start(bf16[256,3072]{1,0:T(8,128)(2,1)} %k_own.5), channel_id=1, source_target_pairs={{0,1},{1,0},{2,3},{3,2},{4,5},{5,4},{6,7},{7,6},{8,9},{9,8},{10,11... | collective-permute-start | bytes 4718600 | tf_op jit(solution)/shard_map/ppermute | solution.py:514
  0.7 11.7 %collective-permute-start.4 = (bf16[256,3072]{1,0:T(8,128)(2,1)}, bf16[256,3072]{1,0:T(8,128)(2,1)}, u32[]{:S(2)}, u32[]{:S(2)}) collective-permute-start(bf16[256,3072]{1,0:T(8,128)(2,1)} %v_own.5), channel_id=1, source_target_pairs={{0,1},{1,0},{2,3},{3,2},{4,5},{5,4},{6,7},{7,6},{8,9},{9,8},{10,11... | collective-permute-start | bytes 4718600 | tf_op jit(solution)/shard_map/ppermute | solution.py:514
  1.2 11.2 %collective-permute-start = (s32[2]{0:T(128)}, s32[2]{0:T(128)S(1)}, u32[]{:S(2)}, u32[]{:S(2)}) collective-permute-start(s32[2]{0:T(128)} %counts.5), channel_id=1, source_target_pairs={{0,1},{1,0},{2,3},{3,2},{4,5},{5,4},{6,7},{7,6},{8,9},{9,8},{10,11... | collective-permute-start | bytes 32 | tf_op jit(solution)/shard_map/ppermute | solution.py:514
  1.3 1.4 copy-start
  2.7 1.4 copy-start.3
  4.1 0.7 copy-start.20
  4.8 7.6 %copy-start.21 = (s32[2]{0:T(128)S(1)}, s32[2]{0:T(128)}, u32[]{:S(2)}) copy-start(s32[2]{0:T(128)} %counts.5) | copy-start | bytes 28
  4.8 7.7 %copy-start.1 = (bf16[256,3072]{1,0:T(8,128)(2,1)S(1)}, bf16[256,3072]{1,0:T(8,128)(2,1)}, u32[]{:S(2)}) copy-start(bf16[256,3072]{1,0:T(8,128)(2,1)} %k_own.5) | copy-start | bytes 4718596
  6.4 63.2 %collective-permute-start.1 = (bf16[528,1280]{1,0:T(8,128)(2,1)}, bf16[528,1280]{1,0:T(8,128)(2,1)}, u32[]{:S(2)}, u32[]{:S(2)}) collective-permute-start(bf16[528,1280]{1,0:T(8,128)(2,1)} %pack_chunk.5), channel_id=1, source_target_pairs={{2,6},{3,7},{4,8},{5,9},{6,10},{7,11},{8,12},{9,13},{10,14},{11,15... | collective-permute-start | bytes 4055048 | tf_op jit(solution)/shard_map/ppermute | solution.py:510
  8.3 61.3 %collective-permute-start.2 = (bf16[528,1280]{1,0:T(8,128)(2,1)}, bf16[528,1280]{1,0:T(8,128)(2,1)}, u32[]{:S(2)}, u32[]{:S(2)}) collective-permute-start(bf16[528,1280]{1,0:T(8,128)(2,1)} %pack_chunk.5), channel_id=1, source_target_pairs={{0,12},{1,13},{4,0},{6,2},{7,3},{8,4},{9,5},{10,6},{11,7},{12,8},{... | collective-permute-start | bytes 4055048 | tf_op jit(solution)/shard_map/ppermute | solution.py:510
  12.5 12.3 %copy-start.4 = (bf16[256,3072]{1,0:T(8,128)(2,1)S(1)}, bf16[256,3072]{1,0:T(8,128)(2,1)}, u32[]{:S(2)}) copy-start(bf16[256,3072]{1,0:T(8,128)(2,1)} %v_own.5) | copy-start | bytes 4718596
  12.5 1.5 copy-start.11
  22.1 23.1 %collective-permute-start.5 = (f32[128,1792]{1,0:T(8,128)S(1)}, f32[128,1792]{1,0:T(8,128)S(1)}, u32[]{:S(2)}, u32[]{:S(2)}) collective-permute-start(f32[128,1792]{1,0:T(8,128)S(1)} %get-tuple-element.27), channel_id=1, source_target_pairs={{0,2},{1,3},{2,0},{3,1},{4,6},{5,7},{6,4},{7,5},{8,10},{9,11},{10,... | collective-permute-start | bytes 2752520 | tf_op jit(solution)/shard_map/ppermute | solution.py:526
  26.3 50.9 %copy-start.24 = (s32[16]{0:T(128)S(1)}, s32[16]{0:T(128)}, u32[]{:S(2)}) copy-start(s32[16]{0:T(128)} %constant.74.clone) | copy-start | bytes 196
  46.0 0.8 copy-start.14
  46.7 0.8 copy-start.22
  47.5 39.0 %copy-start.23 = (s32[2,6]{1,0:T(2,128)S(1)}, s32[2,6]{1,0:T(2,128)}, u32[]{:S(2)}) copy-start(s32[2,6]{1,0:T(2,128)} %param.18) | copy-start | bytes 148
  69.6 63.4 %collective-permute-start.7 = (bf16[528,1024]{1,0:T(8,128)(2,1)}, bf16[528,1024]{1,0:T(8,128)(2,1)}, u32[]{:S(2)}, u32[]{:S(2)}) collective-permute-start(bf16[528,1024]{1,0:T(8,128)(2,1)} %pack_chunk.4), channel_id=1, source_target_pairs={{0,12},{1,13},{4,0},{6,2},{7,3},{8,4},{9,5},{10,6},{11,7},{12,8},{... | collective-permute-start | bytes 3244040 | tf_op jit(solution)/shard_map/ppermute | solution.py:510
  71.9 61.1 %collective-permute-start.6 = (bf16[528,1024]{1,0:T(8,128)(2,1)}, bf16[528,1024]{1,0:T(8,128)(2,1)}, u32[]{:S(2)}, u32[]{:S(2)}) collective-permute-start(bf16[528,1024]{1,0:T(8,128)(2,1)} %pack_chunk.4), channel_id=1, source_target_pairs={{2,6},{3,7},{4,8},{5,9},{6,10},{7,11},{8,12},{9,13},{10,14},{11,15... | collective-permute-start | bytes 3244040 | tf_op jit(solution)/shard_map/ppermute | solution.py:510
  80.9 19.7 %collective-permute-start.8 = (bf16[272,1280]{1,0:T(8,128)(2,1)}, bf16[272,1280]{1,0:T(8,128)(2,1)}, u32[]{:S(2)}, u32[]{:S(2)}) collective-permute-start(bf16[272,1280]{1,0:T(8,128)(2,1)} %get-tuple-element.32), channel_id=1, source_target_pairs={{0,3},{3,0},{4,7},{7,4},{8,11},{11,8},{12,15},{15,12},{16,19},{19,... | collective-permute-start | bytes 2088968 | tf_op jit(solution)/shard_map/ppermute | solution.py:546
  82.8 17.8 %collective-permute-start.9 = (bf16[256,1280]{1,0:T(8,128)(2,1)}, bf16[256,1280]{1,0:T(8,128)(2,1)}, u32[]{:S(2)}, u32[]{:S(2)}) collective-permute-start(bf16[256,1280]{1,0:T(8,128)(2,1)} %get-tuple-element.33), channel_id=1, source_target_pairs={{0,3},{3,0},{4,7},{7,4},{8,11},{11,8},{12,15},{15,12},{16,19},{19,... | collective-permute-start | bytes 1966088 | tf_op jit(solution)/shard_map/ppermute | solution.py:546
  87.2 0.9 copy-start.12
  88.4 42.8 %collective-permute-start.10 = (f32[64,1664]{1,0:T(8,128)}, f32[64,1664]{1,0:T(8,128)S(1)}, u32[]{:S(2)}, u32[]{:S(2)}) collective-permute-start(f32[64,1664]{1,0:T(8,128)} %copy-done.22), channel_id=1, source_target_pairs={{0,4},{1,5},{2,6},{3,7},{4,0},{5,1},{6,2},{7,3},{8,12},{9,13},{10,... | collective-permute-start | bytes 1277960 | tf_op jit(solution)/shard_map/ppermute | solution.py:526
  100.6 1.4 copy-start.5
  102.0 29.2 %copy-start.15 = (f32[64,1664]{1,0:T(8,128)S(1)}, f32[64,1664]{1,0:T(8,128)}, u32[]{:S(2)}) copy-start(f32[64,1664]{1,0:T(8,128)} %copy-done.14) | copy-start | bytes 1277956
  102.0 31.0 %copy-start.13 = (bf16[528,768]{1,0:T(8,128)(2,1)S(1)}, bf16[528,768]{1,0:T(8,128)(2,1)}, u32[]{:S(2)}) copy-start(bf16[528,768]{1,0:T(8,128)(2,1)} %copy-done.12) | copy-start | bytes 2433028
  115.3 43.7 %copy-start.6 = (bf16[256,3072]{1,0:T(8,128)(2,1)S(1)}, bf16[256,3072]{1,0:T(8,128)(2,1)}, u32[]{:S(2)}) copy-start(bf16[256,3072]{1,0:T(8,128)(2,1)} %q.7) | copy-start | bytes 4718596
  132.3 0.7 copy-start.16
  133.0 37.0 %collective-permute-start.12 = (bf16[528,768]{1,0:T(8,128)(2,1)S(1)}, bf16[528,768]{1,0:T(8,128)(2,1)S(1)}, u32[]{:S(2)}, u32[]{:S(2)}) collective-permute-start(bf16[528,768]{1,0:T(8,128)(2,1)S(1)} %copy-done.13), channel_id=1, source_target_pairs={{0,12},{1,13},{4,0},{6,2},{7,3},{8,4},{9,5},{10,6},{11,7},{12,8},{... | collective-permute-start | bytes 2433032 | tf_op jit(solution)/shard_map/ppermute | solution.py:510
  135.0 39.2 %collective-permute-start.11 = (bf16[528,768]{1,0:T(8,128)(2,1)S(1)}, bf16[528,768]{1,0:T(8,128)(2,1)S(1)}, u32[]{:S(2)}, u32[]{:S(2)}) collective-permute-start(bf16[528,768]{1,0:T(8,128)(2,1)S(1)} %copy-done.13), channel_id=1, source_target_pairs={{2,6},{3,7},{4,8},{5,9},{6,10},{7,11},{8,12},{9,13},{10,14},{11,15... | collective-permute-start | bytes 2433032 | tf_op jit(solution)/shard_map/ppermute | solution.py:510
  142.6 16.5 %collective-permute-start.13 = (bf16[272,1024]{1,0:T(8,128)(2,1)S(1)}, bf16[272,1024]{1,0:T(8,128)(2,1)S(1)}, u32[]{:S(2)}, u32[]{:S(2)}) collective-permute-start(bf16[272,1024]{1,0:T(8,128)(2,1)S(1)} %get-tuple-element.40), channel_id=1, source_target_pairs={{0,3},{3,0},{4,7},{7,4},{8,11},{11,8},{12,15},{15,12},{16,19},{19,... | collective-permute-start | bytes 1671176 | tf_op jit(solution)/shard_map/ppermute | solution.py:546
  144.5 14.5 %collective-permute-start.14 = (bf16[256,1024]{1,0:T(8,128)(2,1)S(1)}, bf16[256,1024]{1,0:T(8,128)(2,1)S(1)}, u32[]{:S(2)}, u32[]{:S(2)}) collective-permute-start(bf16[256,1024]{1,0:T(8,128)(2,1)S(1)} %get-tuple-element.41), channel_id=1, source_target_pairs={{0,3},{3,0},{4,7},{7,4},{8,11},{11,8},{12,15},{15,12},{16,19},{19,... | collective-permute-start | bytes 1572872 | tf_op jit(solution)/shard_map/ppermute | solution.py:546
  170.0 24.8 %copy-start.2 = (bf16[256,3072]{1,0:T(8,128)(2,1)S(1)}, bf16[256,3072]{1,0:T(8,128)(2,1)}, u32[]{:S(2)}) copy-start(bf16[256,3072]{1,0:T(8,128)(2,1)} %k_own.5) | copy-start | bytes 4718596
  174.2 2.0 copy-start.9
  176.2 0.9 copy-start.7
  177.1 13.8 %collective-permute-start.15 = (bf16[272,768]{1,0:T(8,128)(2,1)}, bf16[272,768]{1,0:T(8,128)(2,1)}, u32[]{:S(2)}, u32[]{:S(2)}) collective-permute-start(bf16[272,768]{1,0:T(8,128)(2,1)} %get-tuple-element.44), channel_id=1, source_target_pairs={{0,3},{3,0},{4,7},{7,4},{8,11},{11,8},{12,15},{15,12},{16,19},{19,... | collective-permute-start | bytes 1253384 | tf_op jit(solution)/shard_map/ppermute | solution.py:546
  179.0 11.9 %collective-permute-start.16 = (bf16[256,768]{1,0:T(8,128)(2,1)}, bf16[256,768]{1,0:T(8,128)(2,1)S(1)}, u32[]{:S(2)}, u32[]{:S(2)}) collective-permute-start(bf16[256,768]{1,0:T(8,128)(2,1)} %get-tuple-element.45), channel_id=1, source_target_pairs={{0,3},{3,0},{4,7},{7,4},{8,11},{11,8},{12,15},{15,12},{16,19},{19,... | collective-permute-start | bytes 1179656 | tf_op jit(solution)/shard_map/ppermute | solution.py:546
  182.9 8.6 %collective-permute-start.17 = (f32[32,1664]{1,0:T(8,128)}, f32[32,1664]{1,0:T(8,128)}, u32[]{:S(2)}, u32[]{:S(2)}) collective-permute-start(f32[32,1664]{1,0:T(8,128)} %get-tuple-element.47), channel_id=1, source_target_pairs={{0,8},{1,9},{2,10},{3,11},{4,12},{5,13},{6,14},{7,15},{8,0},{9,1},... | collective-permute-start | bytes 638984 | tf_op jit(solution)/shard_map/ppermute | solution.py:526
  191.4 0.9 copy-start.17
  194.2 0.6 copy-start.18
  194.8 10.9 %collective-permute-start.18 = (bf16[16,1536]{1,0:T(8,128)(2,1)}, bf16[16,1536]{1,0:T(8,128)(2,1)}, u32[]{:S(2)}, u32[]{:S(2)}) collective-permute-start(bf16[16,1536]{1,0:T(8,128)(2,1)} %get-tuple-element.49), channel_id=1, source_target_pairs={{0,1},{1,0},{2,3},{3,2},{4,5},{5,4},{6,7},{7,6},{8,9},{9,8},{10,11... | collective-permute-start | bytes 147464 | tf_op jit(solution)/shard_map/ppermute | solution.py:561
  194.9 1.1 copy-start.8
  196.0 1.1 copy-start.10
  197.1 8.6 %copy-start.19 = (bf16[16,1536]{1,0:T(8,128)(2,1)S(1)}, bf16[16,1536]{1,0:T(8,128)(2,1)}, u32[]{:S(2)}) copy-start(bf16[16,1536]{1,0:T(8,128)(2,1)} %copy-done.18) | copy-start | bytes 147460

commit v11 on v10

--- a/solution.py
+++ b/solution.py
@@ -13,7 +13,7 @@
 NR = 4
 BLOCKS = 5
 STEP_HEADS = 2
-CHUNK_HEADS = (10, 8, 6)
+CHUNK_HEADS = (12, 8, 4)
 PAD_ROWS = 16
 VMEM_BYTES = 48 * 1024 * 1024
 LOG2E = 1.4426950408889634
@@ -538,7 +538,7 @@
     merge()
     count = len(CHUNK_HEADS)
     for i in range(count):
-        before = outs[i - 1 : i] + ([parts[-1][0]] if halving and i < 2 else [])
+        before = outs[i - 1 : i] + ([parts[-1][0]] if halving and i == 0 else [])
         if i + 1 < count:
             send(i + 1, *direct[i], *before)
         up, down = tie(direct[i][0], *before), tie(direct[i][1], *before)

time: 211 us -> 203 us (0.962)
  local copies, waits for them, and re-layouts: 15.9 us -> 12.7 us
  waiting for transfers between devices: 90.6 us -> 88.3 us
    ppermute x3, waiting for transfers between devices: 35.2 us -> 27.4 us  [exchanged(): lax.ppermute(parts[i][1], 'tiles', [(d, d ^ 2 << i) for d in range(n)])]
    ppermute x6, waiting for transfers between devices: 26.2 us -> 33.5 us  [send(): lax.ppermute(mine, 'tiles', pairs[x])]
    unnamed x52 -> x46, local copies, waits for them, and re-layouts: 14.3 us -> 10.4 us
    ppermute x6, waiting for transfers between devices: 29.1 us -> 26.2 us  [per_device(): lax.ppermute(half, 'tiles', pairs['relayed'])]
  transfers between devices with their start and end apart: 19 -> 19, of which waited for: 8 -> 8; matrix products, arithmetic and copies ran while one was open for 1% -> 2% of each run, Pallas kernels for 25% -> 26%
where the time goes in v11:
time: 203 us; the launch traced here: 201 us
  waiting for transfers between devices  88.3 us (43%)
  Pallas kernels  55.5 us (27%)
  starting transfers between devices  39.8 us (20%)
  local copies, waits for them, and re-layouts  12.7 us (6%)
  other arithmetic  2.8 us (1%)
    ppermute x6, waiting for transfers between devices, send(): lax.ppermute(mine, 'tiles', pairs[x])  33.5 us
    pallas_call x3, Pallas kernels, video_call(): pl.pallas_call(video_kernel, grid=(heads // STEP_HEADS,), in_specs=in_spe...  32.8 us
    ppermute x3, waiting for transfers between devices, exchanged(): lax.ppermute(parts[i][1], 'tiles', [(d, d ^ 2 << i) for d in range(n)])  27.4 us
    ppermute x6, waiting for transfers between devices, per_device(): lax.ppermute(half, 'tiles', pairs['relayed'])  26.2 us
    ppermute x6, starting transfers between devices, send(): lax.ppermute(mine, 'tiles', pairs[x])  21.1 us
    ppermute x6, starting transfers between devices, per_device(): lax.ppermute(half, 'tiles', pairs['relayed'])  15.1 us
    unnamed x46, local copies, waits for them, and re-layouts  10.4 us
    pallas_call x1, Pallas kernels, text_local(): pl.pallas_call(text_kernel, grid_spec=pltpu.PrefetchScalarGridSpec(num_sc...  8.08 us
  transfers between devices with their start and end apart: 19, of which 8 were waited for; matrix products, arithmetic and copies ran while one was open for 2% of the time, Pallas kernels for 26%

profile of v11, /device:TPU:24, one launch (start us, length us, event | category | flops | bytes accessed | tf_op | source)
XLA Modules:
  0.0 200.7 jit_solution(15249321513550244832)
XLA Ops:
  1.2 1.4 copy-done
  2.6 1.4 copy-done.3
  4.0 2.0 %pack_chunk.5 = bf16[528,1536]{1,0:T(8,128)(2,1)} custom-call(s32[2]{0:T(128)} %counts.5, bf16[256,3072]{1,0:T(8,128)(2,1)S(1)} %copy-done, bf16[256,3072]{1,0:T(8,128)(2,1)S(1)} %copy-done.3), custom_call_target="tpu_custom_call" | custom-call | tf_op jit(solution)/shard_map/pack_chunk/pallas_call | solution.py:91
  6.1 1.9 collective-permute-start.1
  8.0 3.9 %collective-permute-start.2 = (bf16[528,1536]{1,0:T(8,128)(2,1)}, bf16[528,1536]{1,0:T(8,128)(2,1)}, u32[]{:S(2)}, u32[]{:S(2)}) collective-permute-start(bf16[528,1536]{1,0:T(8,128)(2,1)} %pack_chunk.5), channel_id=1, source_target_pairs={{0,12},{1,13},{4,0},{6,2},{7,3},{8,4},{9,5},{10,6},{11,7},{12,8},{... | collective-permute-start | bytes 4866056 | tf_op jit(solution)/shard_map/ppermute | solution.py:510
  12.1 1.1 collective-permute-done
  13.2 0.7 pad_add_fusion.2.counts
  14.0 1.5 copy-done.13
  15.5 8.1 %text_partials.1 = (f32[128,1792]{1,0:T(8,128)S(1)}, f32[128,1792]{1,0:T(8,128)S(1)}) custom-call(s32[17]{0:T(128)S(1)} %pad_add_fusion.1.order, s32[4]{0:T(128)S(1)} %pad_add_fusion.2.counts, bf16[256,3072]{1,0:T(8,128)(2,1)S(1)} %copy-done.13, bf16[256,3072]{1,0:T(8,128)(2,1)S(1)} %copy-done.1, bf16[256,3072]{1,0:T(8,128)(2,1)} %v_own.5, ...), custom_call_target="tpu_custom_call" | custom-call | flops 8388608 | bytes 786432 | tf_op jit(solution)/shard_map/text_partials/pallas_call | solution.py:367
  23.6 2.8 %collective-permute-start.5 = (f32[128,1792]{1,0:T(8,128)S(1)}, f32[128,1792]{1,0:T(8,128)S(1)}, u32[]{:S(2)}, u32[]{:S(2)}) collective-permute-start(f32[128,1792]{1,0:T(8,128)S(1)} %get-tuple-element.27), channel_id=1, source_target_pairs={{0,2},{1,3},{2,0},{3,1},{4,6},{5,7},{6,4},{7,5},{8,10},{9,11},{10,... | collective-permute-start | bytes 2752520 | tf_op jit(solution)/shard_map/ppermute | solution.py:526
  26.4 1.7 pack_chunk.4
  28.1 19.0 %collective-permute-done.5.refs_1_ = f32[128,1792]{1,0:T(8,128)S(1)} collective-permute-done((f32[128,1792]{1,0:T(8,128)S(1)}, f32[128,1792]{1,0:T(8,128)S(1)}, u32[]{:S(2)}, u32[]{:S(2)}) %collective-permute-start.5) | collective-permute-done | bytes 917536 | tf_op jit(solution)/shard_map/ppermute | solution.py:526
  47.1 0.8 text_merge.2
  47.9 0.8 copy-done.14
  48.6 0.8 copy-done.18
  49.4 31.0 %collective-permute-done.1.a.rest_0_ = bf16[528,1536]{1,0:T(8,128)(2,1)} collective-permute-done((bf16[528,1536]{1,0:T(8,128)(2,1)}, bf16[528,1536]{1,0:T(8,128)(2,1)}, u32[]{:S(2)}, u32[]{:S(2)}) %collective-permute-start.1) | collective-permute-done | bytes 1622048 | tf_op jit(solution)/shard_map/ppermute | solution.py:510
  80.5 2.3 %collective-permute-start.7 = (bf16[528,1024]{1,0:T(8,128)(2,1)}, bf16[528,1024]{1,0:T(8,128)(2,1)}, u32[]{:S(2)}, u32[]{:S(2)}) collective-permute-start(bf16[528,1024]{1,0:T(8,128)(2,1)} %pack_chunk.4), channel_id=1, source_target_pairs={{0,12},{1,13},{4,0},{6,2},{7,3},{8,4},{9,5},{10,6},{11,7},{12,8},{... | collective-permute-start | bytes 3244040 | tf_op jit(solution)/shard_map/ppermute | solution.py:510
  82.8 5.3 %collective-permute-start.6 = (bf16[528,1024]{1,0:T(8,128)(2,1)}, bf16[528,1024]{1,0:T(8,128)(2,1)}, u32[]{:S(2)}, u32[]{:S(2)}) collective-permute-start(bf16[528,1024]{1,0:T(8,128)(2,1)} %pack_chunk.4), channel_id=1, source_target_pairs={{2,6},{3,7},{4,8},{5,9},{6,10},{7,11},{8,12},{9,13},{10,14},{11,15... | collective-permute-start | bytes 3244040 | tf_op jit(solution)/shard_map/ppermute | solution.py:510
  88.7 3.4 %choose_relayed.3 = (bf16[272,1536]{1,0:T(8,128)(2,1)}, bf16[256,1536]{1,0:T(8,128)(2,1)}) custom-call(s32[1]{0:T(128)} %dynamic_slice.8.second, bf16[528,1536]{1,0:T(8,128)(2,1)} %collective-permute-done.1.a.rest_0_, bf16[528,1536]{1,0:T(8,128)(2,1)} %collective-permute-done.2.b.rest_1_), custom_call_target="tpu_custom_call" | custom-call | tf_op jit(solution)/shard_map/choose_relayed/pallas_call | solution.py:124
  92.1 1.9 collective-permute-start.8
  94.1 3.6 %collective-permute-start.9 = (bf16[256,1536]{1,0:T(8,128)(2,1)}, bf16[256,1536]{1,0:T(8,128)(2,1)}, u32[]{:S(2)}, u32[]{:S(2)}) collective-permute-start(bf16[256,1536]{1,0:T(8,128)(2,1)} %get-tuple-element.33), channel_id=1, source_target_pairs={{0,3},{3,0},{4,7},{7,4},{8,11},{11,8},{12,15},{15,12},{16,19},{19,... | collective-permute-start | bytes 2359304 | tf_op jit(solution)/shard_map/ppermute | solution.py:546
  99.0 0.7 dynamic-slice_bitcast_fusion
  99.7 0.7 concatenate.18.table
  100.5 14.2 %collective-permute-done.9.rest_3_ = bf16[256,1536]{1,0:T(8,128)(2,1)} collective-permute-done((bf16[256,1536]{1,0:T(8,128)(2,1)}, bf16[256,1536]{1,0:T(8,128)(2,1)}, u32[]{:S(2)}, u32[]{:S(2)}) %collective-permute-start.9) | collective-permute-done | bytes 786464 | tf_op jit(solution)/shard_map/ppermute | solution.py:546
  114.7 15.5 %video_attention.3.rest_8_ = bf16[256,3072]{1,0:T(8,128)(2,1)} custom-call(s32[13]{0:T(128)S(1)} %concatenate.18.table, bf16[256,3072]{1,0:T(8,128)(2,1)S(1)} %copy-done.6, bf16[256,3072]{1,0:T(8,128)(2,1)S(1)} %copy-done.1, bf16[256,3072]{1,0:T(8,128)(2,1)} %v_own.5, bf16[528,1536]{1,0:T(8,128)(2,1)} %collective-permute-done.1.a.rest_0_, ...), custom_call_target="tpu_custom_call" | custom-call | flops 113246208 | bytes 393216 | tf_op jit(solution)/shard_map/video_attention/pallas_call | solution.py:275
  130.2 2.5 %collective-permute-done.6.a.rest_0_ = bf16[528,1024]{1,0:T(8,128)(2,1)} collective-permute-done((bf16[528,1024]{1,0:T(8,128)(2,1)}, bf16[528,1024]{1,0:T(8,128)(2,1)}, u32[]{:S(2)}, u32[]{:S(2)}) %collective-permute-start.6) | collective-permute-done | bytes 1081376 | tf_op jit(solution)/shard_map/ppermute | solution.py:510
  132.6 1.9 choose_relayed.4
  134.6 2.1 %collective-permute-start.12 = (bf16[272,1024]{1,0:T(8,128)(2,1)S(1)}, bf16[272,1024]{1,0:T(8,128)(2,1)S(1)}, u32[]{:S(2)}, u32[]{:S(2)}) collective-permute-start(bf16[272,1024]{1,0:T(8,128)(2,1)S(1)} %get-tuple-element.37), channel_id=1, source_target_pairs={{0,3},{3,0},{4,7},{7,4},{8,11},{11,8},{12,15},{15,12},{16,19},{19,... | collective-permute-start | bytes 1671176 | tf_op jit(solution)/shard_map/ppermute | solution.py:546
  136.6 0.8 pack_chunk.3
  137.4 2.5 %collective-permute-start.11 = (bf16[528,512]{1,0:T(8,128)(2,1)S(1)}, bf16[528,512]{1,0:T(8,128)(2,1)S(1)}, u32[]{:S(2)}, u32[]{:S(2)}) collective-permute-start(bf16[528,512]{1,0:T(8,128)(2,1)S(1)} %pack_chunk.3), channel_id=1, source_target_pairs={{0,12},{1,13},{4,0},{6,2},{7,3},{8,4},{9,5},{10,6},{11,7},{12,8},{... | collective-permute-start | bytes 1622024 | tf_op jit(solution)/shard_map/ppermute | solution.py:510
  139.9 5.2 %collective-permute-start.10 = (bf16[528,512]{1,0:T(8,128)(2,1)S(1)}, bf16[528,512]{1,0:T(8,128)(2,1)S(1)}, u32[]{:S(2)}, u32[]{:S(2)}) collective-permute-start(bf16[528,512]{1,0:T(8,128)(2,1)S(1)} %pack_chunk.3), channel_id=1, source_target_pairs={{2,6},{3,7},{4,8},{5,9},{6,10},{7,11},{8,12},{9,13},{10,14},{11,15... | collective-permute-start | bytes 1622024 | tf_op jit(solution)/shard_map/ppermute | solution.py:510
  145.0 1.9 collective-permute-start.13
  147.1 8.5 %collective-permute-done.13.rest_3_ = bf16[256,1024]{1,0:T(8,128)(2,1)S(1)} collective-permute-done((bf16[256,1024]{1,0:T(8,128)(2,1)S(1)}, bf16[256,1024]{1,0:T(8,128)(2,1)S(1)}, u32[]{:S(2)}, u32[]{:S(2)}) %collective-permute-start.13) | collective-permute-done | bytes 524320 | tf_op jit(solution)/shard_map/ppermute | solution.py:546
  155.6 11.1 %video_attention.4.rest_8_ = bf16[256,3072]{1,0:T(8,128)(2,1)} custom-call(s32[13]{0:T(128)S(1)} %concatenate.18.table, bf16[256,3072]{1,0:T(8,128)(2,1)S(1)} %copy-done.7, bf16[256,3072]{1,0:T(8,128)(2,1)} %k_own.5, bf16[256,3072]{1,0:T(8,128)(2,1)} %v_own.5, bf16[528,1024]{1,0:T(8,128)(2,1)} %collective-permute-done.6.a.rest_0_, ...), custom_call_target="tpu_custom_call", output_to_operand_aliasing={{}: (12, {})} | custom-call | flops 75497472 | bytes 262144 | tf_op jit(solution)/shard_map/video_attention/pallas_call | solution.py:275
  166.7 1.7 choose_relayed.5
  168.4 0.8 copy-done.9
  169.2 1.9 collective-permute-start.14
  171.1 3.6 %collective-permute-start.15 = (bf16[256,512]{1,0:T(8,128)(2,1)}, bf16[256,512]{1,0:T(8,128)(2,1)}, u32[]{:S(2)}, u32[]{:S(2)}) collective-permute-start(bf16[256,512]{1,0:T(8,128)(2,1)} %get-tuple-element.42), channel_id=1, source_target_pairs={{0,3},{3,0},{4,7},{7,4},{8,11},{11,8},{12,15},{15,12},{16,19},{19,... | collective-permute-start | bytes 786440 | tf_op jit(solution)/shard_map/ppermute | solution.py:546
  174.8 1.1 text_merge.3
  175.9 0.7 copy-done.16
  176.7 3.5 %collective-permute-done.15.rest_3_ = bf16[256,512]{1,0:T(8,128)(2,1)} collective-permute-done((bf16[256,512]{1,0:T(8,128)(2,1)}, bf16[256,512]{1,0:T(8,128)(2,1)}, u32[]{:S(2)}, u32[]{:S(2)}) %collective-permute-start.15) | collective-permute-done | bytes 262176 | tf_op jit(solution)/shard_map/ppermute | solution.py:546
  180.2 8.3 %collective-permute-done.17.refs_1_ = f32[32,1664]{1,0:T(8,128)} collective-permute-done((f32[32,1664]{1,0:T(8,128)}, f32[32,1664]{1,0:T(8,128)}, u32[]{:S(2)}, u32[]{:S(2)}) %collective-permute-start.17) | collective-permute-done | bytes 213024 | tf_op jit(solution)/shard_map/ppermute | solution.py:526
  188.5 0.9 copy-done.17
  189.4 1.2 text_finish.1
  190.8 1.0 copy-done.10
  191.8 1.0 copy-done.12
  192.9 6.3 %video_attention.5 = bf16[256,3072]{1,0:T(8,128)(2,1)} custom-call(s32[13]{0:T(128)S(1)} %concatenate.18.table, bf16[256,3072]{1,0:T(8,128)(2,1)S(1)} %copy-done.8, bf16[256,3072]{1,0:T(8,128)(2,1)S(1)} %copy-done.2, bf16[256,3072]{1,0:T(8,128)(2,1)} %v_own.5, bf16[528,512]{1,0:T(8,128)(2,1)S(1)} %copy-done.12, ...), custom_call_target="tpu_custom_call", output_to_operand_aliasing={{}: (12, {})} | custom-call | flops 37748736 | bytes 131072 | tf_op jit(solution)/shard_map/video_attention/pallas_call | solution.py:275
  199.2 1.5 maximum_select_fusion
  (66 shorter events, 2.3 us)
Async XLA Ops:
  0.6 11.4 %copy-start.22 = (s32[16]{0:T(128)S(1)}, s32[16]{0:T(128)}, u32[]{:S(2)}) copy-start(s32[16]{0:T(128)} %constant.76.clone) | copy-start | bytes 196
  0.6 13.3 %collective-permute-start.3 = (bf16[256,3072]{1,0:T(8,128)(2,1)}, bf16[256,3072]{1,0:T(8,128)(2,1)}, u32[]{:S(2)}, u32[]{:S(2)}) collective-permute-start(bf16[256,3072]{1,0:T(8,128)(2,1)} %k_own.5), channel_id=1, source_target_pairs={{0,1},{1,0},{2,3},{3,2},{4,5},{5,4},{6,7},{7,6},{8,9},{9,8},{10,11... | collective-permute-start | bytes 4718600 | tf_op jit(solution)/shard_map/ppermute | solution.py:514
  0.7 13.3 %collective-permute-start.4 = (bf16[256,3072]{1,0:T(8,128)(2,1)}, bf16[256,3072]{1,0:T(8,128)(2,1)}, u32[]{:S(2)}, u32[]{:S(2)}) collective-permute-start(bf16[256,3072]{1,0:T(8,128)(2,1)} %v_own.5), channel_id=1, source_target_pairs={{0,1},{1,0},{2,3},{3,2},{4,5},{5,4},{6,7},{7,6},{8,9},{9,8},{10,11... | collective-permute-start | bytes 4718600 | tf_op jit(solution)/shard_map/ppermute | solution.py:514
  1.2 1.4 copy-start
  2.6 1.4 copy-start.3
  4.0 9.9 %copy-start.1 = (bf16[256,3072]{1,0:T(8,128)(2,1)S(1)}, bf16[256,3072]{1,0:T(8,128)(2,1)}, u32[]{:S(2)}) copy-start(bf16[256,3072]{1,0:T(8,128)(2,1)} %k_own.5) | copy-start | bytes 4718596
  6.1 74.4 %collective-permute-start.1 = (bf16[528,1536]{1,0:T(8,128)(2,1)}, bf16[528,1536]{1,0:T(8,128)(2,1)}, u32[]{:S(2)}, u32[]{:S(2)}) collective-permute-start(bf16[528,1536]{1,0:T(8,128)(2,1)} %pack_chunk.5), channel_id=1, source_target_pairs={{2,6},{3,7},{4,8},{5,9},{6,10},{7,11},{8,12},{9,13},{10,14},{11,15... | collective-permute-start | bytes 4866056 | tf_op jit(solution)/shard_map/ppermute | solution.py:510
  8.0 72.5 %collective-permute-start.2 = (bf16[528,1536]{1,0:T(8,128)(2,1)}, bf16[528,1536]{1,0:T(8,128)(2,1)}, u32[]{:S(2)}, u32[]{:S(2)}) collective-permute-start(bf16[528,1536]{1,0:T(8,128)(2,1)} %pack_chunk.5), channel_id=1, source_target_pairs={{0,12},{1,13},{4,0},{6,2},{7,3},{8,4},{9,5},{10,6},{11,7},{12,8},{... | collective-permute-start | bytes 4866056 | tf_op jit(solution)/shard_map/ppermute | solution.py:510
  11.9 1.3 collective-permute-start
  14.0 12.4 %copy-start.4 = (bf16[256,3072]{1,0:T(8,128)(2,1)S(1)}, bf16[256,3072]{1,0:T(8,128)(2,1)}, u32[]{:S(2)}) copy-start(bf16[256,3072]{1,0:T(8,128)(2,1)} %v_own.5) | copy-start | bytes 4718596
  14.0 1.5 copy-start.13
  23.6 23.5 %collective-permute-start.5 = (f32[128,1792]{1,0:T(8,128)S(1)}, f32[128,1792]{1,0:T(8,128)S(1)}, u32[]{:S(2)}, u32[]{:S(2)}) collective-permute-start(f32[128,1792]{1,0:T(8,128)S(1)} %get-tuple-element.27), channel_id=1, source_target_pairs={{0,2},{1,3},{2,0},{3,1},{4,6},{5,7},{6,4},{7,5},{8,10},{9,11},{10,... | collective-permute-start | bytes 2752520 | tf_op jit(solution)/shard_map/ppermute | solution.py:526
  28.0 60.1 %copy-start.21 = (s32[16]{0:T(128)S(1)}, s32[16]{0:T(128)}, u32[]{:S(2)}) copy-start(s32[16]{0:T(128)} %constant.74.clone) | copy-start | bytes 196
  47.9 0.8 copy-start.14
  48.6 0.8 copy-start.18
  80.5 49.7 %collective-permute-start.7 = (bf16[528,1024]{1,0:T(8,128)(2,1)}, bf16[528,1024]{1,0:T(8,128)(2,1)}, u32[]{:S(2)}, u32[]{:S(2)}) collective-permute-start(bf16[528,1024]{1,0:T(8,128)(2,1)} %pack_chunk.4), channel_id=1, source_target_pairs={{0,12},{1,13},{4,0},{6,2},{7,3},{8,4},{9,5},{10,6},{11,7},{12,8},{... | collective-permute-start | bytes 3244040 | tf_op jit(solution)/shard_map/ppermute | solution.py:510
  82.8 49.8 %collective-permute-start.6 = (bf16[528,1024]{1,0:T(8,128)(2,1)}, bf16[528,1024]{1,0:T(8,128)(2,1)}, u32[]{:S(2)}, u32[]{:S(2)}) collective-permute-start(bf16[528,1024]{1,0:T(8,128)(2,1)} %pack_chunk.4), channel_id=1, source_target_pairs={{2,6},{3,7},{4,8},{5,9},{6,10},{7,11},{8,12},{9,13},{10,14},{11,15... | collective-permute-start | bytes 3244040 | tf_op jit(solution)/shard_map/ppermute | solution.py:510
  88.7 9.0 %copy-start.20 = (s32[2,6]{1,0:T(2,128)S(1)}, s32[2,6]{1,0:T(2,128)}, u32[]{:S(2)}) copy-start(s32[2,6]{1,0:T(2,128)} %param.18) | copy-start | bytes 148
  88.7 26.0 %copy-start.6 = (bf16[256,3072]{1,0:T(8,128)(2,1)S(1)}, bf16[256,3072]{1,0:T(8,128)(2,1)}, u32[]{:S(2)}) copy-start(bf16[256,3072]{1,0:T(8,128)(2,1)} %q.7) | copy-start | bytes 4718596
  92.1 22.6 %collective-permute-start.8 = (bf16[272,1536]{1,0:T(8,128)(2,1)}, bf16[272,1536]{1,0:T(8,128)(2,1)}, u32[]{:S(2)}, u32[]{:S(2)}) collective-permute-start(bf16[272,1536]{1,0:T(8,128)(2,1)} %get-tuple-element.32), channel_id=1, source_target_pairs={{0,3},{3,0},{4,7},{7,4},{8,11},{11,8},{12,15},{15,12},{16,19},{19,... | collective-permute-start | bytes 2506760 | tf_op jit(solution)/shard_map/ppermute | solution.py:546
  94.1 20.6 %collective-permute-start.9 = (bf16[256,1536]{1,0:T(8,128)(2,1)}, bf16[256,1536]{1,0:T(8,128)(2,1)}, u32[]{:S(2)}, u32[]{:S(2)}) collective-permute-start(bf16[256,1536]{1,0:T(8,128)(2,1)} %get-tuple-element.33), channel_id=1, source_target_pairs={{0,3},{3,0},{4,7},{7,4},{8,11},{11,8},{12,15},{15,12},{16,19},{19,... | collective-permute-start | bytes 2359304 | tf_op jit(solution)/shard_map/ppermute | solution.py:546
  130.2 6.4 %copy-start.5 = (bf16[256,3072]{1,0:T(8,128)(2,1)S(1)}, bf16[256,3072]{1,0:T(8,128)(2,1)}, u32[]{:S(2)}) copy-start(bf16[256,3072]{1,0:T(8,128)(2,1)} %v_own.5) | copy-start | bytes 4718596
  134.5 12.4 %copy-start.19 = (f32[64,1664]{1,0:T(8,128)S(1)}, f32[64,1664]{1,0:T(8,128)}, u32[]{:S(2)}) copy-start(f32[64,1664]{1,0:T(8,128)} %copy-done.18) | copy-start | bytes 1277956
  134.5 21.0 %copy-start.7 = (bf16[256,3072]{1,0:T(8,128)(2,1)S(1)}, bf16[256,3072]{1,0:T(8,128)(2,1)}, u32[]{:S(2)}) copy-start(bf16[256,3072]{1,0:T(8,128)(2,1)} %q.7) | copy-start | bytes 4718596
  134.6 21.0 %collective-permute-start.12 = (bf16[272,1024]{1,0:T(8,128)(2,1)S(1)}, bf16[272,1024]{1,0:T(8,128)(2,1)S(1)}, u32[]{:S(2)}, u32[]{:S(2)}) collective-permute-start(bf16[272,1024]{1,0:T(8,128)(2,1)S(1)} %get-tuple-element.37), channel_id=1, source_target_pairs={{0,3},{3,0},{4,7},{7,4},{8,11},{11,8},{12,15},{15,12},{16,19},{19,... | collective-permute-start | bytes 1671176 | tf_op jit(solution)/shard_map/ppermute | solution.py:546
  137.4 29.3 %collective-permute-start.11 = (bf16[528,512]{1,0:T(8,128)(2,1)S(1)}, bf16[528,512]{1,0:T(8,128)(2,1)S(1)}, u32[]{:S(2)}, u32[]{:S(2)}) collective-permute-start(bf16[528,512]{1,0:T(8,128)(2,1)S(1)} %pack_chunk.3), channel_id=1, source_target_pairs={{0,12},{1,13},{4,0},{6,2},{7,3},{8,4},{9,5},{10,6},{11,7},{12,8},{... | collective-permute-start | bytes 1622024 | tf_op jit(solution)/shard_map/ppermute | solution.py:510
  139.9 26.8 %collective-permute-start.10 = (bf16[528,512]{1,0:T(8,128)(2,1)S(1)}, bf16[528,512]{1,0:T(8,128)(2,1)S(1)}, u32[]{:S(2)}, u32[]{:S(2)}) collective-permute-start(bf16[528,512]{1,0:T(8,128)(2,1)S(1)} %pack_chunk.3), channel_id=1, source_target_pairs={{2,6},{3,7},{4,8},{5,9},{6,10},{7,11},{8,12},{9,13},{10,14},{11,15... | collective-permute-start | bytes 1622024 | tf_op jit(solution)/shard_map/ppermute | solution.py:510
  145.0 10.5 %collective-permute-start.13 = (bf16[256,1024]{1,0:T(8,128)(2,1)S(1)}, bf16[256,1024]{1,0:T(8,128)(2,1)S(1)}, u32[]{:S(2)}, u32[]{:S(2)}) collective-permute-start(bf16[256,1024]{1,0:T(8,128)(2,1)S(1)} %get-tuple-element.38), channel_id=1, source_target_pairs={{0,3},{3,0},{4,7},{7,4},{8,11},{11,8},{12,15},{15,12},{16,19},{19,... | collective-permute-start | bytes 1572872 | tf_op jit(solution)/shard_map/ppermute | solution.py:546
  147.0 27.8 %copy-start.15 = (f32[64,1664]{1,0:T(8,128)S(1)}, f32[64,1664]{1,0:T(8,128)}, u32[]{:S(2)}) copy-start(f32[64,1664]{1,0:T(8,128)} %copy-done.14) | copy-start | bytes 1277956
  147.0 27.8 %collective-permute-start.16 = (f32[64,1664]{1,0:T(8,128)S(1)}, f32[64,1664]{1,0:T(8,128)S(1)}, u32[]{:S(2)}, u32[]{:S(2)}) collective-permute-start(f32[64,1664]{1,0:T(8,128)S(1)} %copy-done.19), channel_id=1, source_target_pairs={{0,4},{1,5},{2,6},{3,7},{4,0},{5,1},{6,2},{7,3},{8,12},{9,13},{10,... | collective-permute-start | bytes 1277960 | tf_op jit(solution)/shard_map/ppermute | solution.py:526
  155.6 35.2 %copy-start.8 = (bf16[256,3072]{1,0:T(8,128)(2,1)S(1)}, bf16[256,3072]{1,0:T(8,128)(2,1)}, u32[]{:S(2)}) copy-start(bf16[256,3072]{1,0:T(8,128)(2,1)} %q.7) | copy-start | bytes 4718596
  166.6 24.1 %copy-start.2 = (bf16[256,3072]{1,0:T(8,128)(2,1)S(1)}, bf16[256,3072]{1,0:T(8,128)(2,1)}, u32[]{:S(2)}) copy-start(bf16[256,3072]{1,0:T(8,128)(2,1)} %k_own.5) | copy-start | bytes 4718596
  166.7 1.7 copy-start.11
  168.4 0.8 copy-start.9
  169.2 11.0 %collective-permute-start.14 = (bf16[272,512]{1,0:T(8,128)(2,1)}, bf16[272,512]{1,0:T(8,128)(2,1)S(1)}, u32[]{:S(2)}, u32[]{:S(2)}) collective-permute-start(bf16[272,512]{1,0:T(8,128)(2,1)} %get-tuple-element.41), channel_id=1, source_target_pairs={{0,3},{3,0},{4,7},{7,4},{8,11},{11,8},{12,15},{15,12},{16,19},{19,... | collective-permute-start | bytes 835592 | tf_op jit(solution)/shard_map/ppermute | solution.py:546
  171.1 9.1 %collective-permute-start.15 = (bf16[256,512]{1,0:T(8,128)(2,1)}, bf16[256,512]{1,0:T(8,128)(2,1)}, u32[]{:S(2)}, u32[]{:S(2)}) collective-permute-start(bf16[256,512]{1,0:T(8,128)(2,1)} %get-tuple-element.42), channel_id=1, source_target_pairs={{0,3},{3,0},{4,7},{7,4},{8,11},{11,8},{12,15},{15,12},{16,19},{19,... | collective-permute-start | bytes 786440 | tf_op jit(solution)/shard_map/ppermute | solution.py:546
  175.9 0.7 copy-start.16
  176.6 11.9 %collective-permute-start.17 = (f32[32,1664]{1,0:T(8,128)}, f32[32,1664]{1,0:T(8,128)}, u32[]{:S(2)}, u32[]{:S(2)}) collective-permute-start(f32[32,1664]{1,0:T(8,128)} %get-tuple-element.47), channel_id=1, source_target_pairs={{0,8},{1,9},{2,10},{3,11},{4,12},{5,13},{6,14},{7,15},{8,0},{9,1},... | collective-permute-start | bytes 638984 | tf_op jit(solution)/shard_map/ppermute | solution.py:526
  188.5 0.9 copy-start.17
  190.7 8.5 %collective-permute-start.18 = (bf16[16,1536]{1,0:T(8,128)(2,1)S(1)}, bf16[16,1536]{1,0:T(8,128)(2,1)}, u32[]{:S(2)}, u32[]{:S(2)}) collective-permute-start(bf16[16,1536]{1,0:T(8,128)(2,1)S(1)} %get-tuple-element.49), channel_id=1, source_target_pairs={{0,1},{1,0},{2,3},{3,2},{4,5},{5,4},{6,7},{7,6},{8,9},{9,8},{10,11... | collective-permute-start | bytes 147464 | tf_op jit(solution)/shard_map/ppermute | solution.py:561
  190.8 1.0 copy-start.10
  191.8 1.0 copy-start.12

commit v12 on v11

--- a/solution.py
+++ b/solution.py
@@ -396,10 +396,6 @@
     first, second = refs[-2:]
     half = first.shape[0]
     stats = jnp.where(is_top, top, 0.0)
-    if finish:
-        limits = refs[2]
-        row = lax.broadcasted_iota(jnp.int32, (2 * half, 1), 0)
-        valid = row < jnp.where(row < half, limits[0], limits[1] + half)
     for h in range(PAIR_HEADS):
         cols = pl.ds(h * HD, HD)
         at = slice(h, h + 1)
@@ -407,7 +403,7 @@
         total = mine[:, to] * a[:, at] + theirs[:, to] * b[:, at]
         acc = keep[:, cols] * a[:, at] + got[:, cols] * b[:, at]
         if finish:
-            acc = jnp.where(valid, acc / total, 0.0)
+            acc = acc / total
         else:
             stats = jnp.where(lane == STAT_SUMS + h, total, stats)
         first[:, cols] = acc[:half].astype(first.dtype)
@@ -427,26 +423,21 @@
     )(keep, got)
 
 
-def text_finish(keep, got, limits):
+def text_finish(keep, got):
     shape = jax.ShapeDtypeStruct((keep.shape[0] // 2, PAIR_HEADS * HD), jnp.bfloat16)
-    vmem = pl.BlockSpec(memory_space=pltpu.VMEM)
     return pl.pallas_call(
         functools.partial(merge_kernel, True),
-        in_specs=[vmem, vmem, pl.BlockSpec(memory_space=pltpu.SMEM)],
         out_shape=[shape, shape],
         compiler_params=pltpu.CompilerParams(vmem_limit_bytes=VMEM_BYTES),
         name="text_finish",
-    )(keep, got, limits)
-
-
-def text_order(n, position):
-    bits = n.bit_length() - 1
-    masks = [1 << b for b in (*range(1, bits), 0)]
-    owners = [
-        sum(mask for j, mask in enumerate(masks) if i >> (bits - 1 - j) & 1) for i in range(n)
-    ]
-    order = jnp.array(owners, jnp.int32) ^ position
-    first = position % 2 * (PAIR_HEADS // STEP_HEADS)
+    )(keep, got)
+
+
+def text_order(n, base):
+    masks = (4, 8, 1, 2)
+    owners = [sum(mask for j, mask in enumerate(masks) if i >> (3 - j) & 1) for i in range(n)]
+    order = jnp.array(owners, jnp.int32) ^ base
+    first = base % 2 * (PAIR_HEADS // STEP_HEADS)
     return jnp.concatenate([order, first[None]])
 
 
@@ -514,28 +505,27 @@
         lax.ppermute(x, "tiles", pairs["beside"]) for x in (counts, video_k, video_v)
     ]
     table = make_table(window, counts, beside[0], text_count, choices, position)
-    halving = text % (PAD_ROWS * n) == 0 and n & (n - 1) == 0
-    stages = n.bit_length() - 1
+    halving = text % (PAD_ROWS * n) == 0 and n == 16
+    lower = [d for d in range(n) if not d & 2]
+    upper = [d for d in range(n) if d & 2]
     parts = []
     if halving:
-        order = text_order(n, position)
         both = jnp.concatenate([counts, beside[0]])
-        parts.append(text_local(order, both, text_q, video_k, video_v, *beside[1:]))
-
-    def exchanged(i):
-        return lax.ppermute(parts[i][1], "tiles", [(d, d ^ (2 << i)) for d in range(n)])
+        order = text_order(n, position | 2)
+        partial = text_local(order, both, text_q, video_k, video_v, *beside[1:])
+        halves = []
+        for half in partial:
+            got = lax.ppermute(half, "tiles", [(d, d | 2) for d in lower])
+            halves.append(jnp.concatenate(text_merge(half, got), axis=0))
+        parts.append(halves)
 
     def merge(*before):
-        i = len(parts) - 1
-        if 0 <= i < stages - 2:
-            parts.append(text_merge(tie(parts[i][0], *before), exchanged(i)))
-        elif i == stages - 2:
-            share = text // n
-            limits = [text_count - place * share for place in (position, position ^ 1)]
-            limits = jnp.concatenate(limits)
-            parts.append(text_finish(tie(parts[i][0], *before), exchanged(i), limits))
-
-    merge()
+        i = len(parts)
+        if 0 < i < 3:
+            got = lax.ppermute(parts[-1][1], "tiles", [(d, d ^ (2 << i)) for d in upper])
+            keep = tie(parts[-1][0], *before)
+            parts.append(text_merge(keep, got) if i == 1 else text_finish(keep, got))
+
     count = len(CHUNK_HEADS)
     for i in range(count):
         before = outs[i - 1 : i] + ([parts[-1][0]] if halving and i == 0 else [])
@@ -553,14 +543,19 @@
             )
         )
         if i == 0:
-            merge(outs[0])
+            merge(*relays)
         elif i + 1 == count:
             merge(*relays)
     if halving:
         mine, leave = parts[-1]
         got = lax.ppermute(leave, "tiles", [(d, d ^ 1) for d in range(n)])
         low, high = jnp.concatenate([mine, got], axis=1), jnp.concatenate([got, mine], axis=1)
-        text_out = jnp.where(position % 2 == 0, low, high)
+        ready = jnp.where(position % 2 == 0, low, high)
+        share = text // n
+        handed = lax.ppermute(ready[share:], "tiles", [(d, d ^ 2) for d in upper])
+        rows_valid = position * share + jnp.arange(share, dtype=jnp.int32) < text_count[0]
+        text_out = jnp.where((position & 2) == 0, handed, ready[:share])
+        text_out = jnp.where(rows_valid[:, None], text_out, 0)
     if not halving:
         text_out = text_plain(position, n, text_count, text_q, video_k, video_v, counts)
     return (outs[-1], text_out)

time: 203 us -> 200 us (0.985)
  waiting for transfers between devices: 88.3 us -> 77.7 us
  starting transfers between devices: 39.8 us -> 45.9 us
    ppermute x3 -> x5, waiting for transfers between devices: 27.4 us -> 16.5 us  [the longest x2 16.5 us: per_device(): got = lax.ppermute(half, 'tiles', [(d, d | 2) for d in lower])]
    ppermute x6, waiting for transfers between devices: 26.2 us -> 21 us  [per_device(): lax.ppermute(half, 'tiles', pairs['relayed'])]
    ppermute x6, waiting for transfers between devices: 33.5 us -> 38.4 us  [send(): lax.ppermute(mine, 'tiles', pairs[x])]
    ppermute x3 -> x5, starting transfers between devices: 2.84 us -> 7.08 us  [the longest x2 3.55 us: per_device(): got = lax.ppermute(half, 'tiles', [(d, d | 2) for d in lower])]
    pallas_call x2 -> x3, Pallas kernels: 1.9 us -> 5.06 us  [text_merge(): pl.pallas_call(functools.partial(merge_kernel, False), out_shape=[shape,...]
    unnamed x46 -> x45, local copies, waits for them, and re-layouts: 10.4 us -> 9.86 us
  transfers between devices with their start and end apart: 19 -> 21, of which waited for: 8 -> 8; matrix products, arithmetic and copies ran while one was open for 2% -> 2% of each run, Pallas kernels for 26% -> 29%
where the time goes in v12:
time: 200 us; the launch traced here: 198 us
  waiting for transfers between devices  77.7 us (39%)
  Pallas kernels  57.4 us (29%)
  starting transfers between devices  45.9 us (23%)
  local copies, waits for them, and re-layouts  11.5 us (6%)
  other arithmetic  3.24 us (2%)
    ppermute x6, waiting for transfers between devices, send(): lax.ppermute(mine, 'tiles', pairs[x])  38.4 us
    pallas_call x3, Pallas kernels, video_call(): pl.pallas_call(video_kernel, grid=(heads // STEP_HEADS,), in_specs=in_spe...  32.7 us
    ppermute x6, starting transfers between devices, send(): lax.ppermute(mine, 'tiles', pairs[x])  23 us
    ppermute x6, waiting for transfers between devices, per_device(): lax.ppermute(half, 'tiles', pairs['relayed'])  21 us
    ppermute x2, waiting for transfers between devices, per_device(): got = lax.ppermute(half, 'tiles', [(d, d | 2) for d in lower])  16.5 us
    ppermute x6, starting transfers between devices, per_device(): lax.ppermute(half, 'tiles', pairs['relayed'])  15.1 us
    unnamed x45, local copies, waits for them, and re-layouts  9.86 us
    pallas_call x1, Pallas kernels, text_local(): pl.pallas_call(text_kernel, grid_spec=pltpu.PrefetchScalarGridSpec(num_sc...  8.68 us
  transfers between devices with their start and end apart: 21, of which 8 were waited for; matrix products, arithmetic and copies ran while one was open for 2% of the time, Pallas kernels for 29%

profile of v12, /device:TPU:24, one launch (start us, length us, event | category | flops | bytes accessed | tf_op | source)
XLA Modules:
  0.0 197.5 jit_solution(8952651730784318043)
XLA Ops:
  1.3 1.4 copy-done
  2.7 1.4 copy-done.3
  4.8 1.7 pack_chunk.5
  6.5 2.4 %collective-permute-start.2 = (bf16[528,1536]{1,0:T(8,128)(2,1)}, bf16[528,1536]{1,0:T(8,128)(2,1)}, u32[]{:S(2)}, u32[]{:S(2)}) collective-permute-start(bf16[528,1536]{1,0:T(8,128)(2,1)} %pack_chunk.5), channel_id=1, source_target_pairs={{0,12},{1,13},{4,0},{6,2},{7,3},{8,4},{9,5},{10,6},{11,7},{12,8},{... | collective-permute-start | bytes 4866056 | tf_op jit(solution)/shard_map/ppermute | solution.py:501
  8.9 5.3 %collective-permute-start.1 = (bf16[528,1536]{1,0:T(8,128)(2,1)}, bf16[528,1536]{1,0:T(8,128)(2,1)}, u32[]{:S(2)}, u32[]{:S(2)}) collective-permute-start(bf16[528,1536]{1,0:T(8,128)(2,1)} %pack_chunk.5), channel_id=1, source_target_pairs={{2,6},{3,7},{4,8},{5,9},{6,10},{7,11},{8,12},{9,13},{10,14},{11,15... | collective-permute-start | bytes 4866056 | tf_op jit(solution)/shard_map/ppermute | solution.py:501
  14.4 1.5 copy-done.14
  15.9 8.7 %text_partials.1 = (f32[128,1792]{1,0:T(8,128)S(1)}, f32[128,1792]{1,0:T(8,128)}) custom-call(s32[17]{0:T(128)S(1)} %pad_add_fusion.1.order, s32[4]{0:T(128)S(1)} %pad_add_fusion.2.counts, bf16[256,3072]{1,0:T(8,128)(2,1)S(1)} %copy-done.14, bf16[256,3072]{1,0:T(8,128)(2,1)S(1)} %copy-done.1, bf16[256,3072]{1,0:T(8,128)(2,1)} %v_own.5, ...), custom_call_target="tpu_custom_call" | custom-call | flops 8388608 | bytes 786432 | tf_op jit(solution)/shard_map/text_partials/pallas_call | solution.py:367
  24.6 1.3 collective-permute-start.5
  26.0 2.2 %collective-permute-start.16 = (f32[128,1792]{1,0:T(8,128)}, f32[128,1792]{1,0:T(8,128)}, u32[]{:S(2)}, u32[]{:S(2)}) collective-permute-start(f32[128,1792]{1,0:T(8,128)} %get-tuple-element.46.refs_0_), channel_id=1, source_target_pairs={{0,2},{1,3},{4,6},{5,7},{8,10},{9,11},{12,14},{13,15},{16,18},{17,... | collective-permute-start | bytes 2752520 | tf_op jit(solution)/shard_map/ppermute | solution.py:518
  28.2 1.5 pack_chunk.4
  29.7 16.5 %collective-permute-done.5.refs_1_ = f32[128,1792]{1,0:T(8,128)S(1)} collective-permute-done((f32[128,1792]{1,0:T(8,128)S(1)}, f32[128,1792]{1,0:T(8,128)S(1)}, u32[]{:S(2)}, u32[]{:S(2)}) %collective-permute-start.5) | collective-permute-done | bytes 917536 | tf_op jit(solution)/shard_map/ppermute | solution.py:518
  46.3 0.8 text_merge.3
  47.1 0.9 copy-done.12
  48.5 34.6 %collective-permute-done.1.a.rest_0_ = bf16[528,1536]{1,0:T(8,128)(2,1)} collective-permute-done((bf16[528,1536]{1,0:T(8,128)(2,1)}, bf16[528,1536]{1,0:T(8,128)(2,1)}, u32[]{:S(2)}, u32[]{:S(2)}) %collective-permute-start.1) | collective-permute-done | bytes 1622048 | tf_op jit(solution)/shard_map/ppermute | solution.py:501
  83.1 2.5 %collective-permute-start.7 = (bf16[528,1024]{1,0:T(8,128)(2,1)}, bf16[528,1024]{1,0:T(8,128)(2,1)}, u32[]{:S(2)}, u32[]{:S(2)}) collective-permute-start(bf16[528,1024]{1,0:T(8,128)(2,1)} %pack_chunk.4), channel_id=1, source_target_pairs={{0,12},{1,13},{4,0},{6,2},{7,3},{8,4},{9,5},{10,6},{11,7},{12,8},{... | collective-permute-start | bytes 3244040 | tf_op jit(solution)/shard_map/ppermute | solution.py:501
  85.6 5.2 %collective-permute-start.6 = (bf16[528,1024]{1,0:T(8,128)(2,1)}, bf16[528,1024]{1,0:T(8,128)(2,1)}, u32[]{:S(2)}, u32[]{:S(2)}) collective-permute-start(bf16[528,1024]{1,0:T(8,128)(2,1)} %pack_chunk.4), channel_id=1, source_target_pairs={{2,6},{3,7},{4,8},{5,9},{6,10},{7,11},{8,12},{9,13},{10,14},{11,15... | collective-permute-start | bytes 3244040 | tf_op jit(solution)/shard_map/ppermute | solution.py:501
  91.3 3.3 %choose_relayed.3 = (bf16[272,1536]{1,0:T(8,128)(2,1)}, bf16[256,1536]{1,0:T(8,128)(2,1)}) custom-call(s32[1]{0:T(128)} %dynamic_slice.8.second, bf16[528,1536]{1,0:T(8,128)(2,1)} %collective-permute-done.1.a.rest_0_, bf16[528,1536]{1,0:T(8,128)(2,1)} %collective-permute-done.2.b.rest_1_), custom_call_target="tpu_custom_call" | custom-call | tf_op jit(solution)/shard_map/choose_relayed/pallas_call | solution.py:124
  94.6 1.9 collective-permute-start.8
  96.8 3.6 %collective-permute-start.9 = (bf16[256,1536]{1,0:T(8,128)(2,1)}, bf16[256,1536]{1,0:T(8,128)(2,1)}, u32[]{:S(2)}, u32[]{:S(2)}) collective-permute-start(bf16[256,1536]{1,0:T(8,128)(2,1)} %get-tuple-element.35), channel_id=1, source_target_pairs={{0,3},{3,0},{4,7},{7,4},{8,11},{11,8},{12,15},{15,12},{16,19},{19,... | collective-permute-start | bytes 2359304 | tf_op jit(solution)/shard_map/ppermute | solution.py:536
  100.6 2.3 %text_merge.4 = (f32[64,1664]{1,0:T(8,128)S(1)}, f32[64,1664]{1,0:T(8,128)S(1)}) custom-call(f32[128,1792]{1,0:T(8,128)} %get-tuple-element.46.refs_0_, f32[128,1792]{1,0:T(8,128)} %collective-permute-done.16.refs_1_), custom_call_target="tpu_custom_call" | custom-call | tf_op jit(solution)/shard_map/text_merge/pallas_call | solution.py:418
  102.9 1.0 pad_maximum_fusion
  103.9 1.5 collective-permute-start.17
  106.4 0.7 dynamic-slice_bitcast_fusion
  107.2 10.0 %collective-permute-done.9.rest_3_ = bf16[256,1536]{1,0:T(8,128)(2,1)} collective-permute-done((bf16[256,1536]{1,0:T(8,128)(2,1)}, bf16[256,1536]{1,0:T(8,128)(2,1)}, u32[]{:S(2)}, u32[]{:S(2)}) %collective-permute-start.9) | collective-permute-done | bytes 786464 | tf_op jit(solution)/shard_map/ppermute | solution.py:536
  117.2 15.4 %video_attention.3.rest_8_ = bf16[256,3072]{1,0:T(8,128)(2,1)} custom-call(s32[13]{0:T(128)S(1)} %concatenate.21.table, bf16[256,3072]{1,0:T(8,128)(2,1)S(1)} %copy-done.6, bf16[256,3072]{1,0:T(8,128)(2,1)S(1)} %copy-done.1, bf16[256,3072]{1,0:T(8,128)(2,1)} %v_own.5, bf16[528,1536]{1,0:T(8,128)(2,1)} %collective-permute-done.1.a.rest_0_, ...), custom_call_target="tpu_custom_call" | custom-call | flops 113246208 | bytes 393216 | tf_op jit(solution)/shard_map/video_attention/pallas_call | solution.py:275
  132.7 3.4 %collective-permute-done.6.a.rest_0_ = bf16[528,1024]{1,0:T(8,128)(2,1)} collective-permute-done((bf16[528,1024]{1,0:T(8,128)(2,1)}, bf16[528,1024]{1,0:T(8,128)(2,1)}, u32[]{:S(2)}, u32[]{:S(2)}) %collective-permute-start.6) | collective-permute-done | bytes 1081376 | tf_op jit(solution)/shard_map/ppermute | solution.py:501
  136.0 1.9 choose_relayed.4
  137.9 2.1 %collective-permute-start.12 = (bf16[272,1024]{1,0:T(8,128)(2,1)S(1)}, bf16[272,1024]{1,0:T(8,128)(2,1)S(1)}, u32[]{:S(2)}, u32[]{:S(2)}) collective-permute-start(bf16[272,1024]{1,0:T(8,128)(2,1)S(1)} %get-tuple-element.39), channel_id=1, source_target_pairs={{0,3},{3,0},{4,7},{7,4},{8,11},{11,8},{12,15},{15,12},{16,19},{19,... | collective-permute-start | bytes 1671176 | tf_op jit(solution)/shard_map/ppermute | solution.py:536
  140.7 2.6 %collective-permute-start.11 = (bf16[528,512]{1,0:T(8,128)(2,1)S(1)}, bf16[528,512]{1,0:T(8,128)(2,1)S(1)}, u32[]{:S(2)}, u32[]{:S(2)}) collective-permute-start(bf16[528,512]{1,0:T(8,128)(2,1)S(1)} %pack_chunk.3), channel_id=1, source_target_pairs={{0,12},{1,13},{4,0},{6,2},{7,3},{8,4},{9,5},{10,6},{11,7},{12,8},{... | collective-permute-start | bytes 1622024 | tf_op jit(solution)/shard_map/ppermute | solution.py:501
  143.3 5.2 %collective-permute-start.10 = (bf16[528,512]{1,0:T(8,128)(2,1)S(1)}, bf16[528,512]{1,0:T(8,128)(2,1)S(1)}, u32[]{:S(2)}, u32[]{:S(2)}) collective-permute-start(bf16[528,512]{1,0:T(8,128)(2,1)S(1)} %pack_chunk.3), channel_id=1, source_target_pairs={{2,6},{3,7},{4,8},{5,9},{6,10},{7,11},{8,12},{9,13},{10,14},{11,15... | collective-permute-start | bytes 1622024 | tf_op jit(solution)/shard_map/ppermute | solution.py:501
  148.5 1.9 collective-permute-start.13
  150.4 1.9 text_merge.5
  153.0 5.9 %collective-permute-done.13.rest_3_ = bf16[256,1024]{1,0:T(8,128)(2,1)S(1)} collective-permute-done((bf16[256,1024]{1,0:T(8,128)(2,1)S(1)}, bf16[256,1024]{1,0:T(8,128)(2,1)S(1)}, u32[]{:S(2)}, u32[]{:S(2)}) %collective-permute-start.13) | collective-permute-done | bytes 524320 | tf_op jit(solution)/shard_map/ppermute | solution.py:536
  159.0 11.0 %video_attention.4.rest_8_ = bf16[256,3072]{1,0:T(8,128)(2,1)} custom-call(s32[13]{0:T(128)S(1)} %concatenate.21.table, bf16[256,3072]{1,0:T(8,128)(2,1)S(1)} %copy-done.7, bf16[256,3072]{1,0:T(8,128)(2,1)} %k_own.5, bf16[256,3072]{1,0:T(8,128)(2,1)} %v_own.5, bf16[528,1024]{1,0:T(8,128)(2,1)} %collective-permute-done.6.a.rest_0_, ...), custom_call_target="tpu_custom_call", output_to_operand_aliasing={{}: (12, {})} | custom-call | flops 75497472 | bytes 262144 | tf_op jit(solution)/shard_map/video_attention/pallas_call | solution.py:275
  170.0 0.9 choose_relayed.5
  170.9 0.8 copy-done.8
  171.7 1.9 collective-permute-start.14
  173.6 3.6 %collective-permute-start.15 = (bf16[256,512]{1,0:T(8,128)(2,1)S(1)}, bf16[256,512]{1,0:T(8,128)(2,1)S(1)}, u32[]{:S(2)}, u32[]{:S(2)}) collective-permute-start(bf16[256,512]{1,0:T(8,128)(2,1)S(1)} %get-tuple-element.44), channel_id=1, source_target_pairs={{0,3},{3,0},{4,7},{7,4},{8,11},{11,8},{12,15},{15,12},{16,19},{19,... | collective-permute-start | bytes 786440 | tf_op jit(solution)/shard_map/ppermute | solution.py:536
  177.3 5.1 %collective-permute-done.15.rest_3_ = bf16[256,512]{1,0:T(8,128)(2,1)S(1)} collective-permute-done((bf16[256,512]{1,0:T(8,128)(2,1)S(1)}, bf16[256,512]{1,0:T(8,128)(2,1)S(1)}, u32[]{:S(2)}, u32[]{:S(2)}) %collective-permute-start.15) | collective-permute-done | bytes 262176 | tf_op jit(solution)/shard_map/ppermute | solution.py:536
  182.4 1.1 text_finish.1
  183.5 1.6 collective-permute-done.19
  185.1 1.0 maximum_select_fusion
  186.2 1.3 collective-permute-start.20
  187.5 1.0 copy-done.9
  188.6 1.0 copy-done.11
  189.6 0.9 copy-done.16
  190.6 6.2 %video_attention.5 = bf16[256,3072]{1,0:T(8,128)(2,1)} custom-call(s32[13]{0:T(128)S(1)} %concatenate.21.table, bf16[256,3072]{1,0:T(8,128)(2,1)S(1)} %copy-done.7, bf16[256,3072]{1,0:T(8,128)(2,1)S(1)} %copy-done.2, bf16[256,3072]{1,0:T(8,128)(2,1)} %v_own.5, bf16[528,512]{1,0:T(8,128)(2,1)S(1)} %copy-done.11, ...), custom_call_target="tpu_custom_call", output_to_operand_aliasing={{}: (12, {})} | custom-call | flops 37748736 | bytes 131072 | tf_op jit(solution)/shard_map/video_attention/pallas_call | solution.py:275
  196.8 0.7 fusion
  (74 shorter events, 4.7 us)
Async XLA Ops:
  0.6 13.6 %copy-start.21 = (s32[16]{0:T(128)S(1)}, s32[16]{0:T(128)}, u32[]{:S(2)}) copy-start(s32[16]{0:T(128)} %constant.79.clone) | copy-start | bytes 196
  0.6 13.8 %collective-permute-start.3 = (bf16[256,3072]{1,0:T(8,128)(2,1)}, bf16[256,3072]{1,0:T(8,128)(2,1)}, u32[]{:S(2)}, u32[]{:S(2)}) collective-permute-start(bf16[256,3072]{1,0:T(8,128)(2,1)} %k_own.5), channel_id=1, source_target_pairs={{0,1},{1,0},{2,3},{3,2},{4,5},{5,4},{6,7},{7,6},{8,9},{9,8},{10,11... | collective-permute-start | bytes 4718600 | tf_op jit(solution)/shard_map/ppermute | solution.py:505
  0.7 13.7 %collective-permute-start.4 = (bf16[256,3072]{1,0:T(8,128)(2,1)}, bf16[256,3072]{1,0:T(8,128)(2,1)}, u32[]{:S(2)}, u32[]{:S(2)}) collective-permute-start(bf16[256,3072]{1,0:T(8,128)(2,1)} %v_own.5), channel_id=1, source_target_pairs={{0,1},{1,0},{2,3},{3,2},{4,5},{5,4},{6,7},{7,6},{8,9},{9,8},{10,11... | collective-permute-start | bytes 4718600 | tf_op jit(solution)/shard_map/ppermute | solution.py:505
  1.2 13.1 %collective-permute-start = (s32[2]{0:T(128)}, s32[2]{0:T(128)S(1)}, u32[]{:S(2)}, u32[]{:S(2)}) collective-permute-start(s32[2]{0:T(128)} %counts.5), channel_id=1, source_target_pairs={{0,1},{1,0},{2,3},{3,2},{4,5},{5,4},{6,7},{7,6},{8,9},{9,8},{10,11... | collective-permute-start | bytes 32 | tf_op jit(solution)/shard_map/ppermute | solution.py:505
  1.3 1.4 copy-start
  2.7 1.4 copy-start.3
  4.1 0.7 copy-start.17
  4.8 9.5 %copy-start.18 = (s32[2]{0:T(128)S(1)}, s32[2]{0:T(128)}, u32[]{:S(2)}) copy-start(s32[2]{0:T(128)} %counts.5) | copy-start | bytes 28
  4.8 9.6 %copy-start.1 = (bf16[256,3072]{1,0:T(8,128)(2,1)S(1)}, bf16[256,3072]{1,0:T(8,128)(2,1)}, u32[]{:S(2)}) copy-start(bf16[256,3072]{1,0:T(8,128)(2,1)} %k_own.5) | copy-start | bytes 4718596
  6.5 42.0 %collective-permute-start.2 = (bf16[528,1536]{1,0:T(8,128)(2,1)}, bf16[528,1536]{1,0:T(8,128)(2,1)}, u32[]{:S(2)}, u32[]{:S(2)}) collective-permute-start(bf16[528,1536]{1,0:T(8,128)(2,1)} %pack_chunk.5), channel_id=1, source_target_pairs={{0,12},{1,13},{4,0},{6,2},{7,3},{8,4},{9,5},{10,6},{11,7},{12,8},{... | collective-permute-start | bytes 4866056 | tf_op jit(solution)/shard_map/ppermute | solution.py:501
  8.9 74.2 %collective-permute-start.1 = (bf16[528,1536]{1,0:T(8,128)(2,1)}, bf16[528,1536]{1,0:T(8,128)(2,1)}, u32[]{:S(2)}, u32[]{:S(2)}) collective-permute-start(bf16[528,1536]{1,0:T(8,128)(2,1)} %pack_chunk.5), channel_id=1, source_target_pairs={{2,6},{3,7},{4,8},{5,9},{6,10},{7,11},{8,12},{9,13},{10,14},{11,15... | collective-permute-start | bytes 4866056 | tf_op jit(solution)/shard_map/ppermute | solution.py:501
  14.4 13.8 %copy-start.4 = (bf16[256,3072]{1,0:T(8,128)(2,1)S(1)}, bf16[256,3072]{1,0:T(8,128)(2,1)}, u32[]{:S(2)}) copy-start(bf16[256,3072]{1,0:T(8,128)(2,1)} %v_own.5) | copy-start | bytes 4718596
  14.4 1.5 copy-start.14
  24.6 21.7 %collective-permute-start.5 = (f32[128,1792]{1,0:T(8,128)S(1)}, f32[128,1792]{1,0:T(8,128)S(1)}, u32[]{:S(2)}, u32[]{:S(2)}) collective-permute-start(f32[128,1792]{1,0:T(8,128)S(1)} %get-tuple-element.28.refs_0_), channel_id=1, source_target_pairs={{0,2},{1,3},{4,6},{5,7},{8,10},{9,11},{12,14},{13,15},{16,18},{17,... | collective-permute-start | bytes 2752520 | tf_op jit(solution)/shard_map/ppermute | solution.py:518
  26.0 74.6 %collective-permute-start.16 = (f32[128,1792]{1,0:T(8,128)}, f32[128,1792]{1,0:T(8,128)}, u32[]{:S(2)}, u32[]{:S(2)}) collective-permute-start(f32[128,1792]{1,0:T(8,128)} %get-tuple-element.46.refs_0_), channel_id=1, source_target_pairs={{0,2},{1,3},{4,6},{5,7},{8,10},{9,11},{12,14},{13,15},{16,18},{17,... | collective-permute-start | bytes 2752520 | tf_op jit(solution)/shard_map/ppermute | solution.py:518
  29.7 61.0 %copy-start.20 = (s32[16]{0:T(128)S(1)}, s32[16]{0:T(128)}, u32[]{:S(2)}) copy-start(s32[16]{0:T(128)} %constant.77.clone) | copy-start | bytes 196
  47.1 0.9 copy-start.12
  83.1 49.6 %collective-permute-start.7 = (bf16[528,1024]{1,0:T(8,128)(2,1)}, bf16[528,1024]{1,0:T(8,128)(2,1)}, u32[]{:S(2)}, u32[]{:S(2)}) collective-permute-start(bf16[528,1024]{1,0:T(8,128)(2,1)} %pack_chunk.4), channel_id=1, source_target_pairs={{0,12},{1,13},{4,0},{6,2},{7,3},{8,4},{9,5},{10,6},{11,7},{12,8},{... | collective-permute-start | bytes 3244040 | tf_op jit(solution)/shard_map/ppermute | solution.py:501
  85.6 50.5 %collective-permute-start.6 = (bf16[528,1024]{1,0:T(8,128)(2,1)}, bf16[528,1024]{1,0:T(8,128)(2,1)}, u32[]{:S(2)}, u32[]{:S(2)}) collective-permute-start(bf16[528,1024]{1,0:T(8,128)(2,1)} %pack_chunk.4), channel_id=1, source_target_pairs={{2,6},{3,7},{4,8},{5,9},{6,10},{7,11},{8,12},{9,13},{10,14},{11,15... | collective-permute-start | bytes 3244040 | tf_op jit(solution)/shard_map/ppermute | solution.py:501
  91.3 5.2 %copy-start.19 = (s32[2,6]{1,0:T(2,128)S(1)}, s32[2,6]{1,0:T(2,128)}, u32[]{:S(2)}) copy-start(s32[2,6]{1,0:T(2,128)} %param.18) | copy-start | bytes 148
  94.6 22.6 %collective-permute-start.8 = (bf16[272,1536]{1,0:T(8,128)(2,1)}, bf16[272,1536]{1,0:T(8,128)(2,1)}, u32[]{:S(2)}, u32[]{:S(2)}) collective-permute-start(bf16[272,1536]{1,0:T(8,128)(2,1)} %get-tuple-element.34), channel_id=1, source_target_pairs={{0,3},{3,0},{4,7},{7,4},{8,11},{11,8},{12,15},{15,12},{16,19},{19,... | collective-permute-start | bytes 2506760 | tf_op jit(solution)/shard_map/ppermute | solution.py:536
  96.8 20.4 %collective-permute-start.9 = (bf16[256,1536]{1,0:T(8,128)(2,1)}, bf16[256,1536]{1,0:T(8,128)(2,1)}, u32[]{:S(2)}, u32[]{:S(2)}) collective-permute-start(bf16[256,1536]{1,0:T(8,128)(2,1)} %get-tuple-element.35), channel_id=1, source_target_pairs={{0,3},{3,0},{4,7},{7,4},{8,11},{11,8},{12,15},{15,12},{16,19},{19,... | collective-permute-start | bytes 2359304 | tf_op jit(solution)/shard_map/ppermute | solution.py:536
  100.5 16.7 %copy-start.6 = (bf16[256,3072]{1,0:T(8,128)(2,1)S(1)}, bf16[256,3072]{1,0:T(8,128)(2,1)}, u32[]{:S(2)}) copy-start(bf16[256,3072]{1,0:T(8,128)(2,1)} %q.7) | copy-start | bytes 4718596
  103.9 46.5 %collective-permute-start.17 = (f32[128,1664]{1,0:T(8,128)}, f32[128,1664]{1,0:T(8,128)}, u32[]{:S(2)}, u32[]{:S(2)}) collective-permute-start(f32[128,1664]{1,0:T(8,128)} %pad_maximum_fusion), channel_id=1, source_target_pairs={{2,6},{3,7},{6,2},{7,3},{10,14},{11,15},{14,10},{15,11},{18,22},{1... | collective-permute-start | bytes 2555912 | tf_op jit(solution)/shard_map/ppermute | solution.py:525
  132.6 7.4 %copy-start.5 = (bf16[256,3072]{1,0:T(8,128)(2,1)S(1)}, bf16[256,3072]{1,0:T(8,128)(2,1)}, u32[]{:S(2)}) copy-start(bf16[256,3072]{1,0:T(8,128)(2,1)} %v_own.5) | copy-start | bytes 4718596
  137.9 12.5 %copy-start.13 = (f32[128,1664]{1,0:T(8,128)S(1)}, f32[128,1664]{1,0:T(8,128)}, u32[]{:S(2)}) copy-start(f32[128,1664]{1,0:T(8,128)} %copy-done.12) | copy-start | bytes 2555908
  137.9 21.0 %collective-permute-start.12 = (bf16[272,1024]{1,0:T(8,128)(2,1)S(1)}, bf16[272,1024]{1,0:T(8,128)(2,1)S(1)}, u32[]{:S(2)}, u32[]{:S(2)}) collective-permute-start(bf16[272,1024]{1,0:T(8,128)(2,1)S(1)} %get-tuple-element.39), channel_id=1, source_target_pairs={{0,3},{3,0},{4,7},{7,4},{8,11},{11,8},{12,15},{15,12},{16,19},{19,... | collective-permute-start | bytes 1671176 | tf_op jit(solution)/shard_map/ppermute | solution.py:536
  140.7 18.3 %copy-start.7 = (bf16[256,3072]{1,0:T(8,128)(2,1)S(1)}, bf16[256,3072]{1,0:T(8,128)(2,1)}, u32[]{:S(2)}) copy-start(bf16[256,3072]{1,0:T(8,128)(2,1)} %q.7) | copy-start | bytes 4718596
  140.7 29.3 %collective-permute-start.11 = (bf16[528,512]{1,0:T(8,128)(2,1)S(1)}, bf16[528,512]{1,0:T(8,128)(2,1)S(1)}, u32[]{:S(2)}, u32[]{:S(2)}) collective-permute-start(bf16[528,512]{1,0:T(8,128)(2,1)S(1)} %pack_chunk.3), channel_id=1, source_target_pairs={{0,12},{1,13},{4,0},{6,2},{7,3},{8,4},{9,5},{10,6},{11,7},{12,8},{... | collective-permute-start | bytes 1622024 | tf_op jit(solution)/shard_map/ppermute | solution.py:501
  143.3 26.7 %collective-permute-start.10 = (bf16[528,512]{1,0:T(8,128)(2,1)S(1)}, bf16[528,512]{1,0:T(8,128)(2,1)S(1)}, u32[]{:S(2)}, u32[]{:S(2)}) collective-permute-start(bf16[528,512]{1,0:T(8,128)(2,1)S(1)} %pack_chunk.3), channel_id=1, source_target_pairs={{2,6},{3,7},{4,8},{5,9},{6,10},{7,11},{8,12},{9,13},{10,14},{11,15... | collective-permute-start | bytes 1622024 | tf_op jit(solution)/shard_map/ppermute | solution.py:501
  148.5 10.5 %collective-permute-start.13 = (bf16[256,1024]{1,0:T(8,128)(2,1)S(1)}, bf16[256,1024]{1,0:T(8,128)(2,1)S(1)}, u32[]{:S(2)}, u32[]{:S(2)}) collective-permute-start(bf16[256,1024]{1,0:T(8,128)(2,1)S(1)} %get-tuple-element.40), channel_id=1, source_target_pairs={{0,3},{3,0},{4,7},{7,4},{8,11},{11,8},{12,15},{15,12},{16,19},{19,... | collective-permute-start | bytes 1572872 | tf_op jit(solution)/shard_map/ppermute | solution.py:536
  152.4 30.0 %collective-permute-start.18 = (f32[64,1664]{1,0:T(8,128)S(1)}, f32[64,1664]{1,0:T(8,128)S(1)}, u32[]{:S(2)}, u32[]{:S(2)}) collective-permute-start(f32[64,1664]{1,0:T(8,128)S(1)} %get-tuple-element.51), channel_id=1, source_target_pairs={{2,10},{3,11},{6,14},{7,15},{10,2},{11,3},{14,6},{15,7},{18,26},{1... | collective-permute-start | bytes 1277960 | tf_op jit(solution)/shard_map/ppermute | solution.py:525
  170.0 17.5 %copy-start.2 = (bf16[256,3072]{1,0:T(8,128)(2,1)S(1)}, bf16[256,3072]{1,0:T(8,128)(2,1)}, u32[]{:S(2)}) copy-start(bf16[256,3072]{1,0:T(8,128)(2,1)} %k_own.5) | copy-start | bytes 4718596
  170.0 0.9 copy-start.10
  170.9 0.8 copy-start.8
  171.7 10.7 %collective-permute-start.14 = (bf16[272,512]{1,0:T(8,128)(2,1)S(1)}, bf16[272,512]{1,0:T(8,128)(2,1)S(1)}, u32[]{:S(2)}, u32[]{:S(2)}) collective-permute-start(bf16[272,512]{1,0:T(8,128)(2,1)S(1)} %get-tuple-element.43), channel_id=1, source_target_pairs={{0,3},{3,0},{4,7},{7,4},{8,11},{11,8},{12,15},{15,12},{16,19},{19,... | collective-permute-start | bytes 835592 | tf_op jit(solution)/shard_map/ppermute | solution.py:536
  173.6 8.7 %collective-permute-start.15 = (bf16[256,512]{1,0:T(8,128)(2,1)S(1)}, bf16[256,512]{1,0:T(8,128)(2,1)S(1)}, u32[]{:S(2)}, u32[]{:S(2)}) collective-permute-start(bf16[256,512]{1,0:T(8,128)(2,1)S(1)} %get-tuple-element.44), channel_id=1, source_target_pairs={{0,3},{3,0},{4,7},{7,4},{8,11},{11,8},{12,15},{15,12},{16,19},{19,... | collective-permute-start | bytes 786440 | tf_op jit(solution)/shard_map/ppermute | solution.py:536
  182.4 1.1 copy-start.15
  183.5 1.6 collective-permute-start.19
  186.2 10.6 %collective-permute-start.20 = (bf16[16,3072]{1,0:T(8,128)(2,1)S(1)}, bf16[16,3072]{1,0:T(8,128)(2,1)S(1)}, u32[]{:S(2)}, u32[]{:S(2)}) collective-permute-start(bf16[16,3072]{1,0:T(8,128)(2,1)S(1)} %slice.8), channel_id=1, source_target_pairs={{2,0},{3,1},{6,4},{7,5},{10,8},{11,9},{14,12},{15,13},{18,16},{19,... | collective-permute-start | bytes 294920 | tf_op jit(solution)/shard_map/ppermute | solution.py:555
  187.5 1.0 copy-start.9
  188.6 1.0 copy-start.11
  189.6 0.9 copy-start.16

commit v13 on v12

--- a/solution.py
+++ b/solution.py
@@ -13,7 +13,7 @@
 NR = 4
 BLOCKS = 5
 STEP_HEADS = 2
-CHUNK_HEADS = (12, 8, 4)
+CHUNK_HEADS = (14, 8, 2)
 PAD_ROWS = 16
 VMEM_BYTES = 48 * 1024 * 1024
 LOG2E = 1.4426950408889634
@@ -528,24 +528,22 @@
 
     count = len(CHUNK_HEADS)
     for i in range(count):
-        before = outs[i - 1 : i] + ([parts[-1][0]] if halving and i == 0 else [])
+        before = outs[i - 1 : i] + (list(parts[-1]) if halving and i == 0 else [])
         if i + 1 < count:
             send(i + 1, *direct[i], *before)
         up, down = tie(direct[i][0], *before), tie(direct[i][1], *before)
-        relays = [
-            lax.ppermute(half, "tiles", pairs["relayed"])
-            for half in choose(sends_later, up, down, rows + PAD_ROWS)
-        ]
+        chosen = choose(sends_later, up, down, rows + PAD_ROWS)
+        relays = [lax.ppermute(half, "tiles", pairs["relayed"]) for half in chosen]
+        if halving and i < 2:
+            merge(*chosen)
+        if halving and i == 1:
+            table = tie(table, parts[-1][0])
         outs.append(
             video_call(
                 starts[i], CHUNK_HEADS[i], table, video_q, video_k, video_v,
                 [*direct[i], *relays, *beside[1:]], text_k, text_v, outs[-1] if outs else None,
             )
         )
-        if i == 0:
-            merge(*relays)
-        elif i + 1 == count:
-            merge(*relays)
     if halving:
         mine, leave = parts[-1]
         got = lax.ppermute(leave, "tiles", [(d, d ^ 1) for d in range(n)])

time: 200 us -> 197 us (0.985)
  the two profiles are of different devices: /device:TPU:24 before, /device:TPU:0 now
where the time goes in v13:
time: 197 us; the launch traced here: 196 us
  starting transfers between devices  67.7 us (34%)
  Pallas kernels  58.5 us (30%)
  waiting for transfers between devices  55 us (28%)
  local copies, waits for them, and re-layouts  11.1 us (6%)
  other arithmetic  2.28 us (1%)
    ppermute x6, starting transfers between devices, send(): lax.ppermute(mine, 'tiles', pairs[x])  42 us
    ppermute x2, waiting for transfers between devices, per_device(): got = lax.ppermute(half, 'tiles', [(d, d | 2) for d in lower])  38.1 us
    pallas_call x3, Pallas kernels, video_call(): pl.pallas_call(video_kernel, grid=(heads // STEP_HEADS,), in_specs=in_spe...  32.6 us
    ppermute x6, starting transfers between devices, per_device(): relays = [lax.ppermute(half, 'tiles', pairs['relayed']) for half in chosen]  16.8 us
    ppermute x6, waiting for transfers between devices, per_device(): relays = [lax.ppermute(half, 'tiles', pairs['relayed']) for half in chosen]  13.7 us
    unnamed x42, local copies, waits for them, and re-layouts  8.6 us
    pallas_call x1, Pallas kernels, text_local(): pl.pallas_call(text_kernel, grid_spec=pltpu.PrefetchScalarGridSpec(num_sc...  8.08 us
    pallas_call x3, Pallas kernels, choose(): pl.pallas_call(choose_kernel, in_specs=[pl.BlockSpec(memory_space=pltpu.S...  7.43 us
  transfers between devices with their start and end apart: 21, of which 5 were waited for; matrix products, arithmetic and copies ran while one was open for 3% of the time, Pallas kernels for 28%

profile of v13, /device:TPU:0, one launch (start us, length us, event | category | flops | bytes accessed | tf_op | source)
XLA Modules:
  0.0 196.3 jit_solution(8843017772361430599)
XLA Ops:
  1.7 1.4 copy-done
  3.1 1.4 copy-done.3
  4.5 0.7 copy-done.15
  5.2 1.8 pack_chunk.3
  7.0 1.3 collective-permute-start.4
  8.3 7.2 %collective-permute-start.6 = (bf16[528,1792]{1,0:T(8,128)(2,1)}, bf16[528,1792]{1,0:T(8,128)(2,1)}, u32[]{:S(2)}, u32[]{:S(2)}) collective-permute-start(bf16[528,1792]{1,0:T(8,128)(2,1)} %pack_chunk.3), channel_id=1, source_target_pairs={{0,12},{1,13},{4,0},{6,2},{7,3},{8,4},{9,5},{10,6},{11,7},{12,8},{... | collective-permute-start | bytes 5677064 | tf_op jit(solution)/shard_map/ppermute | solution.py:501
  15.7 8.1 %text_partials.1 = (f32[128,1792]{1,0:T(8,128)S(1)}, f32[128,1792]{1,0:T(8,128)S(1)}) custom-call(s32[17]{0:T(128)S(1)} %pad_add_fusion.1.order, s32[4]{0:T(128)S(1)} %pad_add_fusion.2.counts, bf16[256,3072]{1,0:T(8,128)(2,1)S(1)} %copy-done.12, bf16[256,3072]{1,0:T(8,128)(2,1)S(1)} %copy-done.1, bf16[256,3072]{1,0:T(8,128)(2,1)} %v_own.5, ...), custom_call_target="tpu_custom_call" | custom-call | flops 8388608 | bytes 786432 | tf_op jit(solution)/shard_map/text_partials/pallas_call | solution.py:367
  23.8 2.1 %collective-permute-start.3 = (f32[128,1792]{1,0:T(8,128)S(1)}, f32[128,1792]{1,0:T(8,128)S(1)}, u32[]{:S(2)}, u32[]{:S(2)}) collective-permute-start(f32[128,1792]{1,0:T(8,128)S(1)} %get-tuple-element.29.refs_0_), channel_id=1, source_target_pairs={{0,2},{1,3},{4,6},{5,7},{8,10},{9,11},{12,14},{13,15},{16,18},{17,... | collective-permute-start | bytes 2752520 | tf_op jit(solution)/shard_map/ppermute | solution.py:518
  25.9 1.3 collective-permute-start.5
  27.3 19.3 %collective-permute-done.3.refs_1_ = f32[128,1792]{1,0:T(8,128)S(1)} collective-permute-done((f32[128,1792]{1,0:T(8,128)S(1)}, f32[128,1792]{1,0:T(8,128)S(1)}, u32[]{:S(2)}, u32[]{:S(2)}) %collective-permute-start.3) | collective-permute-done | bytes 917536 | tf_op jit(solution)/shard_map/ppermute | solution.py:518
  46.5 0.8 text_merge.3
  47.3 18.9 %collective-permute-done.5.refs_1_ = f32[128,1792]{1,0:T(8,128)S(1)} collective-permute-done((f32[128,1792]{1,0:T(8,128)S(1)}, f32[128,1792]{1,0:T(8,128)S(1)}, u32[]{:S(2)}, u32[]{:S(2)}) %collective-permute-start.5) | collective-permute-done | bytes 917536 | tf_op jit(solution)/shard_map/ppermute | solution.py:518
  66.2 0.8 text_merge.4
  67.0 0.8 constant_dynamic-update-slice_fusion.3
  67.8 0.8 constant_dynamic-update-slice_fusion
  68.6 0.9 copy-done.10
  69.6 1.7 collective-permute-start.7
  71.3 1.6 pack_chunk.4
  72.9 3.1 %collective-permute-done.6.b.rest_1_ = bf16[528,1792]{1,0:T(8,128)(2,1)} collective-permute-done((bf16[528,1792]{1,0:T(8,128)(2,1)}, bf16[528,1792]{1,0:T(8,128)(2,1)}, u32[]{:S(2)}, u32[]{:S(2)}) %collective-permute-start.6) | collective-permute-done | bytes 1892384 | tf_op jit(solution)/shard_map/ppermute | solution.py:501
  76.0 1.3 collective-permute-start.8
  77.3 24.6 %collective-permute-start.11 = (bf16[528,1024]{1,0:T(8,128)(2,1)}, bf16[528,1024]{1,0:T(8,128)(2,1)}, u32[]{:S(2)}, u32[]{:S(2)}) collective-permute-start(bf16[528,1024]{1,0:T(8,128)(2,1)} %pack_chunk.4), channel_id=1, source_target_pairs={{0,12},{1,13},{4,0},{6,2},{7,3},{8,4},{9,5},{10,6},{11,7},{12,8},{... | collective-permute-start | bytes 3244040 | tf_op jit(solution)/shard_map/ppermute | solution.py:501
  102.5 3.4 %choose_relayed.3 = (bf16[272,1792]{1,0:T(8,128)(2,1)}, bf16[256,1792]{1,0:T(8,128)(2,1)}) custom-call(s32[1]{0:T(128)} %dynamic_slice.8.second, bf16[528,1792]{1,0:T(8,128)(2,1)} %collective-permute-done.4.a.rest_0_, bf16[528,1792]{1,0:T(8,128)(2,1)} %collective-permute-done.6.b.rest_1_), custom_call_target="tpu_custom_call" | custom-call | tf_op jit(solution)/shard_map/choose_relayed/pallas_call | solution.py:124
  105.9 2.1 %collective-permute-start.9 = (bf16[272,1792]{1,0:T(8,128)(2,1)}, bf16[272,1792]{1,0:T(8,128)(2,1)}, u32[]{:S(2)}, u32[]{:S(2)}) collective-permute-start(bf16[272,1792]{1,0:T(8,128)(2,1)} %get-tuple-element.37), channel_id=1, source_target_pairs={{0,3},{3,0},{4,7},{7,4},{8,11},{11,8},{12,15},{15,12},{16,19},{19,... | collective-permute-start | bytes 2924552 | tf_op jit(solution)/shard_map/ppermute | solution.py:536
  108.0 3.6 %collective-permute-start.10 = (bf16[256,1792]{1,0:T(8,128)(2,1)}, bf16[256,1792]{1,0:T(8,128)(2,1)}, u32[]{:S(2)}, u32[]{:S(2)}) collective-permute-start(bf16[256,1792]{1,0:T(8,128)(2,1)} %get-tuple-element.38), channel_id=1, source_target_pairs={{0,3},{3,0},{4,7},{7,4},{8,11},{11,8},{12,15},{15,12},{16,19},{19,... | collective-permute-start | bytes 2752520 | tf_op jit(solution)/shard_map/ppermute | solution.py:536
  112.1 1.1 copy-done.11
  113.3 2.7 %text_merge.5 = (f32[64,1664]{1,0:T(8,128)S(1)}, f32[64,1664]{1,0:T(8,128)}) custom-call(f32[128,1664]{1,0:T(8,128)S(1)} %copy-done.11, f32[128,1664]{1,0:T(8,128)} %collective-permute-done.7.refs_1_), custom_call_target="tpu_custom_call" | custom-call | tf_op jit(solution)/shard_map/text_merge/pallas_call | solution.py:418
  116.0 0.8 copy-done.13
  116.7 1.4 collective-permute-start.12
  119.0 0.7 dynamic-slice_bitcast_fusion
  119.8 11.8 %collective-permute-done.10.rest_3_ = bf16[256,1792]{1,0:T(8,128)(2,1)} collective-permute-done((bf16[256,1792]{1,0:T(8,128)(2,1)}, bf16[256,1792]{1,0:T(8,128)(2,1)}, u32[]{:S(2)}, u32[]{:S(2)}) %collective-permute-start.10) | collective-permute-done | bytes 917536 | tf_op jit(solution)/shard_map/ppermute | solution.py:536
  131.6 17.6 %video_attention.3.rest_8_ = bf16[256,3072]{1,0:T(8,128)(2,1)} custom-call(s32[13]{0:T(128)S(1)} %concatenate.21.table, bf16[256,3072]{1,0:T(8,128)(2,1)S(1)} %copy-done.7, bf16[256,3072]{1,0:T(8,128)(2,1)S(1)} %copy-done.1, bf16[256,3072]{1,0:T(8,128)(2,1)} %v_own.5, bf16[528,1792]{1,0:T(8,128)(2,1)} %collective-permute-done.4.a.rest_0_, ...), custom_call_target="tpu_custom_call" | custom-call | flops 132120576 | bytes 458752 | tf_op jit(solution)/shard_map/video_attention/pallas_call | solution.py:275
  149.2 3.0 %choose_relayed.4 = (bf16[272,1024]{1,0:T(8,128)(2,1)}, bf16[256,1024]{1,0:T(8,128)(2,1)}) custom-call(s32[1]{0:T(128)} %dynamic_slice.8.second, bf16[528,1024]{1,0:T(8,128)(2,1)} %collective-permute-done.8.a.rest_0_, bf16[528,1024]{1,0:T(8,128)(2,1)} %collective-permute-done.11.b.rest_1_), custom_call_target="tpu_custom_call" | custom-call | tf_op jit(solution)/shard_map/choose_relayed/pallas_call | solution.py:124
  152.2 2.2 %collective-permute-start.15 = (bf16[272,1024]{1,0:T(8,128)(2,1)}, bf16[272,1024]{1,0:T(8,128)(2,1)}, u32[]{:S(2)}, u32[]{:S(2)}) collective-permute-start(bf16[272,1024]{1,0:T(8,128)(2,1)} %get-tuple-element.44), channel_id=1, source_target_pairs={{0,3},{3,0},{4,7},{7,4},{8,11},{11,8},{12,15},{15,12},{16,19},{19,... | collective-permute-start | bytes 1671176 | tf_op jit(solution)/shard_map/ppermute | solution.py:536
  154.4 2.1 %text_finish.1 = (bf16[32,1536]{1,0:T(8,128)(2,1)S(1)}, bf16[32,1536]{1,0:T(8,128)(2,1)}) custom-call(f32[64,1664]{1,0:T(8,128)S(1)} %copy-done.14, f32[64,1664]{1,0:T(8,128)} %collective-permute-done.12.refs_1_), custom_call_target="tpu_custom_call" | custom-call | tf_op jit(solution)/shard_map/text_finish/pallas_call | solution.py:428
  156.5 3.3 %collective-permute-start.16 = (bf16[256,1024]{1,0:T(8,128)(2,1)}, bf16[256,1024]{1,0:T(8,128)(2,1)}, u32[]{:S(2)}, u32[]{:S(2)}) collective-permute-start(bf16[256,1024]{1,0:T(8,128)(2,1)} %get-tuple-element.45), channel_id=1, source_target_pairs={{0,3},{3,0},{4,7},{7,4},{8,11},{11,8},{12,15},{15,12},{16,19},{19,... | collective-permute-start | bytes 1572872 | tf_op jit(solution)/shard_map/ppermute | solution.py:536
  159.9 0.6 pack_chunk.5
  160.6 1.3 collective-permute-start.13
  161.9 6.3 %collective-permute-start.14 = (bf16[528,256]{1,0:T(8,128)(2,1)S(1)}, bf16[528,256]{1,0:T(8,128)(2,1)S(1)}, u32[]{:S(2)}, u32[]{:S(2)}) collective-permute-start(bf16[528,256]{1,0:T(8,128)(2,1)S(1)} %pack_chunk.5), channel_id=1, source_target_pairs={{0,12},{1,13},{4,0},{6,2},{7,3},{8,4},{9,5},{10,6},{11,7},{12,8},{... | collective-permute-start | bytes 811016 | tf_op jit(solution)/shard_map/ppermute | solution.py:501
  168.2 1.0 maximum_select_fusion
  169.3 1.3 collective-permute-start.20
  170.6 1.4 copy-done.8
  172.0 11.1 %video_attention.4.rest_8_ = bf16[256,3072]{1,0:T(8,128)(2,1)} custom-call(s32[13]{0:T(128)S(1)} %concatenate.21.table, bf16[256,3072]{1,0:T(8,128)(2,1)S(1)} %copy-done.8, bf16[256,3072]{1,0:T(8,128)(2,1)} %k_own.5, bf16[256,3072]{1,0:T(8,128)(2,1)} %v_own.5, bf16[528,1024]{1,0:T(8,128)(2,1)} %collective-permute-done.8.a.rest_0_, ...), custom_call_target="tpu_custom_call", output_to_operand_aliasing={{}: (12, {})} | custom-call | flops 75497472 | bytes 262144 | tf_op jit(solution)/shard_map/video_attention/pallas_call | solution.py:275
  183.1 1.0 choose_relayed.5
  184.1 1.9 collective-permute-start.17
  186.1 3.6 %collective-permute-start.18 = (bf16[256,256]{1,0:T(8,128)(2,1)S(1)}, bf16[256,256]{1,0:T(8,128)(2,1)S(1)}, u32[]{:S(2)}, u32[]{:S(2)}) collective-permute-start(bf16[256,256]{1,0:T(8,128)(2,1)S(1)} %get-tuple-element.54), channel_id=1, source_target_pairs={{0,3},{3,0},{4,7},{7,4},{8,11},{11,8},{12,15},{15,12},{16,19},{19,... | collective-permute-start | bytes 393224 | tf_op jit(solution)/shard_map/ppermute | solution.py:536
  189.7 0.7 fusion
  190.5 1.9 collective-permute-done.18.rest_3_
  192.4 3.9 %video_attention.5 = bf16[256,3072]{1,0:T(8,128)(2,1)} custom-call(s32[13]{0:T(128)S(1)} %concatenate.21.table, bf16[256,3072]{1,0:T(8,128)(2,1)S(1)} %copy-done.9, bf16[256,3072]{1,0:T(8,128)(2,1)S(1)} %copy-done.2, bf16[256,3072]{1,0:T(8,128)(2,1)S(1)} %copy-done.6, ...), custom_call_target="tpu_custom_call", output_to_operand_aliasing={{}: (12, {})} | custom-call | flops 18874368 | bytes 65536 | tf_op jit(solution)/shard_map/video_attention/pallas_call | solution.py:275
  (70 shorter events, 2.7 us)
Async XLA Ops:
  0.6 14.9 %copy-start.19 = (s32[16]{0:T(128)S(1)}, s32[16]{0:T(128)}, u32[]{:S(2)}) copy-start(s32[16]{0:T(128)} %constant.79.clone) | copy-start | bytes 196
  0.6 15.1 %collective-permute-start.1 = (bf16[256,3072]{1,0:T(8,128)(2,1)}, bf16[256,3072]{1,0:T(8,128)(2,1)}, u32[]{:S(2)}, u32[]{:S(2)}) collective-permute-start(bf16[256,3072]{1,0:T(8,128)(2,1)} %k_own.5), channel_id=1, source_target_pairs={{0,1},{1,0},{2,3},{3,2},{4,5},{5,4},{6,7},{7,6},{8,9},{9,8},{10,11... | collective-permute-start | bytes 4718600 | tf_op jit(solution)/shard_map/ppermute | solution.py:505
  1.2 14.6 %collective-permute-start.2 = (bf16[256,3072]{1,0:T(8,128)(2,1)}, bf16[256,3072]{1,0:T(8,128)(2,1)}, u32[]{:S(2)}, u32[]{:S(2)}) collective-permute-start(bf16[256,3072]{1,0:T(8,128)(2,1)} %v_own.5), channel_id=1, source_target_pairs={{0,1},{1,0},{2,3},{3,2},{4,5},{5,4},{6,7},{7,6},{8,9},{9,8},{10,11... | collective-permute-start | bytes 4718600 | tf_op jit(solution)/shard_map/ppermute | solution.py:505
  1.2 14.4 %collective-permute-start = (s32[2]{0:T(128)}, s32[2]{0:T(128)S(1)}, u32[]{:S(2)}, u32[]{:S(2)}) collective-permute-start(s32[2]{0:T(128)} %counts.5), channel_id=1, source_target_pairs={{0,1},{1,0},{2,3},{3,2},{4,5},{5,4},{6,7},{7,6},{8,9},{9,8},{10,11... | collective-permute-start | bytes 32 | tf_op jit(solution)/shard_map/ppermute | solution.py:505
  1.7 1.4 copy-start
  3.1 1.4 copy-start.3
  4.5 0.7 copy-start.15
  5.1 10.5 %copy-start.16 = (s32[2]{0:T(128)S(1)}, s32[2]{0:T(128)}, u32[]{:S(2)}) copy-start(s32[2]{0:T(128)} %counts.5) | copy-start | bytes 28
  5.1 10.6 %copy-start.1 = (bf16[256,3072]{1,0:T(8,128)(2,1)S(1)}, bf16[256,3072]{1,0:T(8,128)(2,1)}, u32[]{:S(2)}) copy-start(bf16[256,3072]{1,0:T(8,128)(2,1)} %k_own.5) | copy-start | bytes 4718596
  5.1 10.6 %copy-start.12 = (bf16[256,3072]{1,0:T(8,128)(2,1)S(1)}, bf16[256,3072]{1,0:T(8,128)(2,1)}, u32[]{:S(2)}) copy-start(bf16[256,3072]{1,0:T(8,128)(2,1)} %q.4) | copy-start | bytes 4718596
  7.0 65.9 %collective-permute-start.4 = (bf16[528,1792]{1,0:T(8,128)(2,1)}, bf16[528,1792]{1,0:T(8,128)(2,1)}, u32[]{:S(2)}, u32[]{:S(2)}) collective-permute-start(bf16[528,1792]{1,0:T(8,128)(2,1)} %pack_chunk.3), channel_id=1, source_target_pairs={{2,6},{3,7},{4,8},{5,9},{6,10},{7,11},{8,12},{9,13},{10,14},{11,15... | collective-permute-start | bytes 5677064 | tf_op jit(solution)/shard_map/ppermute | solution.py:501
  8.3 67.7 %collective-permute-start.6 = (bf16[528,1792]{1,0:T(8,128)(2,1)}, bf16[528,1792]{1,0:T(8,128)(2,1)}, u32[]{:S(2)}, u32[]{:S(2)}) collective-permute-start(bf16[528,1792]{1,0:T(8,128)(2,1)} %pack_chunk.3), channel_id=1, source_target_pairs={{0,12},{1,13},{4,0},{6,2},{7,3},{8,4},{9,5},{10,6},{11,7},{12,8},{... | collective-permute-start | bytes 5677064 | tf_op jit(solution)/shard_map/ppermute | solution.py:501
  23.8 22.7 %collective-permute-start.3 = (f32[128,1792]{1,0:T(8,128)S(1)}, f32[128,1792]{1,0:T(8,128)S(1)}, u32[]{:S(2)}, u32[]{:S(2)}) collective-permute-start(f32[128,1792]{1,0:T(8,128)S(1)} %get-tuple-element.29.refs_0_), channel_id=1, source_target_pairs={{0,2},{1,3},{4,6},{5,7},{8,10},{9,11},{12,14},{13,15},{16,18},{17,... | collective-permute-start | bytes 2752520 | tf_op jit(solution)/shard_map/ppermute | solution.py:518
  25.9 40.3 %collective-permute-start.5 = (f32[128,1792]{1,0:T(8,128)S(1)}, f32[128,1792]{1,0:T(8,128)S(1)}, u32[]{:S(2)}, u32[]{:S(2)}) collective-permute-start(f32[128,1792]{1,0:T(8,128)S(1)} %get-tuple-element.32.refs_0_), channel_id=1, source_target_pairs={{0,2},{1,3},{4,6},{5,7},{8,10},{9,11},{12,14},{13,15},{16,18},{17,... | collective-permute-start | bytes 2752520 | tf_op jit(solution)/shard_map/ppermute | solution.py:518
  67.0 4.3 %copy-start.4 = (bf16[256,3072]{1,0:T(8,128)(2,1)S(1)}, bf16[256,3072]{1,0:T(8,128)(2,1)}, u32[]{:S(2)}) copy-start(bf16[256,3072]{1,0:T(8,128)(2,1)} %v_own.5) | copy-start | bytes 4718596
  68.6 0.9 copy-start.10
  69.6 32.3 %copy-start.18 = (s32[16]{0:T(128)S(1)}, s32[16]{0:T(128)}, u32[]{:S(2)}) copy-start(s32[16]{0:T(128)} %constant.77.clone) | copy-start | bytes 196
  69.6 42.5 %collective-permute-start.7 = (f32[128,1664]{1,0:T(8,128)}, f32[128,1664]{1,0:T(8,128)}, u32[]{:S(2)}, u32[]{:S(2)}) collective-permute-start(f32[128,1664]{1,0:T(8,128)} %get-tuple-element.61), channel_id=1, source_target_pairs={{2,6},{3,7},{6,2},{7,3},{10,14},{11,15},{14,10},{15,11},{18,22},{1... | collective-permute-start | bytes 2555912 | tf_op jit(solution)/shard_map/ppermute | solution.py:525
  76.0 73.2 %collective-permute-start.8 = (bf16[528,1024]{1,0:T(8,128)(2,1)}, bf16[528,1024]{1,0:T(8,128)(2,1)}, u32[]{:S(2)}, u32[]{:S(2)}) collective-permute-start(bf16[528,1024]{1,0:T(8,128)(2,1)} %pack_chunk.4), channel_id=1, source_target_pairs={{2,6},{3,7},{4,8},{5,9},{6,10},{7,11},{8,12},{9,13},{10,14},{11,15... | collective-permute-start | bytes 3244040 | tf_op jit(solution)/shard_map/ppermute | solution.py:501
  77.3 71.9 %collective-permute-start.11 = (bf16[528,1024]{1,0:T(8,128)(2,1)}, bf16[528,1024]{1,0:T(8,128)(2,1)}, u32[]{:S(2)}, u32[]{:S(2)}) collective-permute-start(bf16[528,1024]{1,0:T(8,128)(2,1)} %pack_chunk.4), channel_id=1, source_target_pairs={{0,12},{1,13},{4,0},{6,2},{7,3},{8,4},{9,5},{10,6},{11,7},{12,8},{... | collective-permute-start | bytes 3244040 | tf_op jit(solution)/shard_map/ppermute | solution.py:501
  102.5 9.3 %copy-start.17 = (s32[2,6]{1,0:T(2,128)S(1)}, s32[2,6]{1,0:T(2,128)}, u32[]{:S(2)}) copy-start(s32[2,6]{1,0:T(2,128)} %param.18) | copy-start | bytes 148
  105.9 25.6 %copy-start.7 = (bf16[256,3072]{1,0:T(8,128)(2,1)S(1)}, bf16[256,3072]{1,0:T(8,128)(2,1)}, u32[]{:S(2)}) copy-start(bf16[256,3072]{1,0:T(8,128)(2,1)} %q.7) | copy-start | bytes 4718596
  105.9 25.6 %collective-permute-start.9 = (bf16[272,1792]{1,0:T(8,128)(2,1)}, bf16[272,1792]{1,0:T(8,128)(2,1)}, u32[]{:S(2)}, u32[]{:S(2)}) collective-permute-start(bf16[272,1792]{1,0:T(8,128)(2,1)} %get-tuple-element.37), channel_id=1, source_target_pairs={{0,3},{3,0},{4,7},{7,4},{8,11},{11,8},{12,15},{15,12},{16,19},{19,... | collective-permute-start | bytes 2924552 | tf_op jit(solution)/shard_map/ppermute | solution.py:536
  108.0 23.5 %collective-permute-start.10 = (bf16[256,1792]{1,0:T(8,128)(2,1)}, bf16[256,1792]{1,0:T(8,128)(2,1)}, u32[]{:S(2)}, u32[]{:S(2)}) collective-permute-start(bf16[256,1792]{1,0:T(8,128)(2,1)} %get-tuple-element.38), channel_id=1, source_target_pairs={{0,3},{3,0},{4,7},{7,4},{8,11},{11,8},{12,15},{15,12},{16,19},{19,... | collective-permute-start | bytes 2752520 | tf_op jit(solution)/shard_map/ppermute | solution.py:536
  112.1 1.2 copy-start.11
  116.0 0.8 copy-start.13
  116.7 37.7 %collective-permute-start.12 = (f32[64,1664]{1,0:T(8,128)}, f32[64,1664]{1,0:T(8,128)}, u32[]{:S(2)}, u32[]{:S(2)}) collective-permute-start(f32[64,1664]{1,0:T(8,128)} %get-tuple-element.47), channel_id=1, source_target_pairs={{2,10},{3,11},{6,14},{7,15},{10,2},{11,3},{14,6},{15,7},{18,26},{1... | collective-permute-start | bytes 1277960 | tf_op jit(solution)/shard_map/ppermute | solution.py:525
  149.2 5.3 %copy-start.14 = (f32[64,1664]{1,0:T(8,128)S(1)}, f32[64,1664]{1,0:T(8,128)}, u32[]{:S(2)}) copy-start(f32[64,1664]{1,0:T(8,128)} %copy-done.13) | copy-start | bytes 1277956
  149.2 10.7 %copy-start.5 = (bf16[256,3072]{1,0:T(8,128)(2,1)S(1)}, bf16[256,3072]{1,0:T(8,128)(2,1)}, u32[]{:S(2)}) copy-start(bf16[256,3072]{1,0:T(8,128)(2,1)} %v_own.5) | copy-start | bytes 4718596
  152.2 18.4 %collective-permute-start.15 = (bf16[272,1024]{1,0:T(8,128)(2,1)}, bf16[272,1024]{1,0:T(8,128)(2,1)}, u32[]{:S(2)}, u32[]{:S(2)}) collective-permute-start(bf16[272,1024]{1,0:T(8,128)(2,1)} %get-tuple-element.44), channel_id=1, source_target_pairs={{0,3},{3,0},{4,7},{7,4},{8,11},{11,8},{12,15},{15,12},{16,19},{19,... | collective-permute-start | bytes 1671176 | tf_op jit(solution)/shard_map/ppermute | solution.py:536
  156.5 11.7 %collective-permute-start.19 = (bf16[32,1536]{1,0:T(8,128)(2,1)}, bf16[32,1536]{1,0:T(8,128)(2,1)}, u32[]{:S(2)}, u32[]{:S(2)}) collective-permute-start(bf16[32,1536]{1,0:T(8,128)(2,1)} %get-tuple-element.55), channel_id=1, source_target_pairs={{0,1},{1,0},{2,3},{3,2},{4,5},{5,4},{6,7},{7,6},{8,9},{9,8},{10,11... | collective-permute-start | bytes 294920 | tf_op jit(solution)/shard_map/ppermute | solution.py:549
  156.5 14.0 %collective-permute-start.16 = (bf16[256,1024]{1,0:T(8,128)(2,1)}, bf16[256,1024]{1,0:T(8,128)(2,1)}, u32[]{:S(2)}, u32[]{:S(2)}) collective-permute-start(bf16[256,1024]{1,0:T(8,128)(2,1)} %get-tuple-element.45), channel_id=1, source_target_pairs={{0,3},{3,0},{4,7},{7,4},{8,11},{11,8},{12,15},{15,12},{16,19},{19,... | collective-permute-start | bytes 1572872 | tf_op jit(solution)/shard_map/ppermute | solution.py:536
  160.6 22.5 %collective-permute-start.13 = (bf16[528,256]{1,0:T(8,128)(2,1)S(1)}, bf16[528,256]{1,0:T(8,128)(2,1)S(1)}, u32[]{:S(2)}, u32[]{:S(2)}) collective-permute-start(bf16[528,256]{1,0:T(8,128)(2,1)S(1)} %pack_chunk.5), channel_id=1, source_target_pairs={{2,6},{3,7},{4,8},{5,9},{6,10},{7,11},{8,12},{9,13},{10,14},{11,15... | collective-permute-start | bytes 811016 | tf_op jit(solution)/shard_map/ppermute | solution.py:501
  161.9 21.3 %collective-permute-start.14 = (bf16[528,256]{1,0:T(8,128)(2,1)S(1)}, bf16[528,256]{1,0:T(8,128)(2,1)S(1)}, u32[]{:S(2)}, u32[]{:S(2)}) collective-permute-start(bf16[528,256]{1,0:T(8,128)(2,1)S(1)} %pack_chunk.5), channel_id=1, source_target_pairs={{0,12},{1,13},{4,0},{6,2},{7,3},{8,4},{9,5},{10,6},{11,7},{12,8},{... | collective-permute-start | bytes 811016 | tf_op jit(solution)/shard_map/ppermute | solution.py:501
  169.3 20.5 %collective-permute-start.20 = (bf16[16,3072]{1,0:T(8,128)(2,1)S(1)}, bf16[16,3072]{1,0:T(8,128)(2,1)S(1)}, u32[]{:S(2)}, u32[]{:S(2)}) collective-permute-start(bf16[16,3072]{1,0:T(8,128)(2,1)S(1)} %slice.8), channel_id=1, source_target_pairs={{2,0},{3,1},{6,4},{7,5},{10,8},{11,9},{14,12},{15,13},{18,16},{19,... | collective-permute-start | bytes 294920 | tf_op jit(solution)/shard_map/ppermute | solution.py:553
  170.6 1.4 copy-start.8
  172.0 20.4 %copy-start.2 = (bf16[256,3072]{1,0:T(8,128)(2,1)S(1)}, bf16[256,3072]{1,0:T(8,128)(2,1)}, u32[]{:S(2)}) copy-start(bf16[256,3072]{1,0:T(8,128)(2,1)} %k_own.5) | copy-start | bytes 4718596
  172.0 20.4 %copy-start.6 = (bf16[256,3072]{1,0:T(8,128)(2,1)S(1)}, bf16[256,3072]{1,0:T(8,128)(2,1)}, u32[]{:S(2)}) copy-start(bf16[256,3072]{1,0:T(8,128)(2,1)} %v_own.5) | copy-start | bytes 4718596
  172.0 20.4 %copy-start.9 = (bf16[256,3072]{1,0:T(8,128)(2,1)S(1)}, bf16[256,3072]{1,0:T(8,128)(2,1)}, u32[]{:S(2)}) copy-start(bf16[256,3072]{1,0:T(8,128)(2,1)} %q.7) | copy-start | bytes 4718596
  184.1 8.2 %collective-permute-start.17 = (bf16[272,256]{1,0:T(8,128)(2,1)S(1)}, bf16[272,256]{1,0:T(8,128)(2,1)S(1)}, u32[]{:S(2)}, u32[]{:S(2)}) collective-permute-start(bf16[272,256]{1,0:T(8,128)(2,1)S(1)} %get-tuple-element.53), channel_id=1, source_target_pairs={{0,3},{3,0},{4,7},{7,4},{8,11},{11,8},{12,15},{15,12},{16,19},{19,... | collective-permute-start | bytes 417800 | tf_op jit(solution)/shard_map/ppermute | solution.py:536
  186.1 6.3 %collective-permute-start.18 = (bf16[256,256]{1,0:T(8,128)(2,1)S(1)}, bf16[256,256]{1,0:T(8,128)(2,1)S(1)}, u32[]{:S(2)}, u32[]{:S(2)}) collective-permute-start(bf16[256,256]{1,0:T(8,128)(2,1)S(1)} %get-tuple-element.54), channel_id=1, source_target_pairs={{0,3},{3,0},{4,7},{7,4},{8,11},{11,8},{12,15},{15,12},{16,19},{19,... | collective-permute-start | bytes 393224 | tf_op jit(solution)/shard_map/ppermute | solution.py:536

commit v14 on v13

--- a/solution.py
+++ b/solution.py
@@ -13,7 +13,7 @@
 NR = 4
 BLOCKS = 5
 STEP_HEADS = 2
-CHUNK_HEADS = (14, 8, 2)
+CHUNK_HEADS = (14, 10)
 PAD_ROWS = 16
 VMEM_BYTES = 48 * 1024 * 1024
 LOG2E = 1.4426950408889634

time: 197 us -> 211 us (1.071)
  the two profiles are of different devices: /device:TPU:0 before, /device:TPU:24 now
where the time goes in v14:
time: 211 us; the launch traced here: 207 us
  waiting for transfers between devices  91.2 us (43%)
  Pallas kernels  54.8 us (26%)
  starting transfers between devices  45.6 us (22%)
  local copies, waits for them, and re-layouts  12.1 us (6%)
    ppermute x2, waiting for transfers between devices, per_device(): got = lax.ppermute(half, 'tiles', [(d, d | 2) for d in lower])  35.4 us
    pallas_call x2, Pallas kernels, video_call(): pl.pallas_call(video_kernel, grid=(heads // STEP_HEADS,), in_specs=in_spe...  31.2 us
    ppermute x4, waiting for transfers between devices, send(): lax.ppermute(mine, 'tiles', pairs[x])  29.9 us
    ppermute x4, starting transfers between devices, per_device(): relays = [lax.ppermute(half, 'tiles', pairs['relayed']) for half in chosen]  22.9 us
    ppermute x4, waiting for transfers between devices, per_device(): relays = [lax.ppermute(half, 'tiles', pairs['relayed']) for half in chosen]  21.4 us
    ppermute x4, starting transfers between devices, send(): lax.ppermute(mine, 'tiles', pairs[x])  11.7 us
    unnamed x36, local copies, waits for them, and re-layouts  9.67 us
    pallas_call x1, Pallas kernels, text_local(): pl.pallas_call(text_kernel, grid_spec=pltpu.PrefetchScalarGridSpec(num_sc...  8.07 us
  transfers between devices with their start and end apart: 17, of which 7 were waited for; matrix products, arithmetic and copies ran while one was open for 2% of the time, Pallas kernels for 19%

profile of v14, /device:TPU:24, one launch (start us, length us, event | category | flops | bytes accessed | tf_op | source)
XLA Modules:
  0.0 206.6 jit_solution(201290826118624162)
XLA Ops:
  0.7 0.5 collective-permute-start.2
  1.3 1.4 copy-done
  2.7 1.4 copy-done.2
  4.1 0.7 copy-done.10
  4.8 1.9 pack_chunk.2
  6.6 1.9 collective-permute-start.4
  8.6 3.9 %collective-permute-start.6 = (bf16[528,1792]{1,0:T(8,128)(2,1)}, bf16[528,1792]{1,0:T(8,128)(2,1)}, u32[]{:S(2)}, u32[]{:S(2)}) collective-permute-start(bf16[528,1792]{1,0:T(8,128)(2,1)} %pack_chunk.2), channel_id=1, source_target_pairs={{0,12},{1,13},{4,0},{6,2},{7,3},{8,4},{9,5},{10,6},{11,7},{12,8},{... | collective-permute-start | bytes 5677064 | tf_op jit(solution)/shard_map/ppermute | solution.py:501
  12.7 1.1 copy-done.13
  13.9 1.4 copy-done.7
  15.3 8.1 %text_partials.1 = (f32[128,1792]{1,0:T(8,128)S(1)}, f32[128,1792]{1,0:T(8,128)S(1)}) custom-call(s32[17]{0:T(128)S(1)} %pad_add_fusion.1.order, s32[4]{0:T(128)S(1)} %pad_add_fusion.2.counts, bf16[256,3072]{1,0:T(8,128)(2,1)S(1)} %copy-done.7, bf16[256,3072]{1,0:T(8,128)(2,1)S(1)} %copy-done.1, bf16[256,3072]{1,0:T(8,128)(2,1)} %v_own.3, ...), custom_call_target="tpu_custom_call" | custom-call | flops 8388608 | bytes 786432 | tf_op jit(solution)/shard_map/text_partials/pallas_call | solution.py:367
  23.3 4.7 %collective-permute-start.3 = (f32[128,1792]{1,0:T(8,128)S(1)}, f32[128,1792]{1,0:T(8,128)S(1)}, u32[]{:S(2)}, u32[]{:S(2)}) collective-permute-start(f32[128,1792]{1,0:T(8,128)S(1)} %get-tuple-element.24.refs_0_), channel_id=1, source_target_pairs={{0,2},{1,3},{4,6},{5,7},{8,10},{9,11},{12,14},{13,15},{16,18},{17,... | collective-permute-start | bytes 2752520 | tf_op jit(solution)/shard_map/ppermute | solution.py:518
  28.0 1.3 collective-permute-start.5
  29.4 1.6 pack_chunk.3
  31.1 17.7 %collective-permute-done.3.refs_1_ = f32[128,1792]{1,0:T(8,128)S(1)} collective-permute-done((f32[128,1792]{1,0:T(8,128)S(1)}, f32[128,1792]{1,0:T(8,128)S(1)}, u32[]{:S(2)}, u32[]{:S(2)}) %collective-permute-start.3) | collective-permute-done | bytes 917536 | tf_op jit(solution)/shard_map/ppermute | solution.py:518
  48.7 0.8 text_merge.3
  49.5 17.8 %collective-permute-done.5.refs_1_ = f32[128,1792]{1,0:T(8,128)S(1)} collective-permute-done((f32[128,1792]{1,0:T(8,128)S(1)}, f32[128,1792]{1,0:T(8,128)S(1)}, u32[]{:S(2)}, u32[]{:S(2)}) %collective-permute-start.5) | collective-permute-done | bytes 917536 | tf_op jit(solution)/shard_map/ppermute | solution.py:518
  67.3 0.8 text_merge.4
  68.1 0.8 constant_dynamic-update-slice_fusion.3
  68.9 0.8 constant_dynamic-update-slice_fusion
  69.7 0.9 copy-done.5
  70.6 22.4 %collective-permute-done.4.a.rest_0_ = bf16[528,1792]{1,0:T(8,128)(2,1)} collective-permute-done((bf16[528,1792]{1,0:T(8,128)(2,1)}, bf16[528,1792]{1,0:T(8,128)(2,1)}, u32[]{:S(2)}, u32[]{:S(2)}) %collective-permute-start.4) | collective-permute-done | bytes 1892384 | tf_op jit(solution)/shard_map/ppermute | solution.py:501
  93.0 1.9 collective-permute-start.8
  94.9 3.9 %collective-permute-start.11 = (bf16[528,1280]{1,0:T(8,128)(2,1)}, bf16[528,1280]{1,0:T(8,128)(2,1)}, u32[]{:S(2)}, u32[]{:S(2)}) collective-permute-start(bf16[528,1280]{1,0:T(8,128)(2,1)} %pack_chunk.3), channel_id=1, source_target_pairs={{0,12},{1,13},{4,0},{6,2},{7,3},{8,4},{9,5},{10,6},{11,7},{12,8},{... | collective-permute-start | bytes 4055048 | tf_op jit(solution)/shard_map/ppermute | solution.py:501
  98.8 1.6 collective-permute-start.7
  100.4 0.6 dynamic_slice.8.second
  101.0 3.3 %choose_relayed.2 = (bf16[272,1792]{1,0:T(8,128)(2,1)}, bf16[256,1792]{1,0:T(8,128)(2,1)}) custom-call(s32[1]{0:T(128)} %dynamic_slice.8.second, bf16[528,1792]{1,0:T(8,128)(2,1)} %collective-permute-done.4.a.rest_0_, bf16[528,1792]{1,0:T(8,128)(2,1)} %collective-permute-done.6.b.rest_1_), custom_call_target="tpu_custom_call" | custom-call | tf_op jit(solution)/shard_map/choose_relayed/pallas_call | solution.py:124
  104.3 2.1 collective-permute-start.9
  106.4 3.6 %collective-permute-start.10 = (bf16[256,1792]{1,0:T(8,128)(2,1)}, bf16[256,1792]{1,0:T(8,128)(2,1)}, u32[]{:S(2)}, u32[]{:S(2)}) collective-permute-start(bf16[256,1792]{1,0:T(8,128)(2,1)} %get-tuple-element.33), channel_id=1, source_target_pairs={{0,3},{3,0},{4,7},{7,4},{8,11},{11,8},{12,15},{15,12},{16,19},{19,... | collective-permute-start | bytes 2752520 | tf_op jit(solution)/shard_map/ppermute | solution.py:536
  110.1 0.2 reduce_window_sum.11
  110.3 0.1 fusion.1
  110.5 1.1 copy-done.6
  111.6 2.7 %text_merge.5 = (f32[64,1664]{1,0:T(8,128)S(1)}, f32[64,1664]{1,0:T(8,128)}) custom-call(f32[128,1664]{1,0:T(8,128)S(1)} %copy-done.6, f32[128,1664]{1,0:T(8,128)} %collective-permute-done.7.refs_1_), custom_call_target="tpu_custom_call" | custom-call | tf_op jit(solution)/shard_map/text_merge/pallas_call | solution.py:418
  114.3 0.7 copy-done.8
  115.1 1.4 collective-permute-start.12
  116.5 0.1 copy.15
  117.4 0.7 dynamic-slice_bitcast_fusion
  118.2 11.8 %collective-permute-done.10.rest_3_ = bf16[256,1792]{1,0:T(8,128)(2,1)} collective-permute-done((bf16[256,1792]{1,0:T(8,128)(2,1)}, bf16[256,1792]{1,0:T(8,128)(2,1)}, u32[]{:S(2)}, u32[]{:S(2)}) %collective-permute-start.10) | collective-permute-done | bytes 917536 | tf_op jit(solution)/shard_map/ppermute | solution.py:536
  129.9 17.9 %video_attention.2.rest_8_ = bf16[256,3072]{1,0:T(8,128)(2,1)} custom-call(s32[13]{0:T(128)S(1)} %concatenate.21.table, bf16[256,3072]{1,0:T(8,128)(2,1)S(1)} %copy-done.4, bf16[256,3072]{1,0:T(8,128)(2,1)S(1)} %copy-done.1, bf16[256,3072]{1,0:T(8,128)(2,1)} %v_own.3, bf16[528,1792]{1,0:T(8,128)(2,1)} %collective-permute-done.4.a.rest_0_, ...), custom_call_target="tpu_custom_call" | custom-call | flops 132120576 | bytes 458752 | tf_op jit(solution)/shard_map/video_attention/pallas_call | solution.py:275
  147.9 7.5 %collective-permute-done.8.a.rest_0_ = bf16[528,1280]{1,0:T(8,128)(2,1)} collective-permute-done((bf16[528,1280]{1,0:T(8,128)(2,1)}, bf16[528,1280]{1,0:T(8,128)(2,1)}, u32[]{:S(2)}, u32[]{:S(2)}) %collective-permute-start.8) | collective-permute-done | bytes 1351712 | tf_op jit(solution)/shard_map/ppermute | solution.py:501
  155.4 2.7 %choose_relayed.3 = (bf16[272,1280]{1,0:T(8,128)(2,1)}, bf16[256,1280]{1,0:T(8,128)(2,1)S(1)}) custom-call(s32[1]{0:T(128)} %dynamic_slice.8.second, bf16[528,1280]{1,0:T(8,128)(2,1)} %collective-permute-done.8.a.rest_0_, bf16[528,1280]{1,0:T(8,128)(2,1)} %collective-permute-done.11.b.rest_1_), custom_call_target="tpu_custom_call" | custom-call | tf_op jit(solution)/shard_map/choose_relayed/pallas_call | solution.py:124
  158.1 1.7 text_finish.1
  159.9 15.2 %collective-permute-start.13 = (bf16[272,1280]{1,0:T(8,128)(2,1)}, bf16[272,1280]{1,0:T(8,128)(2,1)S(1)}, u32[]{:S(2)}, u32[]{:S(2)}) collective-permute-start(bf16[272,1280]{1,0:T(8,128)(2,1)} %get-tuple-element.39), channel_id=1, source_target_pairs={{0,3},{3,0},{4,7},{7,4},{8,11},{11,8},{12,15},{15,12},{16,19},{19,... | collective-permute-start | bytes 2088968 | tf_op jit(solution)/shard_map/ppermute | solution.py:536
  175.3 1.3 collective-permute-start.16
  176.6 1.9 collective-permute-start.14
  178.5 4.4 %collective-permute-done.16 = bf16[16,3072]{1,0:T(8,128)(2,1)S(1)} collective-permute-done((bf16[16,3072]{1,0:T(8,128)(2,1)S(1)}, bf16[16,3072]{1,0:T(8,128)(2,1)S(1)}, u32[]{:S(2)}, u32[]{:S(2)}) %collective-permute-start.16) | collective-permute-done | bytes 98336 | tf_op jit(solution)/shard_map/ppermute | solution.py:553
  182.9 0.7 fusion
  183.6 9.6 %collective-permute-done.14.rest_3_ = bf16[256,1280]{1,0:T(8,128)(2,1)S(1)} collective-permute-done((bf16[256,1280]{1,0:T(8,128)(2,1)}, bf16[256,1280]{1,0:T(8,128)(2,1)S(1)}, u32[]{:S(2)}, u32[]{:S(2)}) %collective-permute-start.14) | collective-permute-done | bytes 655392 | tf_op jit(solution)/shard_map/ppermute | solution.py:536
  193.2 13.3 %video_attention.3 = bf16[256,3072]{1,0:T(8,128)(2,1)} custom-call(s32[13]{0:T(128)S(1)} %concatenate.21.table, bf16[256,3072]{1,0:T(8,128)(2,1)S(1)} %copy-done.4, bf16[256,3072]{1,0:T(8,128)(2,1)} %k_own.3, bf16[256,3072]{1,0:T(8,128)(2,1)} %v_own.3, bf16[528,1280]{1,0:T(8,128)(2,1)} %collective-permute-done.8.a.rest_0_, ...), custom_call_target="tpu_custom_call", output_to_operand_aliasing={{}: (12, {})} | custom-call | flops 94371840 | bytes 327680 | tf_op jit(solution)/shard_map/video_attention/pallas_call | solution.py:275
  (53 shorter events, 0.9 us)
Async XLA Ops:
  0.6 11.9 %copy-start.16 = (s32[16]{0:T(128)S(1)}, s32[16]{0:T(128)}, u32[]{:S(2)}) copy-start(s32[16]{0:T(128)} %constant.79.clone) | copy-start | bytes 196
  0.6 12.1 %collective-permute-start.1 = (bf16[256,3072]{1,0:T(8,128)(2,1)}, bf16[256,3072]{1,0:T(8,128)(2,1)S(1)}, u32[]{:S(2)}, u32[]{:S(2)}) collective-permute-start(bf16[256,3072]{1,0:T(8,128)(2,1)} %k_own.3), channel_id=1, source_target_pairs={{0,1},{1,0},{2,3},{3,2},{4,5},{5,4},{6,7},{7,6},{8,9},{9,8},{10,11... | collective-permute-start | bytes 4718600 | tf_op jit(solution)/shard_map/ppermute | solution.py:505
  0.7 12.0 %collective-permute-start.2 = (bf16[256,3072]{1,0:T(8,128)(2,1)}, bf16[256,3072]{1,0:T(8,128)(2,1)}, u32[]{:S(2)}, u32[]{:S(2)}) collective-permute-start(bf16[256,3072]{1,0:T(8,128)(2,1)} %v_own.3), channel_id=1, source_target_pairs={{0,1},{1,0},{2,3},{3,2},{4,5},{5,4},{6,7},{7,6},{8,9},{9,8},{10,11... | collective-permute-start | bytes 4718600 | tf_op jit(solution)/shard_map/ppermute | solution.py:505
  1.2 11.4 %collective-permute-start = (s32[2]{0:T(128)}, s32[2]{0:T(128)S(1)}, u32[]{:S(2)}, u32[]{:S(2)}) collective-permute-start(s32[2]{0:T(128)} %counts.3), channel_id=1, source_target_pairs={{0,1},{1,0},{2,3},{3,2},{4,5},{5,4},{6,7},{7,6},{8,9},{9,8},{10,11... | collective-permute-start | bytes 32 | tf_op jit(solution)/shard_map/ppermute | solution.py:505
  1.3 1.4 copy-start
  2.7 1.4 copy-start.2
  4.1 0.7 copy-start.10
  4.8 7.9 %copy-start.11 = (s32[2]{0:T(128)S(1)}, s32[2]{0:T(128)}, u32[]{:S(2)}) copy-start(s32[2]{0:T(128)} %counts.3) | copy-start | bytes 28
  4.8 9.1 %copy-start.1 = (bf16[256,3072]{1,0:T(8,128)(2,1)S(1)}, bf16[256,3072]{1,0:T(8,128)(2,1)}, u32[]{:S(2)}) copy-start(bf16[256,3072]{1,0:T(8,128)(2,1)} %k_own.3) | copy-start | bytes 4718596
  6.6 86.4 %collective-permute-start.4 = (bf16[528,1792]{1,0:T(8,128)(2,1)}, bf16[528,1792]{1,0:T(8,128)(2,1)}, u32[]{:S(2)}, u32[]{:S(2)}) collective-permute-start(bf16[528,1792]{1,0:T(8,128)(2,1)} %pack_chunk.2), channel_id=1, source_target_pairs={{2,6},{3,7},{4,8},{5,9},{6,10},{7,11},{8,12},{9,13},{10,14},{11,15... | collective-permute-start | bytes 5677064 | tf_op jit(solution)/shard_map/ppermute | solution.py:501
  8.6 84.4 %collective-permute-start.6 = (bf16[528,1792]{1,0:T(8,128)(2,1)}, bf16[528,1792]{1,0:T(8,128)(2,1)}, u32[]{:S(2)}, u32[]{:S(2)}) collective-permute-start(bf16[528,1792]{1,0:T(8,128)(2,1)} %pack_chunk.2), channel_id=1, source_target_pairs={{0,12},{1,13},{4,0},{6,2},{7,3},{8,4},{9,5},{10,6},{11,7},{12,8},{... | collective-permute-start | bytes 5677064 | tf_op jit(solution)/shard_map/ppermute | solution.py:501
  12.7 16.7 %copy-start.3 = (bf16[256,3072]{1,0:T(8,128)(2,1)S(1)}, bf16[256,3072]{1,0:T(8,128)(2,1)}, u32[]{:S(2)}) copy-start(bf16[256,3072]{1,0:T(8,128)(2,1)} %v_own.3) | copy-start | bytes 4718596
  12.7 1.2 copy-start.13
  13.9 1.4 copy-start.7
  23.3 25.4 %collective-permute-start.3 = (f32[128,1792]{1,0:T(8,128)S(1)}, f32[128,1792]{1,0:T(8,128)S(1)}, u32[]{:S(2)}, u32[]{:S(2)}) collective-permute-start(f32[128,1792]{1,0:T(8,128)S(1)} %get-tuple-element.24.refs_0_), channel_id=1, source_target_pairs={{0,2},{1,3},{4,6},{5,7},{8,10},{9,11},{12,14},{13,15},{16,18},{17,... | collective-permute-start | bytes 2752520 | tf_op jit(solution)/shard_map/ppermute | solution.py:518
  28.0 39.2 %collective-permute-start.5 = (f32[128,1792]{1,0:T(8,128)S(1)}, f32[128,1792]{1,0:T(8,128)S(1)}, u32[]{:S(2)}, u32[]{:S(2)}) collective-permute-start(f32[128,1792]{1,0:T(8,128)S(1)} %get-tuple-element.27.refs_0_), channel_id=1, source_target_pairs={{0,2},{1,3},{4,6},{5,7},{8,10},{9,11},{12,14},{13,15},{16,18},{17,... | collective-permute-start | bytes 2752520 | tf_op jit(solution)/shard_map/ppermute | solution.py:518
  68.1 32.4 %copy-start.15 = (s32[16]{0:T(128)S(1)}, s32[16]{0:T(128)}, u32[]{:S(2)}) copy-start(s32[16]{0:T(128)} %constant.77.clone) | copy-start | bytes 196
  69.7 0.9 copy-start.5
  93.0 62.4 %collective-permute-start.8 = (bf16[528,1280]{1,0:T(8,128)(2,1)}, bf16[528,1280]{1,0:T(8,128)(2,1)}, u32[]{:S(2)}, u32[]{:S(2)}) collective-permute-start(bf16[528,1280]{1,0:T(8,128)(2,1)} %pack_chunk.3), channel_id=1, source_target_pairs={{2,6},{3,7},{4,8},{5,9},{6,10},{7,11},{8,12},{9,13},{10,14},{11,15... | collective-permute-start | bytes 4055048 | tf_op jit(solution)/shard_map/ppermute | solution.py:501
  94.9 60.5 %collective-permute-start.11 = (bf16[528,1280]{1,0:T(8,128)(2,1)}, bf16[528,1280]{1,0:T(8,128)(2,1)}, u32[]{:S(2)}, u32[]{:S(2)}) collective-permute-start(bf16[528,1280]{1,0:T(8,128)(2,1)} %pack_chunk.3), channel_id=1, source_target_pairs={{0,12},{1,13},{4,0},{6,2},{7,3},{8,4},{9,5},{10,6},{11,7},{12,8},{... | collective-permute-start | bytes 4055048 | tf_op jit(solution)/shard_map/ppermute | solution.py:501
  98.8 11.6 %collective-permute-start.7 = (f32[128,1664]{1,0:T(8,128)}, f32[128,1664]{1,0:T(8,128)}, u32[]{:S(2)}, u32[]{:S(2)}) collective-permute-start(f32[128,1664]{1,0:T(8,128)} %get-tuple-element.51), channel_id=1, source_target_pairs={{2,6},{3,7},{6,2},{7,3},{10,14},{11,15},{14,10},{15,11},{18,22},{1... | collective-permute-start | bytes 2555912 | tf_op jit(solution)/shard_map/ppermute | solution.py:525
  101.0 9.2 %copy-start.14 = (s32[2,6]{1,0:T(2,128)S(1)}, s32[2,6]{1,0:T(2,128)}, u32[]{:S(2)}) copy-start(s32[2,6]{1,0:T(2,128)} %param.18) | copy-start | bytes 148
  104.3 25.6 %copy-start.4 = (bf16[256,3072]{1,0:T(8,128)(2,1)S(1)}, bf16[256,3072]{1,0:T(8,128)(2,1)}, u32[]{:S(2)}) copy-start(bf16[256,3072]{1,0:T(8,128)(2,1)} %q.5) | copy-start | bytes 4718596
  104.3 25.6 %collective-permute-start.9 = (bf16[272,1792]{1,0:T(8,128)(2,1)}, bf16[272,1792]{1,0:T(8,128)(2,1)}, u32[]{:S(2)}, u32[]{:S(2)}) collective-permute-start(bf16[272,1792]{1,0:T(8,128)(2,1)} %get-tuple-element.32), channel_id=1, source_target_pairs={{0,3},{3,0},{4,7},{7,4},{8,11},{11,8},{12,15},{15,12},{16,19},{19,... | collective-permute-start | bytes 2924552 | tf_op jit(solution)/shard_map/ppermute | solution.py:536
  106.4 23.5 %collective-permute-start.10 = (bf16[256,1792]{1,0:T(8,128)(2,1)}, bf16[256,1792]{1,0:T(8,128)(2,1)}, u32[]{:S(2)}, u32[]{:S(2)}) collective-permute-start(bf16[256,1792]{1,0:T(8,128)(2,1)} %get-tuple-element.33), channel_id=1, source_target_pairs={{0,3},{3,0},{4,7},{7,4},{8,11},{11,8},{12,15},{15,12},{16,19},{19,... | collective-permute-start | bytes 2752520 | tf_op jit(solution)/shard_map/ppermute | solution.py:536
  110.5 1.2 copy-start.6
  114.3 0.7 copy-start.8
  115.1 43.0 %collective-permute-start.12 = (f32[64,1664]{1,0:T(8,128)}, f32[64,1664]{1,0:T(8,128)}, u32[]{:S(2)}, u32[]{:S(2)}) collective-permute-start(f32[64,1664]{1,0:T(8,128)} %get-tuple-element.42), channel_id=1, source_target_pairs={{2,10},{3,11},{6,14},{7,15},{10,2},{11,3},{14,6},{15,7},{18,26},{1... | collective-permute-start | bytes 1277960 | tf_op jit(solution)/shard_map/ppermute | solution.py:525
  147.8 10.3 %copy-start.9 = (f32[64,1664]{1,0:T(8,128)S(1)}, f32[64,1664]{1,0:T(8,128)}, u32[]{:S(2)}) copy-start(f32[64,1664]{1,0:T(8,128)} %copy-done.8) | copy-start | bytes 1277956
  158.1 1.7 copy-start.12
  159.8 15.3 %collective-permute-start.15 = (bf16[32,1536]{1,0:T(8,128)(2,1)S(1)}, bf16[32,1536]{1,0:T(8,128)(2,1)S(1)}, u32[]{:S(2)}, u32[]{:S(2)}) collective-permute-start(bf16[32,1536]{1,0:T(8,128)(2,1)S(1)} %get-tuple-element.45), channel_id=1, source_target_pairs={{0,1},{1,0},{2,3},{3,2},{4,5},{5,4},{6,7},{7,6},{8,9},{9,8},{10,11... | collective-permute-start | bytes 294920 | tf_op jit(solution)/shard_map/ppermute | solution.py:549
  159.9 33.3 %collective-permute-start.13 = (bf16[272,1280]{1,0:T(8,128)(2,1)}, bf16[272,1280]{1,0:T(8,128)(2,1)S(1)}, u32[]{:S(2)}, u32[]{:S(2)}) collective-permute-start(bf16[272,1280]{1,0:T(8,128)(2,1)} %get-tuple-element.39), channel_id=1, source_target_pairs={{0,3},{3,0},{4,7},{7,4},{8,11},{11,8},{12,15},{15,12},{16,19},{19,... | collective-permute-start | bytes 2088968 | tf_op jit(solution)/shard_map/ppermute | solution.py:536
  175.3 7.6 %collective-permute-start.16 = (bf16[16,3072]{1,0:T(8,128)(2,1)S(1)}, bf16[16,3072]{1,0:T(8,128)(2,1)S(1)}, u32[]{:S(2)}, u32[]{:S(2)}) collective-permute-start(bf16[16,3072]{1,0:T(8,128)(2,1)S(1)} %slice.8), channel_id=1, source_target_pairs={{2,0},{3,1},{6,4},{7,5},{10,8},{11,9},{14,12},{15,13},{18,16},{19,... | collective-permute-start | bytes 294920 | tf_op jit(solution)/shard_map/ppermute | solution.py:553
  176.6 16.6 %collective-permute-start.14 = (bf16[256,1280]{1,0:T(8,128)(2,1)}, bf16[256,1280]{1,0:T(8,128)(2,1)S(1)}, u32[]{:S(2)}, u32[]{:S(2)}) collective-permute-start(bf16[256,1280]{1,0:T(8,128)(2,1)} %copy-done.12), channel_id=1, source_target_pairs={{0,3},{3,0},{4,7},{7,4},{8,11},{11,8},{12,15},{15,12},{16,19},{19,... | collective-permute-start | bytes 1966088 | tf_op jit(solution)/shard_map/ppermute | solution.py:536
